TPU v7x, 32 devices: a whole 2x2x4 slice. The times are simulated.
32 devices in a mesh: groups: 2 (over x), dom: 16 (over z, y, core).
Axes of the slice: x: 2, y: 2, z: 4, core: 2. Of those that a mesh axis runs over, the one named last changes fastest.
Arguments:
- start_block: bfloat16 [32, 262144], P(None, ('groups', 'dom')), parts along dimension 1
- tiles: bfloat16 [10240, 128, 128], P(('groups', 'dom')), parts along dimension 0
- tile_src: int32 [10240], P(('groups', 'dom')), parts along dimension 0, may hold values from 0 to 111, as said below
- tile_dst: int32 [10240], P(('groups', 'dom')), parts along dimension 0, may hold values from 0 to 63
- slot_count: int32 [32], P(('groups', 'dom')), parts along dimension 0, may hold values from 112 to 320, as said below
- send_rows: int32 [32, 4, 1536], P(('groups', 'dom')), parts along dimension 0, may hold values from 0 to 8191
Outputs:
- subspace: float32 [32, 262144], P(None, ('groups', 'dom')), parts along dimension 1
There are 2 independent parts, one for each index of `groups`. A program takes and returns all parts, laid end to end along the dimension named above; each array names one. Nothing has to cross between parts.
Inputs may be any that keep to these rules, and one draw needn't show every extreme that they name: `tile_src`: slot t < 64 of every partition has source tile t and target tile t; slot 64 + g for g < 48 has source tile 64 + g, the g-th tile of received boundary rows; the other slots may name any local or received tile. Slots at local positions from slot_count on are ignored. Some partition uses all 320 slots. `send_rows`: indices may repeat.
All inputs are finite; a program needn't handle non-finite values.
Results may differ from a plain program's by a relative error of at most 0.0025.
Values may be sent and summed in bfloat16 or wider, within the bound.
No kernel may reach another device: no remote copies, remote signals or barrier semaphores. Data moves between devices by JAX's collectives and lax.ppermute only.
A program may use at most 64 MiB of HBM per device.

v0:
```python
import jax
import jax.numpy as jnp
from jax import lax
from jax.sharding import PartitionSpec as P

ITERS = 3


def swapped(x, axis, bit):
    return lax.ppermute(x, axis, [(i, i ^ 1 << bit) for i in range(lax.axis_size(axis))])


def on_device(start_block, tiles, tile_src, tile_dst, slot_count, send_rows):
    top_bit = lax.axis_size("dom").bit_length() - 2
    colour_bits = (0, 1, 2, top_bit)
    columns = start_block.shape[0]
    states_dev = start_block.shape[1]
    tile_size = tiles.shape[1]
    local_tiles = states_dev // tile_size
    total_states = states_dev * lax.axis_size("dom")
    live_count = slot_count[0]
    send_lists = send_rows[0]
    current = start_block
    received = []
    for colour in range(len(colour_bits)):
        chosen = jnp.take(current, send_lists[colour], axis=1)
        received.append(swapped(chosen, "dom", colour_bits[colour]))
    ghosts = jnp.concatenate(received, axis=1)
    subspace = None
    for sweep_index in range(ITERS):
        final_turn = sweep_index == ITERS - 1
        slot_pieces = (
            jnp.concatenate([current, ghosts], axis=1)
            .reshape(columns, -1, tile_size)
            .transpose(1, 0, 2)
        )
        slot_chosen = slot_pieces[tile_src]
        partials = jnp.einsum(
            "ski,sij->skj", slot_chosen, tiles, preferred_element_type=jnp.float32
        )
        slot_ids = jnp.arange(tile_src.shape[0], dtype=jnp.int32)
        live_mask = slot_ids < live_count
        onehot = (
            (tile_dst[:, None] == jnp.arange(local_tiles, dtype=jnp.int32)[None, :])
            & live_mask[:, None]
        ).astype(jnp.float32)
        summed = jnp.einsum("st,skj->ktj", onehot, partials, precision=lax.Precision.HIGHEST)
        product = summed.reshape(columns, states_dev)
        partial_gram = jnp.dot(product, product.T, precision=lax.Precision.HIGHEST) / total_states
        gram_sum = lax.psum(partial_gram, "dom")
        lower_factor = jnp.linalg.cholesky(gram_sum)
        inverse = lax.linalg.triangular_solve(
            lower_factor, jnp.eye(columns, dtype=jnp.float32), left_side=True, lower=True
        )
        subspace = jnp.dot(inverse, product, precision=lax.Precision.HIGHEST)
        if not final_turn:
            current = subspace.astype(jnp.bfloat16)
            later_received = []
            for later_colour in range(len(colour_bits)):
                later_chosen = jnp.take(current, send_lists[later_colour], axis=1)
                later_received.append(swapped(later_chosen, "dom", colour_bits[later_colour]))
            ghosts = jnp.concatenate(later_received, axis=1)
    return subspace


def solution(mesh):
    return jax.shard_map(
        on_device,
        mesh=mesh,
        in_specs=(
            P(None, ("groups", "dom")),
            P(("groups", "dom"), None, None),
            P(("groups", "dom")),
            P(("groups", "dom")),
            P(("groups", "dom")),
            P(("groups", "dom"), None, None),
        ),
        out_specs=P(None, ("groups", "dom")),
        check_vma=False,
    )
```

profile of v0, /device:TPU:0, one launch (start us, length us, event | category | flops | bytes accessed | tf_op | source)
XLA Modules:
  0.0 350.3 jit_solution(7511705788882570430)
XLA Ops:
  0.0 1.0 slice_reduce_fusion
  1.0 1.9 copy.81
  3.0 3.2 gather_fusion.4
  6.5 3.0 collective-permute-start.1
  9.5 3.2 gather_fusion.3
  12.7 1.0 select_bitcast_fusion.3
  13.8 3.2 gather_fusion.5
  17.1 1.0 select_bitcast_fusion.1
  18.1 1.6 collective-permute-start.2
  19.7 3.2 gather_fusion.6
  23.2 2.7 collective-permute-start.3
  27.7 1.1 copy.85
  28.9 1.1 copy.86
  30.0 4.8 %collective-permute-done.2 = bf16[32,1536]{0,1:T(8,128)(2,1)} collective-permute-done((bf16[32,1536]{0,1:T(8,128)(2,1)}, bf16[32,1536]{0,1:T(8,128)(2,1)}, u32[]{:S(2)}, u32[]{:S(2)}) %collective-permute-start.2) | collective-permute-done | bytes 98336 | tf_op jit(solution)/shard_map/ppermute | solution.py:10
  34.9 1.1 copy.87
  36.0 7.8 %collective-permute-done.3 = bf16[32,1536]{0,1:T(8,128)(2,1)S(1)} collective-permute-done((bf16[32,1536]{0,1:T(8,128)(2,1)S(1)}, bf16[32,1536]{0,1:T(8,128)(2,1)S(1)}, u32[]{:S(2)}, u32[]{:S(2)}) %collective-permute-start.3) | collective-permute-done | bytes 98336 | tf_op jit(solution)/shard_map/ppermute | solution.py:10
  44.2 2.5 gather_fusion
  46.7 5.7 %fusion.49 = f32[320,32,128]{2,1,0:T(8,128)S(1)} fusion(bf16[320,32,128]{2,1,0:T(8,128)(2,1)S(1)} %gather_fusion, bf16[320,128,128]{2,1,0:T(8,128)(2,1)} %param.12), kind=kOutput, calls=%fused_computation.128 | convolution fusion | flops 335544320 | bytes 18350080 | tf_op jit(solution)/shard_map/ski,sij->skj/dot_general | solution.py:38
  52.4 5.3 %fusion.4 = f32[32,128,64]{1,2,0:T(8,128)S(1)} fusion(f32[320,32,128]{2,1,0:T(8,128)S(1)} %fusion.49, s32[320]{0:T(512)S(1)} %copy-done.20, pred[320]{0:T(512)(128)(4,1)S(1)} %copy-done.23), kind=kOutput, calls=%fused_computation.21 | convolution fusion | flops 1006673920 | bytes 6293056 | tf_op jit(solution)/shard_map/st,skj->ktj/dot_general | solution.py:47
  57.7 1.5 fusion.8
  59.2 59.2 %psum.21 = f32[32,32]{0,1:T(8,128)S(1)} all-reduce(f32[32,32]{0,1:T(8,128)S(1)} %fusion.8), channel_id=1, replica_groups=mesh['groups'=2,'dom'=16] {'dom'}, use_global_device_ids=true, to_apply=%region_0.0 | all-reduce | flops 1024 | bytes 8192 | tf_op jit(solution)/shard_map/psum | solution.py:50
  118.5 2.9 cholesky.59
  122.1 0.7 fusion.36
  122.7 2.4 custom-call.7
  125.4 2.4 constant_dynamic-update-slice_fusion.9
  127.8 1.0 copy.95
  128.9 4.0 %gather_fusion.10 = bf16[1536,32]{1,0:T(8,128)(2,1)} fusion(bf16[32,8192]{0,1:T(8,128)(2,1)S(1)} %copy.95, s32[2048]{0:T(1024)S(1)} %copy-done.5), kind=kCustom, calls=%fused_computation.7.clone | custom fusion | bytes 202752 | tf_op jit(solution)/shard_map/jit(_take)/gather | solution.py:60
  132.9 3.2 gather_fusion.9
  136.1 3.2 gather_fusion.8
  139.3 3.2 gather_fusion.7
  142.6 1.1 copy.102
  145.0 0.8 collective-permute-done.4
  146.4 3.3 collective-permute-done.5
  150.4 0.6 constant_dynamic-update-slice_fusion.6
  151.1 0.6 constant_dynamic-update-slice_fusion.5
  151.7 1.3 bitcast_bitcast_fusion.1
  153.1 2.5 gather_fusion.1
  155.6 5.8 %fusion.50 = f32[320,32,128]{2,1,0:T(8,128)S(1)} fusion(bf16[320,32,128]{2,1,0:T(8,128)(2,1)S(1)} %gather_fusion.1, bf16[320,128,128]{2,1,0:T(8,128)(2,1)} %param.12), kind=kOutput, calls=%fused_computation.129 | convolution fusion | flops 335544320 | bytes 18350080 | tf_op jit(solution)/shard_map/ski,sij->skj/dot_general | solution.py:38
  161.4 5.3 %fusion.2 = f32[32,128,64]{1,2,0:T(8,128)S(1)} fusion(f32[320,32,128]{2,1,0:T(8,128)S(1)} %fusion.50, s32[320]{0:T(512)S(1)} %copy-done.21, pred[320]{0:T(512)(128)(4,1)S(1)} %copy-done.24), kind=kOutput, calls=%fused_computation.19 | convolution fusion | flops 1006673920 | bytes 6293056 | tf_op jit(solution)/shard_map/st,skj->ktj/dot_general | solution.py:47
  166.7 1.5 fusion.7
  168.2 61.6 %psum.22 = f32[32,32]{0,1:T(8,128)S(1)} all-reduce(f32[32,32]{0,1:T(8,128)S(1)} %fusion.7), channel_id=1, replica_groups=mesh['groups'=2,'dom'=16] {'dom'}, use_global_device_ids=true, to_apply=%region_3.0 | all-reduce | flops 1024 | bytes 8192 | tf_op jit(solution)/shard_map/psum | solution.py:50
  229.9 2.9 cholesky.70
  233.5 0.7 fusion.37
  234.2 2.4 custom-call.8
  236.9 2.4 constant_dynamic-update-slice_fusion.14
  239.2 1.0 copy.109
  240.3 4.0 %gather_fusion.14 = bf16[1536,32]{1,0:T(8,128)(2,1)} fusion(bf16[32,8192]{0,1:T(8,128)(2,1)S(1)} %copy.109, s32[2048]{0:T(1024)S(1)} %copy-done.6), kind=kCustom, calls=%fused_computation.11.clone | custom fusion | bytes 202752 | tf_op jit(solution)/shard_map/jit(_take)/gather | solution.py:60
  244.3 3.2 gather_fusion.13
  247.6 3.2 gather_fusion.12
  250.8 3.2 gather_fusion.11
  254.0 1.1 copy.116
  256.4 0.8 collective-permute-done.8
  257.9 3.3 collective-permute-done.9
  261.9 0.6 constant_dynamic-update-slice_fusion.11
  263.2 1.3 bitcast_bitcast_fusion
  264.5 2.3 gather_fusion.2
  266.9 5.7 %fusion.51 = f32[320,32,128]{2,1,0:T(8,128)S(1)} fusion(bf16[320,32,128]{2,1,0:T(8,128)(2,1)S(1)} %gather_fusion.2, bf16[320,128,128]{2,1,0:T(8,128)(2,1)} %param.12), kind=kOutput, calls=%fused_computation.130 | convolution fusion | flops 335544320 | bytes 18350080 | tf_op jit(solution)/shard_map/ski,sij->skj/dot_general | solution.py:38
  272.6 5.3 %fusion = f32[32,128,64]{1,2,0:T(8,128)S(1)} fusion(f32[320,32,128]{2,1,0:T(8,128)S(1)} %fusion.51, s32[320]{0:T(512)S(1)} %copy-done.22, pred[320]{0:T(512)(128)(4,1)S(1)} %copy-done.25), kind=kOutput, calls=%fused_computation.17 | convolution fusion | flops 1006673920 | bytes 6293056 | tf_op jit(solution)/shard_map/st,skj->ktj/dot_general | solution.py:47
  277.9 1.5 fusion.6
  279.4 61.1 %psum.23 = f32[32,32]{0,1:T(8,128)S(1)} all-reduce(f32[32,32]{0,1:T(8,128)S(1)} %fusion.6), channel_id=1, replica_groups=mesh['groups'=2,'dom'=16] {'dom'}, use_global_device_ids=true, to_apply=%region_4.8 | all-reduce | flops 1024 | bytes 8192 | tf_op jit(solution)/shard_map/psum | solution.py:50
  340.6 2.9 cholesky.81
  344.2 0.7 fusion.38
  344.9 2.4 custom-call.9
  347.5 2.5 fusion.9
  (125 shorter events, 10.8 us)
Async XLA Ops:
  1.0 11.8 %copy-start.7 = (pred[1536]{0:T(1024)(128)(4,1)}, pred[1536]{0:T(1024)(128)(4,1)S(1)}, u32[]{:S(2)}) copy-start(pred[1536]{0:T(1024)(128)(4,1)S(1)} %compare_and_fusion.2) | copy-start | bytes 4612
  6.4 19.4 %copy-start = (bf16[32,8192]{1,0:T(8,128)(2,1)S(1)}, bf16[32,8192]{1,0:T(8,128)(2,1)}, u32[]{:S(2)}) copy-start(bf16[32,8192]{1,0:T(8,128)(2,1)} %param.11) | copy-start | bytes 1572868
  6.5 22.4 %collective-permute-start.1 = (bf16[32,1536]{0,1:T(8,128)(2,1)S(1)}, bf16[32,1536]{0,1:T(8,128)(2,1)}, u32[]{:S(2)}, u32[]{:S(2)}) collective-permute-start(bf16[32,1536]{0,1:T(8,128)(2,1)S(1)} %select_bitcast_fusion.2), channel_id=1, source_target_pairs={{0,2},{1,3},{2,0},{3,1},{4,6},{5,7},{6,4},{7,5},{8,10},{9,11},{10,... | collective-permute-start | bytes 294920 | tf_op jit(solution)/shard_map/ppermute | solution.py:10
  9.5 16.4 %copy-start.10 = (pred[1536]{0:T(1024)(128)(4,1)}, pred[1536]{0:T(1024)(128)(4,1)S(1)}, u32[]{:S(2)}) copy-start(pred[1536]{0:T(1024)(128)(4,1)S(1)} %compare_and_fusion.3) | copy-start | bytes 4612
  12.7 13.8 %copy-start.26 = (s32[320]{0:T(512)S(1)}, s32[320]{0:T(512)}, u32[]{:S(2)}) copy-start(s32[320]{0:T(512)} %param.13) | copy-start | bytes 3844
  13.8 13.9 %collective-permute-start = (bf16[32,1536]{0,1:T(8,128)(2,1)}, bf16[32,1536]{0,1:T(8,128)(2,1)}, u32[]{:S(2)}, u32[]{:S(2)}) collective-permute-start(bf16[32,1536]{0,1:T(8,128)(2,1)} %select_bitcast_fusion.3), channel_id=1, source_target_pairs={{0,1},{1,0},{2,3},{3,2},{4,5},{5,4},{6,7},{7,6},{8,9},{9,8},{10,11... | collective-permute-start | bytes 294920 | tf_op jit(solution)/shard_map/ppermute | solution.py:10
  13.8 16.2 %copy-start.13 = (pred[1536]{0:T(1024)(128)(4,1)}, pred[1536]{0:T(1024)(128)(4,1)S(1)}, u32[]{:S(2)}) copy-start(pred[1536]{0:T(1024)(128)(4,1)S(1)} %compare_and_fusion.1) | copy-start | bytes 4612
  13.8 16.2 %copy-start.1 = (s32[2048]{0:T(1024)}, s32[2048]{0:T(1024)S(1)}, u32[]{:S(2)}) copy-start(s32[2048]{0:T(1024)S(1)} %get-tuple-element.17) | copy-start | bytes 24580
  13.8 16.2 %copy-start.4 = (s32[2048]{0:T(1024)}, s32[2048]{0:T(1024)S(1)}, u32[]{:S(2)}) copy-start(s32[2048]{0:T(1024)S(1)} %get-tuple-element.16) | copy-start | bytes 24580
  18.1 16.8 %collective-permute-start.2 = (bf16[32,1536]{0,1:T(8,128)(2,1)}, bf16[32,1536]{0,1:T(8,128)(2,1)}, u32[]{:S(2)}, u32[]{:S(2)}) collective-permute-start(bf16[32,1536]{0,1:T(8,128)(2,1)} %select_bitcast_fusion.1), channel_id=1, source_target_pairs={{0,4},{1,5},{2,6},{3,7},{4,0},{5,1},{6,2},{7,3},{8,12},{9,13},{10,... | collective-permute-start | bytes 294920 | tf_op jit(solution)/shard_map/ppermute | solution.py:10
  19.7 24.3 %copy-start.16 = (pred[1536]{0:T(1024)(128)(4,1)}, pred[1536]{0:T(1024)(128)(4,1)S(1)}, u32[]{:S(2)}) copy-start(pred[1536]{0:T(1024)(128)(4,1)S(1)} %compare_and_fusion) | copy-start | bytes 4612
  23.2 20.7 %collective-permute-start.3 = (bf16[32,1536]{0,1:T(8,128)(2,1)S(1)}, bf16[32,1536]{0,1:T(8,128)(2,1)S(1)}, u32[]{:S(2)}, u32[]{:S(2)}) collective-permute-start(bf16[32,1536]{0,1:T(8,128)(2,1)S(1)} %select_bitcast_fusion), channel_id=1, source_target_pairs={{0,8},{1,9},{2,10},{3,11},{4,12},{5,13},{6,14},{7,15},{8,0},{9,1},... | collective-permute-start | bytes 294920 | tf_op jit(solution)/shard_map/ppermute | solution.py:10
  46.6 5.7 %copy-start.20 = (s32[320]{0:T(512)S(1)}, s32[320]{0:T(512)}, u32[]{:S(2)}) copy-start(s32[320]{0:T(512)} %param.14) | copy-start | bytes 3844
  46.7 5.7 %copy-start.23 = (pred[320]{0:T(512)(128)(4,1)S(1)}, pred[320]{0:T(512)(128)(4,1)}, u32[]{:S(2)}) copy-start(pred[320]{0:T(512)(128)(4,1)} %iota_compare_fusion.6) | copy-start | bytes 964
  59.2 69.6 %copy-start.5 = (s32[2048]{0:T(1024)S(1)}, s32[2048]{0:T(1024)}, u32[]{:S(2)}) copy-start(s32[2048]{0:T(1024)} %copy-done.4) | copy-start | bytes 24580
  125.4 7.5 %copy-start.2 = (s32[2048]{0:T(1024)S(1)}, s32[2048]{0:T(1024)}, u32[]{:S(2)}) copy-start(s32[2048]{0:T(1024)} %copy-done.1) | copy-start | bytes 24580
  128.8 14.9 %copy-start.17 = (pred[1536]{0:T(1024)(128)(4,1)S(1)}, pred[1536]{0:T(1024)(128)(4,1)}, u32[]{:S(2)}) copy-start(pred[1536]{0:T(1024)(128)(4,1)} %copy-done.16) | copy-start | bytes 4612
  128.9 15.1 %copy-start.14 = (pred[1536]{0:T(1024)(128)(4,1)S(1)}, pred[1536]{0:T(1024)(128)(4,1)}, u32[]{:S(2)}) copy-start(pred[1536]{0:T(1024)(128)(4,1)} %copy-done.13) | copy-start | bytes 4612
  132.9 11.5 %copy-start.11 = (pred[1536]{0:T(1024)(128)(4,1)S(1)}, pred[1536]{0:T(1024)(128)(4,1)}, u32[]{:S(2)}) copy-start(pred[1536]{0:T(1024)(128)(4,1)} %copy-done.10) | copy-start | bytes 4612
  132.9 11.6 %copy-start.8 = (pred[1536]{0:T(1024)(128)(4,1)S(1)}, pred[1536]{0:T(1024)(128)(4,1)}, u32[]{:S(2)}) copy-start(pred[1536]{0:T(1024)(128)(4,1)} %copy-done.7) | copy-start | bytes 4612
  143.7 7.3 %collective-permute-start.7 = (bf16[32,1536]{1,0:T(8,128)(2,1)S(1)}, bf16[32,1536]{1,0:T(8,128)(2,1)S(1)}, u32[]{:S(2)}, u32[]{:S(2)}) collective-permute-start(bf16[32,1536]{1,0:T(8,128)(2,1)S(1)} %select_bitcast_fusion.8), channel_id=1, source_target_pairs={{0,8},{1,9},{2,10},{3,11},{4,12},{5,13},{6,14},{7,15},{8,0},{9,1},... | collective-permute-start | bytes 294920 | tf_op jit(solution)/shard_map/ppermute | solution.py:10
  144.0 6.4 %collective-permute-start.6 = (bf16[32,1536]{1,0:T(8,128)(2,1)S(1)}, bf16[32,1536]{1,0:T(8,128)(2,1)S(1)}, u32[]{:S(2)}, u32[]{:S(2)}) collective-permute-start(bf16[32,1536]{1,0:T(8,128)(2,1)S(1)} %select_bitcast_fusion.9), channel_id=1, source_target_pairs={{0,4},{1,5},{2,6},{3,7},{4,0},{5,1},{6,2},{7,3},{8,12},{9,13},{10,... | collective-permute-start | bytes 294920 | tf_op jit(solution)/shard_map/ppermute | solution.py:10
  144.4 1.4 collective-permute-start.4
  144.5 5.2 %collective-permute-start.5 = (bf16[32,1536]{1,0:T(8,128)(2,1)S(1)}, bf16[32,1536]{1,0:T(8,128)(2,1)S(1)}, u32[]{:S(2)}, u32[]{:S(2)}) collective-permute-start(bf16[32,1536]{1,0:T(8,128)(2,1)S(1)} %select_bitcast_fusion.10), channel_id=1, source_target_pairs={{0,2},{1,3},{2,0},{3,1},{4,6},{5,7},{6,4},{7,5},{8,10},{9,11},{10,... | collective-permute-start | bytes 294920 | tf_op jit(solution)/shard_map/ppermute | solution.py:10
  155.5 5.8 %copy-start.21 = (s32[320]{0:T(512)S(1)}, s32[320]{0:T(512)}, u32[]{:S(2)}) copy-start(s32[320]{0:T(512)} %param.14) | copy-start | bytes 3844
  155.6 5.8 %copy-start.24 = (pred[320]{0:T(512)(128)(4,1)S(1)}, pred[320]{0:T(512)(128)(4,1)}, u32[]{:S(2)}) copy-start(pred[320]{0:T(512)(128)(4,1)} %iota_compare_fusion.6) | copy-start | bytes 964
  168.2 72.1 %copy-start.6 = (s32[2048]{0:T(1024)S(1)}, s32[2048]{0:T(1024)}, u32[]{:S(2)}) copy-start(s32[2048]{0:T(1024)} %copy-done.4) | copy-start | bytes 24580
  236.8 7.5 %copy-start.3 = (s32[2048]{0:T(1024)S(1)}, s32[2048]{0:T(1024)}, u32[]{:S(2)}) copy-start(s32[2048]{0:T(1024)} %copy-done.1) | copy-start | bytes 24580
  240.3 14.9 %copy-start.18 = (pred[1536]{0:T(1024)(128)(4,1)S(1)}, pred[1536]{0:T(1024)(128)(4,1)}, u32[]{:S(2)}) copy-start(pred[1536]{0:T(1024)(128)(4,1)} %copy-done.16) | copy-start | bytes 4612
  240.3 15.1 %copy-start.15 = (pred[1536]{0:T(1024)(128)(4,1)S(1)}, pred[1536]{0:T(1024)(128)(4,1)}, u32[]{:S(2)}) copy-start(pred[1536]{0:T(1024)(128)(4,1)} %copy-done.13) | copy-start | bytes 4612
  244.3 11.5 %copy-start.12 = (pred[1536]{0:T(1024)(128)(4,1)S(1)}, pred[1536]{0:T(1024)(128)(4,1)}, u32[]{:S(2)}) copy-start(pred[1536]{0:T(1024)(128)(4,1)} %copy-done.10) | copy-start | bytes 4612
  244.3 11.6 %copy-start.9 = (pred[1536]{0:T(1024)(128)(4,1)S(1)}, pred[1536]{0:T(1024)(128)(4,1)}, u32[]{:S(2)}) copy-start(pred[1536]{0:T(1024)(128)(4,1)} %copy-done.7) | copy-start | bytes 4612
  254.0 10.5 %copy-start.19 = (s32[1024]{0:T(1024)S(1)}, s32[1024]{0:T(1024)}, u32[]{:S(2)}) copy-start(s32[1024]{0:T(1024)} %pad_clamp_fusion.4) | copy-start | bytes 12292
  255.2 7.3 %collective-permute-start.11 = (bf16[32,1536]{1,0:T(8,128)(2,1)S(1)}, bf16[32,1536]{1,0:T(8,128)(2,1)S(1)}, u32[]{:S(2)}, u32[]{:S(2)}) collective-permute-start(bf16[32,1536]{1,0:T(8,128)(2,1)S(1)} %select_bitcast_fusion.4), channel_id=1, source_target_pairs={{0,8},{1,9},{2,10},{3,11},{4,12},{5,13},{6,14},{7,15},{8,0},{9,1},... | collective-permute-start | bytes 294920 | tf_op jit(solution)/shard_map/ppermute | solution.py:10
  255.4 6.4 %collective-permute-start.10 = (bf16[32,1536]{1,0:T(8,128)(2,1)S(1)}, bf16[32,1536]{1,0:T(8,128)(2,1)S(1)}, u32[]{:S(2)}, u32[]{:S(2)}) collective-permute-start(bf16[32,1536]{1,0:T(8,128)(2,1)S(1)} %select_bitcast_fusion.5), channel_id=1, source_target_pairs={{0,4},{1,5},{2,6},{3,7},{4,0},{5,1},{6,2},{7,3},{8,12},{9,13},{10,... | collective-permute-start | bytes 294920 | tf_op jit(solution)/shard_map/ppermute | solution.py:10
  255.9 1.4 collective-permute-start.8
  256.0 5.2 %collective-permute-start.9 = (bf16[32,1536]{1,0:T(8,128)(2,1)S(1)}, bf16[32,1536]{1,0:T(8,128)(2,1)S(1)}, u32[]{:S(2)}, u32[]{:S(2)}) collective-permute-start(bf16[32,1536]{1,0:T(8,128)(2,1)S(1)} %select_bitcast_fusion.6), channel_id=1, source_target_pairs={{0,2},{1,3},{2,0},{3,1},{4,6},{5,7},{6,4},{7,5},{8,10},{9,11},{10,... | collective-permute-start | bytes 294920 | tf_op jit(solution)/shard_map/ppermute | solution.py:10
  266.9 5.7 %copy-start.22 = (s32[320]{0:T(512)S(1)}, s32[320]{0:T(512)}, u32[]{:S(2)}) copy-start(s32[320]{0:T(512)} %param.14) | copy-start | bytes 3844
  266.9 5.7 %copy-start.25 = (pred[320]{0:T(512)(128)(4,1)S(1)}, pred[320]{0:T(512)(128)(4,1)}, u32[]{:S(2)}) copy-start(pred[320]{0:T(512)(128)(4,1)} %iota_compare_fusion.6) | copy-start | bytes 964
where the time goes:
time: 356 us; the launch traced here: 350 us
  blocking collectives  182 us (51%)
  local copies, waits for them, and re-layouts  67.5 us (19%)
  matrix products  45.5 us (13%)
  other arithmetic  24 us (7%)
  waiting for transfers between devices  21 us (6%)
  starting transfers between devices  8.57 us (2%)
    psum x3, blocking collectives, on_device(): gram_sum = lax.psum(partial_gram, 'dom')  182 us
    gather x16, local copies, waits for them, and re-layouts, on_device(): later_chosen = jnp.take(current, send_lists[later_colour], axis=1)  30.5 us
    ppermute x12, waiting for transfers between devices, swapped(): lax.ppermute(x, axis, [(i, i ^ 1 << bit) for i in range(lax.axis_size(axi...  21 us
    dot_general x3, matrix products, on_device(): jnp.einsum('ski,sij->skj', slot_chosen, tiles, preferred_element_type=jnp...  17.2 us
    dot_general x3, matrix products, on_device(): jnp.einsum('st,skj->ktj', onehot, partials, precision=lax.Precision.HIGHEST)  15.8 us
    gather x4, local copies, waits for them, and re-layouts, on_device(): chosen = jnp.take(current, send_lists[colour], axis=1)  12.8 us
    another operation x9, other arithmetic, on_device(): lower_factor = jnp.linalg.cholesky(gram_sum)  10.8 us
    another operation x6, other arithmetic, on_device(): lax.linalg.triangular_solve(lower_factor, jnp.eye(columns, dtype=jnp.floa...  9.26 us
  transfers between devices with their start and end apart: 12, of which 6 were waited for; matrix products, arithmetic and copies ran while one was open for 6% of the time, Pallas kernels for 0%

commit v1 on v0

v1 whole, which is shorter than its diff:
```python
import functools

import jax
import jax.numpy as jnp
from jax import lax
from jax.experimental import pallas as pl
from jax.experimental.pallas import tpu as pltpu
from jax.sharding import PartitionSpec as P

ITERS = 3
LANES = 128
PACK = 4
CHUNK = 1024
F32 = jnp.float32
BF16 = jnp.bfloat16
VMEM = pl.BlockSpec(memory_space=pltpu.VMEM)
SMEM = pl.BlockSpec(memory_space=pltpu.SMEM)
PARAMS = pltpu.CompilerParams(vmem_limit_bytes=32 << 20)


def in_vmem(x):
    return pltpu.with_memory_space_constraint(x, pltpu.VMEM)


def vmem_out(shape, dtype):
    return pltpu.VMEM(shape, dtype)


def swapped(x, mask):
    size = lax.axis_size("dom")
    return lax.ppermute(x, "dom", [(i, i ^ mask) for i in range(size)])


def split3(x):
    high = x.astype(BF16)
    rest = x - high.astype(F32)
    mid = rest.astype(BF16)
    low = (rest - mid.astype(F32)).astype(BF16)
    return high, mid, low


def stack3(x):
    return jnp.concatenate(split3(x), axis=0)


def inverse_factor(gram):
    n = gram.shape[0]
    row = lax.broadcasted_iota(jnp.int32, (n, n), 0)
    col = lax.broadcasted_iota(jnp.int32, (n, n), 1)
    eye = (row == col).astype(F32)
    both = jnp.concatenate([gram, eye, jnp.zeros((n, LANES - 2 * n), F32)], axis=1)
    rows = lax.broadcasted_iota(jnp.int32, (n, LANES), 0)
    scale = jnp.zeros((n, LANES), F32)
    for j in range(n):
        pivot = both[j : j + 1, j : j + 1]
        factor = jnp.broadcast_to(both[:, j : j + 1] / pivot, (n, LANES))
        scale = jnp.where(rows == j, jnp.broadcast_to(1.0 / jnp.sqrt(pivot), (n, LANES)), scale)
        both = both - jnp.where(rows > j, factor, 0.0) * both[j : j + 1, :]
    return (both * scale)[:, n : 2 * n]


def apply_matrix(inverse):
    high, mid, low = (t.astype(F32) for t in split3(inverse))
    zero = jnp.zeros_like(high)
    full = jnp.concatenate(
        [
            jnp.concatenate([high, high, high], axis=1),
            jnp.concatenate([mid, mid, zero], axis=1),
            jnp.concatenate([low, zero, zero], axis=1),
        ],
        axis=0,
    )
    return full.astype(BF16)


def applied(matrix, stacked):
    n = matrix.shape[0] // 3
    terms = jnp.dot(matrix, stacked, preferred_element_type=F32)
    return terms[:n] + (terms[n : 2 * n] + terms[2 * n :])


def gram_of(parts, total_states):
    (a, b), (c, d) = parts[:2], parts[2:]
    return ((a + b) + (c + d)) / total_states


def transposed_into(source, rows_ref):
    for g in range(rows_ref.shape[0] // LANES):
        pieces = [
            source[:, (PACK * g + b) * LANES : (PACK * g + b + 1) * LANES].astype(F32)
            for b in range(PACK)
        ]
        rows_ref[g * LANES : (g + 1) * LANES, :] = jnp.concatenate(pieces, axis=0).T


def gathered_into(unroll, row_ref, part_ref, rows_ref, picked, outs):
    count = picked.shape[0]
    columns = outs[0].shape[0]

    def pick(i, carry):
        for u in range(unroll):
            m = i * unroll + u
            picked[pl.ds(m, 1), :] = rows_ref[pl.ds(row_ref[m], 1), :]
        return carry

    lax.fori_loop(0, count // unroll, pick, 0)
    tiles_out = outs[0].shape[1] // LANES
    for g in range(count // LANES):
        y = picked[g * LANES : (g + 1) * LANES, :].T
        part = jnp.broadcast_to(part_ref[g : g + 1, :], (columns, LANES))
        value = y[:columns]
        for b in range(1, PACK):
            value = jnp.where(part == b, y[b * columns : (b + 1) * columns], value)
        out, t = outs[g // tiles_out], g % tiles_out
        out[:, t * LANES : (t + 1) * LANES] = value.astype(out.dtype)


def gather_kernel(unroll, row_ref, part_ref, rows_ref, *rest):
    gathered_into(unroll, row_ref, part_ref, rows_ref, rest[-1], rest[:-1])


def gather_colours(rows, row_list, part_list, count, dtype):
    indices = row_list.shape[0]
    columns = LANES // PACK
    return pl.pallas_call(
        functools.partial(gather_kernel, 64),
        out_shape=[vmem_out((columns, indices // count), dtype)] * count,
        in_specs=[SMEM, VMEM, VMEM],
        out_specs=[VMEM] * count,
        scratch_shapes=[pltpu.VMEM((indices, LANES), F32)],
        compiler_params=PARAMS,
        cost_estimate=pl.CostEstimate(flops=0, bytes_accessed=8 << 20, transcendentals=0),
        name="gather_rows",
    )(row_list, in_vmem(part_list), in_vmem(rows))


def start_rows_kernel(block_ref, rows_ref):
    transposed_into(block_ref, rows_ref)


def start_rows(block):
    return pl.pallas_call(
        start_rows_kernel,
        out_shape=vmem_out((block.shape[1] // PACK, LANES), F32),
        in_specs=[VMEM],
        out_specs=VMEM,
        compiler_params=PARAMS,
        name="start_rows",
    )(in_vmem(block))


def own_slots(block_ref, tiles_ref, own_ref):
    tile_size = tiles_ref.shape[1]
    for t in range(own_ref.shape[1] // tile_size):
        at = slice(t * tile_size, (t + 1) * tile_size)
        own_ref[:, at] = jnp.dot(block_ref[:, at], tiles_ref[t], preferred_element_type=F32)


def first_own_kernel(block_ref, tiles_ref, own_ref):
    own_slots(block_ref, tiles_ref, own_ref)


def first_own(block, tiles):
    return pl.pallas_call(
        first_own_kernel,
        out_shape=vmem_out(block.shape, F32),
        in_specs=[VMEM] * 2,
        out_specs=VMEM,
        compiler_params=PARAMS,
        name="first_own",
    )(in_vmem(block), in_vmem(tiles))


def later_own_kernel(total_states, *refs):
    grams, stacked, tiles_ref = refs[:4], refs[4], refs[5]
    block_ref, matrix_ref, own_ref = refs[6:]
    matrix = apply_matrix(inverse_factor(gram_of([r[...] for r in grams], total_states)))
    matrix_ref[...] = matrix
    for c in range(0, block_ref.shape[1], CHUNK):
        block_ref[:, c : c + CHUNK] = applied(matrix, stacked[:, c : c + CHUNK]).astype(BF16)
    own_slots(block_ref, tiles_ref, own_ref)


def later_own(grams, stacked, tiles, total_states):
    columns, states = stacked.shape[0] // 3, stacked.shape[1]
    return pl.pallas_call(
        functools.partial(later_own_kernel, total_states),
        out_shape=[
            vmem_out((columns, states), BF16),
            vmem_out((3 * columns, 3 * columns), BF16),
            vmem_out((columns, states), F32),
        ],
        in_specs=[VMEM] * 6,
        out_specs=[VMEM] * 3,
        compiler_params=PARAMS,
        name="later_own",
    )(*[in_vmem(g) for g in grams], in_vmem(stacked), in_vmem(tiles))


def product_kernel(colours, group, with_rows, *refs):
    src_ref, dst_ref, count_ref, block_ref, own_ref = refs[:5]
    ghosts, refs = refs[5 : 5 + colours], refs[5 + colours :]
    matrix_ref = None
    if ghosts[0].dtype == F32:
        matrix_ref, refs = refs[0], refs[1:]
    tiles_ref, refs = refs[0], refs[1:]
    stacked_ref, gram_ref, refs = refs[0], refs[1], refs[2:]
    if with_rows:
        rows_ref, refs = refs[0], refs[1:]
    source, total = refs
    columns, states = block_ref.shape
    slots, tile_size, _ = tiles_ref.shape
    first = states // tile_size
    live = count_ref[0]

    source[:, :states] = block_ref[...]
    at = states
    for ghost in ghosts:
        width = ghost.shape[1]
        value = ghost[...]
        if matrix_ref is not None:
            value = applied(matrix_ref[...], stack3(value)).astype(BF16)
        source[:, at : at + width] = value
        at += width
    source[:, at:] = jnp.zeros((columns, tile_size), BF16)
    nothing = at // tile_size
    total[...] = own_ref[...]

    def tile_at(s):
        index = jnp.where(s < live, src_ref[s], nothing)
        return source[:, pl.ds(pl.multiple_of(index * tile_size, tile_size), tile_size)]

    zero = jnp.zeros((columns, tile_size), BF16)

    def body(i, carry):
        base = first + i * group
        terms = []
        for u in range(0, group, 2):
            pair = jnp.concatenate(
                [
                    jnp.concatenate([tile_at(base + u), zero], axis=1),
                    jnp.concatenate([zero, tile_at(base + u + 1)], axis=1),
                ],
                axis=0,
            )
            weights = tiles_ref[pl.ds(base + u, 2)].reshape(2 * tile_size, tile_size)
            both = jnp.dot(pair, weights, preferred_element_type=F32)
            terms += [both[:columns], both[columns:]]
        for u in range(group):
            where = pl.multiple_of(dst_ref[base + u] * tile_size, tile_size)
            total[:, pl.ds(where, tile_size)] += terms[u]
        return carry

    lax.fori_loop(0, (live - first + group - 1) // group, body, 0)

    gram = jnp.zeros((3 * columns, 3 * columns), F32)
    for c in range(0, states, CHUNK):
        part = stack3(total[:, c : c + CHUNK])
        stacked_ref[:, c : c + CHUNK] = part
        gram += lax.dot_general(part, part, (((1,), (1,)), ((), ())), preferred_element_type=F32)
    blocks = [
        gram[a * columns : (a + 1) * columns, b * columns : (b + 1) * columns]
        for a in range(3)
        for b in range(3)
    ]
    small = blocks[8] + (blocks[5] + blocks[7])
    middle = blocks[4] + (blocks[2] + blocks[6])
    gram_ref[...] = blocks[0] + ((blocks[1] + blocks[3]) + (middle + small))
    if with_rows:
        transposed_into(total, rows_ref)


def product(src, dst, count, block, own, ghosts, matrix, tiles, with_rows):
    columns, states = block.shape
    slots, tile_size, _ = tiles.shape
    rest = slots - states // tile_size
    group = 64
    while rest % group:
        group //= 2
    outs = [vmem_out((3 * columns, states), BF16), vmem_out((columns, columns), F32)]
    if with_rows:
        outs.append(vmem_out((states // PACK, LANES), F32))
    operands = [block, own, *ghosts] + ([] if matrix is None else [matrix]) + [tiles]
    width = states + sum(g.shape[1] for g in ghosts) + tile_size
    return pl.pallas_call(
        functools.partial(product_kernel, len(ghosts), group, with_rows),
        out_shape=outs,
        in_specs=[SMEM] * 3 + [VMEM] * len(operands),
        out_specs=[VMEM] * len(outs),
        scratch_shapes=[pltpu.VMEM((columns, width), BF16), pltpu.VMEM((columns, states), F32)],
        compiler_params=PARAMS,
        name="product",
    )(src, dst, count, *[in_vmem(x) for x in operands])


def final_kernel(total_states, *refs):
    grams, stacked, out_ref = refs[:4], refs[4], refs[5]
    matrix = apply_matrix(inverse_factor(gram_of([r[...] for r in grams], total_states)))
    for c in range(0, out_ref.shape[1], CHUNK):
        out_ref[:, c : c + CHUNK] = applied(matrix, stacked[:, c : c + CHUNK])


def final(grams, stacked, total_states):
    columns, states = stacked.shape[0] // 3, stacked.shape[1]
    return pl.pallas_call(
        functools.partial(final_kernel, total_states),
        out_shape=jax.ShapeDtypeStruct((columns, states), F32),
        in_specs=[VMEM] * 5,
        out_specs=VMEM,
        compiler_params=PARAMS,
        name="final",
    )(*[in_vmem(g) for g in grams], in_vmem(stacked))


def dom_rounds(size):
    rounds, step = [], 1
    while step < size:
        span = min(4, size // step)
        rounds.append([step * k for k in range(1, span)])
        step *= span
    return rounds[::-1]


def gram_parts(gram, rounds):
    parts = [gram]
    for masks in rounds:
        if len(parts) > 1:
            gram = (parts[0] + parts[1]) + (parts[2] + parts[3])
        parts = [gram] + [swapped(gram, mask) for mask in masks]
        parts += [jnp.zeros_like(gram)] * (4 - len(parts))
    return parts


def on_device(start_block, tiles, tile_src, tile_dst, slot_count, send_rows):
    size = lax.axis_size("dom")
    masks = [1, 2, 4, 1 << (size.bit_length() - 2)]
    columns, states = start_block.shape
    total_states = states * size
    rounds = dom_rounds(size)
    lists = send_rows[0]
    pack_states = PACK * LANES
    row_lists = lists // pack_states * LANES + lists % LANES
    part_lists = lists // LANES % PACK
    far = (3, 2)
    near = (1, 0)

    def lists_of(colours):
        rows = jnp.concatenate([row_lists[c] for c in colours])
        parts = jnp.concatenate([part_lists[c] for c in colours]).reshape(-1, LANES)
        return rows, parts

    listed = [lists_of(far), lists_of(near)]

    def exchanged(rows, dtype):
        ghosts = [None] * len(masks)
        for colours, (row_list, part_list) in zip((far, near), listed):
            picked = gather_colours(rows, row_list, part_list, len(colours), dtype)
            for colour, x in zip(colours, picked):
                ghosts[colour] = swapped(x, masks[colour])
        return ghosts

    ghosts = exchanged(start_rows(start_block), BF16)
    block, matrix = start_block, None
    own = first_own(start_block, tiles)
    for turn in range(ITERS):
        last = turn == ITERS - 1
        stacked, gram, *rows = product(
            tile_src, tile_dst, slot_count, block, own, ghosts, matrix, tiles, not last
        )
        parts = gram_parts(gram, rounds)
        if last:
            return final(parts, stacked, total_states)
        ghosts = exchanged(rows[0], F32)
        block, matrix, own = later_own(parts, stacked, tiles, total_states)


def solution(mesh):
    return jax.shard_map(
        on_device,
        mesh=mesh,
        in_specs=(
            P(None, ("groups", "dom")),
            P(("groups", "dom"), None, None),
            P(("groups", "dom")),
            P(("groups", "dom")),
            P(("groups", "dom")),
            P(("groups", "dom"), None, None),
        ),
        out_specs=P(None, ("groups", "dom")),
        check_vma=False,
    )
```

time: 356 us -> 107 us (0.30); the launches traced: 350 us -> 107 us
  blocking collectives: 182 us -> 0 us
  local copies, waits for them, and re-layouts: 67.5 us -> 5.17 us
  matrix products: 45.5 us -> 0 us
  Pallas kernels: 0 us -> 44.5 us
  starting transfers between devices: 8.57 us -> 32.4 us
  other arithmetic: 24 us -> 0.87 us
    psum x3 -> x0, blocking collectives: 182 us -> none  [on_device(): gram_sum = lax.psum(partial_gram, 'dom')]
    gather x23 -> x0, local copies, waits for them, and re-layouts: 50.6 us -> none  [the longest x16 30.5 us: on_device(): later_chosen = jnp.take(current, send_lists[later_colour], axis=1)]
    dot_general x12 -> x0, matrix products: 44.8 us -> none  [the longest x3 17.2 us: on_device(): jnp.einsum('ski,sij->skj', slot_chosen, tiles, preferred_element_type=jnp...]
    pallas_call x0 -> x14, Pallas kernels: none -> 44.5 us  [the longest x6 22.6 us: gather_colours(): pl.pallas_call(functools.partial(gather_kernel, 64), out_shape=[vmem_out(...]
    ppermute x12 -> x30, starting transfers between devices: 8.57 us -> 32.4 us  [swapped(): return lax.ppermute(x, 'dom', [(i, i ^ mask) for i in range(size)])]
    another operation x15 -> x0, other arithmetic: 20 us -> none  [the longest x9 10.8 us: on_device(): lower_factor = jnp.linalg.cholesky(gram_sum)]
    ppermute x4 -> x0, local copies, waits for them, and re-layouts: 3.57 us -> none  [swapped(): lax.ppermute(x, axis, [(i, i ^ 1 << bit) for i in range(lax.axis_size(axi...]
    ppermute x12 -> x30, waiting for transfers between devices: 21 us -> 23.2 us  [swapped(): return lax.ppermute(x, 'dom', [(i, i ^ mask) for i in range(size)])]
  transfers between devices with their start and end apart: 12 -> 30, of which waited for: 6 -> 10; matrix products, arithmetic and copies ran while one was open for 6% -> 0% of each run, Pallas kernels for 0% -> 26%
where the time goes in v1:
time: 107 us
  Pallas kernels  44.5 us (42%)
  starting transfers between devices  32.4 us (30%)
  waiting for transfers between devices  23.2 us (22%)
  local copies, waits for them, and re-layouts  5.17 us (5%)
    ppermute x30, starting transfers between devices, swapped(): return lax.ppermute(x, 'dom', [(i, i ^ mask) for i in range(size)])  32.4 us
    ppermute x30, waiting for transfers between devices, swapped(): return lax.ppermute(x, 'dom', [(i, i ^ mask) for i in range(size)])  23.2 us
    pallas_call x6, Pallas kernels, gather_colours(): pl.pallas_call(functools.partial(gather_kernel, 64), out_shape=[vmem_out(...  22.6 us
    pallas_call x3, Pallas kernels, product(): pl.pallas_call(functools.partial(product_kernel, len(ghosts), group, with...  8.94 us
    pallas_call x2, Pallas kernels, later_own(): pl.pallas_call(functools.partial(later_own_kernel, total_states), out_sha...  7.79 us
    unnamed x14, local copies, waits for them, and re-layouts  5.05 us
    pallas_call x1, Pallas kernels, final(): pl.pallas_call(functools.partial(final_kernel, total_states), out_shape=j...  4.34 us
  transfers between devices with their start and end apart: 30, of which 10 were waited for; matrix products, arithmetic and copies ran while one was open for 0% of the time, Pallas kernels for 26%

profile of v1, /device:TPU:0, one launch (start us, length us, event | category | flops | bytes accessed | tf_op | source)
XLA Modules:
  0.0 107.1 jit_solution(10686880956078858120)
XLA Ops:
  0.0 0.8 add_select_fusion
  0.8 0.0 copy-start.1
  0.8 1.0 copy-done.1
  1.9 0.2 start_rows.1.rows_ref
  2.1 0.1 slice_reduce_fusion.1
  2.2 3.6 %gather_rows.7 = (bf16[32,1536]{1,0:T(8,128)(2,1)S(1)}, bf16[32,1536]{1,0:T(8,128)(2,1)S(1)}) custom-call(s32[3072]{0:T(1024)S(1)} %pad_add_fusion.2.row_ref, s32[24,128]{1,0:T(8,128)S(1)} %pad_add_fusion.3.part_ref, f32[2048,128]{1,0:T(8,128)S(1)} %start_rows.1.rows_ref), custom_call_target="tpu_custom_call" | custom-call | bytes 8388608 | tf_op jit(solution)/shard_map/gather_rows/pallas_call | solution.py:125
  5.9 3.1 %collective-permute-start.2 = (bf16[32,1536]{1,0:T(8,128)(2,1)S(1)}, bf16[32,1536]{1,0:T(8,128)(2,1)S(1)}, u32[]{:S(2)}, u32[]{:S(2)}) collective-permute-start(bf16[32,1536]{1,0:T(8,128)(2,1)S(1)} %get-tuple-element.33), channel_id=1, source_target_pairs={{0,4},{1,5},{2,6},{3,7},{4,0},{5,1},{6,2},{7,3},{8,12},{9,13},{10,... | collective-permute-start | bytes 294920 | tf_op jit(solution)/shard_map/ppermute | solution.py:31
  9.0 2.6 %collective-permute-start.3 = (bf16[32,1536]{1,0:T(8,128)(2,1)S(1)}, bf16[32,1536]{1,0:T(8,128)(2,1)S(1)}, u32[]{:S(2)}, u32[]{:S(2)}) collective-permute-start(bf16[32,1536]{1,0:T(8,128)(2,1)S(1)} %get-tuple-element.34), channel_id=1, source_target_pairs={{0,8},{1,9},{2,10},{3,11},{4,12},{5,13},{6,14},{7,15},{8,0},{9,1},... | collective-permute-start | bytes 294920 | tf_op jit(solution)/shard_map/ppermute | solution.py:31
  11.6 3.6 %gather_rows.6 = (bf16[32,1536]{1,0:T(8,128)(2,1)S(1)}, bf16[32,1536]{1,0:T(8,128)(2,1)S(1)}) custom-call(s32[3072]{0:T(1024)S(1)} %pad_add_fusion.row_ref, s32[24,128]{1,0:T(8,128)S(1)} %pad_add_fusion.1.part_ref, f32[2048,128]{1,0:T(8,128)S(1)} %start_rows.1.rows_ref), custom_call_target="tpu_custom_call" | custom-call | bytes 8388608 | tf_op jit(solution)/shard_map/gather_rows/pallas_call | solution.py:125
  15.2 0.1 collective-permute-start
  15.3 1.6 %collective-permute-start.1 = (bf16[32,1536]{1,0:T(8,128)(2,1)S(1)}, bf16[32,1536]{1,0:T(8,128)(2,1)S(1)}, u32[]{:S(2)}, u32[]{:S(2)}) collective-permute-start(bf16[32,1536]{1,0:T(8,128)(2,1)S(1)} %get-tuple-element.32), channel_id=1, source_target_pairs={{0,2},{1,3},{2,0},{3,1},{4,6},{5,7},{6,4},{7,5},{8,10},{9,11},{10,... | collective-permute-start | bytes 294920 | tf_op jit(solution)/shard_map/ppermute | solution.py:31
  17.5 0.0 copy-start
  17.5 4.0 %copy-done = bf16[320,128,128]{2,1,0:T(8,128)(2,1)S(1)} copy-done((bf16[320,128,128]{2,1,0:T(8,128)(2,1)S(1)}, bf16[320,128,128]{2,1,0:T(8,128)(2,1)}, u32[]{:S(2)}) %copy-start) | copy-done | bytes 10485784
  21.6 0.7 first_own.1.refs_4_
  22.2 0.0 collective-permute-done.2.refs_7_
  22.2 0.0 collective-permute-done.3.refs_8_
  22.2 0.0 collective-permute-done.refs_5_
  22.3 2.8 %product.3 = (bf16[96,8192]{1,0:T(8,128)(2,1)S(1)}, f32[32,32]{1,0:T(8,128)S(1)}, f32[2048,128]{1,0:T(8,128)S(1)}) custom-call(s32[320]{0:T(512)S(1)} %copy-done.2, s32[320]{0:T(512)S(1)} %copy-done.3, s32[1]{0:T(128)S(6)} %copy.7.refs_2_, bf16[32,8192]{1,0:T(8,128)(2,1)S(1)} %copy-done.1, f32[32,8192]{1,0:T(8,128)S(1)} %first_own.1.refs_4_, ...), custom_call_target="tpu_custom_call" | custom-call | tf_op jit(solution)/shard_map/product/pallas_call | solution.py:285
  25.0 0.3 collective-permute-start.6
  25.3 1.7 %collective-permute-start.5 = (f32[32,32]{1,0:T(8,128)S(1)}, f32[32,32]{1,0:T(8,128)S(1)}, u32[]{:S(2)}, u32[]{:S(2)}) collective-permute-start(f32[32,32]{1,0:T(8,128)S(1)} %get-tuple-element.35), channel_id=1, source_target_pairs={{0,8},{1,9},{2,10},{3,11},{4,12},{5,13},{6,14},{7,15},{8,0},{9,1},... | collective-permute-start | bytes 12296 | tf_op jit(solution)/shard_map/ppermute | solution.py:31
  27.0 2.5 %collective-permute-start.4 = (f32[32,32]{1,0:T(8,128)S(1)}, f32[32,32]{1,0:T(8,128)S(1)}, u32[]{:S(2)}, u32[]{:S(2)}) collective-permute-start(f32[32,32]{1,0:T(8,128)S(1)} %get-tuple-element.35), channel_id=1, source_target_pairs={{0,4},{1,5},{2,6},{3,7},{4,0},{5,1},{6,2},{7,3},{8,12},{9,13},{10,... | collective-permute-start | bytes 12296 | tf_op jit(solution)/shard_map/ppermute | solution.py:31
  29.5 3.8 %gather_rows.9 = (f32[32,1536]{1,0:T(8,128)S(1)}, f32[32,1536]{1,0:T(8,128)S(1)}) custom-call(s32[3072]{0:T(1024)S(1)} %pad_add_fusion.2.row_ref, s32[24,128]{1,0:T(8,128)S(1)} %pad_add_fusion.3.part_ref, f32[2048,128]{1,0:T(8,128)S(1)} %get-tuple-element.39.rows_ref), custom_call_target="tpu_custom_call" | custom-call | bytes 8388608 | tf_op jit(solution)/shard_map/gather_rows/pallas_call | solution.py:125
  33.3 3.8 %gather_rows.8 = (f32[32,1536]{1,0:T(8,128)S(1)}, f32[32,1536]{1,0:T(8,128)S(1)}) custom-call(s32[3072]{0:T(1024)S(1)} %pad_add_fusion.row_ref, s32[24,128]{1,0:T(8,128)S(1)} %pad_add_fusion.1.part_ref, f32[2048,128]{1,0:T(8,128)S(1)} %get-tuple-element.39.rows_ref), custom_call_target="tpu_custom_call" | custom-call | bytes 8388608 | tf_op jit(solution)/shard_map/gather_rows/pallas_call | solution.py:125
  37.2 0.1 collective-permute-start.12
  37.2 0.8 collective-permute-start.13
  38.0 0.4 collective-permute-start.11
  38.5 1.5 %collective-permute-start.9 = (f32[32,32]{1,0:T(8,128)S(1)}, f32[32,32]{1,0:T(8,128)S(1)}, u32[]{:S(2)}, u32[]{:S(2)}) collective-permute-start(f32[32,32]{1,0:T(8,128)S(1)} %add_add_fusion.2.refs_0_), channel_id=1, source_target_pairs={{0,3},{1,2},{2,1},{3,0},{4,7},{5,6},{6,5},{7,4},{8,11},{9,10},{10,... | collective-permute-start | bytes 12296 | tf_op jit(solution)/shard_map/ppermute | solution.py:31
  40.0 5.3 %collective-permute-done.9.refs_3_ = f32[32,32]{1,0:T(8,128)S(1)} collective-permute-done((f32[32,32]{1,0:T(8,128)S(1)}, f32[32,32]{1,0:T(8,128)S(1)}, u32[]{:S(2)}, u32[]{:S(2)}) %collective-permute-start.9) | collective-permute-done | bytes 4128 | tf_op jit(solution)/shard_map/ppermute | solution.py:31
  45.2 0.4 collective-permute-start.8
  45.6 3.4 %collective-permute-done.8.refs_2_ = f32[32,32]{1,0:T(8,128)S(1)} collective-permute-done((f32[32,32]{1,0:T(8,128)S(1)}, f32[32,32]{1,0:T(8,128)S(1)}, u32[]{:S(2)}, u32[]{:S(2)}) %collective-permute-start.8) | collective-permute-done | bytes 4128 | tf_op jit(solution)/shard_map/ppermute | solution.py:31
  49.0 0.0 collective-permute-start.7
  49.0 1.2 %collective-permute-done.7.refs_1_ = f32[32,32]{1,0:T(8,128)S(1)} collective-permute-done((f32[32,32]{1,0:T(8,128)S(1)}, f32[32,32]{1,0:T(8,128)S(1)}, u32[]{:S(2)}, u32[]{:S(2)}) %collective-permute-start.7) | collective-permute-done | bytes 4128 | tf_op jit(solution)/shard_map/ppermute | solution.py:31
  50.2 3.9 %later_own.2 = (bf16[32,8192]{1,0:T(8,128)(2,1)S(1)}, bf16[96,96]{1,0:T(8,128)(2,1)S(1)}, f32[32,8192]{1,0:T(8,128)S(1)}) custom-call(f32[32,32]{1,0:T(8,128)S(1)} %add_add_fusion.2.refs_0_, f32[32,32]{1,0:T(8,128)S(1)} %collective-permute-done.7.refs_1_, f32[32,32]{1,0:T(8,128)S(1)} %collective-permute-done.8.refs_2_, ...), custom_call_target="tpu_custom_call" | custom-call | tf_op jit(solution)/shard_map/later_own/pallas_call | solution.py:186
  54.1 0.0 collective-permute-done.12.refs_7_
  54.1 0.0 collective-permute-done.13.refs_8_
  54.1 0.0 collective-permute-done.10.refs_5_
  54.1 3.1 %product.4 = (bf16[96,8192]{1,0:T(8,128)(2,1)S(1)}, f32[32,32]{1,0:T(8,128)S(1)}, f32[2048,128]{1,0:T(8,128)S(1)}) custom-call(s32[320]{0:T(512)S(1)} %copy-done.2, s32[320]{0:T(512)S(1)} %copy-done.3, s32[1]{0:T(128)S(6)} %copy.7.refs_2_, bf16[32,8192]{1,0:T(8,128)(2,1)S(1)} %get-tuple-element.37.refs_3_, f32[32,8192]{1,0:T(8,128)S(1)} %get-tuple-element.38.refs_4_, ...), custom_call_target="tpu_custom_call" | custom-call | tf_op jit(solution)/shard_map/product/pallas_call | solution.py:285
  57.2 3.7 %collective-permute-start.16 = (f32[32,32]{1,0:T(8,128)S(1)}, f32[32,32]{1,0:T(8,128)S(1)}, u32[]{:S(2)}, u32[]{:S(2)}) collective-permute-start(f32[32,32]{1,0:T(8,128)S(1)} %get-tuple-element.45), channel_id=1, source_target_pairs={{0,12},{1,13},{2,14},{3,15},{4,8},{5,9},{6,10},{7,11},{8,4},{9,5},... | collective-permute-start | bytes 12296 | tf_op jit(solution)/shard_map/ppermute | solution.py:31
  60.9 0.8 collective-permute-start.14
  61.7 3.8 %gather_rows.11 = (f32[32,1536]{1,0:T(8,128)S(1)}, f32[32,1536]{1,0:T(8,128)S(1)}) custom-call(s32[3072]{0:T(1024)S(1)} %pad_add_fusion.2.row_ref, s32[24,128]{1,0:T(8,128)S(1)} %pad_add_fusion.3.part_ref, f32[2048,128]{1,0:T(8,128)S(1)} %get-tuple-element.49.rows_ref), custom_call_target="tpu_custom_call" | custom-call | bytes 8388608 | tf_op jit(solution)/shard_map/gather_rows/pallas_call | solution.py:125
  65.5 3.8 %gather_rows.10 = (f32[32,1536]{1,0:T(8,128)S(1)}, f32[32,1536]{1,0:T(8,128)S(1)}) custom-call(s32[3072]{0:T(1024)S(1)} %pad_add_fusion.row_ref, s32[24,128]{1,0:T(8,128)S(1)} %pad_add_fusion.1.part_ref, f32[2048,128]{1,0:T(8,128)S(1)} %get-tuple-element.49.rows_ref), custom_call_target="tpu_custom_call" | custom-call | bytes 8388608 | tf_op jit(solution)/shard_map/gather_rows/pallas_call | solution.py:125
  69.4 1.3 %collective-permute-start.22 = (f32[32,1536]{1,0:T(8,128)S(1)}, f32[32,1536]{1,0:T(8,128)S(1)}, u32[]{:S(2)}, u32[]{:S(2)}) collective-permute-start(f32[32,1536]{1,0:T(8,128)S(1)} %get-tuple-element.52), channel_id=1, source_target_pairs={{0,4},{1,5},{2,6},{3,7},{4,0},{5,1},{6,2},{7,3},{8,12},{9,13},{10,... | collective-permute-start | bytes 589832 | tf_op jit(solution)/shard_map/ppermute | solution.py:31
  70.7 2.9 %collective-permute-start.23 = (f32[32,1536]{1,0:T(8,128)S(1)}, f32[32,1536]{1,0:T(8,128)S(1)}, u32[]{:S(2)}, u32[]{:S(2)}) collective-permute-start(f32[32,1536]{1,0:T(8,128)S(1)} %get-tuple-element.53), channel_id=1, source_target_pairs={{0,8},{1,9},{2,10},{3,11},{4,12},{5,13},{6,14},{7,15},{8,0},{9,1},... | collective-permute-start | bytes 589832 | tf_op jit(solution)/shard_map/ppermute | solution.py:31
  73.6 0.0 collective-permute-done.16
  73.6 0.6 collective-permute-start.21
  74.2 1.4 %collective-permute-start.19 = (f32[32,32]{1,0:T(8,128)S(1)}, f32[32,32]{1,0:T(8,128)S(1)}, u32[]{:S(2)}, u32[]{:S(2)}) collective-permute-start(f32[32,32]{1,0:T(8,128)S(1)} %add_add_fusion.1.refs_0_), channel_id=1, source_target_pairs={{0,3},{1,2},{2,1},{3,0},{4,7},{5,6},{6,5},{7,4},{8,11},{9,10},{10,... | collective-permute-start | bytes 12296 | tf_op jit(solution)/shard_map/ppermute | solution.py:31
  75.5 5.3 %collective-permute-done.19.refs_3_ = f32[32,32]{1,0:T(8,128)S(1)} collective-permute-done((f32[32,32]{1,0:T(8,128)S(1)}, f32[32,32]{1,0:T(8,128)S(1)}, u32[]{:S(2)}, u32[]{:S(2)}) %collective-permute-start.19) | collective-permute-done | bytes 4128 | tf_op jit(solution)/shard_map/ppermute | solution.py:31
  80.8 0.5 collective-permute-start.18
  81.3 3.2 %collective-permute-done.18.refs_2_ = f32[32,32]{1,0:T(8,128)S(1)} collective-permute-done((f32[32,32]{1,0:T(8,128)S(1)}, f32[32,32]{1,0:T(8,128)S(1)}, u32[]{:S(2)}, u32[]{:S(2)}) %collective-permute-start.18) | collective-permute-done | bytes 4128 | tf_op jit(solution)/shard_map/ppermute | solution.py:31
  84.5 1.2 %collective-permute-done.17.refs_1_ = f32[32,32]{1,0:T(8,128)S(1)} collective-permute-done((f32[32,32]{1,0:T(8,128)S(1)}, f32[32,32]{1,0:T(8,128)S(1)}, u32[]{:S(2)}, u32[]{:S(2)}) %collective-permute-start.17) | collective-permute-done | bytes 4128 | tf_op jit(solution)/shard_map/ppermute | solution.py:31
  85.7 3.9 %later_own.3 = (bf16[32,8192]{1,0:T(8,128)(2,1)S(1)}, bf16[96,96]{1,0:T(8,128)(2,1)S(1)}, f32[32,8192]{1,0:T(8,128)S(1)}) custom-call(f32[32,32]{1,0:T(8,128)S(1)} %add_add_fusion.1.refs_0_, f32[32,32]{1,0:T(8,128)S(1)} %collective-permute-done.17.refs_1_, f32[32,32]{1,0:T(8,128)S(1)} %collective-permute-done.18.refs_2_, ...), custom_call_target="tpu_custom_call" | custom-call | tf_op jit(solution)/shard_map/later_own/pallas_call | solution.py:186
  89.6 0.0 collective-permute-done.20.refs_5_
  89.7 3.1 %product.5 = (bf16[96,8192]{1,0:T(8,128)(2,1)S(1)}, f32[32,32]{1,0:T(8,128)S(1)}) custom-call(s32[320]{0:T(512)S(1)} %copy-done.2, s32[320]{0:T(512)S(1)} %copy-done.3, s32[1]{0:T(128)S(6)} %copy.7.refs_2_, bf16[32,8192]{1,0:T(8,128)(2,1)S(1)} %get-tuple-element.47.refs_3_, f32[32,8192]{1,0:T(8,128)S(1)} %get-tuple-element.48.refs_4_, ...), custom_call_target="tpu_custom_call" | custom-call | tf_op jit(solution)/shard_map/product/pallas_call | solution.py:285
  92.7 0.2 collective-permute-start.26
  92.9 1.3 %collective-permute-start.25 = (f32[32,32]{1,0:T(8,128)S(1)}, f32[32,32]{1,0:T(8,128)S(1)}, u32[]{:S(2)}, u32[]{:S(2)}) collective-permute-start(f32[32,32]{1,0:T(8,128)S(1)} %get-tuple-element.55), channel_id=1, source_target_pairs={{0,8},{1,9},{2,10},{3,11},{4,12},{5,13},{6,14},{7,15},{8,0},{9,1},... | collective-permute-start | bytes 12296 | tf_op jit(solution)/shard_map/ppermute | solution.py:31
  94.3 2.9 %collective-permute-start.24 = (f32[32,32]{1,0:T(8,128)S(1)}, f32[32,32]{1,0:T(8,128)S(1)}, u32[]{:S(2)}, u32[]{:S(2)}) collective-permute-start(f32[32,32]{1,0:T(8,128)S(1)} %get-tuple-element.55), channel_id=1, source_target_pairs={{0,4},{1,5},{2,6},{3,7},{4,0},{5,1},{6,2},{7,3},{8,12},{9,13},{10,... | collective-permute-start | bytes 12296 | tf_op jit(solution)/shard_map/ppermute | solution.py:31
  97.1 1.1 %collective-permute-done.26 = f32[32,32]{1,0:T(8,128)S(1)} collective-permute-done((f32[32,32]{1,0:T(8,128)S(1)}, f32[32,32]{1,0:T(8,128)S(1)}, u32[]{:S(2)}, u32[]{:S(2)}) %collective-permute-start.26) | collective-permute-done | bytes 4128 | tf_op jit(solution)/shard_map/ppermute | solution.py:31
  98.3 0.6 collective-permute-done.24
  98.8 0.1 collective-permute-start.29
  98.9 0.7 collective-permute-start.28
  99.6 1.2 %collective-permute-start.27 = (f32[32,32]{1,0:T(8,128)S(1)}, f32[32,32]{1,0:T(8,128)S(1)}, u32[]{:S(2)}, u32[]{:S(2)}) collective-permute-start(f32[32,32]{1,0:T(8,128)S(1)} %add_add_fusion.refs_0_), channel_id=1, source_target_pairs={{0,1},{1,0},{2,3},{3,2},{4,5},{5,4},{6,7},{7,6},{8,9},{9,8},{10,11... | collective-permute-start | bytes 12296 | tf_op jit(solution)/shard_map/ppermute | solution.py:31
  100.8 1.3 %collective-permute-done.29.refs_3_ = f32[32,32]{1,0:T(8,128)S(1)} collective-permute-done((f32[32,32]{1,0:T(8,128)S(1)}, f32[32,32]{1,0:T(8,128)S(1)}, u32[]{:S(2)}, u32[]{:S(2)}) %collective-permute-start.29) | collective-permute-done | bytes 4128 | tf_op jit(solution)/shard_map/ppermute | solution.py:31
  102.1 0.7 collective-permute-done.28.refs_2_
  102.7 4.3 %final.1 = f32[32,8192]{1,0:T(8,128)} custom-call(f32[32,32]{1,0:T(8,128)S(1)} %add_add_fusion.refs_0_, f32[32,32]{1,0:T(8,128)S(1)} %collective-permute-done.27.refs_1_, f32[32,32]{1,0:T(8,128)S(1)} %collective-permute-done.28.refs_2_, f32[32,32]{1,0:T(8,128)S(1)} %collective-permute-done.29.refs_3_, bf16[96,8192]{1,0:T(8,128)(2,1)S(1)} %get-tuple-element.56.refs_4_), custom_call_target="tpu_custom_call" | custom-call | tf_op jit(solution)/shard_map/final/pallas_call | solution.py:305
  (34 shorter events, 0.1 us)
Async XLA Ops:
  0.8 1.0 copy-start.1
  5.9 16.3 %collective-permute-start.2 = (bf16[32,1536]{1,0:T(8,128)(2,1)S(1)}, bf16[32,1536]{1,0:T(8,128)(2,1)S(1)}, u32[]{:S(2)}, u32[]{:S(2)}) collective-permute-start(bf16[32,1536]{1,0:T(8,128)(2,1)S(1)} %get-tuple-element.33), channel_id=1, source_target_pairs={{0,4},{1,5},{2,6},{3,7},{4,0},{5,1},{6,2},{7,3},{8,12},{9,13},{10,... | collective-permute-start | bytes 294920 | tf_op jit(solution)/shard_map/ppermute | solution.py:31
  9.0 13.2 %collective-permute-start.3 = (bf16[32,1536]{1,0:T(8,128)(2,1)S(1)}, bf16[32,1536]{1,0:T(8,128)(2,1)S(1)}, u32[]{:S(2)}, u32[]{:S(2)}) collective-permute-start(bf16[32,1536]{1,0:T(8,128)(2,1)S(1)} %get-tuple-element.34), channel_id=1, source_target_pairs={{0,8},{1,9},{2,10},{3,11},{4,12},{5,13},{6,14},{7,15},{8,0},{9,1},... | collective-permute-start | bytes 294920 | tf_op jit(solution)/shard_map/ppermute | solution.py:31
  15.2 7.0 %collective-permute-start = (bf16[32,1536]{1,0:T(8,128)(2,1)S(1)}, bf16[32,1536]{1,0:T(8,128)(2,1)S(1)}, u32[]{:S(2)}, u32[]{:S(2)}) collective-permute-start(bf16[32,1536]{1,0:T(8,128)(2,1)S(1)} %get-tuple-element.31), channel_id=1, source_target_pairs={{0,1},{1,0},{2,3},{3,2},{4,5},{5,4},{6,7},{7,6},{8,9},{9,8},{10,11... | collective-permute-start | bytes 294920 | tf_op jit(solution)/shard_map/ppermute | solution.py:31
  15.3 6.9 %collective-permute-start.1 = (bf16[32,1536]{1,0:T(8,128)(2,1)S(1)}, bf16[32,1536]{1,0:T(8,128)(2,1)S(1)}, u32[]{:S(2)}, u32[]{:S(2)}) collective-permute-start(bf16[32,1536]{1,0:T(8,128)(2,1)S(1)} %get-tuple-element.32), channel_id=1, source_target_pairs={{0,2},{1,3},{2,0},{3,1},{4,6},{5,7},{6,4},{7,5},{8,10},{9,11},{10,... | collective-permute-start | bytes 294920 | tf_op jit(solution)/shard_map/ppermute | solution.py:31
  17.5 4.0 %copy-start = (bf16[320,128,128]{2,1,0:T(8,128)(2,1)S(1)}, bf16[320,128,128]{2,1,0:T(8,128)(2,1)}, u32[]{:S(2)}) copy-start(bf16[320,128,128]{2,1,0:T(8,128)(2,1)} %refs_10_.3) | copy-start | bytes 31457284
  21.5 0.7 copy-start.2
  21.5 0.7 copy-start.3
  21.5 28.6 %slice-start = ((s8[10485760]{0:T(1024)(128)(4,1)}), s8[4194304]{0:T(1024)(128)(4,1)S(1)}, s32[]{:S(2)}) async-start(s8[10485760]{0:T(1024)(128)(4,1)} %bitcast.22), calls=%async_computation | async-start | bytes 8388608
  21.5 28.6 %slice-start.1 = ((s8[10485760]{0:T(1024)(128)(4,1)}), s8[4194304]{0:T(1024)(128)(4,1)S(1)}, s32[]{:S(2)}) async-start(s8[10485760]{0:T(1024)(128)(4,1)} %bitcast.22), calls=%async_computation.1 | async-start | bytes 8388608
  22.2 27.9 %slice-start.2 = ((s8[10485760]{0:T(1024)(128)(4,1)}), s8[2097152]{0:T(1024)(128)(4,1)S(1)}, s32[]{:S(2)}) async-start(s8[10485760]{0:T(1024)(128)(4,1)} %bitcast.22), calls=%async_computation.2 | async-start | bytes 4194304
  25.0 13.0 %collective-permute-start.6 = (f32[32,32]{1,0:T(8,128)S(1)}, f32[32,32]{1,0:T(8,128)S(1)}, u32[]{:S(2)}, u32[]{:S(2)}) collective-permute-start(f32[32,32]{1,0:T(8,128)S(1)} %get-tuple-element.35), channel_id=1, source_target_pairs={{0,12},{1,13},{2,14},{3,15},{4,8},{5,9},{6,10},{7,11},{8,4},{9,5},... | collective-permute-start | bytes 12296 | tf_op jit(solution)/shard_map/ppermute | solution.py:31
  25.3 12.7 %collective-permute-start.5 = (f32[32,32]{1,0:T(8,128)S(1)}, f32[32,32]{1,0:T(8,128)S(1)}, u32[]{:S(2)}, u32[]{:S(2)}) collective-permute-start(f32[32,32]{1,0:T(8,128)S(1)} %get-tuple-element.35), channel_id=1, source_target_pairs={{0,8},{1,9},{2,10},{3,11},{4,12},{5,13},{6,14},{7,15},{8,0},{9,1},... | collective-permute-start | bytes 12296 | tf_op jit(solution)/shard_map/ppermute | solution.py:31
  27.0 11.5 %collective-permute-start.4 = (f32[32,32]{1,0:T(8,128)S(1)}, f32[32,32]{1,0:T(8,128)S(1)}, u32[]{:S(2)}, u32[]{:S(2)}) collective-permute-start(f32[32,32]{1,0:T(8,128)S(1)} %get-tuple-element.35), channel_id=1, source_target_pairs={{0,4},{1,5},{2,6},{3,7},{4,0},{5,1},{6,2},{7,3},{8,12},{9,13},{10,... | collective-permute-start | bytes 12296 | tf_op jit(solution)/shard_map/ppermute | solution.py:31
  37.2 16.9 %collective-permute-start.12 = (f32[32,1536]{1,0:T(8,128)S(1)}, f32[32,1536]{1,0:T(8,128)S(1)}, u32[]{:S(2)}, u32[]{:S(2)}) collective-permute-start(f32[32,1536]{1,0:T(8,128)S(1)} %get-tuple-element.42), channel_id=1, source_target_pairs={{0,4},{1,5},{2,6},{3,7},{4,0},{5,1},{6,2},{7,3},{8,12},{9,13},{10,... | collective-permute-start | bytes 589832 | tf_op jit(solution)/shard_map/ppermute | solution.py:31
  37.2 16.8 %collective-permute-start.13 = (f32[32,1536]{1,0:T(8,128)S(1)}, f32[32,1536]{1,0:T(8,128)S(1)}, u32[]{:S(2)}, u32[]{:S(2)}) collective-permute-start(f32[32,1536]{1,0:T(8,128)S(1)} %get-tuple-element.43), channel_id=1, source_target_pairs={{0,8},{1,9},{2,10},{3,11},{4,12},{5,13},{6,14},{7,15},{8,0},{9,1},... | collective-permute-start | bytes 589832 | tf_op jit(solution)/shard_map/ppermute | solution.py:31
  38.0 16.1 %collective-permute-start.10 = (f32[32,1536]{1,0:T(8,128)S(1)}, f32[32,1536]{1,0:T(8,128)S(1)}, u32[]{:S(2)}, u32[]{:S(2)}) collective-permute-start(f32[32,1536]{1,0:T(8,128)S(1)} %get-tuple-element.40), channel_id=1, source_target_pairs={{0,1},{1,0},{2,3},{3,2},{4,5},{5,4},{6,7},{7,6},{8,9},{9,8},{10,11... | collective-permute-start | bytes 589832 | tf_op jit(solution)/shard_map/ppermute | solution.py:31
  38.0 16.1 %collective-permute-start.11 = (f32[32,1536]{1,0:T(8,128)S(1)}, f32[32,1536]{1,0:T(8,128)S(1)}, u32[]{:S(2)}, u32[]{:S(2)}) collective-permute-start(f32[32,1536]{1,0:T(8,128)S(1)} %get-tuple-element.41), channel_id=1, source_target_pairs={{0,2},{1,3},{2,0},{3,1},{4,6},{5,7},{6,4},{7,5},{8,10},{9,11},{10,... | collective-permute-start | bytes 589832 | tf_op jit(solution)/shard_map/ppermute | solution.py:31
  38.5 6.8 %collective-permute-start.9 = (f32[32,32]{1,0:T(8,128)S(1)}, f32[32,32]{1,0:T(8,128)S(1)}, u32[]{:S(2)}, u32[]{:S(2)}) collective-permute-start(f32[32,32]{1,0:T(8,128)S(1)} %add_add_fusion.2.refs_0_), channel_id=1, source_target_pairs={{0,3},{1,2},{2,1},{3,0},{4,7},{5,6},{6,5},{7,4},{8,11},{9,10},{10,... | collective-permute-start | bytes 12296 | tf_op jit(solution)/shard_map/ppermute | solution.py:31
  45.2 3.7 %collective-permute-start.8 = (f32[32,32]{1,0:T(8,128)S(1)}, f32[32,32]{1,0:T(8,128)S(1)}, u32[]{:S(2)}, u32[]{:S(2)}) collective-permute-start(f32[32,32]{1,0:T(8,128)S(1)} %add_add_fusion.2.refs_0_), channel_id=1, source_target_pairs={{0,2},{1,3},{2,0},{3,1},{4,6},{5,7},{6,4},{7,5},{8,10},{9,11},{10,... | collective-permute-start | bytes 12296 | tf_op jit(solution)/shard_map/ppermute | solution.py:31
  49.0 1.2 %collective-permute-start.7 = (f32[32,32]{1,0:T(8,128)S(1)}, f32[32,32]{1,0:T(8,128)S(1)}, u32[]{:S(2)}, u32[]{:S(2)}) collective-permute-start(f32[32,32]{1,0:T(8,128)S(1)} %add_add_fusion.2.refs_0_), channel_id=1, source_target_pairs={{0,1},{1,0},{2,3},{3,2},{4,5},{5,4},{6,7},{7,6},{8,9},{9,8},{10,11... | collective-permute-start | bytes 12296 | tf_op jit(solution)/shard_map/ppermute | solution.py:31
  57.2 16.4 %collective-permute-start.16 = (f32[32,32]{1,0:T(8,128)S(1)}, f32[32,32]{1,0:T(8,128)S(1)}, u32[]{:S(2)}, u32[]{:S(2)}) collective-permute-start(f32[32,32]{1,0:T(8,128)S(1)} %get-tuple-element.45), channel_id=1, source_target_pairs={{0,12},{1,13},{2,14},{3,15},{4,8},{5,9},{6,10},{7,11},{8,4},{9,5},... | collective-permute-start | bytes 12296 | tf_op jit(solution)/shard_map/ppermute | solution.py:31
  60.9 12.7 %collective-permute-start.15 = (f32[32,32]{1,0:T(8,128)S(1)}, f32[32,32]{1,0:T(8,128)S(1)}, u32[]{:S(2)}, u32[]{:S(2)}) collective-permute-start(f32[32,32]{1,0:T(8,128)S(1)} %get-tuple-element.45), channel_id=1, source_target_pairs={{0,8},{1,9},{2,10},{3,11},{4,12},{5,13},{6,14},{7,15},{8,0},{9,1},... | collective-permute-start | bytes 12296 | tf_op jit(solution)/shard_map/ppermute | solution.py:31
  60.9 13.3 %collective-permute-start.14 = (f32[32,32]{1,0:T(8,128)S(1)}, f32[32,32]{1,0:T(8,128)S(1)}, u32[]{:S(2)}, u32[]{:S(2)}) collective-permute-start(f32[32,32]{1,0:T(8,128)S(1)} %get-tuple-element.45), channel_id=1, source_target_pairs={{0,4},{1,5},{2,6},{3,7},{4,0},{5,1},{6,2},{7,3},{8,12},{9,13},{10,... | collective-permute-start | bytes 12296 | tf_op jit(solution)/shard_map/ppermute | solution.py:31
  69.4 20.3 %collective-permute-start.22 = (f32[32,1536]{1,0:T(8,128)S(1)}, f32[32,1536]{1,0:T(8,128)S(1)}, u32[]{:S(2)}, u32[]{:S(2)}) collective-permute-start(f32[32,1536]{1,0:T(8,128)S(1)} %get-tuple-element.52), channel_id=1, source_target_pairs={{0,4},{1,5},{2,6},{3,7},{4,0},{5,1},{6,2},{7,3},{8,12},{9,13},{10,... | collective-permute-start | bytes 589832 | tf_op jit(solution)/shard_map/ppermute | solution.py:31
  70.7 19.0 %collective-permute-start.23 = (f32[32,1536]{1,0:T(8,128)S(1)}, f32[32,1536]{1,0:T(8,128)S(1)}, u32[]{:S(2)}, u32[]{:S(2)}) collective-permute-start(f32[32,1536]{1,0:T(8,128)S(1)} %get-tuple-element.53), channel_id=1, source_target_pairs={{0,8},{1,9},{2,10},{3,11},{4,12},{5,13},{6,14},{7,15},{8,0},{9,1},... | collective-permute-start | bytes 589832 | tf_op jit(solution)/shard_map/ppermute | solution.py:31
  73.6 16.0 %collective-permute-start.20 = (f32[32,1536]{1,0:T(8,128)S(1)}, f32[32,1536]{1,0:T(8,128)S(1)}, u32[]{:S(2)}, u32[]{:S(2)}) collective-permute-start(f32[32,1536]{1,0:T(8,128)S(1)} %get-tuple-element.50), channel_id=1, source_target_pairs={{0,1},{1,0},{2,3},{3,2},{4,5},{5,4},{6,7},{7,6},{8,9},{9,8},{10,11... | collective-permute-start | bytes 589832 | tf_op jit(solution)/shard_map/ppermute | solution.py:31
  73.6 16.0 %collective-permute-start.21 = (f32[32,1536]{1,0:T(8,128)S(1)}, f32[32,1536]{1,0:T(8,128)S(1)}, u32[]{:S(2)}, u32[]{:S(2)}) collective-permute-start(f32[32,1536]{1,0:T(8,128)S(1)} %get-tuple-element.51), channel_id=1, source_target_pairs={{0,2},{1,3},{2,0},{3,1},{4,6},{5,7},{6,4},{7,5},{8,10},{9,11},{10,... | collective-permute-start | bytes 589832 | tf_op jit(solution)/shard_map/ppermute | solution.py:31
  74.2 6.6 %collective-permute-start.19 = (f32[32,32]{1,0:T(8,128)S(1)}, f32[32,32]{1,0:T(8,128)S(1)}, u32[]{:S(2)}, u32[]{:S(2)}) collective-permute-start(f32[32,32]{1,0:T(8,128)S(1)} %add_add_fusion.1.refs_0_), channel_id=1, source_target_pairs={{0,3},{1,2},{2,1},{3,0},{4,7},{5,6},{6,5},{7,4},{8,11},{9,10},{10,... | collective-permute-start | bytes 12296 | tf_op jit(solution)/shard_map/ppermute | solution.py:31
  80.8 3.7 %collective-permute-start.18 = (f32[32,32]{1,0:T(8,128)S(1)}, f32[32,32]{1,0:T(8,128)S(1)}, u32[]{:S(2)}, u32[]{:S(2)}) collective-permute-start(f32[32,32]{1,0:T(8,128)S(1)} %add_add_fusion.1.refs_0_), channel_id=1, source_target_pairs={{0,2},{1,3},{2,0},{3,1},{4,6},{5,7},{6,4},{7,5},{8,10},{9,11},{10,... | collective-permute-start | bytes 12296 | tf_op jit(solution)/shard_map/ppermute | solution.py:31
  84.5 1.2 %collective-permute-start.17 = (f32[32,32]{1,0:T(8,128)S(1)}, f32[32,32]{1,0:T(8,128)S(1)}, u32[]{:S(2)}, u32[]{:S(2)}) collective-permute-start(f32[32,32]{1,0:T(8,128)S(1)} %add_add_fusion.1.refs_0_), channel_id=1, source_target_pairs={{0,1},{1,0},{2,3},{3,2},{4,5},{5,4},{6,7},{7,6},{8,9},{9,8},{10,11... | collective-permute-start | bytes 12296 | tf_op jit(solution)/shard_map/ppermute | solution.py:31
  92.7 5.5 %collective-permute-start.26 = (f32[32,32]{1,0:T(8,128)S(1)}, f32[32,32]{1,0:T(8,128)S(1)}, u32[]{:S(2)}, u32[]{:S(2)}) collective-permute-start(f32[32,32]{1,0:T(8,128)S(1)} %get-tuple-element.55), channel_id=1, source_target_pairs={{0,12},{1,13},{2,14},{3,15},{4,8},{5,9},{6,10},{7,11},{8,4},{9,5},... | collective-permute-start | bytes 12296 | tf_op jit(solution)/shard_map/ppermute | solution.py:31
  92.9 5.3 %collective-permute-start.25 = (f32[32,32]{1,0:T(8,128)S(1)}, f32[32,32]{1,0:T(8,128)S(1)}, u32[]{:S(2)}, u32[]{:S(2)}) collective-permute-start(f32[32,32]{1,0:T(8,128)S(1)} %get-tuple-element.55), channel_id=1, source_target_pairs={{0,8},{1,9},{2,10},{3,11},{4,12},{5,13},{6,14},{7,15},{8,0},{9,1},... | collective-permute-start | bytes 12296 | tf_op jit(solution)/shard_map/ppermute | solution.py:31
  94.3 4.6 %collective-permute-start.24 = (f32[32,32]{1,0:T(8,128)S(1)}, f32[32,32]{1,0:T(8,128)S(1)}, u32[]{:S(2)}, u32[]{:S(2)}) collective-permute-start(f32[32,32]{1,0:T(8,128)S(1)} %get-tuple-element.55), channel_id=1, source_target_pairs={{0,4},{1,5},{2,6},{3,7},{4,0},{5,1},{6,2},{7,3},{8,12},{9,13},{10,... | collective-permute-start | bytes 12296 | tf_op jit(solution)/shard_map/ppermute | solution.py:31
  98.8 3.2 %collective-permute-start.29 = (f32[32,32]{1,0:T(8,128)S(1)}, f32[32,32]{1,0:T(8,128)S(1)}, u32[]{:S(2)}, u32[]{:S(2)}) collective-permute-start(f32[32,32]{1,0:T(8,128)S(1)} %add_add_fusion.refs_0_), channel_id=1, source_target_pairs={{0,3},{1,2},{2,1},{3,0},{4,7},{5,6},{6,5},{7,4},{8,11},{9,10},{10,... | collective-permute-start | bytes 12296 | tf_op jit(solution)/shard_map/ppermute | solution.py:31
  98.9 3.8 %collective-permute-start.28 = (f32[32,32]{1,0:T(8,128)S(1)}, f32[32,32]{1,0:T(8,128)S(1)}, u32[]{:S(2)}, u32[]{:S(2)}) collective-permute-start(f32[32,32]{1,0:T(8,128)S(1)} %add_add_fusion.refs_0_), channel_id=1, source_target_pairs={{0,2},{1,3},{2,0},{3,1},{4,6},{5,7},{6,4},{7,5},{8,10},{9,11},{10,... | collective-permute-start | bytes 12296 | tf_op jit(solution)/shard_map/ppermute | solution.py:31
  99.6 3.1 %collective-permute-start.27 = (f32[32,32]{1,0:T(8,128)S(1)}, f32[32,32]{1,0:T(8,128)S(1)}, u32[]{:S(2)}, u32[]{:S(2)}) collective-permute-start(f32[32,32]{1,0:T(8,128)S(1)} %add_add_fusion.refs_0_), channel_id=1, source_target_pairs={{0,1},{1,0},{2,3},{3,2},{4,5},{5,4},{6,7},{7,6},{8,9},{9,8},{10,11... | collective-permute-start | bytes 12296 | tf_op jit(solution)/shard_map/ppermute | solution.py:31

commit v2 on v1

--- a/solution.py
+++ b/solution.py
@@ -11,6 +11,9 @@
 LANES = 128
 PACK = 4
 CHUNK = 1024
+SUBLANES = 8
+STEP = 4
+COPIES = 8
 F32 = jnp.float32
 BF16 = jnp.bfloat16
 VMEM = pl.BlockSpec(memory_space=pltpu.VMEM)
@@ -49,14 +52,42 @@
     col = lax.broadcasted_iota(jnp.int32, (n, n), 1)
     eye = (row == col).astype(F32)
     both = jnp.concatenate([gram, eye, jnp.zeros((n, LANES - 2 * n), F32)], axis=1)
-    rows = lax.broadcasted_iota(jnp.int32, (n, LANES), 0)
-    scale = jnp.zeros((n, LANES), F32)
-    for j in range(n):
-        pivot = both[j : j + 1, j : j + 1]
-        factor = jnp.broadcast_to(both[:, j : j + 1] / pivot, (n, LANES))
-        scale = jnp.where(rows == j, jnp.broadcast_to(1.0 / jnp.sqrt(pivot), (n, LANES)), scale)
-        both = both - jnp.where(rows > j, factor, 0.0) * both[j : j + 1, :]
-    return (both * scale)[:, n : 2 * n]
+    full = (SUBLANES, LANES)
+    parts = [both[q : q + SUBLANES] for q in range(0, n, SUBLANES)]
+    sub = lax.broadcasted_iota(jnp.int32, full, 0)
+    scales = [jnp.zeros(full, F32) for _ in parts]
+    for j in range(0, n, STEP):
+        home, at = j // SUBLANES, j % SUBLANES
+        live = range(home, len(parts))
+        cols = [
+            {q: jnp.broadcast_to(parts[q][:, j + a : j + a + 1], full) for q in live}
+            for a in range(STEP)
+        ]
+        rows = [jnp.broadcast_to(parts[home][at + a : at + a + 1], full) for a in range(STEP)]
+        entry = {
+            (a, b): jnp.broadcast_to(cols[b][home][at + a : at + a + 1], full)
+            for a in range(STEP)
+            for b in range(a + 1)
+        }
+        for a in range(STEP):
+            over = 1.0 / entry[a, a]
+            ratio = {c: entry[c, a] * over for c in range(a + 1, STEP)}
+            for c in range(a + 1, STEP):
+                for d in range(a + 1, c + 1):
+                    entry[c, d] = entry[c, d] - ratio[c] * entry[d, a]
+            for c in range(a + 1, STEP):
+                rows[c] = rows[c] - ratio[c] * rows[a]
+                for q in live:
+                    cols[c][q] = cols[c][q] - ratio[c] * cols[a][q]
+            root = 1.0 / jnp.sqrt(entry[a, a])
+            scales[home] = jnp.where(sub == at + a, root, scales[home])
+            for q in live:
+                factor = cols[a][q] * over
+                if q == home:
+                    factor = jnp.where(sub > at + a, factor, 0.0)
+                parts[q] = parts[q] - factor * rows[a]
+    done = jnp.concatenate([p * s for p, s in zip(parts, scales)], axis=0)
+    return done[:, n : 2 * n]
 
 
 def apply_matrix(inverse):
@@ -80,8 +111,7 @@
 
 
 def gram_of(parts, total_states):
-    (a, b), (c, d) = parts[:2], parts[2:]
-    return ((a + b) + (c + d)) / total_states
+    return paired_sum(parts) / total_states
 
 
 def transposed_into(source, rows_ref):
@@ -115,16 +145,16 @@
         out[:, t * LANES : (t + 1) * LANES] = value.astype(out.dtype)
 
 
-def gather_kernel(unroll, row_ref, part_ref, rows_ref, *rest):
-    gathered_into(unroll, row_ref, part_ref, rows_ref, rest[-1], rest[:-1])
-
-
-def gather_colours(rows, row_list, part_list, count, dtype):
+def gather_kernel(row_ref, part_ref, rows_ref, *rest):
+    gathered_into(64, row_ref, part_ref, rows_ref, rest[-1], rest[:-1])
+
+
+def gather_colours(rows, row_list, part_list, count):
     indices = row_list.shape[0]
     columns = LANES // PACK
     return pl.pallas_call(
-        functools.partial(gather_kernel, 64),
-        out_shape=[vmem_out((columns, indices // count), dtype)] * count,
+        gather_kernel,
+        out_shape=[vmem_out((columns, indices // count), F32)] * count,
         in_specs=[SMEM, VMEM, VMEM],
         out_specs=[VMEM] * count,
         scratch_shapes=[pltpu.VMEM((indices, LANES), F32)],
@@ -134,19 +164,45 @@
     )(row_list, in_vmem(part_list), in_vmem(rows))
 
 
-def start_rows_kernel(block_ref, rows_ref):
-    transposed_into(block_ref, rows_ref)
-
-
-def start_rows(block):
-    return pl.pallas_call(
-        start_rows_kernel,
-        out_shape=vmem_out((block.shape[1] // PACK, LANES), F32),
-        in_specs=[VMEM],
-        out_specs=VMEM,
-        compiler_params=PARAMS,
-        name="start_rows",
-    )(in_vmem(block))
+def start_kernel(count, first, make_rows, row_ref, part_ref, source_ref, tiles_ref, *refs):
+    outs, kept_ref, refs = refs[:count], refs[count], refs[count + 1 :]
+    picked, sems = refs[-2:]
+    size = kept_ref.shape[0] // COPIES
+    copies = [
+        pltpu.make_async_copy(
+            tiles_ref.at[pl.ds(first + c * size, size)],
+            kept_ref.at[pl.ds(c * size, size)],
+            sems.at[c],
+        )
+        for c in range(COPIES)
+    ]
+    for copy in copies:
+        copy.start()
+    rows_ref = source_ref
+    if make_rows:
+        rows_ref = refs[0]
+        transposed_into(source_ref, rows_ref)
+    gathered_into(64, row_ref, part_ref, rows_ref, picked, outs)
+    for copy in copies:
+        copy.wait()
+
+
+def start_gather(source, row_list, part_list, count, tiles, first, kept, make_rows):
+    indices = row_list.shape[0]
+    columns = LANES // PACK
+    outs = [vmem_out((columns, indices // count), BF16)] * count
+    outs.append(vmem_out((kept, *tiles.shape[1:]), tiles.dtype))
+    if make_rows:
+        outs.append(vmem_out((source.shape[1] // PACK, LANES), F32))
+    return pl.pallas_call(
+        functools.partial(start_kernel, count, first, make_rows),
+        out_shape=outs,
+        in_specs=[SMEM, VMEM, VMEM, pl.BlockSpec(memory_space=pl.ANY)],
+        out_specs=[VMEM] * len(outs),
+        scratch_shapes=[pltpu.VMEM((indices, LANES), F32), pltpu.SemaphoreType.DMA((COPIES,))],
+        compiler_params=PARAMS,
+        name="start_gather",
+    )(row_list, in_vmem(part_list), in_vmem(source), tiles)
 
 
 def own_slots(block_ref, tiles_ref, own_ref):
@@ -209,7 +265,7 @@
         rows_ref, refs = refs[0], refs[1:]
     source, total = refs
     columns, states = block_ref.shape
-    slots, tile_size, _ = tiles_ref.shape
+    tile_size = tiles_ref.shape[1]
     first = states // tile_size
     live = count_ref[0]
 
@@ -243,7 +299,7 @@
                 ],
                 axis=0,
             )
-            weights = tiles_ref[pl.ds(base + u, 2)].reshape(2 * tile_size, tile_size)
+            weights = tiles_ref[pl.ds(base + u - first, 2)].reshape(2 * tile_size, tile_size)
             both = jnp.dot(pair, weights, preferred_element_type=F32)
             terms += [both[:columns], both[columns:]]
         for u in range(group):
@@ -272,8 +328,7 @@
 
 def product(src, dst, count, block, own, ghosts, matrix, tiles, with_rows):
     columns, states = block.shape
-    slots, tile_size, _ = tiles.shape
-    rest = slots - states // tile_size
+    rest, tile_size, _ = tiles.shape
     group = 64
     while rest % group:
         group //= 2
@@ -321,14 +376,13 @@
     return rounds[::-1]
 
 
-def gram_parts(gram, rounds):
-    parts = [gram]
-    for masks in rounds:
-        if len(parts) > 1:
-            gram = (parts[0] + parts[1]) + (parts[2] + parts[3])
-        parts = [gram] + [swapped(gram, mask) for mask in masks]
-        parts += [jnp.zeros_like(gram)] * (4 - len(parts))
-    return parts
+def paired_sum(parts):
+    return (parts[0] + parts[1]) + (parts[2] + parts[3])
+
+
+def gram_round(gram, masks):
+    parts = [gram] + [swapped(gram, mask) for mask in masks]
+    return parts + [jnp.zeros_like(gram)] * (4 - len(parts))
 
 
 def on_device(start_block, tiles, tile_src, tile_dst, slot_count, send_rows):
@@ -351,27 +405,41 @@
 
     listed = [lists_of(far), lists_of(near)]
 
-    def exchanged(rows, dtype):
-        ghosts = [None] * len(masks)
-        for colours, (row_list, part_list) in zip((far, near), listed):
-            picked = gather_colours(rows, row_list, part_list, len(colours), dtype)
-            for colour, x in zip(colours, picked):
-                ghosts[colour] = swapped(x, masks[colour])
-        return ghosts
-
-    ghosts = exchanged(start_rows(start_block), BF16)
+    def sent(ghosts, colours, picked):
+        for colour, x in zip(colours, picked):
+            ghosts[colour] = swapped(x, masks[colour])
+
+    own_count = states // tiles.shape[1]
+    ghosts = [None] * len(masks)
+    *picked, rest_tiles, start_rows = start_gather(
+        start_block, *listed[0], len(far), tiles, own_count, tiles.shape[0] - own_count, True
+    )
+    sent(ghosts, far, picked)
+    *picked, own_tiles = start_gather(
+        start_rows, *listed[1], len(near), tiles, 0, own_count, False
+    )
+    sent(ghosts, near, picked)
     block, matrix = start_block, None
-    own = first_own(start_block, tiles)
+    own = first_own(start_block, own_tiles)
     for turn in range(ITERS):
         last = turn == ITERS - 1
         stacked, gram, *rows = product(
-            tile_src, tile_dst, slot_count, block, own, ghosts, matrix, tiles, not last
+            tile_src, tile_dst, slot_count, block, own, ghosts, matrix, rest_tiles, not last
         )
-        parts = gram_parts(gram, rounds)
+        for masks_now in rounds[:-1]:
+            gram = paired_sum(gram_round(gram, masks_now))
         if last:
-            return final(parts, stacked, total_states)
-        ghosts = exchanged(rows[0], F32)
-        block, matrix, own = later_own(parts, stacked, tiles, total_states)
+            return final(gram_round(gram, rounds[-1]), stacked, total_states)
+        ghosts = [None] * len(masks)
+        picked = gather_colours(rows[0], *listed[0], len(far))
+        gram, near_rows, *picked = lax.optimization_barrier((gram, rows[0], *picked))
+        parts = gram_round(gram, rounds[-1])
+        sent(ghosts, far, picked)
+        picked = gather_colours(near_rows, *listed[1], len(near))
+        gathered = lax.optimization_barrier((*parts, *picked))
+        parts, picked = gathered[: len(parts)], gathered[len(parts) :]
+        sent(ghosts, near, picked)
+        block, matrix, own = later_own(parts, stacked, own_tiles, total_states)
 
 
 def solution(mesh):

time: 107 us -> 106 us (level)
  local copies, waits for them, and re-layouts: 5.17 us -> 9.17 us
  Pallas kernels: 44.5 us -> 41.4 us
  waiting for transfers between devices: 23.2 us -> 21.7 us
    unnamed x14 -> x12, local copies, waits for them, and re-layouts: 5.05 us -> 9.05 us
    pallas_call x2, Pallas kernels: 7.79 us -> 4.99 us  [later_own(): pl.pallas_call(functools.partial(later_own_kernel, total_states), out_sha...]
    ppermute x30, waiting for transfers between devices: 23.2 us -> 21.7 us  [swapped(): return lax.ppermute(x, 'dom', [(i, i ^ mask) for i in range(size)])]
    pallas_call x1, Pallas kernels: 4.34 us -> 2.94 us  [final(): pl.pallas_call(functools.partial(final_kernel, total_states), out_shape=j...]
    pallas_call x7 -> x6, Pallas kernels: 22.8 us -> 23.7 us  [the longest x4 15.3 us: gather_colours(): pl.pallas_call(gather_kernel, out_shape=[vmem_out((columns, indices // co...]
  transfers between devices with their start and end apart: 30 -> 30, of which waited for: 10 -> 9; matrix products, arithmetic and copies ran while one was open for 0% -> 0% of each run, Pallas kernels for 26% -> 23%
where the time goes in v2:
time: 106 us; the launch traced here: 107 us
  Pallas kernels  41.4 us (39%)
  starting transfers between devices  32.5 us (31%)
  waiting for transfers between devices  21.7 us (20%)
  local copies, waits for them, and re-layouts  9.17 us (9%)
    ppermute x30, starting transfers between devices, swapped(): return lax.ppermute(x, 'dom', [(i, i ^ mask) for i in range(size)])  32.5 us
    ppermute x30, waiting for transfers between devices, swapped(): return lax.ppermute(x, 'dom', [(i, i ^ mask) for i in range(size)])  21.7 us
    pallas_call x4, Pallas kernels, gather_colours(): pl.pallas_call(gather_kernel, out_shape=[vmem_out((columns, indices // co...  15.3 us
    pallas_call x3, Pallas kernels, product(): pl.pallas_call(functools.partial(product_kernel, len(ghosts), group, with...  9.12 us
    unnamed x12, local copies, waits for them, and re-layouts  9.05 us
    pallas_call x2, Pallas kernels, start_gather(): pl.pallas_call(functools.partial(start_kernel, count, first, make_rows),...  8.35 us
    pallas_call x2, Pallas kernels, later_own(): pl.pallas_call(functools.partial(later_own_kernel, total_states), out_sha...  4.99 us
    pallas_call x1, Pallas kernels, final(): pl.pallas_call(functools.partial(final_kernel, total_states), out_shape=j...  2.94 us
  transfers between devices with their start and end apart: 30, of which 9 were waited for; matrix products, arithmetic and copies ran while one was open for 0% of the time, Pallas kernels for 23%

profile of v2, /device:TPU:0, one launch (start us, length us, event | category | flops | bytes accessed | tf_op | source)
XLA Modules:
  0.0 106.5 jit_solution(8828655151113944050)
XLA Ops:
  0.0 0.8 add_select_fusion
  0.8 0.1 slice_reduce_fusion.1
  1.0 0.0 copy-start
  1.0 4.0 %copy-done = bf16[320,128,128]{2,1,0:T(8,128)(2,1)S(1)} copy-done((bf16[320,128,128]{2,1,0:T(8,128)(2,1)S(1)}, bf16[320,128,128]{2,1,0:T(8,128)(2,1)}, u32[]{:S(2)}) %copy-start) | copy-done | bytes 10485784
  5.0 1.0 copy-done.2
  6.0 4.5 %start_gather.2 = (bf16[32,1536]{1,0:T(8,128)(2,1)S(1)}, bf16[32,1536]{1,0:T(8,128)(2,1)S(1)}, bf16[256,128,128]{2,1,0:T(8,128)(2,1)S(1)}, f32[2048,128]{1,0:T(8,128)S(1)}) custom-call(s32[3072]{0:T(1024)S(1)} %pad_add_fusion.2.row_ref, s32[24,128]{1,0:T(8,128)S(1)} %pad_add_fusion.3.part_ref, bf16[32,8192]{1,0:T(8,128)(2,1)S(1)} %copy-done.2, ...), custom_call_target="tpu_custom_call" | custom-call | tf_op jit(solution)/shard_map/start_gather/pallas_call | solution.py:197
  10.5 3.1 %collective-permute-start.2 = (bf16[32,1536]{1,0:T(8,128)(2,1)S(1)}, bf16[32,1536]{1,0:T(8,128)(2,1)S(1)}, u32[]{:S(2)}, u32[]{:S(2)}) collective-permute-start(bf16[32,1536]{1,0:T(8,128)(2,1)S(1)} %get-tuple-element.58), channel_id=1, source_target_pairs={{0,4},{1,5},{2,6},{3,7},{4,0},{5,1},{6,2},{7,3},{8,12},{9,13},{10,... | collective-permute-start | bytes 294920 | tf_op jit(solution)/shard_map/ppermute | solution.py:34
  13.6 2.6 %collective-permute-start.3 = (bf16[32,1536]{1,0:T(8,128)(2,1)S(1)}, bf16[32,1536]{1,0:T(8,128)(2,1)S(1)}, u32[]{:S(2)}, u32[]{:S(2)}) collective-permute-start(bf16[32,1536]{1,0:T(8,128)(2,1)S(1)} %get-tuple-element.59), channel_id=1, source_target_pairs={{0,8},{1,9},{2,10},{3,11},{4,12},{5,13},{6,14},{7,15},{8,0},{9,1},... | collective-permute-start | bytes 294920 | tf_op jit(solution)/shard_map/ppermute | solution.py:34
  16.2 0.0 copy-start.1
  16.2 4.0 %copy-done.1 = bf16[320,128,128]{2,1,0:T(8,128)(2,1)S(1)} copy-done((bf16[320,128,128]{2,1,0:T(8,128)(2,1)S(1)}, bf16[320,128,128]{2,1,0:T(8,128)(2,1)}, u32[]{:S(2)}) %copy-start.1) | copy-done | bytes 10485784
  20.2 3.9 %start_gather.3 = (bf16[32,1536]{1,0:T(8,128)(2,1)S(1)}, bf16[32,1536]{1,0:T(8,128)(2,1)S(1)}, bf16[64,128,128]{2,1,0:T(8,128)(2,1)S(1)}) custom-call(s32[3072]{0:T(1024)S(1)} %pad_add_fusion.row_ref, s32[24,128]{1,0:T(8,128)S(1)} %pad_add_fusion.1.part_ref, f32[2048,128]{1,0:T(8,128)S(1)} %get-tuple-element.54.source_ref, bf16[320,128,128]{2,1,0:T(8,128)(2,1)S(1)} %copy-done.1), custom_call_target="tpu_custom_call" | custom-call | tf_op jit(solution)/shard_map/start_gather/pallas_call | solution.py:197
  24.1 0.0 copy-start.4
  24.1 0.0 copy-start.5
  24.1 0.1 collective-permute-start
  24.2 1.6 %collective-permute-start.1 = (bf16[32,1536]{1,0:T(8,128)(2,1)S(1)}, bf16[32,1536]{1,0:T(8,128)(2,1)S(1)}, u32[]{:S(2)}, u32[]{:S(2)}) collective-permute-start(bf16[32,1536]{1,0:T(8,128)(2,1)S(1)} %get-tuple-element.57), channel_id=1, source_target_pairs={{0,2},{1,3},{2,0},{3,1},{4,6},{5,7},{6,4},{7,5},{8,10},{9,11},{10,... | collective-permute-start | bytes 294920 | tf_op jit(solution)/shard_map/ppermute | solution.py:34
  26.5 0.7 first_own.1.refs_4_
  27.1 0.0 collective-permute-done.3.refs_8_
  27.1 0.0 collective-permute-done.refs_5_
  27.1 2.3 %collective-permute-done.1.refs_6_ = bf16[32,1536]{1,0:T(8,128)(2,1)S(1)} collective-permute-done((bf16[32,1536]{1,0:T(8,128)(2,1)S(1)}, bf16[32,1536]{1,0:T(8,128)(2,1)S(1)}, u32[]{:S(2)}, u32[]{:S(2)}) %collective-permute-start.1) | collective-permute-done | bytes 98336 | tf_op jit(solution)/shard_map/ppermute | solution.py:34
  29.4 2.8 %product.3 = (bf16[96,8192]{1,0:T(8,128)(2,1)S(1)}, f32[32,32]{1,0:T(8,128)S(1)}, f32[2048,128]{1,0:T(8,128)S(1)}) custom-call(s32[320]{0:T(512)S(1)} %copy-done.4, s32[320]{0:T(512)S(1)} %copy-done.5, s32[1]{0:T(128)S(6)} %copy.7.refs_2_, bf16[32,8192]{1,0:T(8,128)(2,1)S(1)} %copy-done.3, f32[32,8192]{1,0:T(8,128)S(1)} %first_own.1.refs_4_, ...), custom_call_target="tpu_custom_call" | custom-call | tf_op jit(solution)/shard_map/product/pallas_call | solution.py:340
  32.2 1.2 %collective-permute-start.6 = (f32[32,32]{1,0:T(8,128)S(1)}, f32[32,32]{1,0:T(8,128)S(1)}, u32[]{:S(2)}, u32[]{:S(2)}) collective-permute-start(f32[32,32]{1,0:T(8,128)S(1)} %get-tuple-element.61), channel_id=1, source_target_pairs={{0,12},{1,13},{2,14},{3,15},{4,8},{5,9},{6,10},{7,11},{8,4},{9,5},... | collective-permute-start | bytes 12296 | tf_op jit(solution)/shard_map/ppermute | solution.py:34
  33.4 0.1 collective-permute-start.5
  33.6 3.1 %collective-permute-start.4 = (f32[32,32]{1,0:T(8,128)S(1)}, f32[32,32]{1,0:T(8,128)S(1)}, u32[]{:S(2)}, u32[]{:S(2)}) collective-permute-start(f32[32,32]{1,0:T(8,128)S(1)} %get-tuple-element.61), channel_id=1, source_target_pairs={{0,4},{1,5},{2,6},{3,7},{4,0},{5,1},{6,2},{7,3},{8,12},{9,13},{10,... | collective-permute-start | bytes 12296 | tf_op jit(solution)/shard_map/ppermute | solution.py:34
  36.6 3.8 %gather_rows.4 = (f32[32,1536]{1,0:T(8,128)S(1)}, f32[32,1536]{1,0:T(8,128)S(1)}) custom-call(s32[3072]{0:T(1024)S(1)} %pad_add_fusion.2.row_ref, s32[24,128]{1,0:T(8,128)S(1)} %pad_add_fusion.3.part_ref, f32[2048,128]{1,0:T(8,128)S(1)} %get-tuple-element.66.rows_ref), custom_call_target="tpu_custom_call" | custom-call | bytes 8388608 | tf_op jit(solution)/shard_map/gather_rows/pallas_call | solution.py:155
  40.5 0.0 collective-permute-done.5
  40.5 0.0 collective-permute-done.4
  40.5 0.1 collective-permute-start.9
  40.6 1.6 %collective-permute-start.8 = (f32[32,32]{1,0:T(8,128)S(1)}, f32[32,32]{1,0:T(8,128)S(1)}, u32[]{:S(2)}, u32[]{:S(2)}) collective-permute-start(f32[32,32]{1,0:T(8,128)S(1)} %add_add_fusion.2.refs_0_), channel_id=1, source_target_pairs={{0,2},{1,3},{2,0},{3,1},{4,6},{5,7},{6,4},{7,5},{8,10},{9,11},{10,... | collective-permute-start | bytes 12296 | tf_op jit(solution)/shard_map/ppermute | solution.py:34
  42.2 0.3 collective-permute-start.7
  42.4 3.8 %gather_rows.5 = (f32[32,1536]{1,0:T(8,128)S(1)}, f32[32,1536]{1,0:T(8,128)S(1)}) custom-call(s32[3072]{0:T(1024)S(1)} %pad_add_fusion.row_ref, s32[24,128]{1,0:T(8,128)S(1)} %pad_add_fusion.1.part_ref, f32[2048,128]{1,0:T(8,128)S(1)} %get-tuple-element.66.rows_ref), custom_call_target="tpu_custom_call" | custom-call | bytes 8388608 | tf_op jit(solution)/shard_map/gather_rows/pallas_call | solution.py:155
  46.3 0.1 collective-permute-start.12
  46.4 1.7 %collective-permute-start.13 = (f32[32,1536]{1,0:T(8,128)S(1)}, f32[32,1536]{1,0:T(8,128)S(1)}, u32[]{:S(2)}, u32[]{:S(2)}) collective-permute-start(f32[32,1536]{1,0:T(8,128)S(1)} %get-tuple-element.79), channel_id=1, source_target_pairs={{0,8},{1,9},{2,10},{3,11},{4,12},{5,13},{6,14},{7,15},{8,0},{9,1},... | collective-permute-start | bytes 589832 | tf_op jit(solution)/shard_map/ppermute | solution.py:34
  48.1 0.0 collective-permute-done.9.refs_3_
  48.1 0.1 collective-permute-start.10
  48.2 0.6 collective-permute-start.11
  48.8 2.5 %later_own.2 = (bf16[32,8192]{1,0:T(8,128)(2,1)S(1)}, bf16[96,96]{1,0:T(8,128)(2,1)S(1)}, f32[32,8192]{1,0:T(8,128)S(1)}) custom-call(f32[32,32]{1,0:T(8,128)S(1)} %add_add_fusion.2.refs_0_, f32[32,32]{1,0:T(8,128)S(1)} %collective-permute-done.7.refs_1_, f32[32,32]{1,0:T(8,128)S(1)} %collective-permute-done.8.refs_2_, ...), custom_call_target="tpu_custom_call" | custom-call | tf_op jit(solution)/shard_map/later_own/pallas_call | solution.py:242
  51.3 4.8 %collective-permute-done.12.refs_7_ = f32[32,1536]{1,0:T(8,128)S(1)} collective-permute-done((f32[32,1536]{1,0:T(8,128)S(1)}, f32[32,1536]{1,0:T(8,128)S(1)}, u32[]{:S(2)}, u32[]{:S(2)}) %collective-permute-start.12) | collective-permute-done | bytes 196640 | tf_op jit(solution)/shard_map/ppermute | solution.py:34
  56.1 2.5 %collective-permute-done.13.refs_8_ = f32[32,1536]{1,0:T(8,128)S(1)} collective-permute-done((f32[32,1536]{1,0:T(8,128)S(1)}, f32[32,1536]{1,0:T(8,128)S(1)}, u32[]{:S(2)}, u32[]{:S(2)}) %collective-permute-start.13) | collective-permute-done | bytes 196640 | tf_op jit(solution)/shard_map/ppermute | solution.py:34
  58.7 3.3 %product.4 = (bf16[96,8192]{1,0:T(8,128)(2,1)S(1)}, f32[32,32]{1,0:T(8,128)S(1)}, f32[2048,128]{1,0:T(8,128)S(1)}) custom-call(s32[320]{0:T(512)S(1)} %copy-done.4, s32[320]{0:T(512)S(1)} %copy-done.5, s32[1]{0:T(128)S(6)} %copy.7.refs_2_, bf16[32,8192]{1,0:T(8,128)(2,1)S(1)} %get-tuple-element.74.refs_3_, f32[32,8192]{1,0:T(8,128)S(1)} %get-tuple-element.75.refs_4_, ...), custom_call_target="tpu_custom_call" | custom-call | tf_op jit(solution)/shard_map/product/pallas_call | solution.py:340
  62.0 2.6 %collective-permute-start.16 = (f32[32,32]{1,0:T(8,128)S(1)}, f32[32,32]{1,0:T(8,128)S(1)}, u32[]{:S(2)}, u32[]{:S(2)}) collective-permute-start(f32[32,32]{1,0:T(8,128)S(1)} %get-tuple-element.81), channel_id=1, source_target_pairs={{0,12},{1,13},{2,14},{3,15},{4,8},{5,9},{6,10},{7,11},{8,4},{9,5},... | collective-permute-start | bytes 12296 | tf_op jit(solution)/shard_map/ppermute | solution.py:34
  64.6 1.8 %collective-permute-start.14 = (f32[32,32]{1,0:T(8,128)S(1)}, f32[32,32]{1,0:T(8,128)S(1)}, u32[]{:S(2)}, u32[]{:S(2)}) collective-permute-start(f32[32,32]{1,0:T(8,128)S(1)} %get-tuple-element.81), channel_id=1, source_target_pairs={{0,4},{1,5},{2,6},{3,7},{4,0},{5,1},{6,2},{7,3},{8,12},{9,13},{10,... | collective-permute-start | bytes 12296 | tf_op jit(solution)/shard_map/ppermute | solution.py:34
  66.4 3.8 %gather_rows.6 = (f32[32,1536]{1,0:T(8,128)S(1)}, f32[32,1536]{1,0:T(8,128)S(1)}) custom-call(s32[3072]{0:T(1024)S(1)} %pad_add_fusion.2.row_ref, s32[24,128]{1,0:T(8,128)S(1)} %pad_add_fusion.3.part_ref, f32[2048,128]{1,0:T(8,128)S(1)} %get-tuple-element.86.rows_ref), custom_call_target="tpu_custom_call" | custom-call | bytes 8388608 | tf_op jit(solution)/shard_map/gather_rows/pallas_call | solution.py:155
  70.3 0.1 collective-permute-start.19
  70.4 1.3 %collective-permute-start.18 = (f32[32,32]{1,0:T(8,128)S(1)}, f32[32,32]{1,0:T(8,128)S(1)}, u32[]{:S(2)}, u32[]{:S(2)}) collective-permute-start(f32[32,32]{1,0:T(8,128)S(1)} %add_add_fusion.1.refs_0_), channel_id=1, source_target_pairs={{0,2},{1,3},{2,0},{3,1},{4,6},{5,7},{6,4},{7,5},{8,10},{9,11},{10,... | collective-permute-start | bytes 12296 | tf_op jit(solution)/shard_map/ppermute | solution.py:34
  71.7 0.5 collective-permute-start.17
  72.2 3.8 %gather_rows.7 = (f32[32,1536]{1,0:T(8,128)S(1)}, f32[32,1536]{1,0:T(8,128)S(1)}) custom-call(s32[3072]{0:T(1024)S(1)} %pad_add_fusion.row_ref, s32[24,128]{1,0:T(8,128)S(1)} %pad_add_fusion.1.part_ref, f32[2048,128]{1,0:T(8,128)S(1)} %get-tuple-element.86.rows_ref), custom_call_target="tpu_custom_call" | custom-call | bytes 8388608 | tf_op jit(solution)/shard_map/gather_rows/pallas_call | solution.py:155
  76.1 0.3 collective-permute-start.22
  76.4 2.9 %collective-permute-start.23 = (f32[32,1536]{1,0:T(8,128)S(1)}, f32[32,1536]{1,0:T(8,128)S(1)}, u32[]{:S(2)}, u32[]{:S(2)}) collective-permute-start(f32[32,1536]{1,0:T(8,128)S(1)} %get-tuple-element.99), channel_id=1, source_target_pairs={{0,8},{1,9},{2,10},{3,11},{4,12},{5,13},{6,14},{7,15},{8,0},{9,1},... | collective-permute-start | bytes 589832 | tf_op jit(solution)/shard_map/ppermute | solution.py:34
  79.3 0.1 collective-permute-start.20
  79.4 0.3 collective-permute-start.21
  79.7 2.5 %later_own.3 = (bf16[32,8192]{1,0:T(8,128)(2,1)S(1)}, bf16[96,96]{1,0:T(8,128)(2,1)S(1)}, f32[32,8192]{1,0:T(8,128)S(1)}) custom-call(f32[32,32]{1,0:T(8,128)S(1)} %add_add_fusion.1.refs_0_, f32[32,32]{1,0:T(8,128)S(1)} %collective-permute-done.17.refs_1_, f32[32,32]{1,0:T(8,128)S(1)} %collective-permute-done.18.refs_2_, ...), custom_call_target="tpu_custom_call" | custom-call | tf_op jit(solution)/shard_map/later_own/pallas_call | solution.py:242
  82.2 4.7 %collective-permute-done.22.refs_7_ = f32[32,1536]{1,0:T(8,128)S(1)} collective-permute-done((f32[32,1536]{1,0:T(8,128)S(1)}, f32[32,1536]{1,0:T(8,128)S(1)}, u32[]{:S(2)}, u32[]{:S(2)}) %collective-permute-start.22) | collective-permute-done | bytes 196640 | tf_op jit(solution)/shard_map/ppermute | solution.py:34
  86.9 1.4 %collective-permute-done.23.refs_8_ = f32[32,1536]{1,0:T(8,128)S(1)} collective-permute-done((f32[32,1536]{1,0:T(8,128)S(1)}, f32[32,1536]{1,0:T(8,128)S(1)}, u32[]{:S(2)}, u32[]{:S(2)}) %collective-permute-start.23) | collective-permute-done | bytes 196640 | tf_op jit(solution)/shard_map/ppermute | solution.py:34
  88.3 3.1 %product.5 = (bf16[96,8192]{1,0:T(8,128)(2,1)S(1)}, f32[32,32]{1,0:T(8,128)S(1)}) custom-call(s32[320]{0:T(512)S(1)} %copy-done.4, s32[320]{0:T(512)S(1)} %copy-done.5, s32[1]{0:T(128)S(6)} %copy.7.refs_2_, bf16[32,8192]{1,0:T(8,128)(2,1)S(1)} %get-tuple-element.94.refs_3_, f32[32,8192]{1,0:T(8,128)S(1)} %get-tuple-element.95.refs_4_, ...), custom_call_target="tpu_custom_call" | custom-call | tf_op jit(solution)/shard_map/product/pallas_call | solution.py:340
  91.4 3.6 %collective-permute-start.26 = (f32[32,32]{1,0:T(8,128)S(1)}, f32[32,32]{1,0:T(8,128)S(1)}, u32[]{:S(2)}, u32[]{:S(2)}) collective-permute-start(f32[32,32]{1,0:T(8,128)S(1)} %get-tuple-element.101), channel_id=1, source_target_pairs={{0,12},{1,13},{2,14},{3,15},{4,8},{5,9},{6,10},{7,11},{8,4},{9,5},... | collective-permute-start | bytes 12296 | tf_op jit(solution)/shard_map/ppermute | solution.py:34
  95.0 0.8 collective-permute-start.24
  95.8 1.1 %collective-permute-done.26 = f32[32,32]{1,0:T(8,128)S(1)} collective-permute-done((f32[32,32]{1,0:T(8,128)S(1)}, f32[32,32]{1,0:T(8,128)S(1)}, u32[]{:S(2)}, u32[]{:S(2)}) %collective-permute-start.26) | collective-permute-done | bytes 4128 | tf_op jit(solution)/shard_map/ppermute | solution.py:34
  96.9 2.7 %collective-permute-done.25 = f32[32,32]{1,0:T(8,128)S(1)} collective-permute-done((f32[32,32]{1,0:T(8,128)S(1)}, f32[32,32]{1,0:T(8,128)S(1)}, u32[]{:S(2)}, u32[]{:S(2)}) %collective-permute-start.25) | collective-permute-done | bytes 4128 | tf_op jit(solution)/shard_map/ppermute | solution.py:34
  99.7 0.1 collective-permute-start.29
  99.8 0.1 collective-permute-start.28
  99.9 1.8 %collective-permute-start.27 = (f32[32,32]{1,0:T(8,128)S(1)}, f32[32,32]{1,0:T(8,128)S(1)}, u32[]{:S(2)}, u32[]{:S(2)}) collective-permute-start(f32[32,32]{1,0:T(8,128)S(1)} %add_add_fusion.refs_0_), channel_id=1, source_target_pairs={{0,1},{1,0},{2,3},{3,2},{4,5},{5,4},{6,7},{7,6},{8,9},{9,8},{10,11... | collective-permute-start | bytes 12296 | tf_op jit(solution)/shard_map/ppermute | solution.py:34
  101.6 1.3 %collective-permute-done.29.refs_3_ = f32[32,32]{1,0:T(8,128)S(1)} collective-permute-done((f32[32,32]{1,0:T(8,128)S(1)}, f32[32,32]{1,0:T(8,128)S(1)}, u32[]{:S(2)}, u32[]{:S(2)}) %collective-permute-start.29) | collective-permute-done | bytes 4128 | tf_op jit(solution)/shard_map/ppermute | solution.py:34
  102.9 0.7 collective-permute-done.28.refs_2_
  103.6 2.9 %final.1 = f32[32,8192]{1,0:T(8,128)} custom-call(f32[32,32]{1,0:T(8,128)S(1)} %add_add_fusion.refs_0_, f32[32,32]{1,0:T(8,128)S(1)} %collective-permute-done.27.refs_1_, f32[32,32]{1,0:T(8,128)S(1)} %collective-permute-done.28.refs_2_, f32[32,32]{1,0:T(8,128)S(1)} %collective-permute-done.29.refs_3_, bf16[96,8192]{1,0:T(8,128)(2,1)S(1)} %get-tuple-element.102.refs_4_), custom_call_target="tpu_custom_call" | custom-call | tf_op jit(solution)/shard_map/final/pallas_call | solution.py:360
  (30 shorter events, 0.1 us)
Async XLA Ops:
  1.0 4.0 %copy-start = (bf16[320,128,128]{2,1,0:T(8,128)(2,1)S(1)}, bf16[320,128,128]{2,1,0:T(8,128)(2,1)}, u32[]{:S(2)}) copy-start(bf16[320,128,128]{2,1,0:T(8,128)(2,1)} %tiles_ref.3) | copy-start | bytes 31457284
  5.0 1.0 copy-start.2
  10.5 16.6 %collective-permute-start.2 = (bf16[32,1536]{1,0:T(8,128)(2,1)S(1)}, bf16[32,1536]{1,0:T(8,128)(2,1)S(1)}, u32[]{:S(2)}, u32[]{:S(2)}) collective-permute-start(bf16[32,1536]{1,0:T(8,128)(2,1)S(1)} %get-tuple-element.58), channel_id=1, source_target_pairs={{0,4},{1,5},{2,6},{3,7},{4,0},{5,1},{6,2},{7,3},{8,12},{9,13},{10,... | collective-permute-start | bytes 294920 | tf_op jit(solution)/shard_map/ppermute | solution.py:34
  13.6 13.5 %collective-permute-start.3 = (bf16[32,1536]{1,0:T(8,128)(2,1)S(1)}, bf16[32,1536]{1,0:T(8,128)(2,1)S(1)}, u32[]{:S(2)}, u32[]{:S(2)}) collective-permute-start(bf16[32,1536]{1,0:T(8,128)(2,1)S(1)} %get-tuple-element.59), channel_id=1, source_target_pairs={{0,8},{1,9},{2,10},{3,11},{4,12},{5,13},{6,14},{7,15},{8,0},{9,1},... | collective-permute-start | bytes 294920 | tf_op jit(solution)/shard_map/ppermute | solution.py:34
  16.2 4.0 %copy-start.1 = (bf16[320,128,128]{2,1,0:T(8,128)(2,1)S(1)}, bf16[320,128,128]{2,1,0:T(8,128)(2,1)}, u32[]{:S(2)}) copy-start(bf16[320,128,128]{2,1,0:T(8,128)(2,1)} %tiles_ref.3) | copy-start | bytes 31457284
  20.2 6.2 %copy-start.3 = (bf16[32,8192]{1,0:T(8,128)(2,1)S(1)}, bf16[32,8192]{1,0:T(8,128)(2,1)}, u32[]{:S(2)}) copy-start(bf16[32,8192]{1,0:T(8,128)(2,1)} %refs_3_.1) | copy-start | bytes 1572868
  24.1 5.3 %copy-start.4 = (s32[320]{0:T(512)S(1)}, s32[320]{0:T(512)}, u32[]{:S(2)}) copy-start(s32[320]{0:T(512)} %refs_0_.5) | copy-start | bytes 3844
  24.1 5.3 %copy-start.5 = (s32[320]{0:T(512)S(1)}, s32[320]{0:T(512)}, u32[]{:S(2)}) copy-start(s32[320]{0:T(512)} %refs_1_.5) | copy-start | bytes 3844
  24.1 3.0 %collective-permute-start = (bf16[32,1536]{1,0:T(8,128)(2,1)S(1)}, bf16[32,1536]{1,0:T(8,128)(2,1)S(1)}, u32[]{:S(2)}, u32[]{:S(2)}) collective-permute-start(bf16[32,1536]{1,0:T(8,128)(2,1)S(1)} %get-tuple-element.56), channel_id=1, source_target_pairs={{0,1},{1,0},{2,3},{3,2},{4,5},{5,4},{6,7},{7,6},{8,9},{9,8},{10,11... | collective-permute-start | bytes 294920 | tf_op jit(solution)/shard_map/ppermute | solution.py:34
  24.2 5.2 %collective-permute-start.1 = (bf16[32,1536]{1,0:T(8,128)(2,1)S(1)}, bf16[32,1536]{1,0:T(8,128)(2,1)S(1)}, u32[]{:S(2)}, u32[]{:S(2)}) collective-permute-start(bf16[32,1536]{1,0:T(8,128)(2,1)S(1)} %get-tuple-element.57), channel_id=1, source_target_pairs={{0,2},{1,3},{2,0},{3,1},{4,6},{5,7},{6,4},{7,5},{8,10},{9,11},{10,... | collective-permute-start | bytes 294920 | tf_op jit(solution)/shard_map/ppermute | solution.py:34
  32.2 8.3 %collective-permute-start.6 = (f32[32,32]{1,0:T(8,128)S(1)}, f32[32,32]{1,0:T(8,128)S(1)}, u32[]{:S(2)}, u32[]{:S(2)}) collective-permute-start(f32[32,32]{1,0:T(8,128)S(1)} %get-tuple-element.61), channel_id=1, source_target_pairs={{0,12},{1,13},{2,14},{3,15},{4,8},{5,9},{6,10},{7,11},{8,4},{9,5},... | collective-permute-start | bytes 12296 | tf_op jit(solution)/shard_map/ppermute | solution.py:34
  33.4 7.1 %collective-permute-start.5 = (f32[32,32]{1,0:T(8,128)S(1)}, f32[32,32]{1,0:T(8,128)S(1)}, u32[]{:S(2)}, u32[]{:S(2)}) collective-permute-start(f32[32,32]{1,0:T(8,128)S(1)} %get-tuple-element.61), channel_id=1, source_target_pairs={{0,8},{1,9},{2,10},{3,11},{4,12},{5,13},{6,14},{7,15},{8,0},{9,1},... | collective-permute-start | bytes 12296 | tf_op jit(solution)/shard_map/ppermute | solution.py:34
  33.6 6.9 %collective-permute-start.4 = (f32[32,32]{1,0:T(8,128)S(1)}, f32[32,32]{1,0:T(8,128)S(1)}, u32[]{:S(2)}, u32[]{:S(2)}) collective-permute-start(f32[32,32]{1,0:T(8,128)S(1)} %get-tuple-element.61), channel_id=1, source_target_pairs={{0,4},{1,5},{2,6},{3,7},{4,0},{5,1},{6,2},{7,3},{8,12},{9,13},{10,... | collective-permute-start | bytes 12296 | tf_op jit(solution)/shard_map/ppermute | solution.py:34
  40.5 7.6 %collective-permute-start.9 = (f32[32,32]{1,0:T(8,128)S(1)}, f32[32,32]{1,0:T(8,128)S(1)}, u32[]{:S(2)}, u32[]{:S(2)}) collective-permute-start(f32[32,32]{1,0:T(8,128)S(1)} %add_add_fusion.2.refs_0_), channel_id=1, source_target_pairs={{0,3},{1,2},{2,1},{3,0},{4,7},{5,6},{6,5},{7,4},{8,11},{9,10},{10,... | collective-permute-start | bytes 12296 | tf_op jit(solution)/shard_map/ppermute | solution.py:34
  40.6 7.5 %collective-permute-start.8 = (f32[32,32]{1,0:T(8,128)S(1)}, f32[32,32]{1,0:T(8,128)S(1)}, u32[]{:S(2)}, u32[]{:S(2)}) collective-permute-start(f32[32,32]{1,0:T(8,128)S(1)} %add_add_fusion.2.refs_0_), channel_id=1, source_target_pairs={{0,2},{1,3},{2,0},{3,1},{4,6},{5,7},{6,4},{7,5},{8,10},{9,11},{10,... | collective-permute-start | bytes 12296 | tf_op jit(solution)/shard_map/ppermute | solution.py:34
  42.2 5.9 %collective-permute-start.7 = (f32[32,32]{1,0:T(8,128)S(1)}, f32[32,32]{1,0:T(8,128)S(1)}, u32[]{:S(2)}, u32[]{:S(2)}) collective-permute-start(f32[32,32]{1,0:T(8,128)S(1)} %add_add_fusion.2.refs_0_), channel_id=1, source_target_pairs={{0,1},{1,0},{2,3},{3,2},{4,5},{5,4},{6,7},{7,6},{8,9},{9,8},{10,11... | collective-permute-start | bytes 12296 | tf_op jit(solution)/shard_map/ppermute | solution.py:34
  46.3 9.8 %collective-permute-start.12 = (f32[32,1536]{1,0:T(8,128)S(1)}, f32[32,1536]{1,0:T(8,128)S(1)}, u32[]{:S(2)}, u32[]{:S(2)}) collective-permute-start(f32[32,1536]{1,0:T(8,128)S(1)} %get-tuple-element.78), channel_id=1, source_target_pairs={{0,4},{1,5},{2,6},{3,7},{4,0},{5,1},{6,2},{7,3},{8,12},{9,13},{10,... | collective-permute-start | bytes 589832 | tf_op jit(solution)/shard_map/ppermute | solution.py:34
  46.4 12.3 %collective-permute-start.13 = (f32[32,1536]{1,0:T(8,128)S(1)}, f32[32,1536]{1,0:T(8,128)S(1)}, u32[]{:S(2)}, u32[]{:S(2)}) collective-permute-start(f32[32,1536]{1,0:T(8,128)S(1)} %get-tuple-element.79), channel_id=1, source_target_pairs={{0,8},{1,9},{2,10},{3,11},{4,12},{5,13},{6,14},{7,15},{8,0},{9,1},... | collective-permute-start | bytes 589832 | tf_op jit(solution)/shard_map/ppermute | solution.py:34
  48.1 10.5 %collective-permute-start.10 = (f32[32,1536]{1,0:T(8,128)S(1)}, f32[32,1536]{1,0:T(8,128)S(1)}, u32[]{:S(2)}, u32[]{:S(2)}) collective-permute-start(f32[32,1536]{1,0:T(8,128)S(1)} %get-tuple-element.76), channel_id=1, source_target_pairs={{0,1},{1,0},{2,3},{3,2},{4,5},{5,4},{6,7},{7,6},{8,9},{9,8},{10,11... | collective-permute-start | bytes 589832 | tf_op jit(solution)/shard_map/ppermute | solution.py:34
  48.2 10.5 %collective-permute-start.11 = (f32[32,1536]{1,0:T(8,128)S(1)}, f32[32,1536]{1,0:T(8,128)S(1)}, u32[]{:S(2)}, u32[]{:S(2)}) collective-permute-start(f32[32,1536]{1,0:T(8,128)S(1)} %get-tuple-element.77), channel_id=1, source_target_pairs={{0,2},{1,3},{2,0},{3,1},{4,6},{5,7},{6,4},{7,5},{8,10},{9,11},{10,... | collective-permute-start | bytes 589832 | tf_op jit(solution)/shard_map/ppermute | solution.py:34
  62.0 8.3 %collective-permute-start.16 = (f32[32,32]{1,0:T(8,128)S(1)}, f32[32,32]{1,0:T(8,128)S(1)}, u32[]{:S(2)}, u32[]{:S(2)}) collective-permute-start(f32[32,32]{1,0:T(8,128)S(1)} %get-tuple-element.81), channel_id=1, source_target_pairs={{0,12},{1,13},{2,14},{3,15},{4,8},{5,9},{6,10},{7,11},{8,4},{9,5},... | collective-permute-start | bytes 12296 | tf_op jit(solution)/shard_map/ppermute | solution.py:34
  64.6 5.7 %collective-permute-start.15 = (f32[32,32]{1,0:T(8,128)S(1)}, f32[32,32]{1,0:T(8,128)S(1)}, u32[]{:S(2)}, u32[]{:S(2)}) collective-permute-start(f32[32,32]{1,0:T(8,128)S(1)} %get-tuple-element.81), channel_id=1, source_target_pairs={{0,8},{1,9},{2,10},{3,11},{4,12},{5,13},{6,14},{7,15},{8,0},{9,1},... | collective-permute-start | bytes 12296 | tf_op jit(solution)/shard_map/ppermute | solution.py:34
  64.6 5.7 %collective-permute-start.14 = (f32[32,32]{1,0:T(8,128)S(1)}, f32[32,32]{1,0:T(8,128)S(1)}, u32[]{:S(2)}, u32[]{:S(2)}) collective-permute-start(f32[32,32]{1,0:T(8,128)S(1)} %get-tuple-element.81), channel_id=1, source_target_pairs={{0,4},{1,5},{2,6},{3,7},{4,0},{5,1},{6,2},{7,3},{8,12},{9,13},{10,... | collective-permute-start | bytes 12296 | tf_op jit(solution)/shard_map/ppermute | solution.py:34
  70.3 9.0 %collective-permute-start.19 = (f32[32,32]{1,0:T(8,128)S(1)}, f32[32,32]{1,0:T(8,128)S(1)}, u32[]{:S(2)}, u32[]{:S(2)}) collective-permute-start(f32[32,32]{1,0:T(8,128)S(1)} %add_add_fusion.1.refs_0_), channel_id=1, source_target_pairs={{0,3},{1,2},{2,1},{3,0},{4,7},{5,6},{6,5},{7,4},{8,11},{9,10},{10,... | collective-permute-start | bytes 12296 | tf_op jit(solution)/shard_map/ppermute | solution.py:34
  70.4 8.9 %collective-permute-start.18 = (f32[32,32]{1,0:T(8,128)S(1)}, f32[32,32]{1,0:T(8,128)S(1)}, u32[]{:S(2)}, u32[]{:S(2)}) collective-permute-start(f32[32,32]{1,0:T(8,128)S(1)} %add_add_fusion.1.refs_0_), channel_id=1, source_target_pairs={{0,2},{1,3},{2,0},{3,1},{4,6},{5,7},{6,4},{7,5},{8,10},{9,11},{10,... | collective-permute-start | bytes 12296 | tf_op jit(solution)/shard_map/ppermute | solution.py:34
  71.7 7.6 %collective-permute-start.17 = (f32[32,32]{1,0:T(8,128)S(1)}, f32[32,32]{1,0:T(8,128)S(1)}, u32[]{:S(2)}, u32[]{:S(2)}) collective-permute-start(f32[32,32]{1,0:T(8,128)S(1)} %add_add_fusion.1.refs_0_), channel_id=1, source_target_pairs={{0,1},{1,0},{2,3},{3,2},{4,5},{5,4},{6,7},{7,6},{8,9},{9,8},{10,11... | collective-permute-start | bytes 12296 | tf_op jit(solution)/shard_map/ppermute | solution.py:34
  76.1 10.9 %collective-permute-start.22 = (f32[32,1536]{1,0:T(8,128)S(1)}, f32[32,1536]{1,0:T(8,128)S(1)}, u32[]{:S(2)}, u32[]{:S(2)}) collective-permute-start(f32[32,1536]{1,0:T(8,128)S(1)} %get-tuple-element.98), channel_id=1, source_target_pairs={{0,4},{1,5},{2,6},{3,7},{4,0},{5,1},{6,2},{7,3},{8,12},{9,13},{10,... | collective-permute-start | bytes 589832 | tf_op jit(solution)/shard_map/ppermute | solution.py:34
  76.4 12.0 %collective-permute-start.23 = (f32[32,1536]{1,0:T(8,128)S(1)}, f32[32,1536]{1,0:T(8,128)S(1)}, u32[]{:S(2)}, u32[]{:S(2)}) collective-permute-start(f32[32,1536]{1,0:T(8,128)S(1)} %get-tuple-element.99), channel_id=1, source_target_pairs={{0,8},{1,9},{2,10},{3,11},{4,12},{5,13},{6,14},{7,15},{8,0},{9,1},... | collective-permute-start | bytes 589832 | tf_op jit(solution)/shard_map/ppermute | solution.py:34
  79.3 9.0 %collective-permute-start.20 = (f32[32,1536]{1,0:T(8,128)S(1)}, f32[32,1536]{1,0:T(8,128)S(1)}, u32[]{:S(2)}, u32[]{:S(2)}) collective-permute-start(f32[32,1536]{1,0:T(8,128)S(1)} %get-tuple-element.96), channel_id=1, source_target_pairs={{0,1},{1,0},{2,3},{3,2},{4,5},{5,4},{6,7},{7,6},{8,9},{9,8},{10,11... | collective-permute-start | bytes 589832 | tf_op jit(solution)/shard_map/ppermute | solution.py:34
  79.4 9.0 %collective-permute-start.21 = (f32[32,1536]{1,0:T(8,128)S(1)}, f32[32,1536]{1,0:T(8,128)S(1)}, u32[]{:S(2)}, u32[]{:S(2)}) collective-permute-start(f32[32,1536]{1,0:T(8,128)S(1)} %get-tuple-element.97), channel_id=1, source_target_pairs={{0,2},{1,3},{2,0},{3,1},{4,6},{5,7},{6,4},{7,5},{8,10},{9,11},{10,... | collective-permute-start | bytes 589832 | tf_op jit(solution)/shard_map/ppermute | solution.py:34
  91.4 5.5 %collective-permute-start.26 = (f32[32,32]{1,0:T(8,128)S(1)}, f32[32,32]{1,0:T(8,128)S(1)}, u32[]{:S(2)}, u32[]{:S(2)}) collective-permute-start(f32[32,32]{1,0:T(8,128)S(1)} %get-tuple-element.101), channel_id=1, source_target_pairs={{0,12},{1,13},{2,14},{3,15},{4,8},{5,9},{6,10},{7,11},{8,4},{9,5},... | collective-permute-start | bytes 12296 | tf_op jit(solution)/shard_map/ppermute | solution.py:34
  95.0 4.6 %collective-permute-start.25 = (f32[32,32]{1,0:T(8,128)S(1)}, f32[32,32]{1,0:T(8,128)S(1)}, u32[]{:S(2)}, u32[]{:S(2)}) collective-permute-start(f32[32,32]{1,0:T(8,128)S(1)} %get-tuple-element.101), channel_id=1, source_target_pairs={{0,8},{1,9},{2,10},{3,11},{4,12},{5,13},{6,14},{7,15},{8,0},{9,1},... | collective-permute-start | bytes 12296 | tf_op jit(solution)/shard_map/ppermute | solution.py:34
  95.0 4.6 %collective-permute-start.24 = (f32[32,32]{1,0:T(8,128)S(1)}, f32[32,32]{1,0:T(8,128)S(1)}, u32[]{:S(2)}, u32[]{:S(2)}) collective-permute-start(f32[32,32]{1,0:T(8,128)S(1)} %get-tuple-element.101), channel_id=1, source_target_pairs={{0,4},{1,5},{2,6},{3,7},{4,0},{5,1},{6,2},{7,3},{8,12},{9,13},{10,... | collective-permute-start | bytes 12296 | tf_op jit(solution)/shard_map/ppermute | solution.py:34
  99.7 3.2 %collective-permute-start.29 = (f32[32,32]{1,0:T(8,128)S(1)}, f32[32,32]{1,0:T(8,128)S(1)}, u32[]{:S(2)}, u32[]{:S(2)}) collective-permute-start(f32[32,32]{1,0:T(8,128)S(1)} %add_add_fusion.refs_0_), channel_id=1, source_target_pairs={{0,3},{1,2},{2,1},{3,0},{4,7},{5,6},{6,5},{7,4},{8,11},{9,10},{10,... | collective-permute-start | bytes 12296 | tf_op jit(solution)/shard_map/ppermute | solution.py:34
  99.8 3.8 %collective-permute-start.28 = (f32[32,32]{1,0:T(8,128)S(1)}, f32[32,32]{1,0:T(8,128)S(1)}, u32[]{:S(2)}, u32[]{:S(2)}) collective-permute-start(f32[32,32]{1,0:T(8,128)S(1)} %add_add_fusion.refs_0_), channel_id=1, source_target_pairs={{0,2},{1,3},{2,0},{3,1},{4,6},{5,7},{6,4},{7,5},{8,10},{9,11},{10,... | collective-permute-start | bytes 12296 | tf_op jit(solution)/shard_map/ppermute | solution.py:34
  99.9 3.7 %collective-permute-start.27 = (f32[32,32]{1,0:T(8,128)S(1)}, f32[32,32]{1,0:T(8,128)S(1)}, u32[]{:S(2)}, u32[]{:S(2)}) collective-permute-start(f32[32,32]{1,0:T(8,128)S(1)} %add_add_fusion.refs_0_), channel_id=1, source_target_pairs={{0,1},{1,0},{2,3},{3,2},{4,5},{5,4},{6,7},{7,6},{8,9},{9,8},{10,11... | collective-permute-start | bytes 12296 | tf_op jit(solution)/shard_map/ppermute | solution.py:34

commit v3 on v2

--- a/solution.py
+++ b/solution.py
@@ -18,11 +18,16 @@
 BF16 = jnp.bfloat16
 VMEM = pl.BlockSpec(memory_space=pltpu.VMEM)
 SMEM = pl.BlockSpec(memory_space=pltpu.SMEM)
+CHEAP = pl.CostEstimate(flops=0, bytes_accessed=1024, transcendentals=0)
 PARAMS = pltpu.CompilerParams(vmem_limit_bytes=32 << 20)
 
 
 def in_vmem(x):
     return pltpu.with_memory_space_constraint(x, pltpu.VMEM)
+
+
+def in_hbm(x):
+    return pltpu.with_memory_space_constraint(x, pltpu.HBM)
 
 
 def vmem_out(shape, dtype):
@@ -159,7 +164,7 @@
         out_specs=[VMEM] * count,
         scratch_shapes=[pltpu.VMEM((indices, LANES), F32)],
         compiler_params=PARAMS,
-        cost_estimate=pl.CostEstimate(flops=0, bytes_accessed=8 << 20, transcendentals=0),
+        cost_estimate=CHEAP,
         name="gather_rows",
     )(row_list, in_vmem(part_list), in_vmem(rows))
 
@@ -197,12 +202,13 @@
     return pl.pallas_call(
         functools.partial(start_kernel, count, first, make_rows),
         out_shape=outs,
-        in_specs=[SMEM, VMEM, VMEM, pl.BlockSpec(memory_space=pl.ANY)],
+        in_specs=[SMEM, VMEM, VMEM, pl.BlockSpec(memory_space=pltpu.HBM)],
         out_specs=[VMEM] * len(outs),
         scratch_shapes=[pltpu.VMEM((indices, LANES), F32), pltpu.SemaphoreType.DMA((COPIES,))],
         compiler_params=PARAMS,
+        cost_estimate=CHEAP,
         name="start_gather",
-    )(row_list, in_vmem(part_list), in_vmem(source), tiles)
+    )(row_list, in_vmem(part_list), source if make_rows else in_vmem(source), in_hbm(tiles))
 
 
 def own_slots(block_ref, tiles_ref, own_ref):
@@ -223,6 +229,7 @@
         in_specs=[VMEM] * 2,
         out_specs=VMEM,
         compiler_params=PARAMS,
+        cost_estimate=CHEAP,
         name="first_own",
     )(in_vmem(block), in_vmem(tiles))
 
@@ -249,6 +256,7 @@
         in_specs=[VMEM] * 6,
         out_specs=[VMEM] * 3,
         compiler_params=PARAMS,
+        cost_estimate=CHEAP,
         name="later_own",
     )(*[in_vmem(g) for g in grams], in_vmem(stacked), in_vmem(tiles))
 
@@ -344,6 +352,7 @@
         out_specs=[VMEM] * len(outs),
         scratch_shapes=[pltpu.VMEM((columns, width), BF16), pltpu.VMEM((columns, states), F32)],
         compiler_params=PARAMS,
+        cost_estimate=CHEAP,
         name="product",
     )(src, dst, count, *[in_vmem(x) for x in operands])
 
@@ -363,6 +372,7 @@
         in_specs=[VMEM] * 5,
         out_specs=VMEM,
         compiler_params=PARAMS,
+        cost_estimate=CHEAP,
         name="final",
     )(*[in_vmem(g) for g in grams], in_vmem(stacked))
 
@@ -432,13 +442,11 @@
             return final(gram_round(gram, rounds[-1]), stacked, total_states)
         ghosts = [None] * len(masks)
         picked = gather_colours(rows[0], *listed[0], len(far))
-        gram, near_rows, *picked = lax.optimization_barrier((gram, rows[0], *picked))
+        gram, *picked = lax.optimization_barrier((gram, *picked))
         parts = gram_round(gram, rounds[-1])
         sent(ghosts, far, picked)
-        picked = gather_colours(near_rows, *listed[1], len(near))
-        gathered = lax.optimization_barrier((*parts, *picked))
-        parts, picked = gathered[: len(parts)], gathered[len(parts) :]
-        sent(ghosts, near, picked)
+        near_rows, *parts = lax.optimization_barrier((rows[0], *parts))
+        sent(ghosts, near, gather_colours(near_rows, *listed[1], len(near)))
         block, matrix, own = later_own(parts, stacked, own_tiles, total_states)
 
 

time: 106 us -> 91.6 us (0.86)
  local copies, waits for them, and re-layouts: 9.17 us -> 1.18 us
  waiting for transfers between devices: 21.7 us -> 13.9 us
    unnamed x12 -> x8, local copies, waits for them, and re-layouts: 9.05 us -> 1.06 us
    ppermute x30, waiting for transfers between devices: 21.7 us -> 13.9 us  [swapped(): return lax.ppermute(x, 'dom', [(i, i ^ mask) for i in range(size)])]
  transfers between devices with their start and end apart: 30 -> 30, of which waited for: 9 -> 12; matrix products, arithmetic and copies ran while one was open for 0% -> 0% of each run, Pallas kernels for 23% -> 27%
where the time goes in v3:
time: 91.6 us; the launch traced here: 91.2 us
  Pallas kernels  40.8 us (45%)
  starting transfers between devices  33.5 us (37%)
  waiting for transfers between devices  13.9 us (15%)
  local copies, waits for them, and re-layouts  1.18 us (1%)
  between operations  0.93 us (1%)
    ppermute x30, starting transfers between devices, swapped(): return lax.ppermute(x, 'dom', [(i, i ^ mask) for i in range(size)])  33.5 us
    pallas_call x4, Pallas kernels, gather_colours(): pl.pallas_call(gather_kernel, out_shape=[vmem_out((columns, indices // co...  15.3 us
    ppermute x30, waiting for transfers between devices, swapped(): return lax.ppermute(x, 'dom', [(i, i ^ mask) for i in range(size)])  13.9 us
    pallas_call x3, Pallas kernels, product(): pl.pallas_call(functools.partial(product_kernel, len(ghosts), group, with...  8.91 us
    pallas_call x2, Pallas kernels, start_gather(): pl.pallas_call(functools.partial(start_kernel, count, first, make_rows),...  7.97 us
    pallas_call x2, Pallas kernels, later_own(): pl.pallas_call(functools.partial(later_own_kernel, total_states), out_sha...  5 us
    pallas_call x1, Pallas kernels, final(): pl.pallas_call(functools.partial(final_kernel, total_states), out_shape=j...  2.93 us
  transfers between devices with their start and end apart: 30, of which 12 were waited for; matrix products, arithmetic and copies ran while one was open for 0% of the time, Pallas kernels for 27%

profile of v3, /device:TPU:0, one launch (start us, length us, event | category | flops | bytes accessed | tf_op | source)
XLA Modules:
  0.0 91.2 jit_solution(11994645472091286246)
XLA Ops:
  0.0 0.8 add_select_fusion
  0.8 0.1 slice_reduce_fusion.1
  1.0 0.0 copy-start
  1.0 1.0 %copy-done = bf16[32,8192]{1,0:T(8,128)(2,1)S(1)} copy-done((bf16[32,8192]{1,0:T(8,128)(2,1)S(1)}, bf16[32,8192]{1,0:T(8,128)(2,1)}, u32[]{:S(2)}) %copy-start) | copy-done | bytes 524312
  2.0 4.2 %start_gather.2 = (bf16[32,1536]{1,0:T(8,128)(2,1)S(1)}, bf16[32,1536]{1,0:T(8,128)(2,1)S(1)}, bf16[256,128,128]{2,1,0:T(8,128)(2,1)S(1)}, f32[2048,128]{1,0:T(8,128)S(1)}) custom-call(s32[3072]{0:T(1024)S(1)} %pad_add_fusion.2.row_ref, s32[24,128]{1,0:T(8,128)S(1)} %pad_add_fusion.3.part_ref, bf16[32,8192]{1,0:T(8,128)(2,1)S(1)} %copy-done, ...), custom_call_target="tpu_custom_call" | custom-call | bytes 1024 | tf_op jit(solution)/shard_map/start_gather/pallas_call | solution.py:202
  6.3 3.1 %collective-permute-start.2 = (bf16[32,1536]{1,0:T(8,128)(2,1)S(1)}, bf16[32,1536]{1,0:T(8,128)(2,1)S(1)}, u32[]{:S(2)}, u32[]{:S(2)}) collective-permute-start(bf16[32,1536]{1,0:T(8,128)(2,1)S(1)} %get-tuple-element.54), channel_id=1, source_target_pairs={{0,4},{1,5},{2,6},{3,7},{4,0},{5,1},{6,2},{7,3},{8,12},{9,13},{10,... | collective-permute-start | bytes 294920 | tf_op jit(solution)/shard_map/ppermute | solution.py:39
  9.4 2.6 %collective-permute-start.3 = (bf16[32,1536]{1,0:T(8,128)(2,1)S(1)}, bf16[32,1536]{1,0:T(8,128)(2,1)S(1)}, u32[]{:S(2)}, u32[]{:S(2)}) collective-permute-start(bf16[32,1536]{1,0:T(8,128)(2,1)S(1)} %get-tuple-element.55), channel_id=1, source_target_pairs={{0,8},{1,9},{2,10},{3,11},{4,12},{5,13},{6,14},{7,15},{8,0},{9,1},... | collective-permute-start | bytes 294920 | tf_op jit(solution)/shard_map/ppermute | solution.py:39
  12.0 0.0 copy-start.1
  12.0 3.7 %start_gather.3 = (bf16[32,1536]{1,0:T(8,128)(2,1)S(1)}, bf16[32,1536]{1,0:T(8,128)(2,1)S(1)}, bf16[64,128,128]{2,1,0:T(8,128)(2,1)S(1)}) custom-call(s32[3072]{0:T(1024)S(1)} %pad_add_fusion.row_ref, s32[24,128]{1,0:T(8,128)S(1)} %pad_add_fusion.1.part_ref, f32[2048,128]{1,0:T(8,128)S(1)} %get-tuple-element.50.source_ref, bf16[320,128,128]{2,1,0:T(8,128)(2,1)} %tiles_ref.3), custom_call_target="tpu_custom_call" | custom-call | bytes 1024 | tf_op jit(solution)/shard_map/start_gather/pallas_call | solution.py:202
  15.7 0.0 copy-start.2
  15.7 0.0 copy-start.3
  15.7 0.1 collective-permute-start
  15.8 1.6 %collective-permute-start.1 = (bf16[32,1536]{1,0:T(8,128)(2,1)S(1)}, bf16[32,1536]{1,0:T(8,128)(2,1)S(1)}, u32[]{:S(2)}, u32[]{:S(2)}) collective-permute-start(bf16[32,1536]{1,0:T(8,128)(2,1)S(1)} %get-tuple-element.53), channel_id=1, source_target_pairs={{0,2},{1,3},{2,0},{3,1},{4,6},{5,7},{6,4},{7,5},{8,10},{9,11},{10,... | collective-permute-start | bytes 294920 | tf_op jit(solution)/shard_map/ppermute | solution.py:39
  18.1 0.7 first_own.1.refs_4_
  18.7 0.0 collective-permute-done.refs_5_
  18.8 2.3 %collective-permute-done.1.refs_6_ = bf16[32,1536]{1,0:T(8,128)(2,1)S(1)} collective-permute-done((bf16[32,1536]{1,0:T(8,128)(2,1)S(1)}, bf16[32,1536]{1,0:T(8,128)(2,1)S(1)}, u32[]{:S(2)}, u32[]{:S(2)}) %collective-permute-start.1) | collective-permute-done | bytes 98336 | tf_op jit(solution)/shard_map/ppermute | solution.py:39
  21.0 2.7 %product.3 = (bf16[96,8192]{1,0:T(8,128)(2,1)S(1)}, f32[32,32]{1,0:T(8,128)S(1)}, f32[2048,128]{1,0:T(8,128)S(1)}) custom-call(s32[320]{0:T(512)S(1)} %copy-done.2, s32[320]{0:T(512)S(1)} %copy-done.3, s32[1]{0:T(128)S(6)} %copy.7.refs_2_, bf16[32,8192]{1,0:T(8,128)(2,1)S(1)} %copy-done.1, f32[32,8192]{1,0:T(8,128)S(1)} %first_own.1.refs_4_, ...), custom_call_target="tpu_custom_call" | custom-call | bytes 1024 | tf_op jit(solution)/shard_map/product/pallas_call | solution.py:348
  23.8 0.1 collective-permute-start.6
  23.9 3.1 %collective-permute-start.5 = (f32[32,32]{1,0:T(8,128)S(1)}, f32[32,32]{1,0:T(8,128)S(1)}, u32[]{:S(2)}, u32[]{:S(2)}) collective-permute-start(f32[32,32]{1,0:T(8,128)S(1)} %get-tuple-element.58), channel_id=1, source_target_pairs={{0,8},{1,9},{2,10},{3,11},{4,12},{5,13},{6,14},{7,15},{8,0},{9,1},... | collective-permute-start | bytes 12296 | tf_op jit(solution)/shard_map/ppermute | solution.py:39
  27.0 1.3 %collective-permute-start.4 = (f32[32,32]{1,0:T(8,128)S(1)}, f32[32,32]{1,0:T(8,128)S(1)}, u32[]{:S(2)}, u32[]{:S(2)}) collective-permute-start(f32[32,32]{1,0:T(8,128)S(1)} %get-tuple-element.58), channel_id=1, source_target_pairs={{0,4},{1,5},{2,6},{3,7},{4,0},{5,1},{6,2},{7,3},{8,12},{9,13},{10,... | collective-permute-start | bytes 12296 | tf_op jit(solution)/shard_map/ppermute | solution.py:39
  28.2 3.8 %gather_rows.4 = (f32[32,1536]{1,0:T(8,128)S(1)}, f32[32,1536]{1,0:T(8,128)S(1)}) custom-call(s32[3072]{0:T(1024)S(1)} %pad_add_fusion.2.row_ref, s32[24,128]{1,0:T(8,128)S(1)} %pad_add_fusion.3.part_ref, f32[2048,128]{1,0:T(8,128)S(1)} %get-tuple-element.69.rows_ref), custom_call_target="tpu_custom_call" | custom-call | bytes 1024 | tf_op jit(solution)/shard_map/gather_rows/pallas_call | solution.py:160
  32.1 0.0 collective-permute-done.4
  32.1 0.1 collective-permute-start.9
  32.2 1.6 %collective-permute-start.8 = (f32[32,32]{1,0:T(8,128)S(1)}, f32[32,32]{1,0:T(8,128)S(1)}, u32[]{:S(2)}, u32[]{:S(2)}) collective-permute-start(f32[32,32]{1,0:T(8,128)S(1)} %add_add_fusion.2.refs_0_), channel_id=1, source_target_pairs={{0,2},{1,3},{2,0},{3,1},{4,6},{5,7},{6,4},{7,5},{8,10},{9,11},{10,... | collective-permute-start | bytes 12296 | tf_op jit(solution)/shard_map/ppermute | solution.py:39
  33.8 0.3 collective-permute-start.7
  34.1 0.8 collective-permute-start.12
  34.8 0.0 collective-permute-start.13
  34.8 0.6 collective-permute-done.9.refs_3_
  35.5 0.6 collective-permute-done.8.refs_2_
  36.0 3.8 %gather_rows.5 = (f32[32,1536]{1,0:T(8,128)S(1)}, f32[32,1536]{1,0:T(8,128)S(1)}) custom-call(s32[3072]{0:T(1024)S(1)} %pad_add_fusion.row_ref, s32[24,128]{1,0:T(8,128)S(1)} %pad_add_fusion.1.part_ref, f32[2048,128]{1,0:T(8,128)S(1)} %get-tuple-element.69.rows_ref), custom_call_target="tpu_custom_call" | custom-call | bytes 1024 | tf_op jit(solution)/shard_map/gather_rows/pallas_call | solution.py:160
  39.9 0.5 collective-permute-start.10
  40.3 1.2 %collective-permute-start.11 = (f32[32,1536]{1,0:T(8,128)S(1)}, f32[32,1536]{1,0:T(8,128)S(1)}, u32[]{:S(2)}, u32[]{:S(2)}) collective-permute-start(f32[32,1536]{1,0:T(8,128)S(1)} %get-tuple-element.71), channel_id=1, source_target_pairs={{0,2},{1,3},{2,0},{3,1},{4,6},{5,7},{6,4},{7,5},{8,10},{9,11},{10,... | collective-permute-start | bytes 589832 | tf_op jit(solution)/shard_map/ppermute | solution.py:39
  41.5 2.5 %later_own.2 = (bf16[32,8192]{1,0:T(8,128)(2,1)S(1)}, bf16[96,96]{1,0:T(8,128)(2,1)S(1)}, f32[32,8192]{1,0:T(8,128)S(1)}) custom-call(f32[32,32]{1,0:T(8,128)S(1)} %add_add_fusion.2.refs_0_, f32[32,32]{1,0:T(8,128)S(1)} %collective-permute-done.7.refs_1_, f32[32,32]{1,0:T(8,128)S(1)} %collective-permute-done.8.refs_2_, ...), custom_call_target="tpu_custom_call" | custom-call | bytes 1024 | tf_op jit(solution)/shard_map/later_own/pallas_call | solution.py:249
  44.0 2.5 %collective-permute-done.13.refs_8_ = f32[32,1536]{1,0:T(8,128)S(1)} collective-permute-done((f32[32,1536]{1,0:T(8,128)S(1)}, f32[32,1536]{1,0:T(8,128)S(1)}, u32[]{:S(2)}, u32[]{:S(2)}) %collective-permute-start.13) | collective-permute-done | bytes 196640 | tf_op jit(solution)/shard_map/ppermute | solution.py:39
  46.5 0.7 collective-permute-done.11.refs_6_
  47.2 3.1 %product.4 = (bf16[96,8192]{1,0:T(8,128)(2,1)S(1)}, f32[32,32]{1,0:T(8,128)S(1)}, f32[2048,128]{1,0:T(8,128)S(1)}) custom-call(s32[320]{0:T(512)S(1)} %copy-done.2, s32[320]{0:T(512)S(1)} %copy-done.3, s32[1]{0:T(128)S(6)} %copy.7.refs_2_, bf16[32,8192]{1,0:T(8,128)(2,1)S(1)} %get-tuple-element.67.refs_3_, f32[32,8192]{1,0:T(8,128)S(1)} %get-tuple-element.68.refs_4_, ...), custom_call_target="tpu_custom_call" | custom-call | bytes 1024 | tf_op jit(solution)/shard_map/product/pallas_call | solution.py:348
  50.4 2.5 %collective-permute-start.16 = (f32[32,32]{1,0:T(8,128)S(1)}, f32[32,32]{1,0:T(8,128)S(1)}, u32[]{:S(2)}, u32[]{:S(2)}) collective-permute-start(f32[32,32]{1,0:T(8,128)S(1)} %get-tuple-element.76), channel_id=1, source_target_pairs={{0,12},{1,13},{2,14},{3,15},{4,8},{5,9},{6,10},{7,11},{8,4},{9,5},... | collective-permute-start | bytes 12296 | tf_op jit(solution)/shard_map/ppermute | solution.py:39
  52.9 1.0 %collective-permute-start.15 = (f32[32,32]{1,0:T(8,128)S(1)}, f32[32,32]{1,0:T(8,128)S(1)}, u32[]{:S(2)}, u32[]{:S(2)}) collective-permute-start(f32[32,32]{1,0:T(8,128)S(1)} %get-tuple-element.76), channel_id=1, source_target_pairs={{0,8},{1,9},{2,10},{3,11},{4,12},{5,13},{6,14},{7,15},{8,0},{9,1},... | collective-permute-start | bytes 12296 | tf_op jit(solution)/shard_map/ppermute | solution.py:39
  53.9 0.9 %collective-permute-start.14 = (f32[32,32]{1,0:T(8,128)S(1)}, f32[32,32]{1,0:T(8,128)S(1)}, u32[]{:S(2)}, u32[]{:S(2)}) collective-permute-start(f32[32,32]{1,0:T(8,128)S(1)} %get-tuple-element.76), channel_id=1, source_target_pairs={{0,4},{1,5},{2,6},{3,7},{4,0},{5,1},{6,2},{7,3},{8,12},{9,13},{10,... | collective-permute-start | bytes 12296 | tf_op jit(solution)/shard_map/ppermute | solution.py:39
  54.8 3.8 %gather_rows.6 = (f32[32,1536]{1,0:T(8,128)S(1)}, f32[32,1536]{1,0:T(8,128)S(1)}) custom-call(s32[3072]{0:T(1024)S(1)} %pad_add_fusion.2.row_ref, s32[24,128]{1,0:T(8,128)S(1)} %pad_add_fusion.3.part_ref, f32[2048,128]{1,0:T(8,128)S(1)} %get-tuple-element.87.rows_ref), custom_call_target="tpu_custom_call" | custom-call | bytes 1024 | tf_op jit(solution)/shard_map/gather_rows/pallas_call | solution.py:160
  58.7 0.1 collective-permute-start.19
  58.8 1.6 %collective-permute-start.18 = (f32[32,32]{1,0:T(8,128)S(1)}, f32[32,32]{1,0:T(8,128)S(1)}, u32[]{:S(2)}, u32[]{:S(2)}) collective-permute-start(f32[32,32]{1,0:T(8,128)S(1)} %add_add_fusion.1.refs_0_), channel_id=1, source_target_pairs={{0,2},{1,3},{2,0},{3,1},{4,6},{5,7},{6,4},{7,5},{8,10},{9,11},{10,... | collective-permute-start | bytes 12296 | tf_op jit(solution)/shard_map/ppermute | solution.py:39
  60.4 0.3 collective-permute-start.17
  60.6 1.1 %collective-permute-start.22 = (f32[32,1536]{1,0:T(8,128)S(1)}, f32[32,1536]{1,0:T(8,128)S(1)}, u32[]{:S(2)}, u32[]{:S(2)}) collective-permute-start(f32[32,1536]{1,0:T(8,128)S(1)} %get-tuple-element.90), channel_id=1, source_target_pairs={{0,4},{1,5},{2,6},{3,7},{4,0},{5,1},{6,2},{7,3},{8,12},{9,13},{10,... | collective-permute-start | bytes 589832 | tf_op jit(solution)/shard_map/ppermute | solution.py:39
  61.7 1.9 %collective-permute-start.23 = (f32[32,1536]{1,0:T(8,128)S(1)}, f32[32,1536]{1,0:T(8,128)S(1)}, u32[]{:S(2)}, u32[]{:S(2)}) collective-permute-start(f32[32,1536]{1,0:T(8,128)S(1)} %get-tuple-element.91), channel_id=1, source_target_pairs={{0,8},{1,9},{2,10},{3,11},{4,12},{5,13},{6,14},{7,15},{8,0},{9,1},... | collective-permute-start | bytes 589832 | tf_op jit(solution)/shard_map/ppermute | solution.py:39
  63.7 3.8 %gather_rows.7 = (f32[32,1536]{1,0:T(8,128)S(1)}, f32[32,1536]{1,0:T(8,128)S(1)}) custom-call(s32[3072]{0:T(1024)S(1)} %pad_add_fusion.row_ref, s32[24,128]{1,0:T(8,128)S(1)} %pad_add_fusion.1.part_ref, f32[2048,128]{1,0:T(8,128)S(1)} %get-tuple-element.87.rows_ref), custom_call_target="tpu_custom_call" | custom-call | bytes 1024 | tf_op jit(solution)/shard_map/gather_rows/pallas_call | solution.py:160
  67.5 0.1 collective-permute-start.20
  67.6 1.6 %collective-permute-start.21 = (f32[32,1536]{1,0:T(8,128)S(1)}, f32[32,1536]{1,0:T(8,128)S(1)}, u32[]{:S(2)}, u32[]{:S(2)}) collective-permute-start(f32[32,1536]{1,0:T(8,128)S(1)} %get-tuple-element.89), channel_id=1, source_target_pairs={{0,2},{1,3},{2,0},{3,1},{4,6},{5,7},{6,4},{7,5},{8,10},{9,11},{10,... | collective-permute-start | bytes 589832 | tf_op jit(solution)/shard_map/ppermute | solution.py:39
  69.2 2.5 %later_own.3 = (bf16[32,8192]{1,0:T(8,128)(2,1)S(1)}, bf16[96,96]{1,0:T(8,128)(2,1)S(1)}, f32[32,8192]{1,0:T(8,128)S(1)}) custom-call(f32[32,32]{1,0:T(8,128)S(1)} %add_add_fusion.1.refs_0_, f32[32,32]{1,0:T(8,128)S(1)} %collective-permute-done.17.refs_1_, f32[32,32]{1,0:T(8,128)S(1)} %collective-permute-done.18.refs_2_, ...), custom_call_target="tpu_custom_call" | custom-call | bytes 1024 | tf_op jit(solution)/shard_map/later_own/pallas_call | solution.py:249
  71.7 1.7 %collective-permute-done.23.refs_8_ = f32[32,1536]{1,0:T(8,128)S(1)} collective-permute-done((f32[32,1536]{1,0:T(8,128)S(1)}, f32[32,1536]{1,0:T(8,128)S(1)}, u32[]{:S(2)}, u32[]{:S(2)}) %collective-permute-start.23) | collective-permute-done | bytes 196640 | tf_op jit(solution)/shard_map/ppermute | solution.py:39
  73.4 1.5 %collective-permute-done.21.refs_6_ = f32[32,1536]{1,0:T(8,128)S(1)} collective-permute-done((f32[32,1536]{1,0:T(8,128)S(1)}, f32[32,1536]{1,0:T(8,128)S(1)}, u32[]{:S(2)}, u32[]{:S(2)}) %collective-permute-start.21) | collective-permute-done | bytes 196640 | tf_op jit(solution)/shard_map/ppermute | solution.py:39
  74.9 3.1 %product.5 = (bf16[96,8192]{1,0:T(8,128)(2,1)S(1)}, f32[32,32]{1,0:T(8,128)S(1)}) custom-call(s32[320]{0:T(512)S(1)} %copy-done.2, s32[320]{0:T(512)S(1)} %copy-done.3, s32[1]{0:T(128)S(6)} %copy.7.refs_2_, bf16[32,8192]{1,0:T(8,128)(2,1)S(1)} %get-tuple-element.85.refs_3_, f32[32,8192]{1,0:T(8,128)S(1)} %get-tuple-element.86.refs_4_, ...), custom_call_target="tpu_custom_call" | custom-call | bytes 1024 | tf_op jit(solution)/shard_map/product/pallas_call | solution.py:348
  78.0 1.4 %collective-permute-start.26 = (f32[32,32]{1,0:T(8,128)S(1)}, f32[32,32]{1,0:T(8,128)S(1)}, u32[]{:S(2)}, u32[]{:S(2)}) collective-permute-start(f32[32,32]{1,0:T(8,128)S(1)} %get-tuple-element.93), channel_id=1, source_target_pairs={{0,12},{1,13},{2,14},{3,15},{4,8},{5,9},{6,10},{7,11},{8,4},{9,5},... | collective-permute-start | bytes 12296 | tf_op jit(solution)/shard_map/ppermute | solution.py:39
  79.3 1.3 %collective-permute-start.25 = (f32[32,32]{1,0:T(8,128)S(1)}, f32[32,32]{1,0:T(8,128)S(1)}, u32[]{:S(2)}, u32[]{:S(2)}) collective-permute-start(f32[32,32]{1,0:T(8,128)S(1)} %get-tuple-element.93), channel_id=1, source_target_pairs={{0,8},{1,9},{2,10},{3,11},{4,12},{5,13},{6,14},{7,15},{8,0},{9,1},... | collective-permute-start | bytes 12296 | tf_op jit(solution)/shard_map/ppermute | solution.py:39
  80.6 1.7 %collective-permute-start.24 = (f32[32,32]{1,0:T(8,128)S(1)}, f32[32,32]{1,0:T(8,128)S(1)}, u32[]{:S(2)}, u32[]{:S(2)}) collective-permute-start(f32[32,32]{1,0:T(8,128)S(1)} %get-tuple-element.93), channel_id=1, source_target_pairs={{0,4},{1,5},{2,6},{3,7},{4,0},{5,1},{6,2},{7,3},{8,12},{9,13},{10,... | collective-permute-start | bytes 12296 | tf_op jit(solution)/shard_map/ppermute | solution.py:39
  82.4 1.1 %collective-permute-done.26 = f32[32,32]{1,0:T(8,128)S(1)} collective-permute-done((f32[32,32]{1,0:T(8,128)S(1)}, f32[32,32]{1,0:T(8,128)S(1)}, u32[]{:S(2)}, u32[]{:S(2)}) %collective-permute-start.26) | collective-permute-done | bytes 4128 | tf_op jit(solution)/shard_map/ppermute | solution.py:39
  83.5 0.5 collective-permute-done.25
  84.0 0.4 collective-permute-done.24
  84.4 0.1 collective-permute-start.29
  84.5 1.4 %collective-permute-start.28 = (f32[32,32]{1,0:T(8,128)S(1)}, f32[32,32]{1,0:T(8,128)S(1)}, u32[]{:S(2)}, u32[]{:S(2)}) collective-permute-start(f32[32,32]{1,0:T(8,128)S(1)} %add_add_fusion.refs_0_), channel_id=1, source_target_pairs={{0,2},{1,3},{2,0},{3,1},{4,6},{5,7},{6,4},{7,5},{8,10},{9,11},{10,... | collective-permute-start | bytes 12296 | tf_op jit(solution)/shard_map/ppermute | solution.py:39
  85.8 0.5 collective-permute-start.27
  86.3 1.3 %collective-permute-done.29.refs_3_ = f32[32,32]{1,0:T(8,128)S(1)} collective-permute-done((f32[32,32]{1,0:T(8,128)S(1)}, f32[32,32]{1,0:T(8,128)S(1)}, u32[]{:S(2)}, u32[]{:S(2)}) %collective-permute-start.29) | collective-permute-done | bytes 4128 | tf_op jit(solution)/shard_map/ppermute | solution.py:39
  87.7 0.6 collective-permute-done.28.refs_2_
  88.3 2.9 %final.1 = f32[32,8192]{1,0:T(8,128)} custom-call(f32[32,32]{1,0:T(8,128)S(1)} %add_add_fusion.refs_0_, f32[32,32]{1,0:T(8,128)S(1)} %collective-permute-done.27.refs_1_, f32[32,32]{1,0:T(8,128)S(1)} %collective-permute-done.28.refs_2_, f32[32,32]{1,0:T(8,128)S(1)} %collective-permute-done.29.refs_3_, bf16[96,8192]{1,0:T(8,128)(2,1)S(1)} %get-tuple-element.94.refs_4_), custom_call_target="tpu_custom_call" | custom-call | bytes 1024 | tf_op jit(solution)/shard_map/final/pallas_call | solution.py:369
  (26 shorter events, 0.1 us)
Async XLA Ops:
  1.0 1.0 %copy-start = (bf16[32,8192]{1,0:T(8,128)(2,1)S(1)}, bf16[32,8192]{1,0:T(8,128)(2,1)}, u32[]{:S(2)}) copy-start(bf16[32,8192]{1,0:T(8,128)(2,1)} %refs_3_.1) | copy-start | bytes 1572868
  6.3 12.5 %collective-permute-start.2 = (bf16[32,1536]{1,0:T(8,128)(2,1)S(1)}, bf16[32,1536]{1,0:T(8,128)(2,1)S(1)}, u32[]{:S(2)}, u32[]{:S(2)}) collective-permute-start(bf16[32,1536]{1,0:T(8,128)(2,1)S(1)} %get-tuple-element.54), channel_id=1, source_target_pairs={{0,4},{1,5},{2,6},{3,7},{4,0},{5,1},{6,2},{7,3},{8,12},{9,13},{10,... | collective-permute-start | bytes 294920 | tf_op jit(solution)/shard_map/ppermute | solution.py:39
  9.4 9.4 %collective-permute-start.3 = (bf16[32,1536]{1,0:T(8,128)(2,1)S(1)}, bf16[32,1536]{1,0:T(8,128)(2,1)S(1)}, u32[]{:S(2)}, u32[]{:S(2)}) collective-permute-start(bf16[32,1536]{1,0:T(8,128)(2,1)S(1)} %get-tuple-element.55), channel_id=1, source_target_pairs={{0,8},{1,9},{2,10},{3,11},{4,12},{5,13},{6,14},{7,15},{8,0},{9,1},... | collective-permute-start | bytes 294920 | tf_op jit(solution)/shard_map/ppermute | solution.py:39
  12.0 6.1 %copy-start.1 = (bf16[32,8192]{1,0:T(8,128)(2,1)S(1)}, bf16[32,8192]{1,0:T(8,128)(2,1)}, u32[]{:S(2)}) copy-start(bf16[32,8192]{1,0:T(8,128)(2,1)} %refs_3_.1) | copy-start | bytes 1572868
  15.7 5.3 %copy-start.2 = (s32[320]{0:T(512)S(1)}, s32[320]{0:T(512)}, u32[]{:S(2)}) copy-start(s32[320]{0:T(512)} %refs_0_.5) | copy-start | bytes 3844
  15.7 5.3 %copy-start.3 = (s32[320]{0:T(512)S(1)}, s32[320]{0:T(512)}, u32[]{:S(2)}) copy-start(s32[320]{0:T(512)} %refs_1_.5) | copy-start | bytes 3844
  15.7 3.0 %collective-permute-start = (bf16[32,1536]{1,0:T(8,128)(2,1)S(1)}, bf16[32,1536]{1,0:T(8,128)(2,1)S(1)}, u32[]{:S(2)}, u32[]{:S(2)}) collective-permute-start(bf16[32,1536]{1,0:T(8,128)(2,1)S(1)} %get-tuple-element.52), channel_id=1, source_target_pairs={{0,1},{1,0},{2,3},{3,2},{4,5},{5,4},{6,7},{7,6},{8,9},{9,8},{10,11... | collective-permute-start | bytes 294920 | tf_op jit(solution)/shard_map/ppermute | solution.py:39
  15.8 5.2 %collective-permute-start.1 = (bf16[32,1536]{1,0:T(8,128)(2,1)S(1)}, bf16[32,1536]{1,0:T(8,128)(2,1)S(1)}, u32[]{:S(2)}, u32[]{:S(2)}) collective-permute-start(bf16[32,1536]{1,0:T(8,128)(2,1)S(1)} %get-tuple-element.53), channel_id=1, source_target_pairs={{0,2},{1,3},{2,0},{3,1},{4,6},{5,7},{6,4},{7,5},{8,10},{9,11},{10,... | collective-permute-start | bytes 294920 | tf_op jit(solution)/shard_map/ppermute | solution.py:39
  23.8 8.3 %collective-permute-start.6 = (f32[32,32]{1,0:T(8,128)S(1)}, f32[32,32]{1,0:T(8,128)S(1)}, u32[]{:S(2)}, u32[]{:S(2)}) collective-permute-start(f32[32,32]{1,0:T(8,128)S(1)} %get-tuple-element.58), channel_id=1, source_target_pairs={{0,12},{1,13},{2,14},{3,15},{4,8},{5,9},{6,10},{7,11},{8,4},{9,5},... | collective-permute-start | bytes 12296 | tf_op jit(solution)/shard_map/ppermute | solution.py:39
  23.9 8.2 %collective-permute-start.5 = (f32[32,32]{1,0:T(8,128)S(1)}, f32[32,32]{1,0:T(8,128)S(1)}, u32[]{:S(2)}, u32[]{:S(2)}) collective-permute-start(f32[32,32]{1,0:T(8,128)S(1)} %get-tuple-element.58), channel_id=1, source_target_pairs={{0,8},{1,9},{2,10},{3,11},{4,12},{5,13},{6,14},{7,15},{8,0},{9,1},... | collective-permute-start | bytes 12296 | tf_op jit(solution)/shard_map/ppermute | solution.py:39
  27.0 5.1 %collective-permute-start.4 = (f32[32,32]{1,0:T(8,128)S(1)}, f32[32,32]{1,0:T(8,128)S(1)}, u32[]{:S(2)}, u32[]{:S(2)}) collective-permute-start(f32[32,32]{1,0:T(8,128)S(1)} %get-tuple-element.58), channel_id=1, source_target_pairs={{0,4},{1,5},{2,6},{3,7},{4,0},{5,1},{6,2},{7,3},{8,12},{9,13},{10,... | collective-permute-start | bytes 12296 | tf_op jit(solution)/shard_map/ppermute | solution.py:39
  32.1 3.3 %collective-permute-start.9 = (f32[32,32]{1,0:T(8,128)S(1)}, f32[32,32]{1,0:T(8,128)S(1)}, u32[]{:S(2)}, u32[]{:S(2)}) collective-permute-start(f32[32,32]{1,0:T(8,128)S(1)} %add_add_fusion.2.refs_0_), channel_id=1, source_target_pairs={{0,3},{1,2},{2,1},{3,0},{4,7},{5,6},{6,5},{7,4},{8,11},{9,10},{10,... | collective-permute-start | bytes 12296 | tf_op jit(solution)/shard_map/ppermute | solution.py:39
  32.2 3.8 %collective-permute-start.8 = (f32[32,32]{1,0:T(8,128)S(1)}, f32[32,32]{1,0:T(8,128)S(1)}, u32[]{:S(2)}, u32[]{:S(2)}) collective-permute-start(f32[32,32]{1,0:T(8,128)S(1)} %add_add_fusion.2.refs_0_), channel_id=1, source_target_pairs={{0,2},{1,3},{2,0},{3,1},{4,6},{5,7},{6,4},{7,5},{8,10},{9,11},{10,... | collective-permute-start | bytes 12296 | tf_op jit(solution)/shard_map/ppermute | solution.py:39
  33.8 2.2 %collective-permute-start.7 = (f32[32,32]{1,0:T(8,128)S(1)}, f32[32,32]{1,0:T(8,128)S(1)}, u32[]{:S(2)}, u32[]{:S(2)}) collective-permute-start(f32[32,32]{1,0:T(8,128)S(1)} %add_add_fusion.2.refs_0_), channel_id=1, source_target_pairs={{0,1},{1,0},{2,3},{3,2},{4,5},{5,4},{6,7},{7,6},{8,9},{9,8},{10,11... | collective-permute-start | bytes 12296 | tf_op jit(solution)/shard_map/ppermute | solution.py:39
  34.1 10.0 %collective-permute-start.12 = (f32[32,1536]{1,0:T(8,128)S(1)}, f32[32,1536]{1,0:T(8,128)S(1)}, u32[]{:S(2)}, u32[]{:S(2)}) collective-permute-start(f32[32,1536]{1,0:T(8,128)S(1)} %get-tuple-element.72), channel_id=1, source_target_pairs={{0,4},{1,5},{2,6},{3,7},{4,0},{5,1},{6,2},{7,3},{8,12},{9,13},{10,... | collective-permute-start | bytes 589832 | tf_op jit(solution)/shard_map/ppermute | solution.py:39
  34.8 11.7 %collective-permute-start.13 = (f32[32,1536]{1,0:T(8,128)S(1)}, f32[32,1536]{1,0:T(8,128)S(1)}, u32[]{:S(2)}, u32[]{:S(2)}) collective-permute-start(f32[32,1536]{1,0:T(8,128)S(1)} %get-tuple-element.73), channel_id=1, source_target_pairs={{0,8},{1,9},{2,10},{3,11},{4,12},{5,13},{6,14},{7,15},{8,0},{9,1},... | collective-permute-start | bytes 589832 | tf_op jit(solution)/shard_map/ppermute | solution.py:39
  39.9 6.6 %collective-permute-start.10 = (f32[32,1536]{1,0:T(8,128)S(1)}, f32[32,1536]{1,0:T(8,128)S(1)}, u32[]{:S(2)}, u32[]{:S(2)}) collective-permute-start(f32[32,1536]{1,0:T(8,128)S(1)} %get-tuple-element.70), channel_id=1, source_target_pairs={{0,1},{1,0},{2,3},{3,2},{4,5},{5,4},{6,7},{7,6},{8,9},{9,8},{10,11... | collective-permute-start | bytes 589832 | tf_op jit(solution)/shard_map/ppermute | solution.py:39
  40.3 6.9 %collective-permute-start.11 = (f32[32,1536]{1,0:T(8,128)S(1)}, f32[32,1536]{1,0:T(8,128)S(1)}, u32[]{:S(2)}, u32[]{:S(2)}) collective-permute-start(f32[32,1536]{1,0:T(8,128)S(1)} %get-tuple-element.71), channel_id=1, source_target_pairs={{0,2},{1,3},{2,0},{3,1},{4,6},{5,7},{6,4},{7,5},{8,10},{9,11},{10,... | collective-permute-start | bytes 589832 | tf_op jit(solution)/shard_map/ppermute | solution.py:39
  50.4 8.3 %collective-permute-start.16 = (f32[32,32]{1,0:T(8,128)S(1)}, f32[32,32]{1,0:T(8,128)S(1)}, u32[]{:S(2)}, u32[]{:S(2)}) collective-permute-start(f32[32,32]{1,0:T(8,128)S(1)} %get-tuple-element.76), channel_id=1, source_target_pairs={{0,12},{1,13},{2,14},{3,15},{4,8},{5,9},{6,10},{7,11},{8,4},{9,5},... | collective-permute-start | bytes 12296 | tf_op jit(solution)/shard_map/ppermute | solution.py:39
  52.9 5.8 %collective-permute-start.15 = (f32[32,32]{1,0:T(8,128)S(1)}, f32[32,32]{1,0:T(8,128)S(1)}, u32[]{:S(2)}, u32[]{:S(2)}) collective-permute-start(f32[32,32]{1,0:T(8,128)S(1)} %get-tuple-element.76), channel_id=1, source_target_pairs={{0,8},{1,9},{2,10},{3,11},{4,12},{5,13},{6,14},{7,15},{8,0},{9,1},... | collective-permute-start | bytes 12296 | tf_op jit(solution)/shard_map/ppermute | solution.py:39
  53.9 4.8 %collective-permute-start.14 = (f32[32,32]{1,0:T(8,128)S(1)}, f32[32,32]{1,0:T(8,128)S(1)}, u32[]{:S(2)}, u32[]{:S(2)}) collective-permute-start(f32[32,32]{1,0:T(8,128)S(1)} %get-tuple-element.76), channel_id=1, source_target_pairs={{0,4},{1,5},{2,6},{3,7},{4,0},{5,1},{6,2},{7,3},{8,12},{9,13},{10,... | collective-permute-start | bytes 12296 | tf_op jit(solution)/shard_map/ppermute | solution.py:39
  58.7 4.9 %collective-permute-start.19 = (f32[32,32]{1,0:T(8,128)S(1)}, f32[32,32]{1,0:T(8,128)S(1)}, u32[]{:S(2)}, u32[]{:S(2)}) collective-permute-start(f32[32,32]{1,0:T(8,128)S(1)} %add_add_fusion.1.refs_0_), channel_id=1, source_target_pairs={{0,3},{1,2},{2,1},{3,0},{4,7},{5,6},{6,5},{7,4},{8,11},{9,10},{10,... | collective-permute-start | bytes 12296 | tf_op jit(solution)/shard_map/ppermute | solution.py:39
  58.8 4.9 %collective-permute-start.18 = (f32[32,32]{1,0:T(8,128)S(1)}, f32[32,32]{1,0:T(8,128)S(1)}, u32[]{:S(2)}, u32[]{:S(2)}) collective-permute-start(f32[32,32]{1,0:T(8,128)S(1)} %add_add_fusion.1.refs_0_), channel_id=1, source_target_pairs={{0,2},{1,3},{2,0},{3,1},{4,6},{5,7},{6,4},{7,5},{8,10},{9,11},{10,... | collective-permute-start | bytes 12296 | tf_op jit(solution)/shard_map/ppermute | solution.py:39
  60.4 3.3 %collective-permute-start.17 = (f32[32,32]{1,0:T(8,128)S(1)}, f32[32,32]{1,0:T(8,128)S(1)}, u32[]{:S(2)}, u32[]{:S(2)}) collective-permute-start(f32[32,32]{1,0:T(8,128)S(1)} %add_add_fusion.1.refs_0_), channel_id=1, source_target_pairs={{0,1},{1,0},{2,3},{3,2},{4,5},{5,4},{6,7},{7,6},{8,9},{9,8},{10,11... | collective-permute-start | bytes 12296 | tf_op jit(solution)/shard_map/ppermute | solution.py:39
  60.6 11.1 %collective-permute-start.22 = (f32[32,1536]{1,0:T(8,128)S(1)}, f32[32,1536]{1,0:T(8,128)S(1)}, u32[]{:S(2)}, u32[]{:S(2)}) collective-permute-start(f32[32,1536]{1,0:T(8,128)S(1)} %get-tuple-element.90), channel_id=1, source_target_pairs={{0,4},{1,5},{2,6},{3,7},{4,0},{5,1},{6,2},{7,3},{8,12},{9,13},{10,... | collective-permute-start | bytes 589832 | tf_op jit(solution)/shard_map/ppermute | solution.py:39
  61.7 11.7 %collective-permute-start.23 = (f32[32,1536]{1,0:T(8,128)S(1)}, f32[32,1536]{1,0:T(8,128)S(1)}, u32[]{:S(2)}, u32[]{:S(2)}) collective-permute-start(f32[32,1536]{1,0:T(8,128)S(1)} %get-tuple-element.91), channel_id=1, source_target_pairs={{0,8},{1,9},{2,10},{3,11},{4,12},{5,13},{6,14},{7,15},{8,0},{9,1},... | collective-permute-start | bytes 589832 | tf_op jit(solution)/shard_map/ppermute | solution.py:39
  67.5 5.9 %collective-permute-start.20 = (f32[32,1536]{1,0:T(8,128)S(1)}, f32[32,1536]{1,0:T(8,128)S(1)}, u32[]{:S(2)}, u32[]{:S(2)}) collective-permute-start(f32[32,1536]{1,0:T(8,128)S(1)} %get-tuple-element.88), channel_id=1, source_target_pairs={{0,1},{1,0},{2,3},{3,2},{4,5},{5,4},{6,7},{7,6},{8,9},{9,8},{10,11... | collective-permute-start | bytes 589832 | tf_op jit(solution)/shard_map/ppermute | solution.py:39
  67.6 7.3 %collective-permute-start.21 = (f32[32,1536]{1,0:T(8,128)S(1)}, f32[32,1536]{1,0:T(8,128)S(1)}, u32[]{:S(2)}, u32[]{:S(2)}) collective-permute-start(f32[32,1536]{1,0:T(8,128)S(1)} %get-tuple-element.89), channel_id=1, source_target_pairs={{0,2},{1,3},{2,0},{3,1},{4,6},{5,7},{6,4},{7,5},{8,10},{9,11},{10,... | collective-permute-start | bytes 589832 | tf_op jit(solution)/shard_map/ppermute | solution.py:39
  78.0 5.5 %collective-permute-start.26 = (f32[32,32]{1,0:T(8,128)S(1)}, f32[32,32]{1,0:T(8,128)S(1)}, u32[]{:S(2)}, u32[]{:S(2)}) collective-permute-start(f32[32,32]{1,0:T(8,128)S(1)} %get-tuple-element.93), channel_id=1, source_target_pairs={{0,12},{1,13},{2,14},{3,15},{4,8},{5,9},{6,10},{7,11},{8,4},{9,5},... | collective-permute-start | bytes 12296 | tf_op jit(solution)/shard_map/ppermute | solution.py:39
  79.3 4.6 %collective-permute-start.25 = (f32[32,32]{1,0:T(8,128)S(1)}, f32[32,32]{1,0:T(8,128)S(1)}, u32[]{:S(2)}, u32[]{:S(2)}) collective-permute-start(f32[32,32]{1,0:T(8,128)S(1)} %get-tuple-element.93), channel_id=1, source_target_pairs={{0,8},{1,9},{2,10},{3,11},{4,12},{5,13},{6,14},{7,15},{8,0},{9,1},... | collective-permute-start | bytes 12296 | tf_op jit(solution)/shard_map/ppermute | solution.py:39
  80.6 3.7 %collective-permute-start.24 = (f32[32,32]{1,0:T(8,128)S(1)}, f32[32,32]{1,0:T(8,128)S(1)}, u32[]{:S(2)}, u32[]{:S(2)}) collective-permute-start(f32[32,32]{1,0:T(8,128)S(1)} %get-tuple-element.93), channel_id=1, source_target_pairs={{0,4},{1,5},{2,6},{3,7},{4,0},{5,1},{6,2},{7,3},{8,12},{9,13},{10,... | collective-permute-start | bytes 12296 | tf_op jit(solution)/shard_map/ppermute | solution.py:39
  84.4 3.3 %collective-permute-start.29 = (f32[32,32]{1,0:T(8,128)S(1)}, f32[32,32]{1,0:T(8,128)S(1)}, u32[]{:S(2)}, u32[]{:S(2)}) collective-permute-start(f32[32,32]{1,0:T(8,128)S(1)} %add_add_fusion.refs_0_), channel_id=1, source_target_pairs={{0,3},{1,2},{2,1},{3,0},{4,7},{5,6},{6,5},{7,4},{8,11},{9,10},{10,... | collective-permute-start | bytes 12296 | tf_op jit(solution)/shard_map/ppermute | solution.py:39
  84.5 3.8 %collective-permute-start.28 = (f32[32,32]{1,0:T(8,128)S(1)}, f32[32,32]{1,0:T(8,128)S(1)}, u32[]{:S(2)}, u32[]{:S(2)}) collective-permute-start(f32[32,32]{1,0:T(8,128)S(1)} %add_add_fusion.refs_0_), channel_id=1, source_target_pairs={{0,2},{1,3},{2,0},{3,1},{4,6},{5,7},{6,4},{7,5},{8,10},{9,11},{10,... | collective-permute-start | bytes 12296 | tf_op jit(solution)/shard_map/ppermute | solution.py:39
  85.8 2.4 %collective-permute-start.27 = (f32[32,32]{1,0:T(8,128)S(1)}, f32[32,32]{1,0:T(8,128)S(1)}, u32[]{:S(2)}, u32[]{:S(2)}) collective-permute-start(f32[32,32]{1,0:T(8,128)S(1)} %add_add_fusion.refs_0_), channel_id=1, source_target_pairs={{0,1},{1,0},{2,3},{3,2},{4,5},{5,4},{6,7},{7,6},{8,9},{9,8},{10,11... | collective-permute-start | bytes 12296 | tf_op jit(solution)/shard_map/ppermute | solution.py:39

commit v4 on v3

--- a/solution.py
+++ b/solution.py
@@ -405,8 +405,8 @@
     pack_states = PACK * LANES
     row_lists = lists // pack_states * LANES + lists % LANES
     part_lists = lists // LANES % PACK
-    far = (3, 2)
-    near = (1, 0)
+    far = (3, 0)
+    near = (2, 1)
 
     def lists_of(colours):
         rows = jnp.concatenate([row_lists[c] for c in colours])

time: 91.6 us -> 98.1 us (1.071)
  the two profiles are of different devices: /device:TPU:0 before, /device:TPU:3 now
where the time goes in v4:
time: 98.1 us; the launch traced here: 97.4 us
  Pallas kernels  40.8 us (42%)
  starting transfers between devices  35.7 us (36%)
  waiting for transfers between devices  18 us (18%)
  local copies, waits for them, and re-layouts  1.18 us (1%)
    ppermute x30, starting transfers between devices, swapped(): return lax.ppermute(x, 'dom', [(i, i ^ mask) for i in range(size)])  35.7 us
    ppermute x30, waiting for transfers between devices, swapped(): return lax.ppermute(x, 'dom', [(i, i ^ mask) for i in range(size)])  18 us
    pallas_call x4, Pallas kernels, gather_colours(): pl.pallas_call(gather_kernel, out_shape=[vmem_out((columns, indices // co...  15.3 us
    pallas_call x3, Pallas kernels, product(): pl.pallas_call(functools.partial(product_kernel, len(ghosts), group, with...  8.92 us
    pallas_call x2, Pallas kernels, start_gather(): pl.pallas_call(functools.partial(start_kernel, count, first, make_rows),...  7.97 us
    pallas_call x2, Pallas kernels, later_own(): pl.pallas_call(functools.partial(later_own_kernel, total_states), out_sha...  5 us
    pallas_call x1, Pallas kernels, final(): pl.pallas_call(functools.partial(final_kernel, total_states), out_shape=j...  2.94 us
  transfers between devices with their start and end apart: 30, of which 12 were waited for; matrix products, arithmetic and copies ran while one was open for 0% of the time, Pallas kernels for 25%

profile of v4, /device:TPU:3, one launch (start us, length us, event | category | flops | bytes accessed | tf_op | source)
XLA Modules:
  0.0 97.4 jit_solution(15845467064408085010)
XLA Ops:
  0.0 0.8 add_select_fusion
  0.8 0.1 slice_reduce_fusion.1
  1.0 0.0 copy-start
  1.0 1.0 %copy-done = bf16[32,8192]{1,0:T(8,128)(2,1)S(1)} copy-done((bf16[32,8192]{1,0:T(8,128)(2,1)S(1)}, bf16[32,8192]{1,0:T(8,128)(2,1)}, u32[]{:S(2)}) %copy-start) | copy-done | bytes 524312
  2.0 4.2 %start_gather.2 = (bf16[32,1536]{1,0:T(8,128)(2,1)S(1)}, bf16[32,1536]{1,0:T(8,128)(2,1)S(1)}, bf16[256,128,128]{2,1,0:T(8,128)(2,1)S(1)}, f32[2048,128]{1,0:T(8,128)S(1)}) custom-call(s32[3072]{0:T(1024)S(1)} %pad_add_fusion.2.row_ref, s32[24,128]{1,0:T(8,128)S(1)} %pad_add_fusion.3.part_ref, bf16[32,8192]{1,0:T(8,128)(2,1)S(1)} %copy-done, ...), custom_call_target="tpu_custom_call" | custom-call | bytes 1024 | tf_op jit(solution)/shard_map/start_gather/pallas_call | solution.py:202
  6.3 0.7 collective-permute-start
  7.0 2.3 %collective-permute-start.3 = (bf16[32,1536]{1,0:T(8,128)(2,1)S(1)}, bf16[32,1536]{1,0:T(8,128)(2,1)S(1)}, u32[]{:S(2)}, u32[]{:S(2)}) collective-permute-start(bf16[32,1536]{1,0:T(8,128)(2,1)S(1)} %get-tuple-element.55), channel_id=1, source_target_pairs={{0,8},{1,9},{2,10},{3,11},{4,12},{5,13},{6,14},{7,15},{8,0},{9,1},... | collective-permute-start | bytes 294920 | tf_op jit(solution)/shard_map/ppermute | solution.py:39
  9.4 0.0 copy-start.1
  9.4 3.7 %start_gather.3 = (bf16[32,1536]{1,0:T(8,128)(2,1)S(1)}, bf16[32,1536]{1,0:T(8,128)(2,1)S(1)}, bf16[64,128,128]{2,1,0:T(8,128)(2,1)S(1)}) custom-call(s32[3072]{0:T(1024)S(1)} %pad_add_fusion.row_ref, s32[24,128]{1,0:T(8,128)S(1)} %pad_add_fusion.1.part_ref, f32[2048,128]{1,0:T(8,128)S(1)} %get-tuple-element.50.source_ref, bf16[320,128,128]{2,1,0:T(8,128)(2,1)} %tiles_ref.3), custom_call_target="tpu_custom_call" | custom-call | bytes 1024 | tf_op jit(solution)/shard_map/start_gather/pallas_call | solution.py:202
  13.1 0.0 copy-start.2
  13.1 0.0 copy-start.3
  13.1 1.3 %collective-permute-start.1 = (bf16[32,1536]{1,0:T(8,128)(2,1)S(1)}, bf16[32,1536]{1,0:T(8,128)(2,1)S(1)}, u32[]{:S(2)}, u32[]{:S(2)}) collective-permute-start(bf16[32,1536]{1,0:T(8,128)(2,1)S(1)} %get-tuple-element.53), channel_id=1, source_target_pairs={{0,2},{1,3},{2,0},{3,1},{4,6},{5,7},{6,4},{7,5},{8,10},{9,11},{10,... | collective-permute-start | bytes 294920 | tf_op jit(solution)/shard_map/ppermute | solution.py:39
  14.4 1.3 %collective-permute-start.2 = (bf16[32,1536]{1,0:T(8,128)(2,1)S(1)}, bf16[32,1536]{1,0:T(8,128)(2,1)S(1)}, u32[]{:S(2)}, u32[]{:S(2)}) collective-permute-start(bf16[32,1536]{1,0:T(8,128)(2,1)S(1)} %get-tuple-element.54), channel_id=1, source_target_pairs={{0,4},{1,5},{2,6},{3,7},{4,0},{5,1},{6,2},{7,3},{8,12},{9,13},{10,... | collective-permute-start | bytes 294920 | tf_op jit(solution)/shard_map/ppermute | solution.py:39
  16.4 0.7 first_own.1.refs_4_
  17.1 0.0 collective-permute-done.refs_5_
  17.1 0.0 collective-permute-done.3.refs_8_
  17.1 0.2 collective-permute-done.1.refs_6_
  17.2 0.8 collective-permute-done.2.refs_7_
  18.0 2.7 %product.3 = (bf16[96,8192]{1,0:T(8,128)(2,1)S(1)}, f32[32,32]{1,0:T(8,128)S(1)}, f32[2048,128]{1,0:T(8,128)S(1)}) custom-call(s32[320]{0:T(512)S(1)} %copy-done.2, s32[320]{0:T(512)S(1)} %copy-done.3, s32[1]{0:T(128)S(6)} %copy.7.refs_2_, bf16[32,8192]{1,0:T(8,128)(2,1)S(1)} %copy-done.1, f32[32,8192]{1,0:T(8,128)S(1)} %first_own.1.refs_4_, ...), custom_call_target="tpu_custom_call" | custom-call | bytes 1024 | tf_op jit(solution)/shard_map/product/pallas_call | solution.py:348
  20.8 1.1 %collective-permute-start.6 = (f32[32,32]{1,0:T(8,128)S(1)}, f32[32,32]{1,0:T(8,128)S(1)}, u32[]{:S(2)}, u32[]{:S(2)}) collective-permute-start(f32[32,32]{1,0:T(8,128)S(1)} %get-tuple-element.58), channel_id=1, source_target_pairs={{0,12},{1,13},{2,14},{3,15},{4,8},{5,9},{6,10},{7,11},{8,4},{9,5},... | collective-permute-start | bytes 12296 | tf_op jit(solution)/shard_map/ppermute | solution.py:39
  21.9 0.8 collective-permute-start.5
  22.7 1.7 %collective-permute-start.4 = (f32[32,32]{1,0:T(8,128)S(1)}, f32[32,32]{1,0:T(8,128)S(1)}, u32[]{:S(2)}, u32[]{:S(2)}) collective-permute-start(f32[32,32]{1,0:T(8,128)S(1)} %get-tuple-element.58), channel_id=1, source_target_pairs={{0,4},{1,5},{2,6},{3,7},{4,0},{5,1},{6,2},{7,3},{8,12},{9,13},{10,... | collective-permute-start | bytes 12296 | tf_op jit(solution)/shard_map/ppermute | solution.py:39
  24.4 3.8 %gather_rows.4 = (f32[32,1536]{1,0:T(8,128)S(1)}, f32[32,1536]{1,0:T(8,128)S(1)}) custom-call(s32[3072]{0:T(1024)S(1)} %pad_add_fusion.2.row_ref, s32[24,128]{1,0:T(8,128)S(1)} %pad_add_fusion.3.part_ref, f32[2048,128]{1,0:T(8,128)S(1)} %get-tuple-element.70.rows_ref), custom_call_target="tpu_custom_call" | custom-call | bytes 1024 | tf_op jit(solution)/shard_map/gather_rows/pallas_call | solution.py:160
  28.2 0.0 collective-permute-done.6
  28.3 2.7 %collective-permute-start.9 = (f32[32,32]{1,0:T(8,128)S(1)}, f32[32,32]{1,0:T(8,128)S(1)}, u32[]{:S(2)}, u32[]{:S(2)}) collective-permute-start(f32[32,32]{1,0:T(8,128)S(1)} %add_add_fusion.2.refs_0_), channel_id=1, source_target_pairs={{0,3},{1,2},{2,1},{3,0},{4,7},{5,6},{6,5},{7,4},{8,11},{9,10},{10,... | collective-permute-start | bytes 12296 | tf_op jit(solution)/shard_map/ppermute | solution.py:39
  31.0 1.2 %collective-permute-start.8 = (f32[32,32]{1,0:T(8,128)S(1)}, f32[32,32]{1,0:T(8,128)S(1)}, u32[]{:S(2)}, u32[]{:S(2)}) collective-permute-start(f32[32,32]{1,0:T(8,128)S(1)} %add_add_fusion.2.refs_0_), channel_id=1, source_target_pairs={{0,2},{1,3},{2,0},{3,1},{4,6},{5,7},{6,4},{7,5},{8,10},{9,11},{10,... | collective-permute-start | bytes 12296 | tf_op jit(solution)/shard_map/ppermute | solution.py:39
  32.2 0.0 collective-permute-start.7
  32.2 0.5 collective-permute-start.10
  32.7 0.4 collective-permute-start.13
  33.1 0.0 collective-permute-done.9.refs_3_
  33.1 0.5 collective-permute-done.8.refs_2_
  33.6 3.8 %gather_rows.5 = (f32[32,1536]{1,0:T(8,128)S(1)}, f32[32,1536]{1,0:T(8,128)S(1)}) custom-call(s32[3072]{0:T(1024)S(1)} %pad_add_fusion.row_ref, s32[24,128]{1,0:T(8,128)S(1)} %pad_add_fusion.1.part_ref, f32[2048,128]{1,0:T(8,128)S(1)} %get-tuple-element.70.rows_ref), custom_call_target="tpu_custom_call" | custom-call | bytes 1024 | tf_op jit(solution)/shard_map/gather_rows/pallas_call | solution.py:160
  37.5 1.3 %collective-permute-start.11 = (f32[32,1536]{1,0:T(8,128)S(1)}, f32[32,1536]{1,0:T(8,128)S(1)}, u32[]{:S(2)}, u32[]{:S(2)}) collective-permute-start(f32[32,1536]{1,0:T(8,128)S(1)} %get-tuple-element.71), channel_id=1, source_target_pairs={{0,2},{1,3},{2,0},{3,1},{4,6},{5,7},{6,4},{7,5},{8,10},{9,11},{10,... | collective-permute-start | bytes 589832 | tf_op jit(solution)/shard_map/ppermute | solution.py:39
  38.7 1.5 %collective-permute-start.12 = (f32[32,1536]{1,0:T(8,128)S(1)}, f32[32,1536]{1,0:T(8,128)S(1)}, u32[]{:S(2)}, u32[]{:S(2)}) collective-permute-start(f32[32,1536]{1,0:T(8,128)S(1)} %get-tuple-element.72), channel_id=1, source_target_pairs={{0,4},{1,5},{2,6},{3,7},{4,0},{5,1},{6,2},{7,3},{8,12},{9,13},{10,... | collective-permute-start | bytes 589832 | tf_op jit(solution)/shard_map/ppermute | solution.py:39
  40.2 2.5 %later_own.2 = (bf16[32,8192]{1,0:T(8,128)(2,1)S(1)}, bf16[96,96]{1,0:T(8,128)(2,1)S(1)}, f32[32,8192]{1,0:T(8,128)S(1)}) custom-call(f32[32,32]{1,0:T(8,128)S(1)} %add_add_fusion.2.refs_0_, f32[32,32]{1,0:T(8,128)S(1)} %collective-permute-done.7.refs_1_, f32[32,32]{1,0:T(8,128)S(1)} %collective-permute-done.8.refs_2_, ...), custom_call_target="tpu_custom_call" | custom-call | bytes 1024 | tf_op jit(solution)/shard_map/later_own/pallas_call | solution.py:249
  42.7 0.0 collective-permute-done.10.refs_5_
  42.7 1.8 %collective-permute-done.13.refs_8_ = f32[32,1536]{1,0:T(8,128)S(1)} collective-permute-done((f32[32,1536]{1,0:T(8,128)S(1)}, f32[32,1536]{1,0:T(8,128)S(1)}, u32[]{:S(2)}, u32[]{:S(2)}) %collective-permute-start.13) | collective-permute-done | bytes 196640 | tf_op jit(solution)/shard_map/ppermute | solution.py:39
  44.6 0.0 collective-permute-done.11.refs_6_
  44.6 4.3 %collective-permute-done.12.refs_7_ = f32[32,1536]{1,0:T(8,128)S(1)} collective-permute-done((f32[32,1536]{1,0:T(8,128)S(1)}, f32[32,1536]{1,0:T(8,128)S(1)}, u32[]{:S(2)}, u32[]{:S(2)}) %collective-permute-start.12) | collective-permute-done | bytes 196640 | tf_op jit(solution)/shard_map/ppermute | solution.py:39
  48.9 3.1 %product.4 = (bf16[96,8192]{1,0:T(8,128)(2,1)S(1)}, f32[32,32]{1,0:T(8,128)S(1)}, f32[2048,128]{1,0:T(8,128)S(1)}) custom-call(s32[320]{0:T(512)S(1)} %copy-done.2, s32[320]{0:T(512)S(1)} %copy-done.3, s32[1]{0:T(128)S(6)} %copy.7.refs_2_, bf16[32,8192]{1,0:T(8,128)(2,1)S(1)} %get-tuple-element.67.refs_3_, f32[32,8192]{1,0:T(8,128)S(1)} %get-tuple-element.68.refs_4_, ...), custom_call_target="tpu_custom_call" | custom-call | bytes 1024 | tf_op jit(solution)/shard_map/product/pallas_call | solution.py:348
  52.0 1.3 %collective-permute-start.16 = (f32[32,32]{1,0:T(8,128)S(1)}, f32[32,32]{1,0:T(8,128)S(1)}, u32[]{:S(2)}, u32[]{:S(2)}) collective-permute-start(f32[32,32]{1,0:T(8,128)S(1)} %get-tuple-element.76), channel_id=1, source_target_pairs={{0,12},{1,13},{2,14},{3,15},{4,8},{5,9},{6,10},{7,11},{8,4},{9,5},... | collective-permute-start | bytes 12296 | tf_op jit(solution)/shard_map/ppermute | solution.py:39
  53.3 2.3 %collective-permute-start.14 = (f32[32,32]{1,0:T(8,128)S(1)}, f32[32,32]{1,0:T(8,128)S(1)}, u32[]{:S(2)}, u32[]{:S(2)}) collective-permute-start(f32[32,32]{1,0:T(8,128)S(1)} %get-tuple-element.76), channel_id=1, source_target_pairs={{0,4},{1,5},{2,6},{3,7},{4,0},{5,1},{6,2},{7,3},{8,12},{9,13},{10,... | collective-permute-start | bytes 12296 | tf_op jit(solution)/shard_map/ppermute | solution.py:39
  55.6 3.8 %gather_rows.6 = (f32[32,1536]{1,0:T(8,128)S(1)}, f32[32,1536]{1,0:T(8,128)S(1)}) custom-call(s32[3072]{0:T(1024)S(1)} %pad_add_fusion.2.row_ref, s32[24,128]{1,0:T(8,128)S(1)} %pad_add_fusion.3.part_ref, f32[2048,128]{1,0:T(8,128)S(1)} %get-tuple-element.88.rows_ref), custom_call_target="tpu_custom_call" | custom-call | bytes 1024 | tf_op jit(solution)/shard_map/gather_rows/pallas_call | solution.py:160
  59.5 1.9 %collective-permute-start.19 = (f32[32,32]{1,0:T(8,128)S(1)}, f32[32,32]{1,0:T(8,128)S(1)}, u32[]{:S(2)}, u32[]{:S(2)}) collective-permute-start(f32[32,32]{1,0:T(8,128)S(1)} %add_add_fusion.1.refs_0_), channel_id=1, source_target_pairs={{0,3},{1,2},{2,1},{3,0},{4,7},{5,6},{6,5},{7,4},{8,11},{9,10},{10,... | collective-permute-start | bytes 12296 | tf_op jit(solution)/shard_map/ppermute | solution.py:39
  61.4 0.9 collective-permute-start.18
  62.2 0.5 collective-permute-start.20
  62.7 1.0 %collective-permute-start.23 = (f32[32,1536]{1,0:T(8,128)S(1)}, f32[32,1536]{1,0:T(8,128)S(1)}, u32[]{:S(2)}, u32[]{:S(2)}) collective-permute-start(f32[32,1536]{1,0:T(8,128)S(1)} %get-tuple-element.91), channel_id=1, source_target_pairs={{0,8},{1,9},{2,10},{3,11},{4,12},{5,13},{6,14},{7,15},{8,0},{9,1},... | collective-permute-start | bytes 589832 | tf_op jit(solution)/shard_map/ppermute | solution.py:39
  63.8 0.6 collective-permute-done.18.refs_2_
  64.4 3.8 %gather_rows.7 = (f32[32,1536]{1,0:T(8,128)S(1)}, f32[32,1536]{1,0:T(8,128)S(1)}) custom-call(s32[3072]{0:T(1024)S(1)} %pad_add_fusion.row_ref, s32[24,128]{1,0:T(8,128)S(1)} %pad_add_fusion.1.part_ref, f32[2048,128]{1,0:T(8,128)S(1)} %get-tuple-element.88.rows_ref), custom_call_target="tpu_custom_call" | custom-call | bytes 1024 | tf_op jit(solution)/shard_map/gather_rows/pallas_call | solution.py:160
  68.2 0.9 collective-permute-start.21
  69.1 1.7 %collective-permute-start.22 = (f32[32,1536]{1,0:T(8,128)S(1)}, f32[32,1536]{1,0:T(8,128)S(1)}, u32[]{:S(2)}, u32[]{:S(2)}) collective-permute-start(f32[32,1536]{1,0:T(8,128)S(1)} %get-tuple-element.90), channel_id=1, source_target_pairs={{0,4},{1,5},{2,6},{3,7},{4,0},{5,1},{6,2},{7,3},{8,12},{9,13},{10,... | collective-permute-start | bytes 589832 | tf_op jit(solution)/shard_map/ppermute | solution.py:39
  70.9 2.5 %later_own.3 = (bf16[32,8192]{1,0:T(8,128)(2,1)S(1)}, bf16[96,96]{1,0:T(8,128)(2,1)S(1)}, f32[32,8192]{1,0:T(8,128)S(1)}) custom-call(f32[32,32]{1,0:T(8,128)S(1)} %add_add_fusion.1.refs_0_, f32[32,32]{1,0:T(8,128)S(1)} %collective-permute-done.17.refs_1_, f32[32,32]{1,0:T(8,128)S(1)} %collective-permute-done.18.refs_2_, ...), custom_call_target="tpu_custom_call" | custom-call | bytes 1024 | tf_op jit(solution)/shard_map/later_own/pallas_call | solution.py:249
  73.4 1.2 %collective-permute-done.23.refs_8_ = f32[32,1536]{1,0:T(8,128)S(1)} collective-permute-done((f32[32,1536]{1,0:T(8,128)S(1)}, f32[32,1536]{1,0:T(8,128)S(1)}, u32[]{:S(2)}, u32[]{:S(2)}) %collective-permute-start.23) | collective-permute-done | bytes 196640 | tf_op jit(solution)/shard_map/ppermute | solution.py:39
  74.6 4.3 %collective-permute-done.22.refs_7_ = f32[32,1536]{1,0:T(8,128)S(1)} collective-permute-done((f32[32,1536]{1,0:T(8,128)S(1)}, f32[32,1536]{1,0:T(8,128)S(1)}, u32[]{:S(2)}, u32[]{:S(2)}) %collective-permute-start.22) | collective-permute-done | bytes 196640 | tf_op jit(solution)/shard_map/ppermute | solution.py:39
  78.9 3.1 %product.5 = (bf16[96,8192]{1,0:T(8,128)(2,1)S(1)}, f32[32,32]{1,0:T(8,128)S(1)}) custom-call(s32[320]{0:T(512)S(1)} %copy-done.2, s32[320]{0:T(512)S(1)} %copy-done.3, s32[1]{0:T(128)S(6)} %copy.7.refs_2_, bf16[32,8192]{1,0:T(8,128)(2,1)S(1)} %get-tuple-element.85.refs_3_, f32[32,8192]{1,0:T(8,128)S(1)} %get-tuple-element.86.refs_4_, ...), custom_call_target="tpu_custom_call" | custom-call | bytes 1024 | tf_op jit(solution)/shard_map/product/pallas_call | solution.py:348
  82.0 1.9 %collective-permute-start.26 = (f32[32,32]{1,0:T(8,128)S(1)}, f32[32,32]{1,0:T(8,128)S(1)}, u32[]{:S(2)}, u32[]{:S(2)}) collective-permute-start(f32[32,32]{1,0:T(8,128)S(1)} %get-tuple-element.93), channel_id=1, source_target_pairs={{0,12},{1,13},{2,14},{3,15},{4,8},{5,9},{6,10},{7,11},{8,4},{9,5},... | collective-permute-start | bytes 12296 | tf_op jit(solution)/shard_map/ppermute | solution.py:39
  83.9 1.7 %collective-permute-start.24 = (f32[32,32]{1,0:T(8,128)S(1)}, f32[32,32]{1,0:T(8,128)S(1)}, u32[]{:S(2)}, u32[]{:S(2)}) collective-permute-start(f32[32,32]{1,0:T(8,128)S(1)} %get-tuple-element.93), channel_id=1, source_target_pairs={{0,4},{1,5},{2,6},{3,7},{4,0},{5,1},{6,2},{7,3},{8,12},{9,13},{10,... | collective-permute-start | bytes 12296 | tf_op jit(solution)/shard_map/ppermute | solution.py:39
  85.5 0.8 collective-permute-done.26
  86.4 1.3 %collective-permute-done.25 = f32[32,32]{1,0:T(8,128)S(1)} collective-permute-done((f32[32,32]{1,0:T(8,128)S(1)}, f32[32,32]{1,0:T(8,128)S(1)}, u32[]{:S(2)}, u32[]{:S(2)}) %collective-permute-start.25) | collective-permute-done | bytes 4128 | tf_op jit(solution)/shard_map/ppermute | solution.py:39
  87.7 4.2 %collective-permute-start.29 = (f32[32,32]{1,0:T(8,128)S(1)}, f32[32,32]{1,0:T(8,128)S(1)}, u32[]{:S(2)}, u32[]{:S(2)}) collective-permute-start(f32[32,32]{1,0:T(8,128)S(1)} %add_add_fusion.refs_0_), channel_id=1, source_target_pairs={{0,3},{1,2},{2,1},{3,0},{4,7},{5,6},{6,5},{7,4},{8,11},{9,10},{10,... | collective-permute-start | bytes 12296 | tf_op jit(solution)/shard_map/ppermute | solution.py:39
  91.9 0.5 collective-permute-start.27
  92.4 0.9 collective-permute-done.29.refs_3_
  93.3 1.2 %collective-permute-done.28.refs_2_ = f32[32,32]{1,0:T(8,128)S(1)} collective-permute-done((f32[32,32]{1,0:T(8,128)S(1)}, f32[32,32]{1,0:T(8,128)S(1)}, u32[]{:S(2)}, u32[]{:S(2)}) %collective-permute-start.28) | collective-permute-done | bytes 4128 | tf_op jit(solution)/shard_map/ppermute | solution.py:39
  94.5 2.9 %final.1 = f32[32,8192]{1,0:T(8,128)} custom-call(f32[32,32]{1,0:T(8,128)S(1)} %add_add_fusion.refs_0_, f32[32,32]{1,0:T(8,128)S(1)} %collective-permute-done.27.refs_1_, f32[32,32]{1,0:T(8,128)S(1)} %collective-permute-done.28.refs_2_, f32[32,32]{1,0:T(8,128)S(1)} %collective-permute-done.29.refs_3_, bf16[96,8192]{1,0:T(8,128)(2,1)S(1)} %get-tuple-element.94.refs_4_), custom_call_target="tpu_custom_call" | custom-call | bytes 1024 | tf_op jit(solution)/shard_map/final/pallas_call | solution.py:369
  (26 shorter events, 0.1 us)
Async XLA Ops:
  1.0 1.0 %copy-start = (bf16[32,8192]{1,0:T(8,128)(2,1)S(1)}, bf16[32,8192]{1,0:T(8,128)(2,1)}, u32[]{:S(2)}) copy-start(bf16[32,8192]{1,0:T(8,128)(2,1)} %refs_3_.1) | copy-start | bytes 1572868
  6.3 10.8 %collective-permute-start = (bf16[32,1536]{1,0:T(8,128)(2,1)S(1)}, bf16[32,1536]{1,0:T(8,128)(2,1)S(1)}, u32[]{:S(2)}, u32[]{:S(2)}) collective-permute-start(bf16[32,1536]{1,0:T(8,128)(2,1)S(1)} %get-tuple-element.52), channel_id=1, source_target_pairs={{0,1},{1,0},{2,3},{3,2},{4,5},{5,4},{6,7},{7,6},{8,9},{9,8},{10,11... | collective-permute-start | bytes 294920 | tf_op jit(solution)/shard_map/ppermute | solution.py:39
  7.0 10.0 %collective-permute-start.3 = (bf16[32,1536]{1,0:T(8,128)(2,1)S(1)}, bf16[32,1536]{1,0:T(8,128)(2,1)S(1)}, u32[]{:S(2)}, u32[]{:S(2)}) collective-permute-start(bf16[32,1536]{1,0:T(8,128)(2,1)S(1)} %get-tuple-element.55), channel_id=1, source_target_pairs={{0,8},{1,9},{2,10},{3,11},{4,12},{5,13},{6,14},{7,15},{8,0},{9,1},... | collective-permute-start | bytes 294920 | tf_op jit(solution)/shard_map/ppermute | solution.py:39
  9.4 7.0 %copy-start.1 = (bf16[32,8192]{1,0:T(8,128)(2,1)S(1)}, bf16[32,8192]{1,0:T(8,128)(2,1)}, u32[]{:S(2)}) copy-start(bf16[32,8192]{1,0:T(8,128)(2,1)} %refs_3_.1) | copy-start | bytes 1572868
  13.1 4.9 %copy-start.2 = (s32[320]{0:T(512)S(1)}, s32[320]{0:T(512)}, u32[]{:S(2)}) copy-start(s32[320]{0:T(512)} %refs_0_.5) | copy-start | bytes 3844
  13.1 4.9 %copy-start.3 = (s32[320]{0:T(512)S(1)}, s32[320]{0:T(512)}, u32[]{:S(2)}) copy-start(s32[320]{0:T(512)} %refs_1_.5) | copy-start | bytes 3844
  13.1 4.1 %collective-permute-start.1 = (bf16[32,1536]{1,0:T(8,128)(2,1)S(1)}, bf16[32,1536]{1,0:T(8,128)(2,1)S(1)}, u32[]{:S(2)}, u32[]{:S(2)}) collective-permute-start(bf16[32,1536]{1,0:T(8,128)(2,1)S(1)} %get-tuple-element.53), channel_id=1, source_target_pairs={{0,2},{1,3},{2,0},{3,1},{4,6},{5,7},{6,4},{7,5},{8,10},{9,11},{10,... | collective-permute-start | bytes 294920 | tf_op jit(solution)/shard_map/ppermute | solution.py:39
  14.4 3.6 %collective-permute-start.2 = (bf16[32,1536]{1,0:T(8,128)(2,1)S(1)}, bf16[32,1536]{1,0:T(8,128)(2,1)S(1)}, u32[]{:S(2)}, u32[]{:S(2)}) collective-permute-start(bf16[32,1536]{1,0:T(8,128)(2,1)S(1)} %get-tuple-element.54), channel_id=1, source_target_pairs={{0,4},{1,5},{2,6},{3,7},{4,0},{5,1},{6,2},{7,3},{8,12},{9,13},{10,... | collective-permute-start | bytes 294920 | tf_op jit(solution)/shard_map/ppermute | solution.py:39
  20.8 7.5 %collective-permute-start.6 = (f32[32,32]{1,0:T(8,128)S(1)}, f32[32,32]{1,0:T(8,128)S(1)}, u32[]{:S(2)}, u32[]{:S(2)}) collective-permute-start(f32[32,32]{1,0:T(8,128)S(1)} %get-tuple-element.58), channel_id=1, source_target_pairs={{0,12},{1,13},{2,14},{3,15},{4,8},{5,9},{6,10},{7,11},{8,4},{9,5},... | collective-permute-start | bytes 12296 | tf_op jit(solution)/shard_map/ppermute | solution.py:39
  21.9 6.3 %collective-permute-start.5 = (f32[32,32]{1,0:T(8,128)S(1)}, f32[32,32]{1,0:T(8,128)S(1)}, u32[]{:S(2)}, u32[]{:S(2)}) collective-permute-start(f32[32,32]{1,0:T(8,128)S(1)} %get-tuple-element.58), channel_id=1, source_target_pairs={{0,8},{1,9},{2,10},{3,11},{4,12},{5,13},{6,14},{7,15},{8,0},{9,1},... | collective-permute-start | bytes 12296 | tf_op jit(solution)/shard_map/ppermute | solution.py:39
  22.7 5.5 %collective-permute-start.4 = (f32[32,32]{1,0:T(8,128)S(1)}, f32[32,32]{1,0:T(8,128)S(1)}, u32[]{:S(2)}, u32[]{:S(2)}) collective-permute-start(f32[32,32]{1,0:T(8,128)S(1)} %get-tuple-element.58), channel_id=1, source_target_pairs={{0,4},{1,5},{2,6},{3,7},{4,0},{5,1},{6,2},{7,3},{8,12},{9,13},{10,... | collective-permute-start | bytes 12296 | tf_op jit(solution)/shard_map/ppermute | solution.py:39
  28.3 4.8 %collective-permute-start.9 = (f32[32,32]{1,0:T(8,128)S(1)}, f32[32,32]{1,0:T(8,128)S(1)}, u32[]{:S(2)}, u32[]{:S(2)}) collective-permute-start(f32[32,32]{1,0:T(8,128)S(1)} %add_add_fusion.2.refs_0_), channel_id=1, source_target_pairs={{0,3},{1,2},{2,1},{3,0},{4,7},{5,6},{6,5},{7,4},{8,11},{9,10},{10,... | collective-permute-start | bytes 12296 | tf_op jit(solution)/shard_map/ppermute | solution.py:39
  31.0 2.7 %collective-permute-start.8 = (f32[32,32]{1,0:T(8,128)S(1)}, f32[32,32]{1,0:T(8,128)S(1)}, u32[]{:S(2)}, u32[]{:S(2)}) collective-permute-start(f32[32,32]{1,0:T(8,128)S(1)} %add_add_fusion.2.refs_0_), channel_id=1, source_target_pairs={{0,2},{1,3},{2,0},{3,1},{4,6},{5,7},{6,4},{7,5},{8,10},{9,11},{10,... | collective-permute-start | bytes 12296 | tf_op jit(solution)/shard_map/ppermute | solution.py:39
  32.2 1.4 %collective-permute-start.7 = (f32[32,32]{1,0:T(8,128)S(1)}, f32[32,32]{1,0:T(8,128)S(1)}, u32[]{:S(2)}, u32[]{:S(2)}) collective-permute-start(f32[32,32]{1,0:T(8,128)S(1)} %add_add_fusion.2.refs_0_), channel_id=1, source_target_pairs={{0,1},{1,0},{2,3},{3,2},{4,5},{5,4},{6,7},{7,6},{8,9},{9,8},{10,11... | collective-permute-start | bytes 12296 | tf_op jit(solution)/shard_map/ppermute | solution.py:39
  32.2 10.5 %collective-permute-start.10 = (f32[32,1536]{1,0:T(8,128)S(1)}, f32[32,1536]{1,0:T(8,128)S(1)}, u32[]{:S(2)}, u32[]{:S(2)}) collective-permute-start(f32[32,1536]{1,0:T(8,128)S(1)} %get-tuple-element.69), channel_id=1, source_target_pairs={{0,1},{1,0},{2,3},{3,2},{4,5},{5,4},{6,7},{7,6},{8,9},{9,8},{10,11... | collective-permute-start | bytes 589832 | tf_op jit(solution)/shard_map/ppermute | solution.py:39
  32.7 11.9 %collective-permute-start.13 = (f32[32,1536]{1,0:T(8,128)S(1)}, f32[32,1536]{1,0:T(8,128)S(1)}, u32[]{:S(2)}, u32[]{:S(2)}) collective-permute-start(f32[32,1536]{1,0:T(8,128)S(1)} %get-tuple-element.73), channel_id=1, source_target_pairs={{0,8},{1,9},{2,10},{3,11},{4,12},{5,13},{6,14},{7,15},{8,0},{9,1},... | collective-permute-start | bytes 589832 | tf_op jit(solution)/shard_map/ppermute | solution.py:39
  37.5 7.1 %collective-permute-start.11 = (f32[32,1536]{1,0:T(8,128)S(1)}, f32[32,1536]{1,0:T(8,128)S(1)}, u32[]{:S(2)}, u32[]{:S(2)}) collective-permute-start(f32[32,1536]{1,0:T(8,128)S(1)} %get-tuple-element.71), channel_id=1, source_target_pairs={{0,2},{1,3},{2,0},{3,1},{4,6},{5,7},{6,4},{7,5},{8,10},{9,11},{10,... | collective-permute-start | bytes 589832 | tf_op jit(solution)/shard_map/ppermute | solution.py:39
  38.7 10.2 %collective-permute-start.12 = (f32[32,1536]{1,0:T(8,128)S(1)}, f32[32,1536]{1,0:T(8,128)S(1)}, u32[]{:S(2)}, u32[]{:S(2)}) collective-permute-start(f32[32,1536]{1,0:T(8,128)S(1)} %get-tuple-element.72), channel_id=1, source_target_pairs={{0,4},{1,5},{2,6},{3,7},{4,0},{5,1},{6,2},{7,3},{8,12},{9,13},{10,... | collective-permute-start | bytes 589832 | tf_op jit(solution)/shard_map/ppermute | solution.py:39
  52.0 7.5 %collective-permute-start.16 = (f32[32,32]{1,0:T(8,128)S(1)}, f32[32,32]{1,0:T(8,128)S(1)}, u32[]{:S(2)}, u32[]{:S(2)}) collective-permute-start(f32[32,32]{1,0:T(8,128)S(1)} %get-tuple-element.76), channel_id=1, source_target_pairs={{0,12},{1,13},{2,14},{3,15},{4,8},{5,9},{6,10},{7,11},{8,4},{9,5},... | collective-permute-start | bytes 12296 | tf_op jit(solution)/shard_map/ppermute | solution.py:39
  53.3 6.2 %collective-permute-start.15 = (f32[32,32]{1,0:T(8,128)S(1)}, f32[32,32]{1,0:T(8,128)S(1)}, u32[]{:S(2)}, u32[]{:S(2)}) collective-permute-start(f32[32,32]{1,0:T(8,128)S(1)} %get-tuple-element.76), channel_id=1, source_target_pairs={{0,8},{1,9},{2,10},{3,11},{4,12},{5,13},{6,14},{7,15},{8,0},{9,1},... | collective-permute-start | bytes 12296 | tf_op jit(solution)/shard_map/ppermute | solution.py:39
  53.3 6.2 %collective-permute-start.14 = (f32[32,32]{1,0:T(8,128)S(1)}, f32[32,32]{1,0:T(8,128)S(1)}, u32[]{:S(2)}, u32[]{:S(2)}) collective-permute-start(f32[32,32]{1,0:T(8,128)S(1)} %get-tuple-element.76), channel_id=1, source_target_pairs={{0,4},{1,5},{2,6},{3,7},{4,0},{5,1},{6,2},{7,3},{8,12},{9,13},{10,... | collective-permute-start | bytes 12296 | tf_op jit(solution)/shard_map/ppermute | solution.py:39
  59.5 4.3 %collective-permute-start.19 = (f32[32,32]{1,0:T(8,128)S(1)}, f32[32,32]{1,0:T(8,128)S(1)}, u32[]{:S(2)}, u32[]{:S(2)}) collective-permute-start(f32[32,32]{1,0:T(8,128)S(1)} %add_add_fusion.1.refs_0_), channel_id=1, source_target_pairs={{0,3},{1,2},{2,1},{3,0},{4,7},{5,6},{6,5},{7,4},{8,11},{9,10},{10,... | collective-permute-start | bytes 12296 | tf_op jit(solution)/shard_map/ppermute | solution.py:39
  61.4 3.0 %collective-permute-start.18 = (f32[32,32]{1,0:T(8,128)S(1)}, f32[32,32]{1,0:T(8,128)S(1)}, u32[]{:S(2)}, u32[]{:S(2)}) collective-permute-start(f32[32,32]{1,0:T(8,128)S(1)} %add_add_fusion.1.refs_0_), channel_id=1, source_target_pairs={{0,2},{1,3},{2,0},{3,1},{4,6},{5,7},{6,4},{7,5},{8,10},{9,11},{10,... | collective-permute-start | bytes 12296 | tf_op jit(solution)/shard_map/ppermute | solution.py:39
  62.2 2.1 %collective-permute-start.17 = (f32[32,32]{1,0:T(8,128)S(1)}, f32[32,32]{1,0:T(8,128)S(1)}, u32[]{:S(2)}, u32[]{:S(2)}) collective-permute-start(f32[32,32]{1,0:T(8,128)S(1)} %add_add_fusion.1.refs_0_), channel_id=1, source_target_pairs={{0,1},{1,0},{2,3},{3,2},{4,5},{5,4},{6,7},{7,6},{8,9},{9,8},{10,11... | collective-permute-start | bytes 12296 | tf_op jit(solution)/shard_map/ppermute | solution.py:39
  62.2 11.2 %collective-permute-start.20 = (f32[32,1536]{1,0:T(8,128)S(1)}, f32[32,1536]{1,0:T(8,128)S(1)}, u32[]{:S(2)}, u32[]{:S(2)}) collective-permute-start(f32[32,1536]{1,0:T(8,128)S(1)} %get-tuple-element.87), channel_id=1, source_target_pairs={{0,1},{1,0},{2,3},{3,2},{4,5},{5,4},{6,7},{7,6},{8,9},{9,8},{10,11... | collective-permute-start | bytes 589832 | tf_op jit(solution)/shard_map/ppermute | solution.py:39
  62.7 11.9 %collective-permute-start.23 = (f32[32,1536]{1,0:T(8,128)S(1)}, f32[32,1536]{1,0:T(8,128)S(1)}, u32[]{:S(2)}, u32[]{:S(2)}) collective-permute-start(f32[32,1536]{1,0:T(8,128)S(1)} %get-tuple-element.91), channel_id=1, source_target_pairs={{0,8},{1,9},{2,10},{3,11},{4,12},{5,13},{6,14},{7,15},{8,0},{9,1},... | collective-permute-start | bytes 589832 | tf_op jit(solution)/shard_map/ppermute | solution.py:39
  68.2 6.4 %collective-permute-start.21 = (f32[32,1536]{1,0:T(8,128)S(1)}, f32[32,1536]{1,0:T(8,128)S(1)}, u32[]{:S(2)}, u32[]{:S(2)}) collective-permute-start(f32[32,1536]{1,0:T(8,128)S(1)} %get-tuple-element.89), channel_id=1, source_target_pairs={{0,2},{1,3},{2,0},{3,1},{4,6},{5,7},{6,4},{7,5},{8,10},{9,11},{10,... | collective-permute-start | bytes 589832 | tf_op jit(solution)/shard_map/ppermute | solution.py:39
  69.1 9.8 %collective-permute-start.22 = (f32[32,1536]{1,0:T(8,128)S(1)}, f32[32,1536]{1,0:T(8,128)S(1)}, u32[]{:S(2)}, u32[]{:S(2)}) collective-permute-start(f32[32,1536]{1,0:T(8,128)S(1)} %get-tuple-element.90), channel_id=1, source_target_pairs={{0,4},{1,5},{2,6},{3,7},{4,0},{5,1},{6,2},{7,3},{8,12},{9,13},{10,... | collective-permute-start | bytes 589832 | tf_op jit(solution)/shard_map/ppermute | solution.py:39
  82.0 4.4 %collective-permute-start.26 = (f32[32,32]{1,0:T(8,128)S(1)}, f32[32,32]{1,0:T(8,128)S(1)}, u32[]{:S(2)}, u32[]{:S(2)}) collective-permute-start(f32[32,32]{1,0:T(8,128)S(1)} %get-tuple-element.93), channel_id=1, source_target_pairs={{0,12},{1,13},{2,14},{3,15},{4,8},{5,9},{6,10},{7,11},{8,4},{9,5},... | collective-permute-start | bytes 12296 | tf_op jit(solution)/shard_map/ppermute | solution.py:39
  83.9 3.8 %collective-permute-start.25 = (f32[32,32]{1,0:T(8,128)S(1)}, f32[32,32]{1,0:T(8,128)S(1)}, u32[]{:S(2)}, u32[]{:S(2)}) collective-permute-start(f32[32,32]{1,0:T(8,128)S(1)} %get-tuple-element.93), channel_id=1, source_target_pairs={{0,8},{1,9},{2,10},{3,11},{4,12},{5,13},{6,14},{7,15},{8,0},{9,1},... | collective-permute-start | bytes 12296 | tf_op jit(solution)/shard_map/ppermute | solution.py:39
  83.9 3.8 %collective-permute-start.24 = (f32[32,32]{1,0:T(8,128)S(1)}, f32[32,32]{1,0:T(8,128)S(1)}, u32[]{:S(2)}, u32[]{:S(2)}) collective-permute-start(f32[32,32]{1,0:T(8,128)S(1)} %get-tuple-element.93), channel_id=1, source_target_pairs={{0,4},{1,5},{2,6},{3,7},{4,0},{5,1},{6,2},{7,3},{8,12},{9,13},{10,... | collective-permute-start | bytes 12296 | tf_op jit(solution)/shard_map/ppermute | solution.py:39
  87.7 5.7 %collective-permute-start.29 = (f32[32,32]{1,0:T(8,128)S(1)}, f32[32,32]{1,0:T(8,128)S(1)}, u32[]{:S(2)}, u32[]{:S(2)}) collective-permute-start(f32[32,32]{1,0:T(8,128)S(1)} %add_add_fusion.refs_0_), channel_id=1, source_target_pairs={{0,3},{1,2},{2,1},{3,0},{4,7},{5,6},{6,5},{7,4},{8,11},{9,10},{10,... | collective-permute-start | bytes 12296 | tf_op jit(solution)/shard_map/ppermute | solution.py:39
  91.9 2.6 %collective-permute-start.28 = (f32[32,32]{1,0:T(8,128)S(1)}, f32[32,32]{1,0:T(8,128)S(1)}, u32[]{:S(2)}, u32[]{:S(2)}) collective-permute-start(f32[32,32]{1,0:T(8,128)S(1)} %add_add_fusion.refs_0_), channel_id=1, source_target_pairs={{0,2},{1,3},{2,0},{3,1},{4,6},{5,7},{6,4},{7,5},{8,10},{9,11},{10,... | collective-permute-start | bytes 12296 | tf_op jit(solution)/shard_map/ppermute | solution.py:39
  91.9 2.6 %collective-permute-start.27 = (f32[32,32]{1,0:T(8,128)S(1)}, f32[32,32]{1,0:T(8,128)S(1)}, u32[]{:S(2)}, u32[]{:S(2)}) collective-permute-start(f32[32,32]{1,0:T(8,128)S(1)} %add_add_fusion.refs_0_), channel_id=1, source_target_pairs={{0,1},{1,0},{2,3},{3,2},{4,5},{5,4},{6,7},{7,6},{8,9},{9,8},{10,11... | collective-permute-start | bytes 12296 | tf_op jit(solution)/shard_map/ppermute | solution.py:39

commit v5 on v3

--- a/solution.py
+++ b/solution.py
@@ -18,6 +18,7 @@
 BF16 = jnp.bfloat16
 VMEM = pl.BlockSpec(memory_space=pltpu.VMEM)
 SMEM = pl.BlockSpec(memory_space=pltpu.SMEM)
+HBM = pl.BlockSpec(memory_space=pltpu.HBM)
 CHEAP = pl.CostEstimate(flops=0, bytes_accessed=1024, transcendentals=0)
 PARAMS = pltpu.CompilerParams(vmem_limit_bytes=32 << 20)
 
@@ -115,8 +116,22 @@
     return terms[:n] + (terms[n : 2 * n] + terms[2 * n :])
 
 
+def packed(square):
+    n = square.shape[0]
+    count = LANES // n
+    step = n // count
+    return jnp.concatenate([square[q * step : (q + 1) * step] for q in range(count)], axis=1)
+
+
+def unpacked(wide):
+    step = wide.shape[0]
+    n = LANES // PACK
+    count = n // step
+    return jnp.concatenate([wide[:, q * n : (q + 1) * n] for q in range(count)], axis=0)
+
+
 def gram_of(parts, total_states):
-    return paired_sum(parts) / total_states
+    return unpacked(paired_sum(parts)) / total_states
 
 
 def transposed_into(source, rows_ref):
@@ -181,12 +196,18 @@
         )
         for c in range(COPIES)
     ]
+    if make_rows:
+        block_ref = refs[1]
+        block_copy = pltpu.make_async_copy(source_ref, block_ref, sems.at[COPIES])
+        block_copy.start()
     for copy in copies:
         copy.start()
+    if make_rows:
+        block_copy.wait()
     rows_ref = source_ref
     if make_rows:
         rows_ref = refs[0]
-        transposed_into(source_ref, rows_ref)
+        transposed_into(block_ref, rows_ref)
     gathered_into(64, row_ref, part_ref, rows_ref, picked, outs)
     for copy in copies:
         copy.wait()
@@ -199,16 +220,18 @@
     outs.append(vmem_out((kept, *tiles.shape[1:]), tiles.dtype))
     if make_rows:
         outs.append(vmem_out((source.shape[1] // PACK, LANES), F32))
+        outs.append(vmem_out(source.shape, source.dtype))
+    source = in_hbm(source) if make_rows else in_vmem(source)
     return pl.pallas_call(
         functools.partial(start_kernel, count, first, make_rows),
         out_shape=outs,
-        in_specs=[SMEM, VMEM, VMEM, pl.BlockSpec(memory_space=pltpu.HBM)],
+        in_specs=[SMEM, VMEM, HBM if make_rows else VMEM, HBM],
         out_specs=[VMEM] * len(outs),
-        scratch_shapes=[pltpu.VMEM((indices, LANES), F32), pltpu.SemaphoreType.DMA((COPIES,))],
+        scratch_shapes=[pltpu.VMEM((indices, LANES), F32), pltpu.SemaphoreType.DMA((COPIES + 1,))],
         compiler_params=PARAMS,
         cost_estimate=CHEAP,
         name="start_gather",
-    )(row_list, in_vmem(part_list), source if make_rows else in_vmem(source), in_hbm(tiles))
+    )(row_list, in_vmem(part_list), source, in_hbm(tiles))
 
 
 def own_slots(block_ref, tiles_ref, own_ref):
@@ -329,7 +352,7 @@
     ]
     small = blocks[8] + (blocks[5] + blocks[7])
     middle = blocks[4] + (blocks[2] + blocks[6])
-    gram_ref[...] = blocks[0] + ((blocks[1] + blocks[3]) + (middle + small))
+    gram_ref[...] = packed(blocks[0] + ((blocks[1] + blocks[3]) + (middle + small)))
     if with_rows:
         transposed_into(total, rows_ref)
 
@@ -340,7 +363,7 @@
     group = 64
     while rest % group:
         group //= 2
-    outs = [vmem_out((3 * columns, states), BF16), vmem_out((columns, columns), F32)]
+    outs = [vmem_out((3 * columns, states), BF16), vmem_out((columns * columns // LANES, LANES), F32)]
     if with_rows:
         outs.append(vmem_out((states // PACK, LANES), F32))
     operands = [block, own, *ghosts] + ([] if matrix is None else [matrix]) + [tiles]
@@ -358,10 +381,16 @@
 
 
 def final_kernel(total_states, *refs):
-    grams, stacked, out_ref = refs[:4], refs[4], refs[5]
+    grams, stacked, out_ref, ready, sems = refs[:4], *refs[4:]
     matrix = apply_matrix(inverse_factor(gram_of([r[...] for r in grams], total_states)))
-    for c in range(0, out_ref.shape[1], CHUNK):
-        out_ref[:, c : c + CHUNK] = applied(matrix, stacked[:, c : c + CHUNK])
+    copies = []
+    for n, c in enumerate(range(0, out_ref.shape[1], CHUNK)):
+        at = pl.ds(c, CHUNK)
+        ready[:, at] = applied(matrix, stacked[:, at])
+        copies.append(pltpu.make_async_copy(ready.at[:, at], out_ref.at[:, at], sems.at[n]))
+        copies[-1].start()
+    for copy in copies:
+        copy.wait()
 
 
 def final(grams, stacked, total_states):
@@ -370,7 +399,11 @@
         functools.partial(final_kernel, total_states),
         out_shape=jax.ShapeDtypeStruct((columns, states), F32),
         in_specs=[VMEM] * 5,
-        out_specs=VMEM,
+        out_specs=HBM,
+        scratch_shapes=[
+            pltpu.VMEM((columns, states), F32),
+            pltpu.SemaphoreType.DMA((states // CHUNK,)),
+        ],
         compiler_params=PARAMS,
         cost_estimate=CHEAP,
         name="final",
@@ -421,7 +454,7 @@
 
     own_count = states // tiles.shape[1]
     ghosts = [None] * len(masks)
-    *picked, rest_tiles, start_rows = start_gather(
+    *picked, rest_tiles, start_rows, block = start_gather(
         start_block, *listed[0], len(far), tiles, own_count, tiles.shape[0] - own_count, True
     )
     sent(ghosts, far, picked)
@@ -429,8 +462,8 @@
         start_rows, *listed[1], len(near), tiles, 0, own_count, False
     )
     sent(ghosts, near, picked)
-    block, matrix = start_block, None
-    own = first_own(start_block, own_tiles)
+    matrix = None
+    own = first_own(block, own_tiles)
     for turn in range(ITERS):
         last = turn == ITERS - 1
         stacked, gram, *rows = product(

time: 91.6 us -> 92 us (level)
  waiting for transfers between devices: 13.9 us -> 16.9 us
  Pallas kernels: 40.8 us -> 39.7 us
  local copies, waits for them, and re-layouts: 1.18 us -> 0.14 us
  starting transfers between devices: 33.5 us -> 32.5 us
    ppermute x30, waiting for transfers between devices: 13.9 us -> 16.9 us  [swapped(): return lax.ppermute(x, 'dom', [(i, i ^ mask) for i in range(size)])]
    pallas_call x3, Pallas kernels: 8.91 us -> 7.3 us  [product(): pl.pallas_call(functools.partial(product_kernel, len(ghosts), group, with...]
    unnamed x8 -> x4, local copies, waits for them, and re-layouts: 1.06 us -> 0.01 us
    ppermute x30, starting transfers between devices: 33.5 us -> 32.5 us  [swapped(): return lax.ppermute(x, 'dom', [(i, i ^ mask) for i in range(size)])]
  transfers between devices with their start and end apart: 30 -> 30, of which waited for: 12 -> 11; matrix products, arithmetic and copies ran while one was open for 0% -> 0% of each run, Pallas kernels for 27% -> 27%
where the time goes in v5:
time: 92 us; the launch traced here: 91 us
  Pallas kernels  39.7 us (43%)
  starting transfers between devices  32.5 us (35%)
  waiting for transfers between devices  16.9 us (18%)
    ppermute x30, starting transfers between devices, swapped(): return lax.ppermute(x, 'dom', [(i, i ^ mask) for i in range(size)])  32.5 us
    ppermute x30, waiting for transfers between devices, swapped(): return lax.ppermute(x, 'dom', [(i, i ^ mask) for i in range(size)])  16.9 us
    pallas_call x4, Pallas kernels, gather_colours(): pl.pallas_call(gather_kernel, out_shape=[vmem_out((columns, indices // co...  15.3 us
    pallas_call x2, Pallas kernels, start_gather(): pl.pallas_call(functools.partial(start_kernel, count, first, make_rows),...  8.72 us
    pallas_call x3, Pallas kernels, product(): pl.pallas_call(functools.partial(product_kernel, len(ghosts), group, with...  7.3 us
    pallas_call x2, Pallas kernels, later_own(): pl.pallas_call(functools.partial(later_own_kernel, total_states), out_sha...  5 us
    pallas_call x1, Pallas kernels, final(): pl.pallas_call(functools.partial(final_kernel, total_states), out_shape=j...  2.7 us
  transfers between devices with their start and end apart: 30, of which 11 were waited for; matrix products, arithmetic and copies ran while one was open for 0% of the time, Pallas kernels for 27%

profile of v5, /device:TPU:0, one launch (start us, length us, event | category | flops | bytes accessed | tf_op | source)
XLA Modules:
  0.0 91.0 jit_solution(4669954892372201188)
XLA Ops:
  0.0 0.8 add_select_fusion
  0.8 0.1 slice_reduce_fusion.1
  1.0 5.0 %start_gather.2 = (bf16[32,1536]{1,0:T(8,128)(2,1)S(1)}, bf16[32,1536]{1,0:T(8,128)(2,1)S(1)}, bf16[256,128,128]{2,1,0:T(8,128)(2,1)S(1)}, f32[2048,128]{1,0:T(8,128)S(1)}, bf16[32,8192]{1,0:T(8,128)(2,1)S(1)}) custom-call(s32[3072]{0:T(1024)S(1)} %pad_add_fusion.row_ref, s32[24,128]{1,0:T(8,128)S(1)} %pad_add_fusion.1.part_ref, ...), custom_call_target="tpu_custom_call" | custom-call | bytes 1024 | tf_op jit(solution)/shard_map/start_gather/pallas_call | solution.py:225
  6.0 3.1 %collective-permute-start.2 = (bf16[32,1536]{1,0:T(8,128)(2,1)S(1)}, bf16[32,1536]{1,0:T(8,128)(2,1)S(1)}, u32[]{:S(2)}, u32[]{:S(2)}) collective-permute-start(bf16[32,1536]{1,0:T(8,128)(2,1)S(1)} %get-tuple-element.56), channel_id=1, source_target_pairs={{0,4},{1,5},{2,6},{3,7},{4,0},{5,1},{6,2},{7,3},{8,12},{9,13},{10,... | collective-permute-start | bytes 294920 | tf_op jit(solution)/shard_map/ppermute | solution.py:40
  9.1 2.6 %collective-permute-start.3 = (bf16[32,1536]{1,0:T(8,128)(2,1)S(1)}, bf16[32,1536]{1,0:T(8,128)(2,1)S(1)}, u32[]{:S(2)}, u32[]{:S(2)}) collective-permute-start(bf16[32,1536]{1,0:T(8,128)(2,1)S(1)} %get-tuple-element.57), channel_id=1, source_target_pairs={{0,8},{1,9},{2,10},{3,11},{4,12},{5,13},{6,14},{7,15},{8,0},{9,1},... | collective-permute-start | bytes 294920 | tf_op jit(solution)/shard_map/ppermute | solution.py:40
  11.7 3.7 %start_gather.3 = (bf16[32,1536]{1,0:T(8,128)(2,1)S(1)}, bf16[32,1536]{1,0:T(8,128)(2,1)S(1)}, bf16[64,128,128]{2,1,0:T(8,128)(2,1)S(1)}) custom-call(s32[3072]{0:T(1024)S(1)} %pad_add_fusion.2.row_ref, s32[24,128]{1,0:T(8,128)S(1)} %pad_add_fusion.3.part_ref, f32[2048,128]{1,0:T(8,128)S(1)} %get-tuple-element.52.source_ref, bf16[320,128,128]{2,1,0:T(8,128)(2,1)} %tiles_ref.3), custom_call_target="tpu_custom_call" | custom-call | bytes 1024 | tf_op jit(solution)/shard_map/start_gather/pallas_call | solution.py:225
  15.4 0.0 copy-start
  15.4 0.0 copy-start.1
  15.4 0.1 collective-permute-start
  15.5 1.6 %collective-permute-start.1 = (bf16[32,1536]{1,0:T(8,128)(2,1)S(1)}, bf16[32,1536]{1,0:T(8,128)(2,1)S(1)}, u32[]{:S(2)}, u32[]{:S(2)}) collective-permute-start(bf16[32,1536]{1,0:T(8,128)(2,1)S(1)} %get-tuple-element.55), channel_id=1, source_target_pairs={{0,2},{1,3},{2,0},{3,1},{4,6},{5,7},{6,4},{7,5},{8,10},{9,11},{10,... | collective-permute-start | bytes 294920 | tf_op jit(solution)/shard_map/ppermute | solution.py:40
  17.8 0.7 first_own.1.refs_4_
  18.4 0.0 collective-permute-done.refs_5_
  18.4 2.3 %collective-permute-done.1.refs_6_ = bf16[32,1536]{1,0:T(8,128)(2,1)S(1)} collective-permute-done((bf16[32,1536]{1,0:T(8,128)(2,1)S(1)}, bf16[32,1536]{1,0:T(8,128)(2,1)S(1)}, u32[]{:S(2)}, u32[]{:S(2)}) %collective-permute-start.1) | collective-permute-done | bytes 98336 | tf_op jit(solution)/shard_map/ppermute | solution.py:40
  20.7 2.2 %product.3 = (bf16[96,8192]{1,0:T(8,128)(2,1)S(1)}, f32[8,128]{1,0:T(8,128)S(1)}, f32[2048,128]{1,0:T(8,128)S(1)}) custom-call(s32[320]{0:T(512)S(1)} %copy-done, s32[320]{0:T(512)S(1)} %copy-done.1, s32[1]{0:T(128)S(6)} %copy.7.refs_2_, bf16[32,8192]{1,0:T(8,128)(2,1)S(1)} %get-tuple-element.51.block_ref.refs_3_, f32[32,8192]{1,0:T(8,128)S(1)} %first_own.1.refs_4_, ...), custom_call_target="tpu_custom_call" | custom-call | bytes 1024 | tf_op jit(solution)/shard_map/product/pallas_call | solution.py:371
  23.0 0.7 collective-permute-start.6
  23.6 1.3 %collective-permute-start.5 = (f32[8,128]{1,0:T(8,128)S(1)}, f32[8,128]{1,0:T(8,128)S(1)}, u32[]{:S(2)}, u32[]{:S(2)}) collective-permute-start(f32[8,128]{1,0:T(8,128)S(1)} %get-tuple-element.60), channel_id=1, source_target_pairs={{0,8},{1,9},{2,10},{3,11},{4,12},{5,13},{6,14},{7,15},{8,0},{9,1},... | collective-permute-start | bytes 12296 | tf_op jit(solution)/shard_map/ppermute | solution.py:40
  24.9 2.5 %collective-permute-start.4 = (f32[8,128]{1,0:T(8,128)S(1)}, f32[8,128]{1,0:T(8,128)S(1)}, u32[]{:S(2)}, u32[]{:S(2)}) collective-permute-start(f32[8,128]{1,0:T(8,128)S(1)} %get-tuple-element.60), channel_id=1, source_target_pairs={{0,4},{1,5},{2,6},{3,7},{4,0},{5,1},{6,2},{7,3},{8,12},{9,13},{10,... | collective-permute-start | bytes 12296 | tf_op jit(solution)/shard_map/ppermute | solution.py:40
  27.4 3.8 %gather_rows.4 = (f32[32,1536]{1,0:T(8,128)S(1)}, f32[32,1536]{1,0:T(8,128)S(1)}) custom-call(s32[3072]{0:T(1024)S(1)} %pad_add_fusion.row_ref, s32[24,128]{1,0:T(8,128)S(1)} %pad_add_fusion.1.part_ref, f32[2048,128]{1,0:T(8,128)S(1)} %get-tuple-element.71.rows_ref), custom_call_target="tpu_custom_call" | custom-call | bytes 1024 | tf_op jit(solution)/shard_map/gather_rows/pallas_call | solution.py:175
  31.2 0.0 collective-permute-done.6
  31.3 1.8 %collective-permute-start.9 = (f32[8,128]{1,0:T(8,128)S(1)}, f32[8,128]{1,0:T(8,128)S(1)}, u32[]{:S(2)}, u32[]{:S(2)}) collective-permute-start(f32[8,128]{1,0:T(8,128)S(1)} %add_add_fusion.2.refs_0_), channel_id=1, source_target_pairs={{0,3},{1,2},{2,1},{3,0},{4,7},{5,6},{6,5},{7,4},{8,11},{9,10},{10,... | collective-permute-start | bytes 12296 | tf_op jit(solution)/shard_map/ppermute | solution.py:40
  33.1 0.5 collective-permute-start.8
  33.6 0.0 collective-permute-start.7
  33.6 0.0 collective-permute-start.12
  33.6 0.8 collective-permute-start.13
  34.4 0.0 collective-permute-done.9.refs_3_
  34.4 2.3 %collective-permute-done.8.refs_2_ = f32[8,128]{1,0:T(8,128)S(1)} collective-permute-done((f32[8,128]{1,0:T(8,128)S(1)}, f32[8,128]{1,0:T(8,128)S(1)}, u32[]{:S(2)}, u32[]{:S(2)}) %collective-permute-start.8) | collective-permute-done | bytes 4128 | tf_op jit(solution)/shard_map/ppermute | solution.py:40
  36.7 0.0 collective-permute-done.7.refs_1_
  36.7 3.8 %gather_rows.5 = (f32[32,1536]{1,0:T(8,128)S(1)}, f32[32,1536]{1,0:T(8,128)S(1)}) custom-call(s32[3072]{0:T(1024)S(1)} %pad_add_fusion.2.row_ref, s32[24,128]{1,0:T(8,128)S(1)} %pad_add_fusion.3.part_ref, f32[2048,128]{1,0:T(8,128)S(1)} %get-tuple-element.71.rows_ref), custom_call_target="tpu_custom_call" | custom-call | bytes 1024 | tf_op jit(solution)/shard_map/gather_rows/pallas_call | solution.py:175
  40.5 0.1 collective-permute-start.10
  40.6 0.5 collective-permute-start.11
  41.2 2.5 %later_own.2 = (bf16[32,8192]{1,0:T(8,128)(2,1)S(1)}, bf16[96,96]{1,0:T(8,128)(2,1)S(1)}, f32[32,8192]{1,0:T(8,128)S(1)}) custom-call(f32[8,128]{1,0:T(8,128)S(1)} %add_add_fusion.2.refs_0_, f32[8,128]{1,0:T(8,128)S(1)} %collective-permute-done.7.refs_1_, f32[8,128]{1,0:T(8,128)S(1)} %collective-permute-done.8.refs_2_, ...), custom_call_target="tpu_custom_call" | custom-call | bytes 1024 | tf_op jit(solution)/shard_map/later_own/pallas_call | solution.py:272
  43.7 0.0 collective-permute-done.12.refs_7_
  43.7 2.4 %collective-permute-done.13.refs_8_ = f32[32,1536]{1,0:T(8,128)S(1)} collective-permute-done((f32[32,1536]{1,0:T(8,128)S(1)}, f32[32,1536]{1,0:T(8,128)S(1)}, u32[]{:S(2)}, u32[]{:S(2)}) %collective-permute-start.13) | collective-permute-done | bytes 196640 | tf_op jit(solution)/shard_map/ppermute | solution.py:40
  46.0 0.0 collective-permute-done.10.refs_5_
  46.0 1.9 %collective-permute-done.11.refs_6_ = f32[32,1536]{1,0:T(8,128)S(1)} collective-permute-done((f32[32,1536]{1,0:T(8,128)S(1)}, f32[32,1536]{1,0:T(8,128)S(1)}, u32[]{:S(2)}, u32[]{:S(2)}) %collective-permute-start.11) | collective-permute-done | bytes 196640 | tf_op jit(solution)/shard_map/ppermute | solution.py:40
  47.9 2.6 %product.4 = (bf16[96,8192]{1,0:T(8,128)(2,1)S(1)}, f32[8,128]{1,0:T(8,128)S(1)}, f32[2048,128]{1,0:T(8,128)S(1)}) custom-call(s32[320]{0:T(512)S(1)} %copy-done, s32[320]{0:T(512)S(1)} %copy-done.1, s32[1]{0:T(128)S(6)} %copy.7.refs_2_, bf16[32,8192]{1,0:T(8,128)(2,1)S(1)} %get-tuple-element.69.refs_3_, f32[32,8192]{1,0:T(8,128)S(1)} %get-tuple-element.70.refs_4_, ...), custom_call_target="tpu_custom_call" | custom-call | bytes 1024 | tf_op jit(solution)/shard_map/product/pallas_call | solution.py:371
  50.5 2.0 %collective-permute-start.16 = (f32[8,128]{1,0:T(8,128)S(1)}, f32[8,128]{1,0:T(8,128)S(1)}, u32[]{:S(2)}, u32[]{:S(2)}) collective-permute-start(f32[8,128]{1,0:T(8,128)S(1)} %get-tuple-element.78), channel_id=1, source_target_pairs={{0,12},{1,13},{2,14},{3,15},{4,8},{5,9},{6,10},{7,11},{8,4},{9,5},... | collective-permute-start | bytes 12296 | tf_op jit(solution)/shard_map/ppermute | solution.py:40
  52.5 0.0 collective-permute-start.15
  52.5 2.5 %collective-permute-start.14 = (f32[8,128]{1,0:T(8,128)S(1)}, f32[8,128]{1,0:T(8,128)S(1)}, u32[]{:S(2)}, u32[]{:S(2)}) collective-permute-start(f32[8,128]{1,0:T(8,128)S(1)} %get-tuple-element.78), channel_id=1, source_target_pairs={{0,4},{1,5},{2,6},{3,7},{4,0},{5,1},{6,2},{7,3},{8,12},{9,13},{10,... | collective-permute-start | bytes 12296 | tf_op jit(solution)/shard_map/ppermute | solution.py:40
  55.0 3.8 %gather_rows.6 = (f32[32,1536]{1,0:T(8,128)S(1)}, f32[32,1536]{1,0:T(8,128)S(1)}) custom-call(s32[3072]{0:T(1024)S(1)} %pad_add_fusion.row_ref, s32[24,128]{1,0:T(8,128)S(1)} %pad_add_fusion.1.part_ref, f32[2048,128]{1,0:T(8,128)S(1)} %get-tuple-element.89.rows_ref), custom_call_target="tpu_custom_call" | custom-call | bytes 1024 | tf_op jit(solution)/shard_map/gather_rows/pallas_call | solution.py:175
  58.8 0.0 collective-permute-done.16
  58.9 0.8 collective-permute-start.19
  59.6 0.5 collective-permute-start.18
  60.1 0.7 collective-permute-start.17
  60.8 0.0 collective-permute-start.22
  60.8 2.5 %collective-permute-start.23 = (f32[32,1536]{1,0:T(8,128)S(1)}, f32[32,1536]{1,0:T(8,128)S(1)}, u32[]{:S(2)}, u32[]{:S(2)}) collective-permute-start(f32[32,1536]{1,0:T(8,128)S(1)} %get-tuple-element.93), channel_id=1, source_target_pairs={{0,8},{1,9},{2,10},{3,11},{4,12},{5,13},{6,14},{7,15},{8,0},{9,1},... | collective-permute-start | bytes 589832 | tf_op jit(solution)/shard_map/ppermute | solution.py:40
  63.3 3.8 %gather_rows.7 = (f32[32,1536]{1,0:T(8,128)S(1)}, f32[32,1536]{1,0:T(8,128)S(1)}) custom-call(s32[3072]{0:T(1024)S(1)} %pad_add_fusion.2.row_ref, s32[24,128]{1,0:T(8,128)S(1)} %pad_add_fusion.3.part_ref, f32[2048,128]{1,0:T(8,128)S(1)} %get-tuple-element.89.rows_ref), custom_call_target="tpu_custom_call" | custom-call | bytes 1024 | tf_op jit(solution)/shard_map/gather_rows/pallas_call | solution.py:175
  67.1 0.1 collective-permute-start.20
  67.2 1.8 %collective-permute-start.21 = (f32[32,1536]{1,0:T(8,128)S(1)}, f32[32,1536]{1,0:T(8,128)S(1)}, u32[]{:S(2)}, u32[]{:S(2)}) collective-permute-start(f32[32,1536]{1,0:T(8,128)S(1)} %get-tuple-element.91), channel_id=1, source_target_pairs={{0,2},{1,3},{2,0},{3,1},{4,6},{5,7},{6,4},{7,5},{8,10},{9,11},{10,... | collective-permute-start | bytes 589832 | tf_op jit(solution)/shard_map/ppermute | solution.py:40
  69.0 2.5 %later_own.3 = (bf16[32,8192]{1,0:T(8,128)(2,1)S(1)}, bf16[96,96]{1,0:T(8,128)(2,1)S(1)}, f32[32,8192]{1,0:T(8,128)S(1)}) custom-call(f32[8,128]{1,0:T(8,128)S(1)} %add_add_fusion.1.refs_0_, f32[8,128]{1,0:T(8,128)S(1)} %collective-permute-done.17.refs_1_, f32[8,128]{1,0:T(8,128)S(1)} %collective-permute-done.18.refs_2_, ...), custom_call_target="tpu_custom_call" | custom-call | bytes 1024 | tf_op jit(solution)/shard_map/later_own/pallas_call | solution.py:272
  71.5 0.1 collective-permute-done.22.refs_7_
  71.6 1.2 %collective-permute-done.23.refs_8_ = f32[32,1536]{1,0:T(8,128)S(1)} collective-permute-done((f32[32,1536]{1,0:T(8,128)S(1)}, f32[32,1536]{1,0:T(8,128)S(1)}, u32[]{:S(2)}, u32[]{:S(2)}) %collective-permute-start.23) | collective-permute-done | bytes 196640 | tf_op jit(solution)/shard_map/ppermute | solution.py:40
  72.8 1.8 %collective-permute-done.21.refs_6_ = f32[32,1536]{1,0:T(8,128)S(1)} collective-permute-done((f32[32,1536]{1,0:T(8,128)S(1)}, f32[32,1536]{1,0:T(8,128)S(1)}, u32[]{:S(2)}, u32[]{:S(2)}) %collective-permute-start.21) | collective-permute-done | bytes 196640 | tf_op jit(solution)/shard_map/ppermute | solution.py:40
  74.5 2.5 %product.5 = (bf16[96,8192]{1,0:T(8,128)(2,1)S(1)}, f32[8,128]{1,0:T(8,128)S(1)}) custom-call(s32[320]{0:T(512)S(1)} %copy-done, s32[320]{0:T(512)S(1)} %copy-done.1, s32[1]{0:T(128)S(6)} %copy.7.refs_2_, bf16[32,8192]{1,0:T(8,128)(2,1)S(1)} %get-tuple-element.87.refs_3_, f32[32,8192]{1,0:T(8,128)S(1)} %get-tuple-element.88.refs_4_, ...), custom_call_target="tpu_custom_call" | custom-call | bytes 1024 | tf_op jit(solution)/shard_map/product/pallas_call | solution.py:371
  77.0 2.5 %collective-permute-start.26 = (f32[8,128]{1,0:T(8,128)S(1)}, f32[8,128]{1,0:T(8,128)S(1)}, u32[]{:S(2)}, u32[]{:S(2)}) collective-permute-start(f32[8,128]{1,0:T(8,128)S(1)} %get-tuple-element.95), channel_id=1, source_target_pairs={{0,12},{1,13},{2,14},{3,15},{4,8},{5,9},{6,10},{7,11},{8,4},{9,5},... | collective-permute-start | bytes 12296 | tf_op jit(solution)/shard_map/ppermute | solution.py:40
  79.6 1.9 %collective-permute-start.24 = (f32[8,128]{1,0:T(8,128)S(1)}, f32[8,128]{1,0:T(8,128)S(1)}, u32[]{:S(2)}, u32[]{:S(2)}) collective-permute-start(f32[8,128]{1,0:T(8,128)S(1)} %get-tuple-element.95), channel_id=1, source_target_pairs={{0,4},{1,5},{2,6},{3,7},{4,0},{5,1},{6,2},{7,3},{8,12},{9,13},{10,... | collective-permute-start | bytes 12296 | tf_op jit(solution)/shard_map/ppermute | solution.py:40
  81.4 1.0 %collective-permute-done.26 = f32[8,128]{1,0:T(8,128)S(1)} collective-permute-done((f32[8,128]{1,0:T(8,128)S(1)}, f32[8,128]{1,0:T(8,128)S(1)}, u32[]{:S(2)}, u32[]{:S(2)}) %collective-permute-start.26) | collective-permute-done | bytes 4128 | tf_op jit(solution)/shard_map/ppermute | solution.py:40
  82.5 1.6 %collective-permute-done.25 = f32[8,128]{1,0:T(8,128)S(1)} collective-permute-done((f32[8,128]{1,0:T(8,128)S(1)}, f32[8,128]{1,0:T(8,128)S(1)}, u32[]{:S(2)}, u32[]{:S(2)}) %collective-permute-start.25) | collective-permute-done | bytes 4128 | tf_op jit(solution)/shard_map/ppermute | solution.py:40
  84.1 0.6 collective-permute-start.29
  84.7 0.7 collective-permute-start.28
  85.4 0.6 collective-permute-start.27
  86.0 1.2 %collective-permute-done.29.refs_3_ = f32[8,128]{1,0:T(8,128)S(1)} collective-permute-done((f32[8,128]{1,0:T(8,128)S(1)}, f32[8,128]{1,0:T(8,128)S(1)}, u32[]{:S(2)}, u32[]{:S(2)}) %collective-permute-start.29) | collective-permute-done | bytes 4128 | tf_op jit(solution)/shard_map/ppermute | solution.py:40
  87.2 1.1 %collective-permute-done.28.refs_2_ = f32[8,128]{1,0:T(8,128)S(1)} collective-permute-done((f32[8,128]{1,0:T(8,128)S(1)}, f32[8,128]{1,0:T(8,128)S(1)}, u32[]{:S(2)}, u32[]{:S(2)}) %collective-permute-start.28) | collective-permute-done | bytes 4128 | tf_op jit(solution)/shard_map/ppermute | solution.py:40
  88.3 2.7 %final.1 = f32[32,8192]{1,0:T(8,128)} custom-call(f32[8,128]{1,0:T(8,128)S(1)} %add_add_fusion.refs_0_, f32[8,128]{1,0:T(8,128)S(1)} %collective-permute-done.27.refs_1_, f32[8,128]{1,0:T(8,128)S(1)} %collective-permute-done.28.refs_2_, f32[8,128]{1,0:T(8,128)S(1)} %collective-permute-done.29.refs_3_, bf16[96,8192]{1,0:T(8,128)(2,1)S(1)} %get-tuple-element.96.refs_4_), custom_call_target="tpu_custom_call" | custom-call | bytes 1024 | tf_op jit(solution)/shard_map/final/pallas_call | solution.py:398
  (22 shorter events, 0.1 us)
Async XLA Ops:
  6.0 12.4 %collective-permute-start.2 = (bf16[32,1536]{1,0:T(8,128)(2,1)S(1)}, bf16[32,1536]{1,0:T(8,128)(2,1)S(1)}, u32[]{:S(2)}, u32[]{:S(2)}) collective-permute-start(bf16[32,1536]{1,0:T(8,128)(2,1)S(1)} %get-tuple-element.56), channel_id=1, source_target_pairs={{0,4},{1,5},{2,6},{3,7},{4,0},{5,1},{6,2},{7,3},{8,12},{9,13},{10,... | collective-permute-start | bytes 294920 | tf_op jit(solution)/shard_map/ppermute | solution.py:40
  9.1 9.4 %collective-permute-start.3 = (bf16[32,1536]{1,0:T(8,128)(2,1)S(1)}, bf16[32,1536]{1,0:T(8,128)(2,1)S(1)}, u32[]{:S(2)}, u32[]{:S(2)}) collective-permute-start(bf16[32,1536]{1,0:T(8,128)(2,1)S(1)} %get-tuple-element.57), channel_id=1, source_target_pairs={{0,8},{1,9},{2,10},{3,11},{4,12},{5,13},{6,14},{7,15},{8,0},{9,1},... | collective-permute-start | bytes 294920 | tf_op jit(solution)/shard_map/ppermute | solution.py:40
  15.4 5.3 %copy-start = (s32[320]{0:T(512)S(1)}, s32[320]{0:T(512)}, u32[]{:S(2)}) copy-start(s32[320]{0:T(512)} %refs_0_.5) | copy-start | bytes 3844
  15.4 5.3 %copy-start.1 = (s32[320]{0:T(512)S(1)}, s32[320]{0:T(512)}, u32[]{:S(2)}) copy-start(s32[320]{0:T(512)} %refs_1_.5) | copy-start | bytes 3844
  15.4 3.0 %collective-permute-start = (bf16[32,1536]{1,0:T(8,128)(2,1)S(1)}, bf16[32,1536]{1,0:T(8,128)(2,1)S(1)}, u32[]{:S(2)}, u32[]{:S(2)}) collective-permute-start(bf16[32,1536]{1,0:T(8,128)(2,1)S(1)} %get-tuple-element.54), channel_id=1, source_target_pairs={{0,1},{1,0},{2,3},{3,2},{4,5},{5,4},{6,7},{7,6},{8,9},{9,8},{10,11... | collective-permute-start | bytes 294920 | tf_op jit(solution)/shard_map/ppermute | solution.py:40
  15.5 5.2 %collective-permute-start.1 = (bf16[32,1536]{1,0:T(8,128)(2,1)S(1)}, bf16[32,1536]{1,0:T(8,128)(2,1)S(1)}, u32[]{:S(2)}, u32[]{:S(2)}) collective-permute-start(bf16[32,1536]{1,0:T(8,128)(2,1)S(1)} %get-tuple-element.55), channel_id=1, source_target_pairs={{0,2},{1,3},{2,0},{3,1},{4,6},{5,7},{6,4},{7,5},{8,10},{9,11},{10,... | collective-permute-start | bytes 294920 | tf_op jit(solution)/shard_map/ppermute | solution.py:40
  23.0 8.3 %collective-permute-start.6 = (f32[8,128]{1,0:T(8,128)S(1)}, f32[8,128]{1,0:T(8,128)S(1)}, u32[]{:S(2)}, u32[]{:S(2)}) collective-permute-start(f32[8,128]{1,0:T(8,128)S(1)} %get-tuple-element.60), channel_id=1, source_target_pairs={{0,12},{1,13},{2,14},{3,15},{4,8},{5,9},{6,10},{7,11},{8,4},{9,5},... | collective-permute-start | bytes 12296 | tf_op jit(solution)/shard_map/ppermute | solution.py:40
  23.6 7.7 %collective-permute-start.5 = (f32[8,128]{1,0:T(8,128)S(1)}, f32[8,128]{1,0:T(8,128)S(1)}, u32[]{:S(2)}, u32[]{:S(2)}) collective-permute-start(f32[8,128]{1,0:T(8,128)S(1)} %get-tuple-element.60), channel_id=1, source_target_pairs={{0,8},{1,9},{2,10},{3,11},{4,12},{5,13},{6,14},{7,15},{8,0},{9,1},... | collective-permute-start | bytes 12296 | tf_op jit(solution)/shard_map/ppermute | solution.py:40
  24.9 6.3 %collective-permute-start.4 = (f32[8,128]{1,0:T(8,128)S(1)}, f32[8,128]{1,0:T(8,128)S(1)}, u32[]{:S(2)}, u32[]{:S(2)}) collective-permute-start(f32[8,128]{1,0:T(8,128)S(1)} %get-tuple-element.60), channel_id=1, source_target_pairs={{0,4},{1,5},{2,6},{3,7},{4,0},{5,1},{6,2},{7,3},{8,12},{9,13},{10,... | collective-permute-start | bytes 12296 | tf_op jit(solution)/shard_map/ppermute | solution.py:40
  31.3 3.1 %collective-permute-start.9 = (f32[8,128]{1,0:T(8,128)S(1)}, f32[8,128]{1,0:T(8,128)S(1)}, u32[]{:S(2)}, u32[]{:S(2)}) collective-permute-start(f32[8,128]{1,0:T(8,128)S(1)} %add_add_fusion.2.refs_0_), channel_id=1, source_target_pairs={{0,3},{1,2},{2,1},{3,0},{4,7},{5,6},{6,5},{7,4},{8,11},{9,10},{10,... | collective-permute-start | bytes 12296 | tf_op jit(solution)/shard_map/ppermute | solution.py:40
  33.1 3.6 %collective-permute-start.8 = (f32[8,128]{1,0:T(8,128)S(1)}, f32[8,128]{1,0:T(8,128)S(1)}, u32[]{:S(2)}, u32[]{:S(2)}) collective-permute-start(f32[8,128]{1,0:T(8,128)S(1)} %add_add_fusion.2.refs_0_), channel_id=1, source_target_pairs={{0,2},{1,3},{2,0},{3,1},{4,6},{5,7},{6,4},{7,5},{8,10},{9,11},{10,... | collective-permute-start | bytes 12296 | tf_op jit(solution)/shard_map/ppermute | solution.py:40
  33.6 3.2 %collective-permute-start.7 = (f32[8,128]{1,0:T(8,128)S(1)}, f32[8,128]{1,0:T(8,128)S(1)}, u32[]{:S(2)}, u32[]{:S(2)}) collective-permute-start(f32[8,128]{1,0:T(8,128)S(1)} %add_add_fusion.2.refs_0_), channel_id=1, source_target_pairs={{0,1},{1,0},{2,3},{3,2},{4,5},{5,4},{6,7},{7,6},{8,9},{9,8},{10,11... | collective-permute-start | bytes 12296 | tf_op jit(solution)/shard_map/ppermute | solution.py:40
  33.6 10.1 %collective-permute-start.12 = (f32[32,1536]{1,0:T(8,128)S(1)}, f32[32,1536]{1,0:T(8,128)S(1)}, u32[]{:S(2)}, u32[]{:S(2)}) collective-permute-start(f32[32,1536]{1,0:T(8,128)S(1)} %get-tuple-element.74), channel_id=1, source_target_pairs={{0,4},{1,5},{2,6},{3,7},{4,0},{5,1},{6,2},{7,3},{8,12},{9,13},{10,... | collective-permute-start | bytes 589832 | tf_op jit(solution)/shard_map/ppermute | solution.py:40
  33.6 12.4 %collective-permute-start.13 = (f32[32,1536]{1,0:T(8,128)S(1)}, f32[32,1536]{1,0:T(8,128)S(1)}, u32[]{:S(2)}, u32[]{:S(2)}) collective-permute-start(f32[32,1536]{1,0:T(8,128)S(1)} %get-tuple-element.75), channel_id=1, source_target_pairs={{0,8},{1,9},{2,10},{3,11},{4,12},{5,13},{6,14},{7,15},{8,0},{9,1},... | collective-permute-start | bytes 589832 | tf_op jit(solution)/shard_map/ppermute | solution.py:40
  40.5 5.5 %collective-permute-start.10 = (f32[32,1536]{1,0:T(8,128)S(1)}, f32[32,1536]{1,0:T(8,128)S(1)}, u32[]{:S(2)}, u32[]{:S(2)}) collective-permute-start(f32[32,1536]{1,0:T(8,128)S(1)} %get-tuple-element.72), channel_id=1, source_target_pairs={{0,1},{1,0},{2,3},{3,2},{4,5},{5,4},{6,7},{7,6},{8,9},{9,8},{10,11... | collective-permute-start | bytes 589832 | tf_op jit(solution)/shard_map/ppermute | solution.py:40
  40.6 7.3 %collective-permute-start.11 = (f32[32,1536]{1,0:T(8,128)S(1)}, f32[32,1536]{1,0:T(8,128)S(1)}, u32[]{:S(2)}, u32[]{:S(2)}) collective-permute-start(f32[32,1536]{1,0:T(8,128)S(1)} %get-tuple-element.73), channel_id=1, source_target_pairs={{0,2},{1,3},{2,0},{3,1},{4,6},{5,7},{6,4},{7,5},{8,10},{9,11},{10,... | collective-permute-start | bytes 589832 | tf_op jit(solution)/shard_map/ppermute | solution.py:40
  50.5 8.3 %collective-permute-start.16 = (f32[8,128]{1,0:T(8,128)S(1)}, f32[8,128]{1,0:T(8,128)S(1)}, u32[]{:S(2)}, u32[]{:S(2)}) collective-permute-start(f32[8,128]{1,0:T(8,128)S(1)} %get-tuple-element.78), channel_id=1, source_target_pairs={{0,12},{1,13},{2,14},{3,15},{4,8},{5,9},{6,10},{7,11},{8,4},{9,5},... | collective-permute-start | bytes 12296 | tf_op jit(solution)/shard_map/ppermute | solution.py:40
  52.5 6.3 %collective-permute-start.15 = (f32[8,128]{1,0:T(8,128)S(1)}, f32[8,128]{1,0:T(8,128)S(1)}, u32[]{:S(2)}, u32[]{:S(2)}) collective-permute-start(f32[8,128]{1,0:T(8,128)S(1)} %get-tuple-element.78), channel_id=1, source_target_pairs={{0,8},{1,9},{2,10},{3,11},{4,12},{5,13},{6,14},{7,15},{8,0},{9,1},... | collective-permute-start | bytes 12296 | tf_op jit(solution)/shard_map/ppermute | solution.py:40
  52.5 6.3 %collective-permute-start.14 = (f32[8,128]{1,0:T(8,128)S(1)}, f32[8,128]{1,0:T(8,128)S(1)}, u32[]{:S(2)}, u32[]{:S(2)}) collective-permute-start(f32[8,128]{1,0:T(8,128)S(1)} %get-tuple-element.78), channel_id=1, source_target_pairs={{0,4},{1,5},{2,6},{3,7},{4,0},{5,1},{6,2},{7,3},{8,12},{9,13},{10,... | collective-permute-start | bytes 12296 | tf_op jit(solution)/shard_map/ppermute | solution.py:40
  58.9 4.4 %collective-permute-start.19 = (f32[8,128]{1,0:T(8,128)S(1)}, f32[8,128]{1,0:T(8,128)S(1)}, u32[]{:S(2)}, u32[]{:S(2)}) collective-permute-start(f32[8,128]{1,0:T(8,128)S(1)} %add_add_fusion.1.refs_0_), channel_id=1, source_target_pairs={{0,3},{1,2},{2,1},{3,0},{4,7},{5,6},{6,5},{7,4},{8,11},{9,10},{10,... | collective-permute-start | bytes 12296 | tf_op jit(solution)/shard_map/ppermute | solution.py:40
  59.6 3.7 %collective-permute-start.18 = (f32[8,128]{1,0:T(8,128)S(1)}, f32[8,128]{1,0:T(8,128)S(1)}, u32[]{:S(2)}, u32[]{:S(2)}) collective-permute-start(f32[8,128]{1,0:T(8,128)S(1)} %add_add_fusion.1.refs_0_), channel_id=1, source_target_pairs={{0,2},{1,3},{2,0},{3,1},{4,6},{5,7},{6,4},{7,5},{8,10},{9,11},{10,... | collective-permute-start | bytes 12296 | tf_op jit(solution)/shard_map/ppermute | solution.py:40
  60.1 3.2 %collective-permute-start.17 = (f32[8,128]{1,0:T(8,128)S(1)}, f32[8,128]{1,0:T(8,128)S(1)}, u32[]{:S(2)}, u32[]{:S(2)}) collective-permute-start(f32[8,128]{1,0:T(8,128)S(1)} %add_add_fusion.1.refs_0_), channel_id=1, source_target_pairs={{0,1},{1,0},{2,3},{3,2},{4,5},{5,4},{6,7},{7,6},{8,9},{9,8},{10,11... | collective-permute-start | bytes 12296 | tf_op jit(solution)/shard_map/ppermute | solution.py:40
  60.8 10.8 %collective-permute-start.22 = (f32[32,1536]{1,0:T(8,128)S(1)}, f32[32,1536]{1,0:T(8,128)S(1)}, u32[]{:S(2)}, u32[]{:S(2)}) collective-permute-start(f32[32,1536]{1,0:T(8,128)S(1)} %get-tuple-element.92), channel_id=1, source_target_pairs={{0,4},{1,5},{2,6},{3,7},{4,0},{5,1},{6,2},{7,3},{8,12},{9,13},{10,... | collective-permute-start | bytes 589832 | tf_op jit(solution)/shard_map/ppermute | solution.py:40
  60.8 12.0 %collective-permute-start.23 = (f32[32,1536]{1,0:T(8,128)S(1)}, f32[32,1536]{1,0:T(8,128)S(1)}, u32[]{:S(2)}, u32[]{:S(2)}) collective-permute-start(f32[32,1536]{1,0:T(8,128)S(1)} %get-tuple-element.93), channel_id=1, source_target_pairs={{0,8},{1,9},{2,10},{3,11},{4,12},{5,13},{6,14},{7,15},{8,0},{9,1},... | collective-permute-start | bytes 589832 | tf_op jit(solution)/shard_map/ppermute | solution.py:40
  67.1 5.6 %collective-permute-start.20 = (f32[32,1536]{1,0:T(8,128)S(1)}, f32[32,1536]{1,0:T(8,128)S(1)}, u32[]{:S(2)}, u32[]{:S(2)}) collective-permute-start(f32[32,1536]{1,0:T(8,128)S(1)} %get-tuple-element.90), channel_id=1, source_target_pairs={{0,1},{1,0},{2,3},{3,2},{4,5},{5,4},{6,7},{7,6},{8,9},{9,8},{10,11... | collective-permute-start | bytes 589832 | tf_op jit(solution)/shard_map/ppermute | solution.py:40
  67.2 7.3 %collective-permute-start.21 = (f32[32,1536]{1,0:T(8,128)S(1)}, f32[32,1536]{1,0:T(8,128)S(1)}, u32[]{:S(2)}, u32[]{:S(2)}) collective-permute-start(f32[32,1536]{1,0:T(8,128)S(1)} %get-tuple-element.91), channel_id=1, source_target_pairs={{0,2},{1,3},{2,0},{3,1},{4,6},{5,7},{6,4},{7,5},{8,10},{9,11},{10,... | collective-permute-start | bytes 589832 | tf_op jit(solution)/shard_map/ppermute | solution.py:40
  77.0 5.4 %collective-permute-start.26 = (f32[8,128]{1,0:T(8,128)S(1)}, f32[8,128]{1,0:T(8,128)S(1)}, u32[]{:S(2)}, u32[]{:S(2)}) collective-permute-start(f32[8,128]{1,0:T(8,128)S(1)} %get-tuple-element.95), channel_id=1, source_target_pairs={{0,12},{1,13},{2,14},{3,15},{4,8},{5,9},{6,10},{7,11},{8,4},{9,5},... | collective-permute-start | bytes 12296 | tf_op jit(solution)/shard_map/ppermute | solution.py:40
  79.6 4.5 %collective-permute-start.25 = (f32[8,128]{1,0:T(8,128)S(1)}, f32[8,128]{1,0:T(8,128)S(1)}, u32[]{:S(2)}, u32[]{:S(2)}) collective-permute-start(f32[8,128]{1,0:T(8,128)S(1)} %get-tuple-element.95), channel_id=1, source_target_pairs={{0,8},{1,9},{2,10},{3,11},{4,12},{5,13},{6,14},{7,15},{8,0},{9,1},... | collective-permute-start | bytes 12296 | tf_op jit(solution)/shard_map/ppermute | solution.py:40
  79.6 4.5 %collective-permute-start.24 = (f32[8,128]{1,0:T(8,128)S(1)}, f32[8,128]{1,0:T(8,128)S(1)}, u32[]{:S(2)}, u32[]{:S(2)}) collective-permute-start(f32[8,128]{1,0:T(8,128)S(1)} %get-tuple-element.95), channel_id=1, source_target_pairs={{0,4},{1,5},{2,6},{3,7},{4,0},{5,1},{6,2},{7,3},{8,12},{9,13},{10,... | collective-permute-start | bytes 12296 | tf_op jit(solution)/shard_map/ppermute | solution.py:40
  84.1 3.1 %collective-permute-start.29 = (f32[8,128]{1,0:T(8,128)S(1)}, f32[8,128]{1,0:T(8,128)S(1)}, u32[]{:S(2)}, u32[]{:S(2)}) collective-permute-start(f32[8,128]{1,0:T(8,128)S(1)} %add_add_fusion.refs_0_), channel_id=1, source_target_pairs={{0,3},{1,2},{2,1},{3,0},{4,7},{5,6},{6,5},{7,4},{8,11},{9,10},{10,... | collective-permute-start | bytes 12296 | tf_op jit(solution)/shard_map/ppermute | solution.py:40
  84.7 3.6 %collective-permute-start.28 = (f32[8,128]{1,0:T(8,128)S(1)}, f32[8,128]{1,0:T(8,128)S(1)}, u32[]{:S(2)}, u32[]{:S(2)}) collective-permute-start(f32[8,128]{1,0:T(8,128)S(1)} %add_add_fusion.refs_0_), channel_id=1, source_target_pairs={{0,2},{1,3},{2,0},{3,1},{4,6},{5,7},{6,4},{7,5},{8,10},{9,11},{10,... | collective-permute-start | bytes 12296 | tf_op jit(solution)/shard_map/ppermute | solution.py:40
  85.4 2.9 %collective-permute-start.27 = (f32[8,128]{1,0:T(8,128)S(1)}, f32[8,128]{1,0:T(8,128)S(1)}, u32[]{:S(2)}, u32[]{:S(2)}) collective-permute-start(f32[8,128]{1,0:T(8,128)S(1)} %add_add_fusion.refs_0_), channel_id=1, source_target_pairs={{0,1},{1,0},{2,3},{3,2},{4,5},{5,4},{6,7},{7,6},{8,9},{9,8},{10,11... | collective-permute-start | bytes 12296 | tf_op jit(solution)/shard_map/ppermute | solution.py:40

commit v6 on v5

--- a/solution.py
+++ b/solution.py
@@ -301,14 +301,14 @@
     live = count_ref[0]
 
     source[:, :states] = block_ref[...]
-    at = states
-    for ghost in ghosts:
-        width = ghost.shape[1]
+    width = ghosts[0].shape[1]
+    for n, ghost in enumerate(ghosts):
+        at = states + (len(ghosts) - 1 - n) * width
         value = ghost[...]
         if matrix_ref is not None:
             value = applied(matrix_ref[...], stack3(value)).astype(BF16)
         source[:, at : at + width] = value
-        at += width
+    at = states + len(ghosts) * width
     source[:, at:] = jnp.zeros((columns, tile_size), BF16)
     nothing = at // tile_size
     total[...] = own_ref[...]
@@ -366,7 +366,7 @@
     outs = [vmem_out((3 * columns, states), BF16), vmem_out((columns * columns // LANES, LANES), F32)]
     if with_rows:
         outs.append(vmem_out((states // PACK, LANES), F32))
-    operands = [block, own, *ghosts] + ([] if matrix is None else [matrix]) + [tiles]
+    operands = [block, own, *ghosts[::-1]] + ([] if matrix is None else [matrix]) + [tiles]
     width = states + sum(g.shape[1] for g in ghosts) + tile_size
     return pl.pallas_call(
         functools.partial(product_kernel, len(ghosts), group, with_rows),

time: 92 us -> 89.3 us (0.971); the launches traced: 91 us -> 89.9 us
  Pallas kernels: 39.7 us -> 45.1 us
  waiting for transfers between devices: 16.9 us -> 12.5 us
  starting transfers between devices: 32.5 us -> 30.3 us
    pallas_call x3, Pallas kernels: 7.3 us -> 12.7 us  [product(): pl.pallas_call(functools.partial(product_kernel, len(ghosts), group, with...]
    ppermute x30, waiting for transfers between devices: 16.9 us -> 12.5 us  [swapped(): return lax.ppermute(x, 'dom', [(i, i ^ mask) for i in range(size)])]
    ppermute x30, starting transfers between devices: 32.5 us -> 30.3 us  [swapped(): return lax.ppermute(x, 'dom', [(i, i ^ mask) for i in range(size)])]
  transfers between devices with their start and end apart: 30 -> 30, of which waited for: 11 -> 12; matrix products, arithmetic and copies ran while one was open for 0% -> 0% of each run, Pallas kernels for 27% -> 27%
where the time goes in v6:
time: 89.3 us; the launch traced here: 89.9 us
  Pallas kernels  45.1 us (51%)
  starting transfers between devices  30.3 us (34%)
  waiting for transfers between devices  12.5 us (14%)
  between operations  0.9 us (1%)
    ppermute x30, starting transfers between devices, swapped(): return lax.ppermute(x, 'dom', [(i, i ^ mask) for i in range(size)])  30.3 us
    pallas_call x4, Pallas kernels, gather_colours(): pl.pallas_call(gather_kernel, out_shape=[vmem_out((columns, indices // co...  15.3 us
    pallas_call x3, Pallas kernels, product(): pl.pallas_call(functools.partial(product_kernel, len(ghosts), group, with...  12.7 us
    ppermute x30, waiting for transfers between devices, swapped(): return lax.ppermute(x, 'dom', [(i, i ^ mask) for i in range(size)])  12.5 us
    pallas_call x2, Pallas kernels, start_gather(): pl.pallas_call(functools.partial(start_kernel, count, first, make_rows),...  8.72 us
    pallas_call x2, Pallas kernels, later_own(): pl.pallas_call(functools.partial(later_own_kernel, total_states), out_sha...  4.98 us
    pallas_call x1, Pallas kernels, final(): pl.pallas_call(functools.partial(final_kernel, total_states), out_shape=j...  2.7 us
  transfers between devices with their start and end apart: 30, of which 12 were waited for; matrix products, arithmetic and copies ran while one was open for 0% of the time, Pallas kernels for 27%

profile of v6, /device:TPU:0, one launch (start us, length us, event | category | flops | bytes accessed | tf_op | source)
XLA Modules:
  0.0 89.9 jit_solution(7271770544542437482)
XLA Ops:
  0.0 0.8 add_select_fusion
  0.8 0.1 slice_reduce_fusion.1
  1.0 5.0 %start_gather.2 = (bf16[32,1536]{1,0:T(8,128)(2,1)S(1)}, bf16[32,1536]{1,0:T(8,128)(2,1)S(1)}, bf16[256,128,128]{2,1,0:T(8,128)(2,1)S(1)}, f32[2048,128]{1,0:T(8,128)S(1)}, bf16[32,8192]{1,0:T(8,128)(2,1)S(1)}) custom-call(s32[3072]{0:T(1024)S(1)} %pad_add_fusion.row_ref, s32[24,128]{1,0:T(8,128)S(1)} %pad_add_fusion.1.part_ref, ...), custom_call_target="tpu_custom_call" | custom-call | bytes 1024 | tf_op jit(solution)/shard_map/start_gather/pallas_call | solution.py:225
  6.0 4.1 %collective-permute-start = (bf16[32,1536]{1,0:T(8,128)(2,1)S(1)}, bf16[32,1536]{1,0:T(8,128)(2,1)S(1)}, u32[]{:S(2)}, u32[]{:S(2)}) collective-permute-start(bf16[32,1536]{1,0:T(8,128)(2,1)S(1)} %get-tuple-element.54), channel_id=1, source_target_pairs={{0,8},{1,9},{2,10},{3,11},{4,12},{5,13},{6,14},{7,15},{8,0},{9,1},... | collective-permute-start | bytes 294920 | tf_op jit(solution)/shard_map/ppermute | solution.py:40
  10.1 1.6 %collective-permute-start.1 = (bf16[32,1536]{1,0:T(8,128)(2,1)S(1)}, bf16[32,1536]{1,0:T(8,128)(2,1)S(1)}, u32[]{:S(2)}, u32[]{:S(2)}) collective-permute-start(bf16[32,1536]{1,0:T(8,128)(2,1)S(1)} %get-tuple-element.55), channel_id=1, source_target_pairs={{0,4},{1,5},{2,6},{3,7},{4,0},{5,1},{6,2},{7,3},{8,12},{9,13},{10,... | collective-permute-start | bytes 294920 | tf_op jit(solution)/shard_map/ppermute | solution.py:40
  11.7 3.7 %start_gather.3 = (bf16[32,1536]{1,0:T(8,128)(2,1)S(1)}, bf16[32,1536]{1,0:T(8,128)(2,1)S(1)}, bf16[64,128,128]{2,1,0:T(8,128)(2,1)S(1)}) custom-call(s32[3072]{0:T(1024)S(1)} %pad_add_fusion.2.row_ref, s32[24,128]{1,0:T(8,128)S(1)} %pad_add_fusion.3.part_ref, f32[2048,128]{1,0:T(8,128)S(1)} %get-tuple-element.52.source_ref, bf16[320,128,128]{2,1,0:T(8,128)(2,1)} %tiles_ref.3), custom_call_target="tpu_custom_call" | custom-call | bytes 1024 | tf_op jit(solution)/shard_map/start_gather/pallas_call | solution.py:225
  15.4 0.0 copy-start
  15.4 0.0 copy-start.1
  15.4 1.6 %collective-permute-start.2 = (bf16[32,1536]{1,0:T(8,128)(2,1)S(1)}, bf16[32,1536]{1,0:T(8,128)(2,1)S(1)}, u32[]{:S(2)}, u32[]{:S(2)}) collective-permute-start(bf16[32,1536]{1,0:T(8,128)(2,1)S(1)} %get-tuple-element.56), channel_id=1, source_target_pairs={{0,2},{1,3},{2,0},{3,1},{4,6},{5,7},{6,4},{7,5},{8,10},{9,11},{10,... | collective-permute-start | bytes 294920 | tf_op jit(solution)/shard_map/ppermute | solution.py:40
  17.7 0.7 first_own.1.refs_4_
  18.3 1.8 %collective-permute-done.2.refs_7_ = bf16[32,1536]{1,0:T(8,128)(2,1)S(1)} collective-permute-done((bf16[32,1536]{1,0:T(8,128)(2,1)S(1)}, bf16[32,1536]{1,0:T(8,128)(2,1)S(1)}, u32[]{:S(2)}, u32[]{:S(2)}) %collective-permute-start.2) | collective-permute-done | bytes 98336 | tf_op jit(solution)/shard_map/ppermute | solution.py:40
  20.1 0.0 collective-permute-done.3.refs_8_
  20.1 4.0 %product.3 = (bf16[96,8192]{1,0:T(8,128)(2,1)S(1)}, f32[8,128]{1,0:T(8,128)S(1)}, f32[2048,128]{1,0:T(8,128)S(1)}) custom-call(s32[320]{0:T(512)S(1)} %copy-done, s32[320]{0:T(512)S(1)} %copy-done.1, s32[1]{0:T(128)S(6)} %copy.7.refs_2_, bf16[32,8192]{1,0:T(8,128)(2,1)S(1)} %get-tuple-element.51.block_ref.refs_3_, f32[32,8192]{1,0:T(8,128)S(1)} %first_own.1.refs_4_, ...), custom_call_target="tpu_custom_call" | custom-call | bytes 1024 | tf_op jit(solution)/shard_map/product/pallas_call | solution.py:371
  24.2 0.1 collective-permute-start.6
  24.2 0.1 collective-permute-start.5
  24.3 4.3 %collective-permute-start.4 = (f32[8,128]{1,0:T(8,128)S(1)}, f32[8,128]{1,0:T(8,128)S(1)}, u32[]{:S(2)}, u32[]{:S(2)}) collective-permute-start(f32[8,128]{1,0:T(8,128)S(1)} %get-tuple-element.60), channel_id=1, source_target_pairs={{0,4},{1,5},{2,6},{3,7},{4,0},{5,1},{6,2},{7,3},{8,12},{9,13},{10,... | collective-permute-start | bytes 12296 | tf_op jit(solution)/shard_map/ppermute | solution.py:40
  28.6 3.8 %gather_rows.4 = (f32[32,1536]{1,0:T(8,128)S(1)}, f32[32,1536]{1,0:T(8,128)S(1)}) custom-call(s32[3072]{0:T(1024)S(1)} %pad_add_fusion.row_ref, s32[24,128]{1,0:T(8,128)S(1)} %pad_add_fusion.1.part_ref, f32[2048,128]{1,0:T(8,128)S(1)} %get-tuple-element.73.rows_ref), custom_call_target="tpu_custom_call" | custom-call | bytes 1024 | tf_op jit(solution)/shard_map/gather_rows/pallas_call | solution.py:175
  32.4 0.0 collective-permute-done.6
  32.5 0.1 collective-permute-start.9
  32.6 0.1 collective-permute-start.8
  32.6 1.8 %collective-permute-start.7 = (f32[8,128]{1,0:T(8,128)S(1)}, f32[8,128]{1,0:T(8,128)S(1)}, u32[]{:S(2)}, u32[]{:S(2)}) collective-permute-start(f32[8,128]{1,0:T(8,128)S(1)} %add_add_fusion.2.refs_0_), channel_id=1, source_target_pairs={{0,1},{1,0},{2,3},{3,2},{4,5},{5,4},{6,7},{7,6},{8,9},{9,8},{10,11... | collective-permute-start | bytes 12296 | tf_op jit(solution)/shard_map/ppermute | solution.py:40
  34.4 0.0 collective-permute-start.10
  34.4 0.6 collective-permute-start.11
  35.1 0.5 collective-permute-done.9.refs_3_
  35.6 0.7 collective-permute-done.8.refs_2_
  36.2 0.0 collective-permute-done.7.refs_1_
  36.2 3.8 %gather_rows.5 = (f32[32,1536]{1,0:T(8,128)S(1)}, f32[32,1536]{1,0:T(8,128)S(1)}) custom-call(s32[3072]{0:T(1024)S(1)} %pad_add_fusion.2.row_ref, s32[24,128]{1,0:T(8,128)S(1)} %pad_add_fusion.3.part_ref, f32[2048,128]{1,0:T(8,128)S(1)} %get-tuple-element.73.rows_ref), custom_call_target="tpu_custom_call" | custom-call | bytes 1024 | tf_op jit(solution)/shard_map/gather_rows/pallas_call | solution.py:175
  40.1 0.1 collective-permute-start.12
  40.2 0.6 collective-permute-start.13
  40.8 2.5 %later_own.2 = (bf16[32,8192]{1,0:T(8,128)(2,1)S(1)}, bf16[96,96]{1,0:T(8,128)(2,1)S(1)}, f32[32,8192]{1,0:T(8,128)S(1)}) custom-call(f32[8,128]{1,0:T(8,128)S(1)} %add_add_fusion.2.refs_0_, f32[8,128]{1,0:T(8,128)S(1)} %collective-permute-done.7.refs_1_, f32[8,128]{1,0:T(8,128)S(1)} %collective-permute-done.8.refs_2_, ...), custom_call_target="tpu_custom_call" | custom-call | bytes 1024 | tf_op jit(solution)/shard_map/later_own/pallas_call | solution.py:272
  43.3 2.5 %collective-permute-done.10.refs_5_ = f32[32,1536]{1,0:T(8,128)S(1)} collective-permute-done((f32[32,1536]{1,0:T(8,128)S(1)}, f32[32,1536]{1,0:T(8,128)S(1)}, u32[]{:S(2)}, u32[]{:S(2)}) %collective-permute-start.10) | collective-permute-done | bytes 196640 | tf_op jit(solution)/shard_map/ppermute | solution.py:40
  45.8 0.0 collective-permute-done.11.refs_6_
  45.8 0.6 collective-permute-done.12.refs_7_
  46.4 0.0 collective-permute-done.13.refs_8_
  46.4 4.4 %product.4 = (bf16[96,8192]{1,0:T(8,128)(2,1)S(1)}, f32[8,128]{1,0:T(8,128)S(1)}, f32[2048,128]{1,0:T(8,128)S(1)}) custom-call(s32[320]{0:T(512)S(1)} %copy-done, s32[320]{0:T(512)S(1)} %copy-done.1, s32[1]{0:T(128)S(6)} %copy.7.refs_2_, bf16[32,8192]{1,0:T(8,128)(2,1)S(1)} %get-tuple-element.69.refs_3_, f32[32,8192]{1,0:T(8,128)S(1)} %get-tuple-element.70.refs_4_, ...), custom_call_target="tpu_custom_call" | custom-call | bytes 1024 | tf_op jit(solution)/shard_map/product/pallas_call | solution.py:371
  50.8 1.4 %collective-permute-start.16 = (f32[8,128]{1,0:T(8,128)S(1)}, f32[8,128]{1,0:T(8,128)S(1)}, u32[]{:S(2)}, u32[]{:S(2)}) collective-permute-start(f32[8,128]{1,0:T(8,128)S(1)} %get-tuple-element.78), channel_id=1, source_target_pairs={{0,12},{1,13},{2,14},{3,15},{4,8},{5,9},{6,10},{7,11},{8,4},{9,5},... | collective-permute-start | bytes 12296 | tf_op jit(solution)/shard_map/ppermute | solution.py:40
  52.2 3.0 %collective-permute-start.14 = (f32[8,128]{1,0:T(8,128)S(1)}, f32[8,128]{1,0:T(8,128)S(1)}, u32[]{:S(2)}, u32[]{:S(2)}) collective-permute-start(f32[8,128]{1,0:T(8,128)S(1)} %get-tuple-element.78), channel_id=1, source_target_pairs={{0,4},{1,5},{2,6},{3,7},{4,0},{5,1},{6,2},{7,3},{8,12},{9,13},{10,... | collective-permute-start | bytes 12296 | tf_op jit(solution)/shard_map/ppermute | solution.py:40
  55.3 3.8 %gather_rows.6 = (f32[32,1536]{1,0:T(8,128)S(1)}, f32[32,1536]{1,0:T(8,128)S(1)}) custom-call(s32[3072]{0:T(1024)S(1)} %pad_add_fusion.row_ref, s32[24,128]{1,0:T(8,128)S(1)} %pad_add_fusion.1.part_ref, f32[2048,128]{1,0:T(8,128)S(1)} %get-tuple-element.91.rows_ref), custom_call_target="tpu_custom_call" | custom-call | bytes 1024 | tf_op jit(solution)/shard_map/gather_rows/pallas_call | solution.py:175
  59.1 0.0 collective-permute-done.15
  59.1 0.0 collective-permute-done.14
  59.1 0.1 collective-permute-start.19
  59.2 0.1 collective-permute-start.18
  59.3 1.8 %collective-permute-start.17 = (f32[8,128]{1,0:T(8,128)S(1)}, f32[8,128]{1,0:T(8,128)S(1)}, u32[]{:S(2)}, u32[]{:S(2)}) collective-permute-start(f32[8,128]{1,0:T(8,128)S(1)} %add_add_fusion.1.refs_0_), channel_id=1, source_target_pairs={{0,1},{1,0},{2,3},{3,2},{4,5},{5,4},{6,7},{7,6},{8,9},{9,8},{10,11... | collective-permute-start | bytes 12296 | tf_op jit(solution)/shard_map/ppermute | solution.py:40
  61.1 0.0 collective-permute-start.20
  61.1 1.9 %collective-permute-start.21 = (f32[32,1536]{1,0:T(8,128)S(1)}, f32[32,1536]{1,0:T(8,128)S(1)}, u32[]{:S(2)}, u32[]{:S(2)}) collective-permute-start(f32[32,1536]{1,0:T(8,128)S(1)} %get-tuple-element.90), channel_id=1, source_target_pairs={{0,4},{1,5},{2,6},{3,7},{4,0},{5,1},{6,2},{7,3},{8,12},{9,13},{10,... | collective-permute-start | bytes 589832 | tf_op jit(solution)/shard_map/ppermute | solution.py:40
  63.0 0.0 collective-permute-done.17.refs_1_
  63.0 3.8 %gather_rows.7 = (f32[32,1536]{1,0:T(8,128)S(1)}, f32[32,1536]{1,0:T(8,128)S(1)}) custom-call(s32[3072]{0:T(1024)S(1)} %pad_add_fusion.2.row_ref, s32[24,128]{1,0:T(8,128)S(1)} %pad_add_fusion.3.part_ref, f32[2048,128]{1,0:T(8,128)S(1)} %get-tuple-element.91.rows_ref), custom_call_target="tpu_custom_call" | custom-call | bytes 1024 | tf_op jit(solution)/shard_map/gather_rows/pallas_call | solution.py:175
  66.8 0.8 collective-permute-start.22
  67.7 0.0 collective-permute-start.23
  67.7 2.5 %later_own.3 = (bf16[32,8192]{1,0:T(8,128)(2,1)S(1)}, bf16[96,96]{1,0:T(8,128)(2,1)S(1)}, f32[32,8192]{1,0:T(8,128)S(1)}) custom-call(f32[8,128]{1,0:T(8,128)S(1)} %add_add_fusion.1.refs_0_, f32[8,128]{1,0:T(8,128)S(1)} %collective-permute-done.17.refs_1_, f32[8,128]{1,0:T(8,128)S(1)} %collective-permute-done.18.refs_2_, ...), custom_call_target="tpu_custom_call" | custom-call | bytes 1024 | tf_op jit(solution)/shard_map/later_own/pallas_call | solution.py:272
  70.2 2.3 %collective-permute-done.20.refs_5_ = f32[32,1536]{1,0:T(8,128)S(1)} collective-permute-done((f32[32,1536]{1,0:T(8,128)S(1)}, f32[32,1536]{1,0:T(8,128)S(1)}, u32[]{:S(2)}, u32[]{:S(2)}) %collective-permute-start.20) | collective-permute-done | bytes 196640 | tf_op jit(solution)/shard_map/ppermute | solution.py:40
  72.4 0.0 collective-permute-done.21.refs_6_
  72.4 0.7 collective-permute-done.22.refs_7_
  73.2 4.3 %product.5 = (bf16[96,8192]{1,0:T(8,128)(2,1)S(1)}, f32[8,128]{1,0:T(8,128)S(1)}) custom-call(s32[320]{0:T(512)S(1)} %copy-done, s32[320]{0:T(512)S(1)} %copy-done.1, s32[1]{0:T(128)S(6)} %copy.7.refs_2_, bf16[32,8192]{1,0:T(8,128)(2,1)S(1)} %get-tuple-element.87.refs_3_, f32[32,8192]{1,0:T(8,128)S(1)} %get-tuple-element.88.refs_4_, ...), custom_call_target="tpu_custom_call" | custom-call | bytes 1024 | tf_op jit(solution)/shard_map/product/pallas_call | solution.py:371
  77.5 1.3 %collective-permute-start.26 = (f32[8,128]{1,0:T(8,128)S(1)}, f32[8,128]{1,0:T(8,128)S(1)}, u32[]{:S(2)}, u32[]{:S(2)}) collective-permute-start(f32[8,128]{1,0:T(8,128)S(1)} %get-tuple-element.95), channel_id=1, source_target_pairs={{0,12},{1,13},{2,14},{3,15},{4,8},{5,9},{6,10},{7,11},{8,4},{9,5},... | collective-permute-start | bytes 12296 | tf_op jit(solution)/shard_map/ppermute | solution.py:40
  78.8 3.1 %collective-permute-start.24 = (f32[8,128]{1,0:T(8,128)S(1)}, f32[8,128]{1,0:T(8,128)S(1)}, u32[]{:S(2)}, u32[]{:S(2)}) collective-permute-start(f32[8,128]{1,0:T(8,128)S(1)} %get-tuple-element.95), channel_id=1, source_target_pairs={{0,4},{1,5},{2,6},{3,7},{4,0},{5,1},{6,2},{7,3},{8,12},{9,13},{10,... | collective-permute-start | bytes 12296 | tf_op jit(solution)/shard_map/ppermute | solution.py:40
  81.9 1.0 %collective-permute-done.26 = f32[8,128]{1,0:T(8,128)S(1)} collective-permute-done((f32[8,128]{1,0:T(8,128)S(1)}, f32[8,128]{1,0:T(8,128)S(1)}, u32[]{:S(2)}, u32[]{:S(2)}) %collective-permute-start.26) | collective-permute-done | bytes 4128 | tf_op jit(solution)/shard_map/ppermute | solution.py:40
  82.9 0.4 collective-permute-done.25
  83.3 0.2 collective-permute-done.24
  83.5 0.7 collective-permute-start.28
  84.2 1.2 %collective-permute-start.27 = (f32[8,128]{1,0:T(8,128)S(1)}, f32[8,128]{1,0:T(8,128)S(1)}, u32[]{:S(2)}, u32[]{:S(2)}) collective-permute-start(f32[8,128]{1,0:T(8,128)S(1)} %add_add_fusion.refs_0_), channel_id=1, source_target_pairs={{0,1},{1,0},{2,3},{3,2},{4,5},{5,4},{6,7},{7,6},{8,9},{9,8},{10,11... | collective-permute-start | bytes 12296 | tf_op jit(solution)/shard_map/ppermute | solution.py:40
  85.3 1.2 %collective-permute-done.29.refs_3_ = f32[8,128]{1,0:T(8,128)S(1)} collective-permute-done((f32[8,128]{1,0:T(8,128)S(1)}, f32[8,128]{1,0:T(8,128)S(1)}, u32[]{:S(2)}, u32[]{:S(2)}) %collective-permute-start.29) | collective-permute-done | bytes 4128 | tf_op jit(solution)/shard_map/ppermute | solution.py:40
  86.5 0.6 collective-permute-done.28.refs_2_
  87.2 2.7 %final.1 = f32[32,8192]{1,0:T(8,128)} custom-call(f32[8,128]{1,0:T(8,128)S(1)} %add_add_fusion.refs_0_, f32[8,128]{1,0:T(8,128)S(1)} %collective-permute-done.27.refs_1_, f32[8,128]{1,0:T(8,128)S(1)} %collective-permute-done.28.refs_2_, f32[8,128]{1,0:T(8,128)S(1)} %collective-permute-done.29.refs_3_, bf16[96,8192]{1,0:T(8,128)(2,1)S(1)} %get-tuple-element.96.refs_4_), custom_call_target="tpu_custom_call" | custom-call | bytes 1024 | tf_op jit(solution)/shard_map/final/pallas_call | solution.py:398
  (22 shorter events, 0.1 us)
Async XLA Ops:
  6.0 12.4 %collective-permute-start = (bf16[32,1536]{1,0:T(8,128)(2,1)S(1)}, bf16[32,1536]{1,0:T(8,128)(2,1)S(1)}, u32[]{:S(2)}, u32[]{:S(2)}) collective-permute-start(bf16[32,1536]{1,0:T(8,128)(2,1)S(1)} %get-tuple-element.54), channel_id=1, source_target_pairs={{0,8},{1,9},{2,10},{3,11},{4,12},{5,13},{6,14},{7,15},{8,0},{9,1},... | collective-permute-start | bytes 294920 | tf_op jit(solution)/shard_map/ppermute | solution.py:40
  10.1 8.3 %collective-permute-start.1 = (bf16[32,1536]{1,0:T(8,128)(2,1)S(1)}, bf16[32,1536]{1,0:T(8,128)(2,1)S(1)}, u32[]{:S(2)}, u32[]{:S(2)}) collective-permute-start(bf16[32,1536]{1,0:T(8,128)(2,1)S(1)} %get-tuple-element.55), channel_id=1, source_target_pairs={{0,4},{1,5},{2,6},{3,7},{4,0},{5,1},{6,2},{7,3},{8,12},{9,13},{10,... | collective-permute-start | bytes 294920 | tf_op jit(solution)/shard_map/ppermute | solution.py:40
  15.4 4.7 %copy-start = (s32[320]{0:T(512)S(1)}, s32[320]{0:T(512)}, u32[]{:S(2)}) copy-start(s32[320]{0:T(512)} %refs_0_.5) | copy-start | bytes 3844
  15.4 4.7 %copy-start.1 = (s32[320]{0:T(512)S(1)}, s32[320]{0:T(512)}, u32[]{:S(2)}) copy-start(s32[320]{0:T(512)} %refs_1_.5) | copy-start | bytes 3844
  15.4 4.7 %collective-permute-start.2 = (bf16[32,1536]{1,0:T(8,128)(2,1)S(1)}, bf16[32,1536]{1,0:T(8,128)(2,1)S(1)}, u32[]{:S(2)}, u32[]{:S(2)}) collective-permute-start(bf16[32,1536]{1,0:T(8,128)(2,1)S(1)} %get-tuple-element.56), channel_id=1, source_target_pairs={{0,2},{1,3},{2,0},{3,1},{4,6},{5,7},{6,4},{7,5},{8,10},{9,11},{10,... | collective-permute-start | bytes 294920 | tf_op jit(solution)/shard_map/ppermute | solution.py:40
  17.0 3.1 %collective-permute-start.3 = (bf16[32,1536]{1,0:T(8,128)(2,1)S(1)}, bf16[32,1536]{1,0:T(8,128)(2,1)S(1)}, u32[]{:S(2)}, u32[]{:S(2)}) collective-permute-start(bf16[32,1536]{1,0:T(8,128)(2,1)S(1)} %get-tuple-element.57), channel_id=1, source_target_pairs={{0,1},{1,0},{2,3},{3,2},{4,5},{5,4},{6,7},{7,6},{8,9},{9,8},{10,11... | collective-permute-start | bytes 294920 | tf_op jit(solution)/shard_map/ppermute | solution.py:40
  24.2 8.3 %collective-permute-start.6 = (f32[8,128]{1,0:T(8,128)S(1)}, f32[8,128]{1,0:T(8,128)S(1)}, u32[]{:S(2)}, u32[]{:S(2)}) collective-permute-start(f32[8,128]{1,0:T(8,128)S(1)} %get-tuple-element.60), channel_id=1, source_target_pairs={{0,12},{1,13},{2,14},{3,15},{4,8},{5,9},{6,10},{7,11},{8,4},{9,5},... | collective-permute-start | bytes 12296 | tf_op jit(solution)/shard_map/ppermute | solution.py:40
  24.2 8.2 %collective-permute-start.5 = (f32[8,128]{1,0:T(8,128)S(1)}, f32[8,128]{1,0:T(8,128)S(1)}, u32[]{:S(2)}, u32[]{:S(2)}) collective-permute-start(f32[8,128]{1,0:T(8,128)S(1)} %get-tuple-element.60), channel_id=1, source_target_pairs={{0,8},{1,9},{2,10},{3,11},{4,12},{5,13},{6,14},{7,15},{8,0},{9,1},... | collective-permute-start | bytes 12296 | tf_op jit(solution)/shard_map/ppermute | solution.py:40
  24.3 8.1 %collective-permute-start.4 = (f32[8,128]{1,0:T(8,128)S(1)}, f32[8,128]{1,0:T(8,128)S(1)}, u32[]{:S(2)}, u32[]{:S(2)}) collective-permute-start(f32[8,128]{1,0:T(8,128)S(1)} %get-tuple-element.60), channel_id=1, source_target_pairs={{0,4},{1,5},{2,6},{3,7},{4,0},{5,1},{6,2},{7,3},{8,12},{9,13},{10,... | collective-permute-start | bytes 12296 | tf_op jit(solution)/shard_map/ppermute | solution.py:40
  32.5 3.1 %collective-permute-start.9 = (f32[8,128]{1,0:T(8,128)S(1)}, f32[8,128]{1,0:T(8,128)S(1)}, u32[]{:S(2)}, u32[]{:S(2)}) collective-permute-start(f32[8,128]{1,0:T(8,128)S(1)} %add_add_fusion.2.refs_0_), channel_id=1, source_target_pairs={{0,3},{1,2},{2,1},{3,0},{4,7},{5,6},{6,5},{7,4},{8,11},{9,10},{10,... | collective-permute-start | bytes 12296 | tf_op jit(solution)/shard_map/ppermute | solution.py:40
  32.6 3.7 %collective-permute-start.8 = (f32[8,128]{1,0:T(8,128)S(1)}, f32[8,128]{1,0:T(8,128)S(1)}, u32[]{:S(2)}, u32[]{:S(2)}) collective-permute-start(f32[8,128]{1,0:T(8,128)S(1)} %add_add_fusion.2.refs_0_), channel_id=1, source_target_pairs={{0,2},{1,3},{2,0},{3,1},{4,6},{5,7},{6,4},{7,5},{8,10},{9,11},{10,... | collective-permute-start | bytes 12296 | tf_op jit(solution)/shard_map/ppermute | solution.py:40
  32.6 3.6 %collective-permute-start.7 = (f32[8,128]{1,0:T(8,128)S(1)}, f32[8,128]{1,0:T(8,128)S(1)}, u32[]{:S(2)}, u32[]{:S(2)}) collective-permute-start(f32[8,128]{1,0:T(8,128)S(1)} %add_add_fusion.2.refs_0_), channel_id=1, source_target_pairs={{0,1},{1,0},{2,3},{3,2},{4,5},{5,4},{6,7},{7,6},{8,9},{9,8},{10,11... | collective-permute-start | bytes 12296 | tf_op jit(solution)/shard_map/ppermute | solution.py:40
  34.4 11.4 %collective-permute-start.10 = (f32[32,1536]{1,0:T(8,128)S(1)}, f32[32,1536]{1,0:T(8,128)S(1)}, u32[]{:S(2)}, u32[]{:S(2)}) collective-permute-start(f32[32,1536]{1,0:T(8,128)S(1)} %get-tuple-element.71), channel_id=1, source_target_pairs={{0,8},{1,9},{2,10},{3,11},{4,12},{5,13},{6,14},{7,15},{8,0},{9,1},... | collective-permute-start | bytes 589832 | tf_op jit(solution)/shard_map/ppermute | solution.py:40
  34.4 11.4 %collective-permute-start.11 = (f32[32,1536]{1,0:T(8,128)S(1)}, f32[32,1536]{1,0:T(8,128)S(1)}, u32[]{:S(2)}, u32[]{:S(2)}) collective-permute-start(f32[32,1536]{1,0:T(8,128)S(1)} %get-tuple-element.72), channel_id=1, source_target_pairs={{0,4},{1,5},{2,6},{3,7},{4,0},{5,1},{6,2},{7,3},{8,12},{9,13},{10,... | collective-permute-start | bytes 589832 | tf_op jit(solution)/shard_map/ppermute | solution.py:40
  40.1 6.3 %collective-permute-start.12 = (f32[32,1536]{1,0:T(8,128)S(1)}, f32[32,1536]{1,0:T(8,128)S(1)}, u32[]{:S(2)}, u32[]{:S(2)}) collective-permute-start(f32[32,1536]{1,0:T(8,128)S(1)} %get-tuple-element.74), channel_id=1, source_target_pairs={{0,2},{1,3},{2,0},{3,1},{4,6},{5,7},{6,4},{7,5},{8,10},{9,11},{10,... | collective-permute-start | bytes 589832 | tf_op jit(solution)/shard_map/ppermute | solution.py:40
  40.2 6.3 %collective-permute-start.13 = (f32[32,1536]{1,0:T(8,128)S(1)}, f32[32,1536]{1,0:T(8,128)S(1)}, u32[]{:S(2)}, u32[]{:S(2)}) collective-permute-start(f32[32,1536]{1,0:T(8,128)S(1)} %get-tuple-element.75), channel_id=1, source_target_pairs={{0,1},{1,0},{2,3},{3,2},{4,5},{5,4},{6,7},{7,6},{8,9},{9,8},{10,11... | collective-permute-start | bytes 589832 | tf_op jit(solution)/shard_map/ppermute | solution.py:40
  50.8 8.3 %collective-permute-start.16 = (f32[8,128]{1,0:T(8,128)S(1)}, f32[8,128]{1,0:T(8,128)S(1)}, u32[]{:S(2)}, u32[]{:S(2)}) collective-permute-start(f32[8,128]{1,0:T(8,128)S(1)} %get-tuple-element.78), channel_id=1, source_target_pairs={{0,12},{1,13},{2,14},{3,15},{4,8},{5,9},{6,10},{7,11},{8,4},{9,5},... | collective-permute-start | bytes 12296 | tf_op jit(solution)/shard_map/ppermute | solution.py:40
  52.2 6.9 %collective-permute-start.15 = (f32[8,128]{1,0:T(8,128)S(1)}, f32[8,128]{1,0:T(8,128)S(1)}, u32[]{:S(2)}, u32[]{:S(2)}) collective-permute-start(f32[8,128]{1,0:T(8,128)S(1)} %get-tuple-element.78), channel_id=1, source_target_pairs={{0,8},{1,9},{2,10},{3,11},{4,12},{5,13},{6,14},{7,15},{8,0},{9,1},... | collective-permute-start | bytes 12296 | tf_op jit(solution)/shard_map/ppermute | solution.py:40
  52.2 6.9 %collective-permute-start.14 = (f32[8,128]{1,0:T(8,128)S(1)}, f32[8,128]{1,0:T(8,128)S(1)}, u32[]{:S(2)}, u32[]{:S(2)}) collective-permute-start(f32[8,128]{1,0:T(8,128)S(1)} %get-tuple-element.78), channel_id=1, source_target_pairs={{0,4},{1,5},{2,6},{3,7},{4,0},{5,1},{6,2},{7,3},{8,12},{9,13},{10,... | collective-permute-start | bytes 12296 | tf_op jit(solution)/shard_map/ppermute | solution.py:40
  59.1 3.9 %collective-permute-start.19 = (f32[8,128]{1,0:T(8,128)S(1)}, f32[8,128]{1,0:T(8,128)S(1)}, u32[]{:S(2)}, u32[]{:S(2)}) collective-permute-start(f32[8,128]{1,0:T(8,128)S(1)} %add_add_fusion.1.refs_0_), channel_id=1, source_target_pairs={{0,3},{1,2},{2,1},{3,0},{4,7},{5,6},{6,5},{7,4},{8,11},{9,10},{10,... | collective-permute-start | bytes 12296 | tf_op jit(solution)/shard_map/ppermute | solution.py:40
  59.2 3.8 %collective-permute-start.18 = (f32[8,128]{1,0:T(8,128)S(1)}, f32[8,128]{1,0:T(8,128)S(1)}, u32[]{:S(2)}, u32[]{:S(2)}) collective-permute-start(f32[8,128]{1,0:T(8,128)S(1)} %add_add_fusion.1.refs_0_), channel_id=1, source_target_pairs={{0,2},{1,3},{2,0},{3,1},{4,6},{5,7},{6,4},{7,5},{8,10},{9,11},{10,... | collective-permute-start | bytes 12296 | tf_op jit(solution)/shard_map/ppermute | solution.py:40
  59.3 3.7 %collective-permute-start.17 = (f32[8,128]{1,0:T(8,128)S(1)}, f32[8,128]{1,0:T(8,128)S(1)}, u32[]{:S(2)}, u32[]{:S(2)}) collective-permute-start(f32[8,128]{1,0:T(8,128)S(1)} %add_add_fusion.1.refs_0_), channel_id=1, source_target_pairs={{0,1},{1,0},{2,3},{3,2},{4,5},{5,4},{6,7},{7,6},{8,9},{9,8},{10,11... | collective-permute-start | bytes 12296 | tf_op jit(solution)/shard_map/ppermute | solution.py:40
  61.1 11.4 %collective-permute-start.20 = (f32[32,1536]{1,0:T(8,128)S(1)}, f32[32,1536]{1,0:T(8,128)S(1)}, u32[]{:S(2)}, u32[]{:S(2)}) collective-permute-start(f32[32,1536]{1,0:T(8,128)S(1)} %get-tuple-element.89), channel_id=1, source_target_pairs={{0,8},{1,9},{2,10},{3,11},{4,12},{5,13},{6,14},{7,15},{8,0},{9,1},... | collective-permute-start | bytes 589832 | tf_op jit(solution)/shard_map/ppermute | solution.py:40
  61.1 11.4 %collective-permute-start.21 = (f32[32,1536]{1,0:T(8,128)S(1)}, f32[32,1536]{1,0:T(8,128)S(1)}, u32[]{:S(2)}, u32[]{:S(2)}) collective-permute-start(f32[32,1536]{1,0:T(8,128)S(1)} %get-tuple-element.90), channel_id=1, source_target_pairs={{0,4},{1,5},{2,6},{3,7},{4,0},{5,1},{6,2},{7,3},{8,12},{9,13},{10,... | collective-permute-start | bytes 589832 | tf_op jit(solution)/shard_map/ppermute | solution.py:40
  66.8 6.3 %collective-permute-start.22 = (f32[32,1536]{1,0:T(8,128)S(1)}, f32[32,1536]{1,0:T(8,128)S(1)}, u32[]{:S(2)}, u32[]{:S(2)}) collective-permute-start(f32[32,1536]{1,0:T(8,128)S(1)} %get-tuple-element.92), channel_id=1, source_target_pairs={{0,2},{1,3},{2,0},{3,1},{4,6},{5,7},{6,4},{7,5},{8,10},{9,11},{10,... | collective-permute-start | bytes 589832 | tf_op jit(solution)/shard_map/ppermute | solution.py:40
  67.7 5.5 %collective-permute-start.23 = (f32[32,1536]{1,0:T(8,128)S(1)}, f32[32,1536]{1,0:T(8,128)S(1)}, u32[]{:S(2)}, u32[]{:S(2)}) collective-permute-start(f32[32,1536]{1,0:T(8,128)S(1)} %get-tuple-element.93), channel_id=1, source_target_pairs={{0,1},{1,0},{2,3},{3,2},{4,5},{5,4},{6,7},{7,6},{8,9},{9,8},{10,11... | collective-permute-start | bytes 589832 | tf_op jit(solution)/shard_map/ppermute | solution.py:40
  77.5 5.4 %collective-permute-start.26 = (f32[8,128]{1,0:T(8,128)S(1)}, f32[8,128]{1,0:T(8,128)S(1)}, u32[]{:S(2)}, u32[]{:S(2)}) collective-permute-start(f32[8,128]{1,0:T(8,128)S(1)} %get-tuple-element.95), channel_id=1, source_target_pairs={{0,12},{1,13},{2,14},{3,15},{4,8},{5,9},{6,10},{7,11},{8,4},{9,5},... | collective-permute-start | bytes 12296 | tf_op jit(solution)/shard_map/ppermute | solution.py:40
  78.8 4.5 %collective-permute-start.25 = (f32[8,128]{1,0:T(8,128)S(1)}, f32[8,128]{1,0:T(8,128)S(1)}, u32[]{:S(2)}, u32[]{:S(2)}) collective-permute-start(f32[8,128]{1,0:T(8,128)S(1)} %get-tuple-element.95), channel_id=1, source_target_pairs={{0,8},{1,9},{2,10},{3,11},{4,12},{5,13},{6,14},{7,15},{8,0},{9,1},... | collective-permute-start | bytes 12296 | tf_op jit(solution)/shard_map/ppermute | solution.py:40
  78.8 4.7 %collective-permute-start.24 = (f32[8,128]{1,0:T(8,128)S(1)}, f32[8,128]{1,0:T(8,128)S(1)}, u32[]{:S(2)}, u32[]{:S(2)}) collective-permute-start(f32[8,128]{1,0:T(8,128)S(1)} %get-tuple-element.95), channel_id=1, source_target_pairs={{0,4},{1,5},{2,6},{3,7},{4,0},{5,1},{6,2},{7,3},{8,12},{9,13},{10,... | collective-permute-start | bytes 12296 | tf_op jit(solution)/shard_map/ppermute | solution.py:40
  83.5 3.0 %collective-permute-start.29 = (f32[8,128]{1,0:T(8,128)S(1)}, f32[8,128]{1,0:T(8,128)S(1)}, u32[]{:S(2)}, u32[]{:S(2)}) collective-permute-start(f32[8,128]{1,0:T(8,128)S(1)} %add_add_fusion.refs_0_), channel_id=1, source_target_pairs={{0,3},{1,2},{2,1},{3,0},{4,7},{5,6},{6,5},{7,4},{8,11},{9,10},{10,... | collective-permute-start | bytes 12296 | tf_op jit(solution)/shard_map/ppermute | solution.py:40
  83.5 3.7 %collective-permute-start.28 = (f32[8,128]{1,0:T(8,128)S(1)}, f32[8,128]{1,0:T(8,128)S(1)}, u32[]{:S(2)}, u32[]{:S(2)}) collective-permute-start(f32[8,128]{1,0:T(8,128)S(1)} %add_add_fusion.refs_0_), channel_id=1, source_target_pairs={{0,2},{1,3},{2,0},{3,1},{4,6},{5,7},{6,4},{7,5},{8,10},{9,11},{10,... | collective-permute-start | bytes 12296 | tf_op jit(solution)/shard_map/ppermute | solution.py:40
  84.2 3.0 %collective-permute-start.27 = (f32[8,128]{1,0:T(8,128)S(1)}, f32[8,128]{1,0:T(8,128)S(1)}, u32[]{:S(2)}, u32[]{:S(2)}) collective-permute-start(f32[8,128]{1,0:T(8,128)S(1)} %add_add_fusion.refs_0_), channel_id=1, source_target_pairs={{0,1},{1,0},{2,3},{3,2},{4,5},{5,4},{6,7},{7,6},{8,9},{9,8},{10,11... | collective-permute-start | bytes 12296 | tf_op jit(solution)/shard_map/ppermute | solution.py:40

commit v7 on v6

--- a/solution.py
+++ b/solution.py
@@ -14,6 +14,8 @@
 SUBLANES = 8
 STEP = 4
 COPIES = 8
+LARGE = 64
+SMALL = 16
 F32 = jnp.float32
 BF16 = jnp.bfloat16
 VMEM = pl.BlockSpec(memory_space=pltpu.VMEM)
@@ -236,109 +238,159 @@
 
 def own_slots(block_ref, tiles_ref, own_ref):
     tile_size = tiles_ref.shape[1]
-    for t in range(own_ref.shape[1] // tile_size):
+    for t in range(tiles_ref.shape[0]):
         at = slice(t * tile_size, (t + 1) * tile_size)
         own_ref[:, at] = jnp.dot(block_ref[:, at], tiles_ref[t], preferred_element_type=F32)
 
 
-def first_own_kernel(block_ref, tiles_ref, own_ref):
-    own_slots(block_ref, tiles_ref, own_ref)
-
-
-def first_own(block, tiles):
+def order_slots(src_ref, dst_ref, count_ref, order_ref, first):
+    rest = order_ref.shape[0] // 4
+    used = jnp.minimum(count_ref[0] - first, rest)
+
+    def place(i, placed):
+        src = src_ref[first + i]
+        local = src < first
+        at = jnp.where(local, placed, used - 1 - (i - placed))
+        order_ref[at] = i
+        order_ref[rest + at] = jnp.where(local, src, src - first)
+        order_ref[2 * rest + at] = dst_ref[first + i]
+        return placed + local.astype(jnp.int32)
+
+    order_ref[3 * rest] = lax.fori_loop(0, used, place, jnp.int32(0))
+    order_ref[3 * rest + 1] = used
+
+
+def add_slots(order_ref, start, stop, source, tiles_ref, total):
+    rest = order_ref.shape[0] // 4
+    tile_size = tiles_ref.shape[1]
+    columns = source.shape[0]
+    spare = total.shape[1] // tile_size - 1
+    zero = jnp.zeros((columns, tile_size), BF16)
+
+    def tile_of(index):
+        return pl.ds(pl.multiple_of(index * tile_size, tile_size), tile_size)
+
+    def chunk(base, size, whole):
+        slots = []
+        for u in range(size):
+            at = base + u
+            if whole:
+                slots.append([order_ref[k * rest + at] for k in range(3)])
+            else:
+                there = at < stop
+                at = jnp.minimum(at, rest - 1)
+                other = (0, 0, spare)
+                slots.append([jnp.where(there, order_ref[k * rest + at], other[k]) for k in range(3)])
+        terms = []
+        for u in range(0, size, 2):
+            (slot_a, src_a, _), (slot_b, src_b, _) = slots[u : u + 2]
+            pair = jnp.concatenate(
+                [
+                    jnp.concatenate([source[:, tile_of(src_a)], zero], axis=1),
+                    jnp.concatenate([zero, source[:, tile_of(src_b)]], axis=1),
+                ],
+                axis=0,
+            )
+            weights = jnp.concatenate([tiles_ref[slot_a], tiles_ref[slot_b]], axis=0)
+            both = jnp.dot(pair, weights, preferred_element_type=F32)
+            terms += [both[:columns], both[columns:]]
+        for (_, _, dst), term in zip(slots, terms):
+            total[:, tile_of(dst)] += term
+
+    def large(i, carry):
+        chunk(start + i * LARGE, LARGE, True)
+        return carry
+
+    wholes = (stop - start) // LARGE
+    lax.fori_loop(0, wholes, large, 0)
+    after = start + wholes * LARGE
+
+    def small(i, carry):
+        chunk(after + i * SMALL, SMALL, False)
+        return carry
+
+    lax.fori_loop(0, (stop - after + SMALL - 1) // SMALL, small, 0)
+
+
+def local_slots(order_ref, block_ref, own_tiles, rest_tiles, own_ref):
+    rest = order_ref.shape[0] // 4
+    own_slots(block_ref, own_tiles, own_ref)
+    states = block_ref.shape[1]
+    own_ref[:, states:] = jnp.zeros((own_ref.shape[0], own_ref.shape[1] - states), F32)
+    add_slots(order_ref, 0, order_ref[3 * rest], block_ref, rest_tiles, own_ref)
+
+
+def first_own_kernel(src_ref, dst_ref, count_ref, block_ref, own_tiles, rest_tiles, own_ref, order_ref):
+    order_slots(src_ref, dst_ref, count_ref, order_ref, own_tiles.shape[0])
+    local_slots(order_ref, block_ref, own_tiles, rest_tiles, own_ref)
+
+
+def own_shape(columns, tiles):
+    count, tile_size, _ = tiles.shape
+    return vmem_out((columns, (count + 1) * tile_size), F32)
+
+
+def first_own(src, dst, count, block, own_tiles, rest_tiles):
     return pl.pallas_call(
         first_own_kernel,
-        out_shape=vmem_out(block.shape, F32),
-        in_specs=[VMEM] * 2,
-        out_specs=VMEM,
+        out_shape=[
+            own_shape(block.shape[0], own_tiles),
+            jax.ShapeDtypeStruct((4 * rest_tiles.shape[0],), jnp.int32),
+        ],
+        in_specs=[SMEM] * 3 + [VMEM] * 3,
+        out_specs=[VMEM, SMEM],
         compiler_params=PARAMS,
         cost_estimate=CHEAP,
         name="first_own",
-    )(in_vmem(block), in_vmem(tiles))
-
-
-def later_own_kernel(total_states, *refs):
-    grams, stacked, tiles_ref = refs[:4], refs[4], refs[5]
-    block_ref, matrix_ref, own_ref = refs[6:]
+    )(src, dst, count, in_vmem(block), in_vmem(own_tiles), in_vmem(rest_tiles))
+
+
+def later_own_kernel(total_states, order_ref, *refs):
+    grams, (stacked, own_tiles, rest_tiles) = refs[:4], refs[4:7]
+    matrix_ref, own_ref, block_ref = refs[7:]
     matrix = apply_matrix(inverse_factor(gram_of([r[...] for r in grams], total_states)))
     matrix_ref[...] = matrix
     for c in range(0, block_ref.shape[1], CHUNK):
         block_ref[:, c : c + CHUNK] = applied(matrix, stacked[:, c : c + CHUNK]).astype(BF16)
-    own_slots(block_ref, tiles_ref, own_ref)
-
-
-def later_own(grams, stacked, tiles, total_states):
+    local_slots(order_ref, block_ref, own_tiles, rest_tiles, own_ref)
+
+
+def later_own(order, grams, stacked, own_tiles, rest_tiles, total_states):
     columns, states = stacked.shape[0] // 3, stacked.shape[1]
+    operands = [*grams, stacked, own_tiles, rest_tiles]
     return pl.pallas_call(
         functools.partial(later_own_kernel, total_states),
-        out_shape=[
-            vmem_out((columns, states), BF16),
-            vmem_out((3 * columns, 3 * columns), BF16),
-            vmem_out((columns, states), F32),
-        ],
-        in_specs=[VMEM] * 6,
-        out_specs=[VMEM] * 3,
+        out_shape=[vmem_out((3 * columns, 3 * columns), BF16), own_shape(columns, own_tiles)],
+        in_specs=[SMEM] + [VMEM] * len(operands),
+        out_specs=[VMEM] * 2,
+        scratch_shapes=[pltpu.VMEM((columns, states), BF16)],
         compiler_params=PARAMS,
         cost_estimate=CHEAP,
         name="later_own",
-    )(*[in_vmem(g) for g in grams], in_vmem(stacked), in_vmem(tiles))
-
-
-def product_kernel(colours, group, with_rows, *refs):
-    src_ref, dst_ref, count_ref, block_ref, own_ref = refs[:5]
-    ghosts, refs = refs[5 : 5 + colours], refs[5 + colours :]
+    )(order, *[in_vmem(x) for x in operands])
+
+
+def product_kernel(colours, with_rows, order_ref, own_ref, *refs):
+    ghosts, refs = refs[:colours], refs[colours:]
     matrix_ref = None
     if ghosts[0].dtype == F32:
         matrix_ref, refs = refs[0], refs[1:]
-    tiles_ref, refs = refs[0], refs[1:]
-    stacked_ref, gram_ref, refs = refs[0], refs[1], refs[2:]
+    tiles_ref, stacked_ref, gram_ref, *refs = refs
     if with_rows:
-        rows_ref, refs = refs[0], refs[1:]
+        rows_ref, *refs = refs
     source, total = refs
-    columns, states = block_ref.shape
-    tile_size = tiles_ref.shape[1]
-    first = states // tile_size
-    live = count_ref[0]
-
-    source[:, :states] = block_ref[...]
+    columns, states = stacked_ref.shape[0] // 3, stacked_ref.shape[1]
+    rest = order_ref.shape[0] // 4
+
     width = ghosts[0].shape[1]
     for n, ghost in enumerate(ghosts):
-        at = states + (len(ghosts) - 1 - n) * width
+        at = (len(ghosts) - 1 - n) * width
         value = ghost[...]
         if matrix_ref is not None:
             value = applied(matrix_ref[...], stack3(value)).astype(BF16)
         source[:, at : at + width] = value
-    at = states + len(ghosts) * width
-    source[:, at:] = jnp.zeros((columns, tile_size), BF16)
-    nothing = at // tile_size
     total[...] = own_ref[...]
-
-    def tile_at(s):
-        index = jnp.where(s < live, src_ref[s], nothing)
-        return source[:, pl.ds(pl.multiple_of(index * tile_size, tile_size), tile_size)]
-
-    zero = jnp.zeros((columns, tile_size), BF16)
-
-    def body(i, carry):
-        base = first + i * group
-        terms = []
-        for u in range(0, group, 2):
-            pair = jnp.concatenate(
-                [
-                    jnp.concatenate([tile_at(base + u), zero], axis=1),
-                    jnp.concatenate([zero, tile_at(base + u + 1)], axis=1),
-                ],
-                axis=0,
-            )
-            weights = tiles_ref[pl.ds(base + u - first, 2)].reshape(2 * tile_size, tile_size)
-            both = jnp.dot(pair, weights, preferred_element_type=F32)
-            terms += [both[:columns], both[columns:]]
-        for u in range(group):
-            where = pl.multiple_of(dst_ref[base + u] * tile_size, tile_size)
-            total[:, pl.ds(where, tile_size)] += terms[u]
-        return carry
-
-    lax.fori_loop(0, (live - first + group - 1) // group, body, 0)
+    add_slots(order_ref, order_ref[3 * rest], order_ref[3 * rest + 1], source, tiles_ref, total)
 
     gram = jnp.zeros((3 * columns, 3 * columns), F32)
     for c in range(0, states, CHUNK):
@@ -357,27 +409,27 @@
         transposed_into(total, rows_ref)
 
 
-def product(src, dst, count, block, own, ghosts, matrix, tiles, with_rows):
-    columns, states = block.shape
-    rest, tile_size, _ = tiles.shape
-    group = 64
-    while rest % group:
-        group //= 2
-    outs = [vmem_out((3 * columns, states), BF16), vmem_out((columns * columns // LANES, LANES), F32)]
+def product(order, own, ghosts, matrix, tiles, with_rows):
+    tile_size = tiles.shape[1]
+    columns, states = own.shape[0], own.shape[1] - tile_size
+    outs = [
+        vmem_out((3 * columns, states), BF16),
+        vmem_out((columns * columns // LANES, LANES), F32),
+    ]
     if with_rows:
         outs.append(vmem_out((states // PACK, LANES), F32))
-    operands = [block, own, *ghosts[::-1]] + ([] if matrix is None else [matrix]) + [tiles]
-    width = states + sum(g.shape[1] for g in ghosts) + tile_size
+    operands = [own, *ghosts[::-1]] + ([] if matrix is None else [matrix]) + [tiles]
+    width = sum(g.shape[1] for g in ghosts)
     return pl.pallas_call(
-        functools.partial(product_kernel, len(ghosts), group, with_rows),
+        functools.partial(product_kernel, len(ghosts), with_rows),
         out_shape=outs,
-        in_specs=[SMEM] * 3 + [VMEM] * len(operands),
+        in_specs=[SMEM] + [VMEM] * len(operands),
         out_specs=[VMEM] * len(outs),
-        scratch_shapes=[pltpu.VMEM((columns, width), BF16), pltpu.VMEM((columns, states), F32)],
+        scratch_shapes=[pltpu.VMEM((columns, width), BF16), pltpu.VMEM(own.shape, F32)],
         compiler_params=PARAMS,
         cost_estimate=CHEAP,
         name="product",
-    )(src, dst, count, *[in_vmem(x) for x in operands])
+    )(order, *[in_vmem(x) for x in operands])
 
 
 def final_kernel(total_states, *refs):
@@ -463,12 +515,10 @@
     )
     sent(ghosts, near, picked)
     matrix = None
-    own = first_own(block, own_tiles)
+    own, order = first_own(tile_src, tile_dst, slot_count, block, own_tiles, rest_tiles)
     for turn in range(ITERS):
         last = turn == ITERS - 1
-        stacked, gram, *rows = product(
-            tile_src, tile_dst, slot_count, block, own, ghosts, matrix, rest_tiles, not last
-        )
+        stacked, gram, *rows = product(order, own, ghosts, matrix, rest_tiles, not last)
         for masks_now in rounds[:-1]:
             gram = paired_sum(gram_round(gram, masks_now))
         if last:
@@ -480,7 +530,7 @@
         sent(ghosts, far, picked)
         near_rows, *parts = lax.optimization_barrier((rows[0], *parts))
         sent(ghosts, near, gather_colours(near_rows, *listed[1], len(near)))
-        block, matrix, own = later_own(parts, stacked, own_tiles, total_states)
+        matrix, own = later_own(order, parts, stacked, own_tiles, rest_tiles, total_states)
 
 
 def solution(mesh):

time: 89.3 us -> 91.5 us (1.025)
  starting transfers between devices: 30.3 us -> 33.9 us
  waiting for transfers between devices: 12.5 us -> 9.93 us
    ppermute x30, starting transfers between devices: 30.3 us -> 33.9 us  [swapped(): return lax.ppermute(x, 'dom', [(i, i ^ mask) for i in range(size)])]
    ppermute x30, waiting for transfers between devices: 12.5 us -> 9.93 us  [swapped(): return lax.ppermute(x, 'dom', [(i, i ^ mask) for i in range(size)])]
    pallas_call x2, Pallas kernels: 4.98 us -> 7.21 us  [later_own(): pl.pallas_call(functools.partial(later_own_kernel, total_states), out_sha...]
    pallas_call x4, Pallas kernels: 13.4 us -> 11.9 us  [the longest x3 8.18 us: product(): pl.pallas_call(functools.partial(product_kernel, len(ghosts), with_rows),...]
  transfers between devices with their start and end apart: 30 -> 30, of which waited for: 12 -> 9; matrix products, arithmetic and copies ran while one was open for 0% -> 0% of each run, Pallas kernels for 27% -> 33%
where the time goes in v7:
time: 91.5 us; the launch traced here: 91.8 us
  Pallas kernels  45.8 us (50%)
  starting transfers between devices  33.9 us (37%)
  waiting for transfers between devices  9.93 us (11%)
  between operations  1.1 us (1%)
    ppermute x30, starting transfers between devices, swapped(): return lax.ppermute(x, 'dom', [(i, i ^ mask) for i in range(size)])  33.9 us
    pallas_call x4, Pallas kernels, gather_colours(): pl.pallas_call(gather_kernel, out_shape=[vmem_out((columns, indices // co...  15.3 us
    ppermute x30, waiting for transfers between devices, swapped(): return lax.ppermute(x, 'dom', [(i, i ^ mask) for i in range(size)])  9.93 us
    pallas_call x2, Pallas kernels, start_gather(): pl.pallas_call(functools.partial(start_kernel, count, first, make_rows),...  8.72 us
    pallas_call x3, Pallas kernels, product(): pl.pallas_call(functools.partial(product_kernel, len(ghosts), with_rows),...  8.18 us
    pallas_call x2, Pallas kernels, later_own(): pl.pallas_call(functools.partial(later_own_kernel, total_states), out_sha...  7.21 us
    pallas_call x1, Pallas kernels, first_own(): pl.pallas_call(first_own_kernel, out_shape=[own_shape(block.shape[0], own...  3.69 us
    pallas_call x1, Pallas kernels, final(): pl.pallas_call(functools.partial(final_kernel, total_states), out_shape=j...  2.7 us
  transfers between devices with their start and end apart: 30, of which 9 were waited for; matrix products, arithmetic and copies ran while one was open for 0% of the time, Pallas kernels for 33%

profile of v7, /device:TPU:0, one launch (start us, length us, event | category | flops | bytes accessed | tf_op | source)
XLA Modules:
  0.0 91.8 jit_solution(11088766474962901231)
XLA Ops:
  0.0 0.8 add_select_fusion
  0.8 0.1 slice_reduce_fusion.1
  1.0 5.0 %start_gather.2 = (bf16[32,1536]{1,0:T(8,128)(2,1)S(1)}, bf16[32,1536]{1,0:T(8,128)(2,1)S(1)}, bf16[256,128,128]{2,1,0:T(8,128)(2,1)S(1)}, f32[2048,128]{1,0:T(8,128)S(1)}, bf16[32,8192]{1,0:T(8,128)(2,1)S(1)}) custom-call(s32[3072]{0:T(1024)S(1)} %pad_add_fusion.row_ref, s32[24,128]{1,0:T(8,128)S(1)} %pad_add_fusion.1.part_ref, ...), custom_call_target="tpu_custom_call" | custom-call | bytes 1024 | tf_op jit(solution)/shard_map/start_gather/pallas_call | solution.py:227
  6.0 4.1 %collective-permute-start = (bf16[32,1536]{1,0:T(8,128)(2,1)S(1)}, bf16[32,1536]{1,0:T(8,128)(2,1)S(1)}, u32[]{:S(2)}, u32[]{:S(2)}) collective-permute-start(bf16[32,1536]{1,0:T(8,128)(2,1)S(1)} %get-tuple-element.57), channel_id=1, source_target_pairs={{0,8},{1,9},{2,10},{3,11},{4,12},{5,13},{6,14},{7,15},{8,0},{9,1},... | collective-permute-start | bytes 294920 | tf_op jit(solution)/shard_map/ppermute | solution.py:42
  10.1 1.6 %collective-permute-start.1 = (bf16[32,1536]{1,0:T(8,128)(2,1)S(1)}, bf16[32,1536]{1,0:T(8,128)(2,1)S(1)}, u32[]{:S(2)}, u32[]{:S(2)}) collective-permute-start(bf16[32,1536]{1,0:T(8,128)(2,1)S(1)} %get-tuple-element.58), channel_id=1, source_target_pairs={{0,4},{1,5},{2,6},{3,7},{4,0},{5,1},{6,2},{7,3},{8,12},{9,13},{10,... | collective-permute-start | bytes 294920 | tf_op jit(solution)/shard_map/ppermute | solution.py:42
  11.7 0.0 copy-start
  11.7 0.0 copy-start.1
  11.7 3.7 %start_gather.3 = (bf16[32,1536]{1,0:T(8,128)(2,1)S(1)}, bf16[32,1536]{1,0:T(8,128)(2,1)S(1)}, bf16[64,128,128]{2,1,0:T(8,128)(2,1)S(1)}) custom-call(s32[3072]{0:T(1024)S(1)} %pad_add_fusion.2.row_ref, s32[24,128]{1,0:T(8,128)S(1)} %pad_add_fusion.3.part_ref, f32[2048,128]{1,0:T(8,128)S(1)} %get-tuple-element.52.source_ref, bf16[320,128,128]{2,1,0:T(8,128)(2,1)} %tiles_ref.3), custom_call_target="tpu_custom_call" | custom-call | bytes 1024 | tf_op jit(solution)/shard_map/start_gather/pallas_call | solution.py:227
  15.4 1.6 %collective-permute-start.2 = (bf16[32,1536]{1,0:T(8,128)(2,1)S(1)}, bf16[32,1536]{1,0:T(8,128)(2,1)S(1)}, u32[]{:S(2)}, u32[]{:S(2)}) collective-permute-start(bf16[32,1536]{1,0:T(8,128)(2,1)S(1)} %get-tuple-element.59), channel_id=1, source_target_pairs={{0,2},{1,3},{2,0},{3,1},{4,6},{5,7},{6,4},{7,5},{8,10},{9,11},{10,... | collective-permute-start | bytes 294920 | tf_op jit(solution)/shard_map/ppermute | solution.py:42
  17.0 0.0 collective-permute-start.3
  17.7 3.7 %first_own.1 = (f32[32,8320]{1,0:T(8,128)S(1)}, s32[1024]{0:T(1024)S(1)}) custom-call(s32[320]{0:T(512)S(1)} %copy-done, s32[320]{0:T(512)S(1)} %copy-done.1, s32[1]{0:T(128)S(6)} %copy.7.count_ref, bf16[32,8192]{1,0:T(8,128)(2,1)S(1)} %get-tuple-element.51.block_ref, bf16[64,128,128]{2,1,0:T(8,128)(2,1)S(1)} %get-tuple-element.53.own_tiles.refs_5_, ...), custom_call_target="tpu_custom_call" | custom-call | bytes 1024 | tf_op jit(solution)/shard_map/first_own/pallas_call | solution.py:334
  21.4 0.0 collective-permute-done.refs_0_
  21.4 0.0 collective-permute-done.2.refs_2_
  21.4 0.0 collective-permute-done.3.refs_3_
  21.4 2.4 %product.3 = (bf16[96,8192]{1,0:T(8,128)(2,1)S(1)}, f32[8,128]{1,0:T(8,128)S(1)}, f32[2048,128]{1,0:T(8,128)S(1)}) custom-call(s32[1024]{0:T(1024)S(1)} %get-tuple-element.55.order_ref, f32[32,8320]{1,0:T(8,128)S(1)} %get-tuple-element.56.own_ref, bf16[32,1536]{1,0:T(8,128)(2,1)S(1)} %collective-permute-done.refs_0_, ...), custom_call_target="tpu_custom_call" | custom-call | bytes 1024 | tf_op jit(solution)/shard_map/product/pallas_call | solution.py:423
  23.9 0.1 collective-permute-start.6
  24.0 1.3 %collective-permute-start.5 = (f32[8,128]{1,0:T(8,128)S(1)}, f32[8,128]{1,0:T(8,128)S(1)}, u32[]{:S(2)}, u32[]{:S(2)}) collective-permute-start(f32[8,128]{1,0:T(8,128)S(1)} %get-tuple-element.62), channel_id=1, source_target_pairs={{0,8},{1,9},{2,10},{3,11},{4,12},{5,13},{6,14},{7,15},{8,0},{9,1},... | collective-permute-start | bytes 12296 | tf_op jit(solution)/shard_map/ppermute | solution.py:42
  25.3 3.1 %collective-permute-start.4 = (f32[8,128]{1,0:T(8,128)S(1)}, f32[8,128]{1,0:T(8,128)S(1)}, u32[]{:S(2)}, u32[]{:S(2)}) collective-permute-start(f32[8,128]{1,0:T(8,128)S(1)} %get-tuple-element.62), channel_id=1, source_target_pairs={{0,4},{1,5},{2,6},{3,7},{4,0},{5,1},{6,2},{7,3},{8,12},{9,13},{10,... | collective-permute-start | bytes 12296 | tf_op jit(solution)/shard_map/ppermute | solution.py:42
  28.4 3.8 %gather_rows.4 = (f32[32,1536]{1,0:T(8,128)S(1)}, f32[32,1536]{1,0:T(8,128)S(1)}) custom-call(s32[3072]{0:T(1024)S(1)} %pad_add_fusion.row_ref, s32[24,128]{1,0:T(8,128)S(1)} %pad_add_fusion.1.part_ref, f32[2048,128]{1,0:T(8,128)S(1)} %get-tuple-element.74.rows_ref), custom_call_target="tpu_custom_call" | custom-call | bytes 1024 | tf_op jit(solution)/shard_map/gather_rows/pallas_call | solution.py:177
  32.2 0.0 collective-permute-done.5
  32.2 0.0 collective-permute-done.4
  32.2 3.6 %collective-permute-start.9 = (f32[8,128]{1,0:T(8,128)S(1)}, f32[8,128]{1,0:T(8,128)S(1)}, u32[]{:S(2)}, u32[]{:S(2)}) collective-permute-start(f32[8,128]{1,0:T(8,128)S(1)} %add_add_fusion.2.refs_0_), channel_id=1, source_target_pairs={{0,3},{1,2},{2,1},{3,0},{4,7},{5,6},{6,5},{7,4},{8,11},{9,10},{10,... | collective-permute-start | bytes 12296 | tf_op jit(solution)/shard_map/ppermute | solution.py:42
  35.8 0.0 collective-permute-start.8
  35.8 0.2 collective-permute-start.7
  36.0 0.3 collective-permute-start.10
  36.3 0.6 collective-permute-start.11
  36.9 0.2 collective-permute-done.9.refs_3_
  37.1 2.3 %collective-permute-done.8.refs_2_ = f32[8,128]{1,0:T(8,128)S(1)} collective-permute-done((f32[8,128]{1,0:T(8,128)S(1)}, f32[8,128]{1,0:T(8,128)S(1)}, u32[]{:S(2)}, u32[]{:S(2)}) %collective-permute-start.8) | collective-permute-done | bytes 4128 | tf_op jit(solution)/shard_map/ppermute | solution.py:42
  39.4 3.8 %gather_rows.5 = (f32[32,1536]{1,0:T(8,128)S(1)}, f32[32,1536]{1,0:T(8,128)S(1)}) custom-call(s32[3072]{0:T(1024)S(1)} %pad_add_fusion.2.row_ref, s32[24,128]{1,0:T(8,128)S(1)} %pad_add_fusion.3.part_ref, f32[2048,128]{1,0:T(8,128)S(1)} %get-tuple-element.74.rows_ref), custom_call_target="tpu_custom_call" | custom-call | bytes 1024 | tf_op jit(solution)/shard_map/gather_rows/pallas_call | solution.py:177
  43.2 0.1 collective-permute-start.12
  43.4 0.0 collective-permute-start.13
  43.4 3.6 %later_own.2 = (bf16[96,96]{1,0:T(8,128)(2,1)S(1)}, f32[32,8320]{1,0:T(8,128)S(1)}) custom-call(s32[1024]{0:T(1024)S(1)} %get-tuple-element.55.order_ref, f32[8,128]{1,0:T(8,128)S(1)} %add_add_fusion.2.refs_0_, f32[8,128]{1,0:T(8,128)S(1)} %collective-permute-done.7.refs_1_, f32[8,128]{1,0:T(8,128)S(1)} %collective-permute-done.8.refs_2_, ...), custom_call_target="tpu_custom_call" | custom-call | bytes 1024 | tf_op jit(solution)/shard_map/later_own/pallas_call | solution.py:361
  47.0 0.9 %collective-permute-done.10.refs_0_ = f32[32,1536]{1,0:T(8,128)S(1)} collective-permute-done((f32[32,1536]{1,0:T(8,128)S(1)}, f32[32,1536]{1,0:T(8,128)S(1)}, u32[]{:S(2)}, u32[]{:S(2)}) %collective-permute-start.10) | collective-permute-done | bytes 196640 | tf_op jit(solution)/shard_map/ppermute | solution.py:42
  47.9 1.0 %collective-permute-done.12.refs_2_ = f32[32,1536]{1,0:T(8,128)S(1)} collective-permute-done((f32[32,1536]{1,0:T(8,128)S(1)}, f32[32,1536]{1,0:T(8,128)S(1)}, u32[]{:S(2)}, u32[]{:S(2)}) %collective-permute-start.12) | collective-permute-done | bytes 196640 | tf_op jit(solution)/shard_map/ppermute | solution.py:42
  49.0 0.0 collective-permute-done.13.refs_3_
  49.0 3.0 %product.4 = (bf16[96,8192]{1,0:T(8,128)(2,1)S(1)}, f32[8,128]{1,0:T(8,128)S(1)}, f32[2048,128]{1,0:T(8,128)S(1)}) custom-call(s32[1024]{0:T(1024)S(1)} %get-tuple-element.55.order_ref, f32[32,8320]{1,0:T(8,128)S(1)} %get-tuple-element.71.own_ref, f32[32,1536]{1,0:T(8,128)S(1)} %collective-permute-done.10.refs_0_, ...), custom_call_target="tpu_custom_call" | custom-call | bytes 1024 | tf_op jit(solution)/shard_map/product/pallas_call | solution.py:423
  52.0 2.4 %collective-permute-start.16 = (f32[8,128]{1,0:T(8,128)S(1)}, f32[8,128]{1,0:T(8,128)S(1)}, u32[]{:S(2)}, u32[]{:S(2)}) collective-permute-start(f32[8,128]{1,0:T(8,128)S(1)} %get-tuple-element.79), channel_id=1, source_target_pairs={{0,12},{1,13},{2,14},{3,15},{4,8},{5,9},{6,10},{7,11},{8,4},{9,5},... | collective-permute-start | bytes 12296 | tf_op jit(solution)/shard_map/ppermute | solution.py:42
  54.4 0.0 collective-permute-start.15
  54.4 2.1 %collective-permute-start.14 = (f32[8,128]{1,0:T(8,128)S(1)}, f32[8,128]{1,0:T(8,128)S(1)}, u32[]{:S(2)}, u32[]{:S(2)}) collective-permute-start(f32[8,128]{1,0:T(8,128)S(1)} %get-tuple-element.79), channel_id=1, source_target_pairs={{0,4},{1,5},{2,6},{3,7},{4,0},{5,1},{6,2},{7,3},{8,12},{9,13},{10,... | collective-permute-start | bytes 12296 | tf_op jit(solution)/shard_map/ppermute | solution.py:42
  56.4 3.8 %gather_rows.6 = (f32[32,1536]{1,0:T(8,128)S(1)}, f32[32,1536]{1,0:T(8,128)S(1)}) custom-call(s32[3072]{0:T(1024)S(1)} %pad_add_fusion.row_ref, s32[24,128]{1,0:T(8,128)S(1)} %pad_add_fusion.1.part_ref, f32[2048,128]{1,0:T(8,128)S(1)} %get-tuple-element.91.rows_ref), custom_call_target="tpu_custom_call" | custom-call | bytes 1024 | tf_op jit(solution)/shard_map/gather_rows/pallas_call | solution.py:177
  60.3 0.0 collective-permute-done.16
  60.3 1.0 %collective-permute-start.19 = (f32[8,128]{1,0:T(8,128)S(1)}, f32[8,128]{1,0:T(8,128)S(1)}, u32[]{:S(2)}, u32[]{:S(2)}) collective-permute-start(f32[8,128]{1,0:T(8,128)S(1)} %add_add_fusion.1.refs_0_), channel_id=1, source_target_pairs={{0,3},{1,2},{2,1},{3,0},{4,7},{5,6},{6,5},{7,4},{8,11},{9,10},{10,... | collective-permute-start | bytes 12296 | tf_op jit(solution)/shard_map/ppermute | solution.py:42
  61.3 0.3 collective-permute-start.18
  61.6 0.6 collective-permute-start.17
  62.2 0.9 collective-permute-start.20
  63.1 2.0 %collective-permute-start.21 = (f32[32,1536]{1,0:T(8,128)S(1)}, f32[32,1536]{1,0:T(8,128)S(1)}, u32[]{:S(2)}, u32[]{:S(2)}) collective-permute-start(f32[32,1536]{1,0:T(8,128)S(1)} %get-tuple-element.90), channel_id=1, source_target_pairs={{0,4},{1,5},{2,6},{3,7},{4,0},{5,1},{6,2},{7,3},{8,12},{9,13},{10,... | collective-permute-start | bytes 589832 | tf_op jit(solution)/shard_map/ppermute | solution.py:42
  65.1 0.0 collective-permute-done.19.refs_3_
  65.2 3.8 %gather_rows.7 = (f32[32,1536]{1,0:T(8,128)S(1)}, f32[32,1536]{1,0:T(8,128)S(1)}) custom-call(s32[3072]{0:T(1024)S(1)} %pad_add_fusion.2.row_ref, s32[24,128]{1,0:T(8,128)S(1)} %pad_add_fusion.3.part_ref, f32[2048,128]{1,0:T(8,128)S(1)} %get-tuple-element.91.rows_ref), custom_call_target="tpu_custom_call" | custom-call | bytes 1024 | tf_op jit(solution)/shard_map/gather_rows/pallas_call | solution.py:177
  69.0 1.8 %collective-permute-start.22 = (f32[32,1536]{1,0:T(8,128)S(1)}, f32[32,1536]{1,0:T(8,128)S(1)}, u32[]{:S(2)}, u32[]{:S(2)}) collective-permute-start(f32[32,1536]{1,0:T(8,128)S(1)} %get-tuple-element.92), channel_id=1, source_target_pairs={{0,2},{1,3},{2,0},{3,1},{4,6},{5,7},{6,4},{7,5},{8,10},{9,11},{10,... | collective-permute-start | bytes 589832 | tf_op jit(solution)/shard_map/ppermute | solution.py:42
  70.8 3.6 %later_own.3 = (bf16[96,96]{1,0:T(8,128)(2,1)S(1)}, f32[32,8320]{1,0:T(8,128)S(1)}) custom-call(s32[1024]{0:T(1024)S(1)} %get-tuple-element.55.order_ref, f32[8,128]{1,0:T(8,128)S(1)} %add_add_fusion.1.refs_0_, f32[8,128]{1,0:T(8,128)S(1)} %collective-permute-done.17.refs_1_, f32[8,128]{1,0:T(8,128)S(1)} %collective-permute-done.18.refs_2_, ...), custom_call_target="tpu_custom_call" | custom-call | bytes 1024 | tf_op jit(solution)/shard_map/later_own/pallas_call | solution.py:361
  74.4 0.0 collective-permute-done.20.refs_0_
  74.4 0.0 collective-permute-done.21.refs_1_
  74.4 1.3 %collective-permute-done.22.refs_2_ = f32[32,1536]{1,0:T(8,128)S(1)} collective-permute-done((f32[32,1536]{1,0:T(8,128)S(1)}, f32[32,1536]{1,0:T(8,128)S(1)}, u32[]{:S(2)}, u32[]{:S(2)}) %collective-permute-start.22) | collective-permute-done | bytes 196640 | tf_op jit(solution)/shard_map/ppermute | solution.py:42
  75.8 2.8 %product.5 = (bf16[96,8192]{1,0:T(8,128)(2,1)S(1)}, f32[8,128]{1,0:T(8,128)S(1)}) custom-call(s32[1024]{0:T(1024)S(1)} %get-tuple-element.55.order_ref, f32[32,8320]{1,0:T(8,128)S(1)} %get-tuple-element.88.own_ref, f32[32,1536]{1,0:T(8,128)S(1)} %collective-permute-done.20.refs_0_, f32[32,1536]{1,0:T(8,128)S(1)} %collective-permute-done.21.refs_1_, ...), custom_call_target="tpu_custom_call" | custom-call | bytes 1024 | tf_op jit(solution)/shard_map/product/pallas_call | solution.py:423
  78.5 2.1 %collective-permute-start.26 = (f32[8,128]{1,0:T(8,128)S(1)}, f32[8,128]{1,0:T(8,128)S(1)}, u32[]{:S(2)}, u32[]{:S(2)}) collective-permute-start(f32[8,128]{1,0:T(8,128)S(1)} %get-tuple-element.95), channel_id=1, source_target_pairs={{0,12},{1,13},{2,14},{3,15},{4,8},{5,9},{6,10},{7,11},{8,4},{9,5},... | collective-permute-start | bytes 12296 | tf_op jit(solution)/shard_map/ppermute | solution.py:42
  80.7 2.3 %collective-permute-start.24 = (f32[8,128]{1,0:T(8,128)S(1)}, f32[8,128]{1,0:T(8,128)S(1)}, u32[]{:S(2)}, u32[]{:S(2)}) collective-permute-start(f32[8,128]{1,0:T(8,128)S(1)} %get-tuple-element.95), channel_id=1, source_target_pairs={{0,4},{1,5},{2,6},{3,7},{4,0},{5,1},{6,2},{7,3},{8,12},{9,13},{10,... | collective-permute-start | bytes 12296 | tf_op jit(solution)/shard_map/ppermute | solution.py:42
  82.9 1.0 %collective-permute-done.26 = f32[8,128]{1,0:T(8,128)S(1)} collective-permute-done((f32[8,128]{1,0:T(8,128)S(1)}, f32[8,128]{1,0:T(8,128)S(1)}, u32[]{:S(2)}, u32[]{:S(2)}) %collective-permute-start.26) | collective-permute-done | bytes 4128 | tf_op jit(solution)/shard_map/ppermute | solution.py:42
  83.9 1.2 %collective-permute-done.25 = f32[8,128]{1,0:T(8,128)S(1)} collective-permute-done((f32[8,128]{1,0:T(8,128)S(1)}, f32[8,128]{1,0:T(8,128)S(1)}, u32[]{:S(2)}, u32[]{:S(2)}) %collective-permute-start.25) | collective-permute-done | bytes 4128 | tf_op jit(solution)/shard_map/ppermute | solution.py:42
  85.2 0.1 collective-permute-start.29
  85.3 0.7 collective-permute-start.28
  86.0 1.1 %collective-permute-start.27 = (f32[8,128]{1,0:T(8,128)S(1)}, f32[8,128]{1,0:T(8,128)S(1)}, u32[]{:S(2)}, u32[]{:S(2)}) collective-permute-start(f32[8,128]{1,0:T(8,128)S(1)} %add_add_fusion.refs_0_), channel_id=1, source_target_pairs={{0,1},{1,0},{2,3},{3,2},{4,5},{5,4},{6,7},{7,6},{8,9},{9,8},{10,11... | collective-permute-start | bytes 12296 | tf_op jit(solution)/shard_map/ppermute | solution.py:42
  87.1 1.2 %collective-permute-done.29.refs_3_ = f32[8,128]{1,0:T(8,128)S(1)} collective-permute-done((f32[8,128]{1,0:T(8,128)S(1)}, f32[8,128]{1,0:T(8,128)S(1)}, u32[]{:S(2)}, u32[]{:S(2)}) %collective-permute-start.29) | collective-permute-done | bytes 4128 | tf_op jit(solution)/shard_map/ppermute | solution.py:42
  88.3 0.7 collective-permute-done.28.refs_2_
  88.9 2.7 %final.1 = f32[32,8192]{1,0:T(8,128)} custom-call(f32[8,128]{1,0:T(8,128)S(1)} %add_add_fusion.refs_0_, f32[8,128]{1,0:T(8,128)S(1)} %collective-permute-done.27.refs_1_, f32[8,128]{1,0:T(8,128)S(1)} %collective-permute-done.28.refs_2_, f32[8,128]{1,0:T(8,128)S(1)} %collective-permute-done.29.refs_3_, bf16[96,8192]{1,0:T(8,128)(2,1)S(1)} %get-tuple-element.96.refs_4_), custom_call_target="tpu_custom_call" | custom-call | bytes 1024 | tf_op jit(solution)/shard_map/final/pallas_call | solution.py:450
  (22 shorter events, 0.1 us)
Async XLA Ops:
  6.0 15.4 %collective-permute-start = (bf16[32,1536]{1,0:T(8,128)(2,1)S(1)}, bf16[32,1536]{1,0:T(8,128)(2,1)S(1)}, u32[]{:S(2)}, u32[]{:S(2)}) collective-permute-start(bf16[32,1536]{1,0:T(8,128)(2,1)S(1)} %get-tuple-element.57), channel_id=1, source_target_pairs={{0,8},{1,9},{2,10},{3,11},{4,12},{5,13},{6,14},{7,15},{8,0},{9,1},... | collective-permute-start | bytes 294920 | tf_op jit(solution)/shard_map/ppermute | solution.py:42
  10.1 11.3 %collective-permute-start.1 = (bf16[32,1536]{1,0:T(8,128)(2,1)S(1)}, bf16[32,1536]{1,0:T(8,128)(2,1)S(1)}, u32[]{:S(2)}, u32[]{:S(2)}) collective-permute-start(bf16[32,1536]{1,0:T(8,128)(2,1)S(1)} %get-tuple-element.58), channel_id=1, source_target_pairs={{0,4},{1,5},{2,6},{3,7},{4,0},{5,1},{6,2},{7,3},{8,12},{9,13},{10,... | collective-permute-start | bytes 294920 | tf_op jit(solution)/shard_map/ppermute | solution.py:42
  11.7 6.0 %copy-start = (s32[320]{0:T(512)S(1)}, s32[320]{0:T(512)}, u32[]{:S(2)}) copy-start(s32[320]{0:T(512)} %src_ref.1) | copy-start | bytes 3844
  11.7 6.0 %copy-start.1 = (s32[320]{0:T(512)S(1)}, s32[320]{0:T(512)}, u32[]{:S(2)}) copy-start(s32[320]{0:T(512)} %dst_ref.1) | copy-start | bytes 3844
  15.4 6.0 %collective-permute-start.2 = (bf16[32,1536]{1,0:T(8,128)(2,1)S(1)}, bf16[32,1536]{1,0:T(8,128)(2,1)S(1)}, u32[]{:S(2)}, u32[]{:S(2)}) collective-permute-start(bf16[32,1536]{1,0:T(8,128)(2,1)S(1)} %get-tuple-element.59), channel_id=1, source_target_pairs={{0,2},{1,3},{2,0},{3,1},{4,6},{5,7},{6,4},{7,5},{8,10},{9,11},{10,... | collective-permute-start | bytes 294920 | tf_op jit(solution)/shard_map/ppermute | solution.py:42
  17.0 4.4 %collective-permute-start.3 = (bf16[32,1536]{1,0:T(8,128)(2,1)S(1)}, bf16[32,1536]{1,0:T(8,128)(2,1)S(1)}, u32[]{:S(2)}, u32[]{:S(2)}) collective-permute-start(bf16[32,1536]{1,0:T(8,128)(2,1)S(1)} %get-tuple-element.60), channel_id=1, source_target_pairs={{0,1},{1,0},{2,3},{3,2},{4,5},{5,4},{6,7},{7,6},{8,9},{9,8},{10,11... | collective-permute-start | bytes 294920 | tf_op jit(solution)/shard_map/ppermute | solution.py:42
  23.9 8.3 %collective-permute-start.6 = (f32[8,128]{1,0:T(8,128)S(1)}, f32[8,128]{1,0:T(8,128)S(1)}, u32[]{:S(2)}, u32[]{:S(2)}) collective-permute-start(f32[8,128]{1,0:T(8,128)S(1)} %get-tuple-element.62), channel_id=1, source_target_pairs={{0,12},{1,13},{2,14},{3,15},{4,8},{5,9},{6,10},{7,11},{8,4},{9,5},... | collective-permute-start | bytes 12296 | tf_op jit(solution)/shard_map/ppermute | solution.py:42
  24.0 8.2 %collective-permute-start.5 = (f32[8,128]{1,0:T(8,128)S(1)}, f32[8,128]{1,0:T(8,128)S(1)}, u32[]{:S(2)}, u32[]{:S(2)}) collective-permute-start(f32[8,128]{1,0:T(8,128)S(1)} %get-tuple-element.62), channel_id=1, source_target_pairs={{0,8},{1,9},{2,10},{3,11},{4,12},{5,13},{6,14},{7,15},{8,0},{9,1},... | collective-permute-start | bytes 12296 | tf_op jit(solution)/shard_map/ppermute | solution.py:42
  25.3 6.9 %collective-permute-start.4 = (f32[8,128]{1,0:T(8,128)S(1)}, f32[8,128]{1,0:T(8,128)S(1)}, u32[]{:S(2)}, u32[]{:S(2)}) collective-permute-start(f32[8,128]{1,0:T(8,128)S(1)} %get-tuple-element.62), channel_id=1, source_target_pairs={{0,4},{1,5},{2,6},{3,7},{4,0},{5,1},{6,2},{7,3},{8,12},{9,13},{10,... | collective-permute-start | bytes 12296 | tf_op jit(solution)/shard_map/ppermute | solution.py:42
  32.2 4.9 %collective-permute-start.9 = (f32[8,128]{1,0:T(8,128)S(1)}, f32[8,128]{1,0:T(8,128)S(1)}, u32[]{:S(2)}, u32[]{:S(2)}) collective-permute-start(f32[8,128]{1,0:T(8,128)S(1)} %add_add_fusion.2.refs_0_), channel_id=1, source_target_pairs={{0,3},{1,2},{2,1},{3,0},{4,7},{5,6},{6,5},{7,4},{8,11},{9,10},{10,... | collective-permute-start | bytes 12296 | tf_op jit(solution)/shard_map/ppermute | solution.py:42
  35.8 3.6 %collective-permute-start.8 = (f32[8,128]{1,0:T(8,128)S(1)}, f32[8,128]{1,0:T(8,128)S(1)}, u32[]{:S(2)}, u32[]{:S(2)}) collective-permute-start(f32[8,128]{1,0:T(8,128)S(1)} %add_add_fusion.2.refs_0_), channel_id=1, source_target_pairs={{0,2},{1,3},{2,0},{3,1},{4,6},{5,7},{6,4},{7,5},{8,10},{9,11},{10,... | collective-permute-start | bytes 12296 | tf_op jit(solution)/shard_map/ppermute | solution.py:42
  35.8 3.6 %collective-permute-start.7 = (f32[8,128]{1,0:T(8,128)S(1)}, f32[8,128]{1,0:T(8,128)S(1)}, u32[]{:S(2)}, u32[]{:S(2)}) collective-permute-start(f32[8,128]{1,0:T(8,128)S(1)} %add_add_fusion.2.refs_0_), channel_id=1, source_target_pairs={{0,1},{1,0},{2,3},{3,2},{4,5},{5,4},{6,7},{7,6},{8,9},{9,8},{10,11... | collective-permute-start | bytes 12296 | tf_op jit(solution)/shard_map/ppermute | solution.py:42
  36.0 12.0 %collective-permute-start.10 = (f32[32,1536]{1,0:T(8,128)S(1)}, f32[32,1536]{1,0:T(8,128)S(1)}, u32[]{:S(2)}, u32[]{:S(2)}) collective-permute-start(f32[32,1536]{1,0:T(8,128)S(1)} %get-tuple-element.72), channel_id=1, source_target_pairs={{0,8},{1,9},{2,10},{3,11},{4,12},{5,13},{6,14},{7,15},{8,0},{9,1},... | collective-permute-start | bytes 589832 | tf_op jit(solution)/shard_map/ppermute | solution.py:42
  36.3 11.7 %collective-permute-start.11 = (f32[32,1536]{1,0:T(8,128)S(1)}, f32[32,1536]{1,0:T(8,128)S(1)}, u32[]{:S(2)}, u32[]{:S(2)}) collective-permute-start(f32[32,1536]{1,0:T(8,128)S(1)} %get-tuple-element.73), channel_id=1, source_target_pairs={{0,4},{1,5},{2,6},{3,7},{4,0},{5,1},{6,2},{7,3},{8,12},{9,13},{10,... | collective-permute-start | bytes 589832 | tf_op jit(solution)/shard_map/ppermute | solution.py:42
  43.2 5.7 %collective-permute-start.12 = (f32[32,1536]{1,0:T(8,128)S(1)}, f32[32,1536]{1,0:T(8,128)S(1)}, u32[]{:S(2)}, u32[]{:S(2)}) collective-permute-start(f32[32,1536]{1,0:T(8,128)S(1)} %get-tuple-element.75), channel_id=1, source_target_pairs={{0,2},{1,3},{2,0},{3,1},{4,6},{5,7},{6,4},{7,5},{8,10},{9,11},{10,... | collective-permute-start | bytes 589832 | tf_op jit(solution)/shard_map/ppermute | solution.py:42
  43.4 5.6 %collective-permute-start.13 = (f32[32,1536]{1,0:T(8,128)S(1)}, f32[32,1536]{1,0:T(8,128)S(1)}, u32[]{:S(2)}, u32[]{:S(2)}) collective-permute-start(f32[32,1536]{1,0:T(8,128)S(1)} %get-tuple-element.76), channel_id=1, source_target_pairs={{0,1},{1,0},{2,3},{3,2},{4,5},{5,4},{6,7},{7,6},{8,9},{9,8},{10,11... | collective-permute-start | bytes 589832 | tf_op jit(solution)/shard_map/ppermute | solution.py:42
  52.0 8.3 %collective-permute-start.16 = (f32[8,128]{1,0:T(8,128)S(1)}, f32[8,128]{1,0:T(8,128)S(1)}, u32[]{:S(2)}, u32[]{:S(2)}) collective-permute-start(f32[8,128]{1,0:T(8,128)S(1)} %get-tuple-element.79), channel_id=1, source_target_pairs={{0,12},{1,13},{2,14},{3,15},{4,8},{5,9},{6,10},{7,11},{8,4},{9,5},... | collective-permute-start | bytes 12296 | tf_op jit(solution)/shard_map/ppermute | solution.py:42
  54.4 5.9 %collective-permute-start.15 = (f32[8,128]{1,0:T(8,128)S(1)}, f32[8,128]{1,0:T(8,128)S(1)}, u32[]{:S(2)}, u32[]{:S(2)}) collective-permute-start(f32[8,128]{1,0:T(8,128)S(1)} %get-tuple-element.79), channel_id=1, source_target_pairs={{0,8},{1,9},{2,10},{3,11},{4,12},{5,13},{6,14},{7,15},{8,0},{9,1},... | collective-permute-start | bytes 12296 | tf_op jit(solution)/shard_map/ppermute | solution.py:42
  54.4 5.9 %collective-permute-start.14 = (f32[8,128]{1,0:T(8,128)S(1)}, f32[8,128]{1,0:T(8,128)S(1)}, u32[]{:S(2)}, u32[]{:S(2)}) collective-permute-start(f32[8,128]{1,0:T(8,128)S(1)} %get-tuple-element.79), channel_id=1, source_target_pairs={{0,4},{1,5},{2,6},{3,7},{4,0},{5,1},{6,2},{7,3},{8,12},{9,13},{10,... | collective-permute-start | bytes 12296 | tf_op jit(solution)/shard_map/ppermute | solution.py:42
  60.3 4.8 %collective-permute-start.19 = (f32[8,128]{1,0:T(8,128)S(1)}, f32[8,128]{1,0:T(8,128)S(1)}, u32[]{:S(2)}, u32[]{:S(2)}) collective-permute-start(f32[8,128]{1,0:T(8,128)S(1)} %add_add_fusion.1.refs_0_), channel_id=1, source_target_pairs={{0,3},{1,2},{2,1},{3,0},{4,7},{5,6},{6,5},{7,4},{8,11},{9,10},{10,... | collective-permute-start | bytes 12296 | tf_op jit(solution)/shard_map/ppermute | solution.py:42
  61.3 3.9 %collective-permute-start.18 = (f32[8,128]{1,0:T(8,128)S(1)}, f32[8,128]{1,0:T(8,128)S(1)}, u32[]{:S(2)}, u32[]{:S(2)}) collective-permute-start(f32[8,128]{1,0:T(8,128)S(1)} %add_add_fusion.1.refs_0_), channel_id=1, source_target_pairs={{0,2},{1,3},{2,0},{3,1},{4,6},{5,7},{6,4},{7,5},{8,10},{9,11},{10,... | collective-permute-start | bytes 12296 | tf_op jit(solution)/shard_map/ppermute | solution.py:42
  61.6 3.5 %collective-permute-start.17 = (f32[8,128]{1,0:T(8,128)S(1)}, f32[8,128]{1,0:T(8,128)S(1)}, u32[]{:S(2)}, u32[]{:S(2)}) collective-permute-start(f32[8,128]{1,0:T(8,128)S(1)} %add_add_fusion.1.refs_0_), channel_id=1, source_target_pairs={{0,1},{1,0},{2,3},{3,2},{4,5},{5,4},{6,7},{7,6},{8,9},{9,8},{10,11... | collective-permute-start | bytes 12296 | tf_op jit(solution)/shard_map/ppermute | solution.py:42
  62.2 12.2 %collective-permute-start.20 = (f32[32,1536]{1,0:T(8,128)S(1)}, f32[32,1536]{1,0:T(8,128)S(1)}, u32[]{:S(2)}, u32[]{:S(2)}) collective-permute-start(f32[32,1536]{1,0:T(8,128)S(1)} %get-tuple-element.89), channel_id=1, source_target_pairs={{0,8},{1,9},{2,10},{3,11},{4,12},{5,13},{6,14},{7,15},{8,0},{9,1},... | collective-permute-start | bytes 589832 | tf_op jit(solution)/shard_map/ppermute | solution.py:42
  63.1 11.3 %collective-permute-start.21 = (f32[32,1536]{1,0:T(8,128)S(1)}, f32[32,1536]{1,0:T(8,128)S(1)}, u32[]{:S(2)}, u32[]{:S(2)}) collective-permute-start(f32[32,1536]{1,0:T(8,128)S(1)} %get-tuple-element.90), channel_id=1, source_target_pairs={{0,4},{1,5},{2,6},{3,7},{4,0},{5,1},{6,2},{7,3},{8,12},{9,13},{10,... | collective-permute-start | bytes 589832 | tf_op jit(solution)/shard_map/ppermute | solution.py:42
  69.0 6.8 %collective-permute-start.22 = (f32[32,1536]{1,0:T(8,128)S(1)}, f32[32,1536]{1,0:T(8,128)S(1)}, u32[]{:S(2)}, u32[]{:S(2)}) collective-permute-start(f32[32,1536]{1,0:T(8,128)S(1)} %get-tuple-element.92), channel_id=1, source_target_pairs={{0,2},{1,3},{2,0},{3,1},{4,6},{5,7},{6,4},{7,5},{8,10},{9,11},{10,... | collective-permute-start | bytes 589832 | tf_op jit(solution)/shard_map/ppermute | solution.py:42
  70.8 5.0 %collective-permute-start.23 = (f32[32,1536]{1,0:T(8,128)S(1)}, f32[32,1536]{1,0:T(8,128)S(1)}, u32[]{:S(2)}, u32[]{:S(2)}) collective-permute-start(f32[32,1536]{1,0:T(8,128)S(1)} %get-tuple-element.93), channel_id=1, source_target_pairs={{0,1},{1,0},{2,3},{3,2},{4,5},{5,4},{6,7},{7,6},{8,9},{9,8},{10,11... | collective-permute-start | bytes 589832 | tf_op jit(solution)/shard_map/ppermute | solution.py:42
  78.5 5.4 %collective-permute-start.26 = (f32[8,128]{1,0:T(8,128)S(1)}, f32[8,128]{1,0:T(8,128)S(1)}, u32[]{:S(2)}, u32[]{:S(2)}) collective-permute-start(f32[8,128]{1,0:T(8,128)S(1)} %get-tuple-element.95), channel_id=1, source_target_pairs={{0,12},{1,13},{2,14},{3,15},{4,8},{5,9},{6,10},{7,11},{8,4},{9,5},... | collective-permute-start | bytes 12296 | tf_op jit(solution)/shard_map/ppermute | solution.py:42
  80.7 4.5 %collective-permute-start.25 = (f32[8,128]{1,0:T(8,128)S(1)}, f32[8,128]{1,0:T(8,128)S(1)}, u32[]{:S(2)}, u32[]{:S(2)}) collective-permute-start(f32[8,128]{1,0:T(8,128)S(1)} %get-tuple-element.95), channel_id=1, source_target_pairs={{0,8},{1,9},{2,10},{3,11},{4,12},{5,13},{6,14},{7,15},{8,0},{9,1},... | collective-permute-start | bytes 12296 | tf_op jit(solution)/shard_map/ppermute | solution.py:42
  80.7 4.5 %collective-permute-start.24 = (f32[8,128]{1,0:T(8,128)S(1)}, f32[8,128]{1,0:T(8,128)S(1)}, u32[]{:S(2)}, u32[]{:S(2)}) collective-permute-start(f32[8,128]{1,0:T(8,128)S(1)} %get-tuple-element.95), channel_id=1, source_target_pairs={{0,4},{1,5},{2,6},{3,7},{4,0},{5,1},{6,2},{7,3},{8,12},{9,13},{10,... | collective-permute-start | bytes 12296 | tf_op jit(solution)/shard_map/ppermute | solution.py:42
  85.2 3.1 %collective-permute-start.29 = (f32[8,128]{1,0:T(8,128)S(1)}, f32[8,128]{1,0:T(8,128)S(1)}, u32[]{:S(2)}, u32[]{:S(2)}) collective-permute-start(f32[8,128]{1,0:T(8,128)S(1)} %add_add_fusion.refs_0_), channel_id=1, source_target_pairs={{0,3},{1,2},{2,1},{3,0},{4,7},{5,6},{6,5},{7,4},{8,11},{9,10},{10,... | collective-permute-start | bytes 12296 | tf_op jit(solution)/shard_map/ppermute | solution.py:42
  85.3 3.7 %collective-permute-start.28 = (f32[8,128]{1,0:T(8,128)S(1)}, f32[8,128]{1,0:T(8,128)S(1)}, u32[]{:S(2)}, u32[]{:S(2)}) collective-permute-start(f32[8,128]{1,0:T(8,128)S(1)} %add_add_fusion.refs_0_), channel_id=1, source_target_pairs={{0,2},{1,3},{2,0},{3,1},{4,6},{5,7},{6,4},{7,5},{8,10},{9,11},{10,... | collective-permute-start | bytes 12296 | tf_op jit(solution)/shard_map/ppermute | solution.py:42
  86.0 2.9 %collective-permute-start.27 = (f32[8,128]{1,0:T(8,128)S(1)}, f32[8,128]{1,0:T(8,128)S(1)}, u32[]{:S(2)}, u32[]{:S(2)}) collective-permute-start(f32[8,128]{1,0:T(8,128)S(1)} %add_add_fusion.refs_0_), channel_id=1, source_target_pairs={{0,1},{1,0},{2,3},{3,2},{4,5},{5,4},{6,7},{7,6},{8,9},{9,8},{10,11... | collective-permute-start | bytes 12296 | tf_op jit(solution)/shard_map/ppermute | solution.py:42

commit v8 on v6

--- a/solution.py
+++ b/solution.py
@@ -12,8 +12,9 @@
 PACK = 4
 CHUNK = 1024
 SUBLANES = 8
-STEP = 4
+STEP = 8
 COPIES = 8
+GROUP = 128
 F32 = jnp.float32
 BF16 = jnp.bfloat16
 VMEM = pl.BlockSpec(memory_space=pltpu.VMEM)
@@ -131,7 +132,9 @@
 
 
 def gram_of(parts, total_states):
-    return unpacked(paired_sum(parts)) / total_states
+    while len(parts) > 1:
+        parts = [a + b for a, b in zip(parts[::2], parts[1::2])] + parts[len(parts) // 2 * 2 :]
+    return unpacked(parts[0]) / total_states
 
 
 def transposed_into(source, rows_ref):
@@ -352,7 +355,12 @@
     ]
     small = blocks[8] + (blocks[5] + blocks[7])
     middle = blocks[4] + (blocks[2] + blocks[6])
-    gram_ref[...] = packed(blocks[0] + ((blocks[1] + blocks[3]) + (middle + small)))
+    gram = packed(blocks[0] + ((blocks[1] + blocks[3]) + (middle + small)))
+    if with_rows:
+        gram_ref[...] = gram
+    else:
+        for n in range(gram_ref.shape[0]):
+            gram_ref[n] = gram
     if with_rows:
         transposed_into(total, rows_ref)
 
@@ -360,10 +368,13 @@
 def product(src, dst, count, block, own, ghosts, matrix, tiles, with_rows):
     columns, states = block.shape
     rest, tile_size, _ = tiles.shape
-    group = 64
+    group = GROUP
     while rest % group:
         group //= 2
-    outs = [vmem_out((3 * columns, states), BF16), vmem_out((columns * columns // LANES, LANES), F32)]
+    gram_shape = (columns * columns // LANES, LANES)
+    if not with_rows:
+        gram_shape = (lax.axis_size("dom"), *gram_shape)
+    outs = [vmem_out((3 * columns, states), BF16), vmem_out(gram_shape, F32)]
     if with_rows:
         outs.append(vmem_out((states // PACK, LANES), F32))
     operands = [block, own, *ghosts[::-1]] + ([] if matrix is None else [matrix]) + [tiles]
@@ -381,8 +392,9 @@
 
 
 def final_kernel(total_states, *refs):
-    grams, stacked, out_ref, ready, sems = refs[:4], *refs[4:]
-    matrix = apply_matrix(inverse_factor(gram_of([r[...] for r in grams], total_states)))
+    grams, stacked, out_ref, ready, sems = refs
+    parts = [grams[n] for n in range(grams.shape[0])]
+    matrix = apply_matrix(inverse_factor(gram_of(parts, total_states)))
     copies = []
     for n, c in enumerate(range(0, out_ref.shape[1], CHUNK)):
         at = pl.ds(c, CHUNK)
@@ -398,7 +410,7 @@
     return pl.pallas_call(
         functools.partial(final_kernel, total_states),
         out_shape=jax.ShapeDtypeStruct((columns, states), F32),
-        in_specs=[VMEM] * 5,
+        in_specs=[VMEM] * 2,
         out_specs=HBM,
         scratch_shapes=[
             pltpu.VMEM((columns, states), F32),
@@ -407,7 +419,7 @@
         compiler_params=PARAMS,
         cost_estimate=CHEAP,
         name="final",
-    )(*[in_vmem(g) for g in grams], in_vmem(stacked))
+    )(in_vmem(grams), in_vmem(stacked))
 
 
 def dom_rounds(size):
@@ -469,10 +481,10 @@
         stacked, gram, *rows = product(
             tile_src, tile_dst, slot_count, block, own, ghosts, matrix, rest_tiles, not last
         )
+        if last:
+            return final(lax.all_to_all(gram, "dom", 0, 0), stacked, total_states)
         for masks_now in rounds[:-1]:
             gram = paired_sum(gram_round(gram, masks_now))
-        if last:
-            return final(gram_round(gram, rounds[-1]), stacked, total_states)
         ghosts = [None] * len(masks)
         picked = gather_colours(rows[0], *listed[0], len(far))
         gram, *picked = lax.optimization_barrier((gram, *picked))

time: 89.3 us -> 88.6 us (level)
  blocking collectives: 0 us -> 10.4 us
  Pallas kernels: 45.1 us -> 40 us
  starting transfers between devices: 30.3 us -> 27 us
  waiting for transfers between devices: 12.5 us -> 9.56 us
    all_to_all x0 -> x1, blocking collectives: none -> 10.4 us  [on_device(): return final(lax.all_to_all(gram, 'dom', 0, 0), stacked, total_states)]
    pallas_call x3, Pallas kernels: 12.7 us -> 8.9 us  [product(): pl.pallas_call(functools.partial(product_kernel, len(ghosts), group, with...]
    ppermute x30 -> x24, starting transfers between devices: 30.3 us -> 27 us  [swapped(): return lax.ppermute(x, 'dom', [(i, i ^ mask) for i in range(size)])]
    ppermute x30 -> x24, waiting for transfers between devices: 12.5 us -> 9.56 us  [swapped(): return lax.ppermute(x, 'dom', [(i, i ^ mask) for i in range(size)])]
  transfers between devices with their start and end apart: 30 -> 24, of which waited for: 12 -> 7; matrix products, arithmetic and copies ran while one was open for 0% -> 0% of each run, Pallas kernels for 27% -> 27%
where the time goes in v8:
time: 88.6 us; the launch traced here: 89 us
  Pallas kernels  40 us (45%)
  starting transfers between devices  27 us (30%)
  blocking collectives  10.4 us (12%)
  waiting for transfers between devices  9.56 us (11%)
  between operations  1.03 us (1%)
    ppermute x24, starting transfers between devices, swapped(): return lax.ppermute(x, 'dom', [(i, i ^ mask) for i in range(size)])  27 us
    pallas_call x4, Pallas kernels, gather_colours(): pl.pallas_call(gather_kernel, out_shape=[vmem_out((columns, indices // co...  15.3 us
    all_to_all x1, blocking collectives, on_device(): return final(lax.all_to_all(gram, 'dom', 0, 0), stacked, total_states)  10.4 us
    ppermute x24, waiting for transfers between devices, swapped(): return lax.ppermute(x, 'dom', [(i, i ^ mask) for i in range(size)])  9.56 us
    pallas_call x3, Pallas kernels, product(): pl.pallas_call(functools.partial(product_kernel, len(ghosts), group, with...  8.9 us
    pallas_call x2, Pallas kernels, start_gather(): pl.pallas_call(functools.partial(start_kernel, count, first, make_rows),...  8.72 us
    pallas_call x2, Pallas kernels, later_own(): pl.pallas_call(functools.partial(later_own_kernel, total_states), out_sha...  4.15 us
    pallas_call x1, Pallas kernels, final(): pl.pallas_call(functools.partial(final_kernel, total_states), out_shape=j...  2.27 us
  transfers between devices with their start and end apart: 24, of which 7 were waited for; matrix products, arithmetic and copies ran while one was open for 0% of the time, Pallas kernels for 27%

profile of v8, /device:TPU:0, one launch (start us, length us, event | category | flops | bytes accessed | tf_op | source)
XLA Modules:
  0.0 89.0 jit_solution(6798794061054879917)
XLA Ops:
  0.0 0.8 add_select_fusion
  0.8 0.1 slice_reduce_fusion.1
  1.0 5.0 %start_gather.2 = (bf16[32,1536]{1,0:T(8,128)(2,1)S(1)}, bf16[32,1536]{1,0:T(8,128)(2,1)S(1)}, bf16[256,128,128]{2,1,0:T(8,128)(2,1)S(1)}, f32[2048,128]{1,0:T(8,128)S(1)}, bf16[32,8192]{1,0:T(8,128)(2,1)S(1)}) custom-call(s32[3072]{0:T(1024)S(1)} %pad_add_fusion.row_ref, s32[24,128]{1,0:T(8,128)S(1)} %pad_add_fusion.1.part_ref, ...), custom_call_target="tpu_custom_call" | custom-call | bytes 1024 | tf_op jit(solution)/shard_map/start_gather/pallas_call | solution.py:228
  6.0 4.1 %collective-permute-start = (bf16[32,1536]{1,0:T(8,128)(2,1)S(1)}, bf16[32,1536]{1,0:T(8,128)(2,1)S(1)}, u32[]{:S(2)}, u32[]{:S(2)}) collective-permute-start(bf16[32,1536]{1,0:T(8,128)(2,1)S(1)} %get-tuple-element.54), channel_id=1, source_target_pairs={{0,8},{1,9},{2,10},{3,11},{4,12},{5,13},{6,14},{7,15},{8,0},{9,1},... | collective-permute-start | bytes 294920 | tf_op jit(solution)/shard_map/ppermute | solution.py:41
  10.1 1.6 %collective-permute-start.1 = (bf16[32,1536]{1,0:T(8,128)(2,1)S(1)}, bf16[32,1536]{1,0:T(8,128)(2,1)S(1)}, u32[]{:S(2)}, u32[]{:S(2)}) collective-permute-start(bf16[32,1536]{1,0:T(8,128)(2,1)S(1)} %get-tuple-element.55), channel_id=1, source_target_pairs={{0,4},{1,5},{2,6},{3,7},{4,0},{5,1},{6,2},{7,3},{8,12},{9,13},{10,... | collective-permute-start | bytes 294920 | tf_op jit(solution)/shard_map/ppermute | solution.py:41
  11.7 3.7 %start_gather.3 = (bf16[32,1536]{1,0:T(8,128)(2,1)S(1)}, bf16[32,1536]{1,0:T(8,128)(2,1)S(1)}, bf16[64,128,128]{2,1,0:T(8,128)(2,1)S(1)}) custom-call(s32[3072]{0:T(1024)S(1)} %pad_add_fusion.2.row_ref, s32[24,128]{1,0:T(8,128)S(1)} %pad_add_fusion.3.part_ref, f32[2048,128]{1,0:T(8,128)S(1)} %get-tuple-element.52.source_ref, bf16[320,128,128]{2,1,0:T(8,128)(2,1)} %tiles_ref.3), custom_call_target="tpu_custom_call" | custom-call | bytes 1024 | tf_op jit(solution)/shard_map/start_gather/pallas_call | solution.py:228
  15.4 0.0 copy-start
  15.4 0.0 copy-start.1
  15.4 1.6 %collective-permute-start.2 = (bf16[32,1536]{1,0:T(8,128)(2,1)S(1)}, bf16[32,1536]{1,0:T(8,128)(2,1)S(1)}, u32[]{:S(2)}, u32[]{:S(2)}) collective-permute-start(bf16[32,1536]{1,0:T(8,128)(2,1)S(1)} %get-tuple-element.56), channel_id=1, source_target_pairs={{0,2},{1,3},{2,0},{3,1},{4,6},{5,7},{6,4},{7,5},{8,10},{9,11},{10,... | collective-permute-start | bytes 294920 | tf_op jit(solution)/shard_map/ppermute | solution.py:41
  17.0 0.0 collective-permute-start.3
  17.7 0.7 first_own.1.refs_4_
  18.3 0.0 collective-permute-done.refs_5_
  18.3 0.0 collective-permute-done.1.refs_6_
  18.3 1.8 %collective-permute-done.2.refs_7_ = bf16[32,1536]{1,0:T(8,128)(2,1)S(1)} collective-permute-done((bf16[32,1536]{1,0:T(8,128)(2,1)S(1)}, bf16[32,1536]{1,0:T(8,128)(2,1)S(1)}, u32[]{:S(2)}, u32[]{:S(2)}) %collective-permute-start.2) | collective-permute-done | bytes 98336 | tf_op jit(solution)/shard_map/ppermute | solution.py:41
  20.1 0.0 collective-permute-done.3.refs_8_
  20.1 2.7 %product.3 = (bf16[96,8192]{1,0:T(8,128)(2,1)S(1)}, f32[8,128]{1,0:T(8,128)S(1)}, f32[2048,128]{1,0:T(8,128)S(1)}) custom-call(s32[320]{0:T(512)S(1)} %copy-done, s32[320]{0:T(512)S(1)} %copy-done.1, s32[1]{0:T(128)S(6)} %copy.7.refs_2_, bf16[32,8192]{1,0:T(8,128)(2,1)S(1)} %get-tuple-element.51.block_ref.refs_3_, f32[32,8192]{1,0:T(8,128)S(1)} %first_own.1.refs_4_, ...), custom_call_target="tpu_custom_call" | custom-call | bytes 1024 | tf_op jit(solution)/shard_map/product/pallas_call | solution.py:382
  22.8 1.1 %collective-permute-start.6 = (f32[8,128]{1,0:T(8,128)S(1)}, f32[8,128]{1,0:T(8,128)S(1)}, u32[]{:S(2)}, u32[]{:S(2)}) collective-permute-start(f32[8,128]{1,0:T(8,128)S(1)} %get-tuple-element.60), channel_id=1, source_target_pairs={{0,12},{1,13},{2,14},{3,15},{4,8},{5,9},{6,10},{7,11},{8,4},{9,5},... | collective-permute-start | bytes 12296 | tf_op jit(solution)/shard_map/ppermute | solution.py:41
  23.9 0.9 collective-permute-start.5
  24.8 2.5 %collective-permute-start.4 = (f32[8,128]{1,0:T(8,128)S(1)}, f32[8,128]{1,0:T(8,128)S(1)}, u32[]{:S(2)}, u32[]{:S(2)}) collective-permute-start(f32[8,128]{1,0:T(8,128)S(1)} %get-tuple-element.60), channel_id=1, source_target_pairs={{0,4},{1,5},{2,6},{3,7},{4,0},{5,1},{6,2},{7,3},{8,12},{9,13},{10,... | collective-permute-start | bytes 12296 | tf_op jit(solution)/shard_map/ppermute | solution.py:41
  27.3 3.8 %gather_rows.4 = (f32[32,1536]{1,0:T(8,128)S(1)}, f32[32,1536]{1,0:T(8,128)S(1)}) custom-call(s32[3072]{0:T(1024)S(1)} %pad_add_fusion.row_ref, s32[24,128]{1,0:T(8,128)S(1)} %pad_add_fusion.1.part_ref, f32[2048,128]{1,0:T(8,128)S(1)} %get-tuple-element.73.rows_ref), custom_call_target="tpu_custom_call" | custom-call | bytes 1024 | tf_op jit(solution)/shard_map/gather_rows/pallas_call | solution.py:178
  31.1 0.0 collective-permute-done.6
  31.1 0.0 collective-permute-done.5
  31.1 0.0 collective-permute-done.4
  31.2 0.1 collective-permute-start.9
  31.2 1.6 %collective-permute-start.8 = (f32[8,128]{1,0:T(8,128)S(1)}, f32[8,128]{1,0:T(8,128)S(1)}, u32[]{:S(2)}, u32[]{:S(2)}) collective-permute-start(f32[8,128]{1,0:T(8,128)S(1)} %add_add_fusion.1.refs_0_), channel_id=1, source_target_pairs={{0,2},{1,3},{2,0},{3,1},{4,6},{5,7},{6,4},{7,5},{8,10},{9,11},{10,... | collective-permute-start | bytes 12296 | tf_op jit(solution)/shard_map/ppermute | solution.py:41
  32.8 0.3 collective-permute-start.7
  33.1 0.0 collective-permute-start.10
  33.1 1.6 %collective-permute-start.11 = (f32[32,1536]{1,0:T(8,128)S(1)}, f32[32,1536]{1,0:T(8,128)S(1)}, u32[]{:S(2)}, u32[]{:S(2)}) collective-permute-start(f32[32,1536]{1,0:T(8,128)S(1)} %get-tuple-element.72), channel_id=1, source_target_pairs={{0,4},{1,5},{2,6},{3,7},{4,0},{5,1},{6,2},{7,3},{8,12},{9,13},{10,... | collective-permute-start | bytes 589832 | tf_op jit(solution)/shard_map/ppermute | solution.py:41
  34.7 0.0 collective-permute-done.9.refs_3_
  34.7 0.2 collective-permute-done.8.refs_2_
  34.9 0.0 collective-permute-done.7.refs_1_
  34.9 3.8 %gather_rows.5 = (f32[32,1536]{1,0:T(8,128)S(1)}, f32[32,1536]{1,0:T(8,128)S(1)}) custom-call(s32[3072]{0:T(1024)S(1)} %pad_add_fusion.2.row_ref, s32[24,128]{1,0:T(8,128)S(1)} %pad_add_fusion.3.part_ref, f32[2048,128]{1,0:T(8,128)S(1)} %get-tuple-element.73.rows_ref), custom_call_target="tpu_custom_call" | custom-call | bytes 1024 | tf_op jit(solution)/shard_map/gather_rows/pallas_call | solution.py:178
  38.8 1.6 %collective-permute-start.12 = (f32[32,1536]{1,0:T(8,128)S(1)}, f32[32,1536]{1,0:T(8,128)S(1)}, u32[]{:S(2)}, u32[]{:S(2)}) collective-permute-start(f32[32,1536]{1,0:T(8,128)S(1)} %get-tuple-element.74), channel_id=1, source_target_pairs={{0,2},{1,3},{2,0},{3,1},{4,6},{5,7},{6,4},{7,5},{8,10},{9,11},{10,... | collective-permute-start | bytes 589832 | tf_op jit(solution)/shard_map/ppermute | solution.py:41
  40.3 0.0 collective-permute-start.13
  40.4 2.1 %later_own.2 = (bf16[32,8192]{1,0:T(8,128)(2,1)S(1)}, bf16[96,96]{1,0:T(8,128)(2,1)S(1)}, f32[32,8192]{1,0:T(8,128)S(1)}) custom-call(f32[8,128]{1,0:T(8,128)S(1)} %add_add_fusion.1.refs_0_, f32[8,128]{1,0:T(8,128)S(1)} %collective-permute-done.7.refs_1_, f32[8,128]{1,0:T(8,128)S(1)} %collective-permute-done.8.refs_2_, ...), custom_call_target="tpu_custom_call" | custom-call | bytes 1024 | tf_op jit(solution)/shard_map/later_own/pallas_call | solution.py:275
  42.4 2.3 %collective-permute-done.10.refs_5_ = f32[32,1536]{1,0:T(8,128)S(1)} collective-permute-done((f32[32,1536]{1,0:T(8,128)S(1)}, f32[32,1536]{1,0:T(8,128)S(1)}, u32[]{:S(2)}, u32[]{:S(2)}) %collective-permute-start.10) | collective-permute-done | bytes 196640 | tf_op jit(solution)/shard_map/ppermute | solution.py:41
  44.7 0.0 collective-permute-done.11.refs_6_
  44.7 1.4 %collective-permute-done.12.refs_7_ = f32[32,1536]{1,0:T(8,128)S(1)} collective-permute-done((f32[32,1536]{1,0:T(8,128)S(1)}, f32[32,1536]{1,0:T(8,128)S(1)}, u32[]{:S(2)}, u32[]{:S(2)}) %collective-permute-start.12) | collective-permute-done | bytes 196640 | tf_op jit(solution)/shard_map/ppermute | solution.py:41
  46.1 0.0 collective-permute-done.13.refs_8_
  46.1 3.2 %product.4 = (bf16[96,8192]{1,0:T(8,128)(2,1)S(1)}, f32[8,128]{1,0:T(8,128)S(1)}, f32[2048,128]{1,0:T(8,128)S(1)}) custom-call(s32[320]{0:T(512)S(1)} %copy-done, s32[320]{0:T(512)S(1)} %copy-done.1, s32[1]{0:T(128)S(6)} %copy.7.refs_2_, bf16[32,8192]{1,0:T(8,128)(2,1)S(1)} %get-tuple-element.69.refs_3_, f32[32,8192]{1,0:T(8,128)S(1)} %get-tuple-element.70.refs_4_, ...), custom_call_target="tpu_custom_call" | custom-call | bytes 1024 | tf_op jit(solution)/shard_map/product/pallas_call | solution.py:382
  49.3 3.0 %collective-permute-start.16 = (f32[8,128]{1,0:T(8,128)S(1)}, f32[8,128]{1,0:T(8,128)S(1)}, u32[]{:S(2)}, u32[]{:S(2)}) collective-permute-start(f32[8,128]{1,0:T(8,128)S(1)} %get-tuple-element.78), channel_id=1, source_target_pairs={{0,12},{1,13},{2,14},{3,15},{4,8},{5,9},{6,10},{7,11},{8,4},{9,5},... | collective-permute-start | bytes 12296 | tf_op jit(solution)/shard_map/ppermute | solution.py:41
  52.3 0.0 collective-permute-start.15
  52.3 1.5 %collective-permute-start.14 = (f32[8,128]{1,0:T(8,128)S(1)}, f32[8,128]{1,0:T(8,128)S(1)}, u32[]{:S(2)}, u32[]{:S(2)}) collective-permute-start(f32[8,128]{1,0:T(8,128)S(1)} %get-tuple-element.78), channel_id=1, source_target_pairs={{0,4},{1,5},{2,6},{3,7},{4,0},{5,1},{6,2},{7,3},{8,12},{9,13},{10,... | collective-permute-start | bytes 12296 | tf_op jit(solution)/shard_map/ppermute | solution.py:41
  53.7 3.8 %gather_rows.6 = (f32[32,1536]{1,0:T(8,128)S(1)}, f32[32,1536]{1,0:T(8,128)S(1)}) custom-call(s32[3072]{0:T(1024)S(1)} %pad_add_fusion.row_ref, s32[24,128]{1,0:T(8,128)S(1)} %pad_add_fusion.1.part_ref, f32[2048,128]{1,0:T(8,128)S(1)} %get-tuple-element.91.rows_ref), custom_call_target="tpu_custom_call" | custom-call | bytes 1024 | tf_op jit(solution)/shard_map/gather_rows/pallas_call | solution.py:178
  57.6 0.0 collective-permute-done.16
  57.6 0.0 collective-permute-done.15
  57.6 0.0 collective-permute-done.14
  57.6 0.1 collective-permute-start.19
  57.7 0.6 collective-permute-start.18
  58.3 1.2 %collective-permute-start.17 = (f32[8,128]{1,0:T(8,128)S(1)}, f32[8,128]{1,0:T(8,128)S(1)}, u32[]{:S(2)}, u32[]{:S(2)}) collective-permute-start(f32[8,128]{1,0:T(8,128)S(1)} %add_add_fusion.refs_0_), channel_id=1, source_target_pairs={{0,1},{1,0},{2,3},{3,2},{4,5},{5,4},{6,7},{7,6},{8,9},{9,8},{10,11... | collective-permute-start | bytes 12296 | tf_op jit(solution)/shard_map/ppermute | solution.py:41
  59.6 1.4 %collective-permute-start.20 = (f32[32,1536]{1,0:T(8,128)S(1)}, f32[32,1536]{1,0:T(8,128)S(1)}, u32[]{:S(2)}, u32[]{:S(2)}) collective-permute-start(f32[32,1536]{1,0:T(8,128)S(1)} %get-tuple-element.89), channel_id=1, source_target_pairs={{0,8},{1,9},{2,10},{3,11},{4,12},{5,13},{6,14},{7,15},{8,0},{9,1},... | collective-permute-start | bytes 589832 | tf_op jit(solution)/shard_map/ppermute | solution.py:41
  61.0 2.0 %collective-permute-start.21 = (f32[32,1536]{1,0:T(8,128)S(1)}, f32[32,1536]{1,0:T(8,128)S(1)}, u32[]{:S(2)}, u32[]{:S(2)}) collective-permute-start(f32[32,1536]{1,0:T(8,128)S(1)} %get-tuple-element.90), channel_id=1, source_target_pairs={{0,4},{1,5},{2,6},{3,7},{4,0},{5,1},{6,2},{7,3},{8,12},{9,13},{10,... | collective-permute-start | bytes 589832 | tf_op jit(solution)/shard_map/ppermute | solution.py:41
  63.0 0.0 collective-permute-done.18.refs_2_
  63.0 0.0 collective-permute-done.17.refs_1_
  63.0 3.8 %gather_rows.7 = (f32[32,1536]{1,0:T(8,128)S(1)}, f32[32,1536]{1,0:T(8,128)S(1)}) custom-call(s32[3072]{0:T(1024)S(1)} %pad_add_fusion.2.row_ref, s32[24,128]{1,0:T(8,128)S(1)} %pad_add_fusion.3.part_ref, f32[2048,128]{1,0:T(8,128)S(1)} %get-tuple-element.91.rows_ref), custom_call_target="tpu_custom_call" | custom-call | bytes 1024 | tf_op jit(solution)/shard_map/gather_rows/pallas_call | solution.py:178
  66.9 0.3 collective-permute-start.22
  67.2 0.0 collective-permute-start.23
  67.2 2.1 %later_own.3 = (bf16[32,8192]{1,0:T(8,128)(2,1)S(1)}, bf16[96,96]{1,0:T(8,128)(2,1)S(1)}, f32[32,8192]{1,0:T(8,128)S(1)}) custom-call(f32[8,128]{1,0:T(8,128)S(1)} %add_add_fusion.refs_0_, f32[8,128]{1,0:T(8,128)S(1)} %collective-permute-done.17.refs_1_, f32[8,128]{1,0:T(8,128)S(1)} %collective-permute-done.18.refs_2_, ...), custom_call_target="tpu_custom_call" | custom-call | bytes 1024 | tf_op jit(solution)/shard_map/later_own/pallas_call | solution.py:275
  69.3 2.3 %collective-permute-done.20.refs_5_ = f32[32,1536]{1,0:T(8,128)S(1)} collective-permute-done((f32[32,1536]{1,0:T(8,128)S(1)}, f32[32,1536]{1,0:T(8,128)S(1)}, u32[]{:S(2)}, u32[]{:S(2)}) %collective-permute-start.20) | collective-permute-done | bytes 196640 | tf_op jit(solution)/shard_map/ppermute | solution.py:41
  71.6 0.1 collective-permute-done.21.refs_6_
  71.7 1.5 %collective-permute-done.22.refs_7_ = f32[32,1536]{1,0:T(8,128)S(1)} collective-permute-done((f32[32,1536]{1,0:T(8,128)S(1)}, f32[32,1536]{1,0:T(8,128)S(1)}, u32[]{:S(2)}, u32[]{:S(2)}) %collective-permute-start.22) | collective-permute-done | bytes 196640 | tf_op jit(solution)/shard_map/ppermute | solution.py:41
  73.2 3.0 %product.5 = (bf16[96,8192]{1,0:T(8,128)(2,1)S(1)}, f32[16,8,128]{2,1,0:T(8,128)S(1)}) custom-call(s32[320]{0:T(512)S(1)} %copy-done, s32[320]{0:T(512)S(1)} %copy-done.1, s32[1]{0:T(128)S(6)} %copy.7.refs_2_, bf16[32,8192]{1,0:T(8,128)(2,1)S(1)} %get-tuple-element.87.refs_3_, f32[32,8192]{1,0:T(8,128)S(1)} %get-tuple-element.88.refs_4_, ...), custom_call_target="tpu_custom_call" | custom-call | bytes 1024 | tf_op jit(solution)/shard_map/product/pallas_call | solution.py:382
  76.2 10.4 %all_to_all.5.refs_0_ = f32[16,8,128]{2,1,0:T(8,128)S(1)} all-to-all(f32[16,8,128]{2,1,0:T(8,128)S(1)} %get-tuple-element.95), channel_id=1, replica_groups=mesh['groups'=2,'dom'=16] {'dom'}, dimensions={0} | all-to-all | bytes 131072 | tf_op jit(solution)/shard_map/all_to_all | solution.py:485
  86.6 2.3 %final.1 = f32[32,8192]{1,0:T(8,128)} custom-call(f32[16,8,128]{2,1,0:T(8,128)S(1)} %all_to_all.5.refs_0_, bf16[96,8192]{1,0:T(8,128)(2,1)S(1)} %get-tuple-element.96.refs_1_), custom_call_target="tpu_custom_call" | custom-call | bytes 1024 | tf_op jit(solution)/shard_map/final/pallas_call | solution.py:410
  (10 shorter events, 0.1 us)
Async XLA Ops:
  6.0 12.4 %collective-permute-start = (bf16[32,1536]{1,0:T(8,128)(2,1)S(1)}, bf16[32,1536]{1,0:T(8,128)(2,1)S(1)}, u32[]{:S(2)}, u32[]{:S(2)}) collective-permute-start(bf16[32,1536]{1,0:T(8,128)(2,1)S(1)} %get-tuple-element.54), channel_id=1, source_target_pairs={{0,8},{1,9},{2,10},{3,11},{4,12},{5,13},{6,14},{7,15},{8,0},{9,1},... | collective-permute-start | bytes 294920 | tf_op jit(solution)/shard_map/ppermute | solution.py:41
  10.1 8.3 %collective-permute-start.1 = (bf16[32,1536]{1,0:T(8,128)(2,1)S(1)}, bf16[32,1536]{1,0:T(8,128)(2,1)S(1)}, u32[]{:S(2)}, u32[]{:S(2)}) collective-permute-start(bf16[32,1536]{1,0:T(8,128)(2,1)S(1)} %get-tuple-element.55), channel_id=1, source_target_pairs={{0,4},{1,5},{2,6},{3,7},{4,0},{5,1},{6,2},{7,3},{8,12},{9,13},{10,... | collective-permute-start | bytes 294920 | tf_op jit(solution)/shard_map/ppermute | solution.py:41
  15.4 4.7 %copy-start = (s32[320]{0:T(512)S(1)}, s32[320]{0:T(512)}, u32[]{:S(2)}) copy-start(s32[320]{0:T(512)} %refs_0_.5) | copy-start | bytes 3844
  15.4 4.7 %copy-start.1 = (s32[320]{0:T(512)S(1)}, s32[320]{0:T(512)}, u32[]{:S(2)}) copy-start(s32[320]{0:T(512)} %refs_1_.5) | copy-start | bytes 3844
  15.4 4.7 %collective-permute-start.2 = (bf16[32,1536]{1,0:T(8,128)(2,1)S(1)}, bf16[32,1536]{1,0:T(8,128)(2,1)S(1)}, u32[]{:S(2)}, u32[]{:S(2)}) collective-permute-start(bf16[32,1536]{1,0:T(8,128)(2,1)S(1)} %get-tuple-element.56), channel_id=1, source_target_pairs={{0,2},{1,3},{2,0},{3,1},{4,6},{5,7},{6,4},{7,5},{8,10},{9,11},{10,... | collective-permute-start | bytes 294920 | tf_op jit(solution)/shard_map/ppermute | solution.py:41
  17.0 3.1 %collective-permute-start.3 = (bf16[32,1536]{1,0:T(8,128)(2,1)S(1)}, bf16[32,1536]{1,0:T(8,128)(2,1)S(1)}, u32[]{:S(2)}, u32[]{:S(2)}) collective-permute-start(bf16[32,1536]{1,0:T(8,128)(2,1)S(1)} %get-tuple-element.57), channel_id=1, source_target_pairs={{0,1},{1,0},{2,3},{3,2},{4,5},{5,4},{6,7},{7,6},{8,9},{9,8},{10,11... | collective-permute-start | bytes 294920 | tf_op jit(solution)/shard_map/ppermute | solution.py:41
  22.8 8.3 %collective-permute-start.6 = (f32[8,128]{1,0:T(8,128)S(1)}, f32[8,128]{1,0:T(8,128)S(1)}, u32[]{:S(2)}, u32[]{:S(2)}) collective-permute-start(f32[8,128]{1,0:T(8,128)S(1)} %get-tuple-element.60), channel_id=1, source_target_pairs={{0,12},{1,13},{2,14},{3,15},{4,8},{5,9},{6,10},{7,11},{8,4},{9,5},... | collective-permute-start | bytes 12296 | tf_op jit(solution)/shard_map/ppermute | solution.py:41
  23.9 7.2 %collective-permute-start.5 = (f32[8,128]{1,0:T(8,128)S(1)}, f32[8,128]{1,0:T(8,128)S(1)}, u32[]{:S(2)}, u32[]{:S(2)}) collective-permute-start(f32[8,128]{1,0:T(8,128)S(1)} %get-tuple-element.60), channel_id=1, source_target_pairs={{0,8},{1,9},{2,10},{3,11},{4,12},{5,13},{6,14},{7,15},{8,0},{9,1},... | collective-permute-start | bytes 12296 | tf_op jit(solution)/shard_map/ppermute | solution.py:41
  24.8 6.3 %collective-permute-start.4 = (f32[8,128]{1,0:T(8,128)S(1)}, f32[8,128]{1,0:T(8,128)S(1)}, u32[]{:S(2)}, u32[]{:S(2)}) collective-permute-start(f32[8,128]{1,0:T(8,128)S(1)} %get-tuple-element.60), channel_id=1, source_target_pairs={{0,4},{1,5},{2,6},{3,7},{4,0},{5,1},{6,2},{7,3},{8,12},{9,13},{10,... | collective-permute-start | bytes 12296 | tf_op jit(solution)/shard_map/ppermute | solution.py:41
  31.2 3.5 %collective-permute-start.9 = (f32[8,128]{1,0:T(8,128)S(1)}, f32[8,128]{1,0:T(8,128)S(1)}, u32[]{:S(2)}, u32[]{:S(2)}) collective-permute-start(f32[8,128]{1,0:T(8,128)S(1)} %add_add_fusion.1.refs_0_), channel_id=1, source_target_pairs={{0,3},{1,2},{2,1},{3,0},{4,7},{5,6},{6,5},{7,4},{8,11},{9,10},{10,... | collective-permute-start | bytes 12296 | tf_op jit(solution)/shard_map/ppermute | solution.py:41
  31.2 3.7 %collective-permute-start.8 = (f32[8,128]{1,0:T(8,128)S(1)}, f32[8,128]{1,0:T(8,128)S(1)}, u32[]{:S(2)}, u32[]{:S(2)}) collective-permute-start(f32[8,128]{1,0:T(8,128)S(1)} %add_add_fusion.1.refs_0_), channel_id=1, source_target_pairs={{0,2},{1,3},{2,0},{3,1},{4,6},{5,7},{6,4},{7,5},{8,10},{9,11},{10,... | collective-permute-start | bytes 12296 | tf_op jit(solution)/shard_map/ppermute | solution.py:41
  32.8 2.1 %collective-permute-start.7 = (f32[8,128]{1,0:T(8,128)S(1)}, f32[8,128]{1,0:T(8,128)S(1)}, u32[]{:S(2)}, u32[]{:S(2)}) collective-permute-start(f32[8,128]{1,0:T(8,128)S(1)} %add_add_fusion.1.refs_0_), channel_id=1, source_target_pairs={{0,1},{1,0},{2,3},{3,2},{4,5},{5,4},{6,7},{7,6},{8,9},{9,8},{10,11... | collective-permute-start | bytes 12296 | tf_op jit(solution)/shard_map/ppermute | solution.py:41
  33.1 11.6 %collective-permute-start.10 = (f32[32,1536]{1,0:T(8,128)S(1)}, f32[32,1536]{1,0:T(8,128)S(1)}, u32[]{:S(2)}, u32[]{:S(2)}) collective-permute-start(f32[32,1536]{1,0:T(8,128)S(1)} %get-tuple-element.71), channel_id=1, source_target_pairs={{0,8},{1,9},{2,10},{3,11},{4,12},{5,13},{6,14},{7,15},{8,0},{9,1},... | collective-permute-start | bytes 589832 | tf_op jit(solution)/shard_map/ppermute | solution.py:41
  33.1 11.6 %collective-permute-start.11 = (f32[32,1536]{1,0:T(8,128)S(1)}, f32[32,1536]{1,0:T(8,128)S(1)}, u32[]{:S(2)}, u32[]{:S(2)}) collective-permute-start(f32[32,1536]{1,0:T(8,128)S(1)} %get-tuple-element.72), channel_id=1, source_target_pairs={{0,4},{1,5},{2,6},{3,7},{4,0},{5,1},{6,2},{7,3},{8,12},{9,13},{10,... | collective-permute-start | bytes 589832 | tf_op jit(solution)/shard_map/ppermute | solution.py:41
  38.8 7.3 %collective-permute-start.12 = (f32[32,1536]{1,0:T(8,128)S(1)}, f32[32,1536]{1,0:T(8,128)S(1)}, u32[]{:S(2)}, u32[]{:S(2)}) collective-permute-start(f32[32,1536]{1,0:T(8,128)S(1)} %get-tuple-element.74), channel_id=1, source_target_pairs={{0,2},{1,3},{2,0},{3,1},{4,6},{5,7},{6,4},{7,5},{8,10},{9,11},{10,... | collective-permute-start | bytes 589832 | tf_op jit(solution)/shard_map/ppermute | solution.py:41
  40.3 5.7 %collective-permute-start.13 = (f32[32,1536]{1,0:T(8,128)S(1)}, f32[32,1536]{1,0:T(8,128)S(1)}, u32[]{:S(2)}, u32[]{:S(2)}) collective-permute-start(f32[32,1536]{1,0:T(8,128)S(1)} %get-tuple-element.75), channel_id=1, source_target_pairs={{0,1},{1,0},{2,3},{3,2},{4,5},{5,4},{6,7},{7,6},{8,9},{9,8},{10,11... | collective-permute-start | bytes 589832 | tf_op jit(solution)/shard_map/ppermute | solution.py:41
  49.3 8.3 %collective-permute-start.16 = (f32[8,128]{1,0:T(8,128)S(1)}, f32[8,128]{1,0:T(8,128)S(1)}, u32[]{:S(2)}, u32[]{:S(2)}) collective-permute-start(f32[8,128]{1,0:T(8,128)S(1)} %get-tuple-element.78), channel_id=1, source_target_pairs={{0,12},{1,13},{2,14},{3,15},{4,8},{5,9},{6,10},{7,11},{8,4},{9,5},... | collective-permute-start | bytes 12296 | tf_op jit(solution)/shard_map/ppermute | solution.py:41
  52.3 5.3 %collective-permute-start.15 = (f32[8,128]{1,0:T(8,128)S(1)}, f32[8,128]{1,0:T(8,128)S(1)}, u32[]{:S(2)}, u32[]{:S(2)}) collective-permute-start(f32[8,128]{1,0:T(8,128)S(1)} %get-tuple-element.78), channel_id=1, source_target_pairs={{0,8},{1,9},{2,10},{3,11},{4,12},{5,13},{6,14},{7,15},{8,0},{9,1},... | collective-permute-start | bytes 12296 | tf_op jit(solution)/shard_map/ppermute | solution.py:41
  52.3 5.3 %collective-permute-start.14 = (f32[8,128]{1,0:T(8,128)S(1)}, f32[8,128]{1,0:T(8,128)S(1)}, u32[]{:S(2)}, u32[]{:S(2)}) collective-permute-start(f32[8,128]{1,0:T(8,128)S(1)} %get-tuple-element.78), channel_id=1, source_target_pairs={{0,4},{1,5},{2,6},{3,7},{4,0},{5,1},{6,2},{7,3},{8,12},{9,13},{10,... | collective-permute-start | bytes 12296 | tf_op jit(solution)/shard_map/ppermute | solution.py:41
  57.6 5.4 %collective-permute-start.19 = (f32[8,128]{1,0:T(8,128)S(1)}, f32[8,128]{1,0:T(8,128)S(1)}, u32[]{:S(2)}, u32[]{:S(2)}) collective-permute-start(f32[8,128]{1,0:T(8,128)S(1)} %add_add_fusion.refs_0_), channel_id=1, source_target_pairs={{0,3},{1,2},{2,1},{3,0},{4,7},{5,6},{6,5},{7,4},{8,11},{9,10},{10,... | collective-permute-start | bytes 12296 | tf_op jit(solution)/shard_map/ppermute | solution.py:41
  57.7 5.3 %collective-permute-start.18 = (f32[8,128]{1,0:T(8,128)S(1)}, f32[8,128]{1,0:T(8,128)S(1)}, u32[]{:S(2)}, u32[]{:S(2)}) collective-permute-start(f32[8,128]{1,0:T(8,128)S(1)} %add_add_fusion.refs_0_), channel_id=1, source_target_pairs={{0,2},{1,3},{2,0},{3,1},{4,6},{5,7},{6,4},{7,5},{8,10},{9,11},{10,... | collective-permute-start | bytes 12296 | tf_op jit(solution)/shard_map/ppermute | solution.py:41
  58.3 4.7 %collective-permute-start.17 = (f32[8,128]{1,0:T(8,128)S(1)}, f32[8,128]{1,0:T(8,128)S(1)}, u32[]{:S(2)}, u32[]{:S(2)}) collective-permute-start(f32[8,128]{1,0:T(8,128)S(1)} %add_add_fusion.refs_0_), channel_id=1, source_target_pairs={{0,1},{1,0},{2,3},{3,2},{4,5},{5,4},{6,7},{7,6},{8,9},{9,8},{10,11... | collective-permute-start | bytes 12296 | tf_op jit(solution)/shard_map/ppermute | solution.py:41
  59.6 12.0 %collective-permute-start.20 = (f32[32,1536]{1,0:T(8,128)S(1)}, f32[32,1536]{1,0:T(8,128)S(1)}, u32[]{:S(2)}, u32[]{:S(2)}) collective-permute-start(f32[32,1536]{1,0:T(8,128)S(1)} %get-tuple-element.89), channel_id=1, source_target_pairs={{0,8},{1,9},{2,10},{3,11},{4,12},{5,13},{6,14},{7,15},{8,0},{9,1},... | collective-permute-start | bytes 589832 | tf_op jit(solution)/shard_map/ppermute | solution.py:41
  61.0 10.7 %collective-permute-start.21 = (f32[32,1536]{1,0:T(8,128)S(1)}, f32[32,1536]{1,0:T(8,128)S(1)}, u32[]{:S(2)}, u32[]{:S(2)}) collective-permute-start(f32[32,1536]{1,0:T(8,128)S(1)} %get-tuple-element.90), channel_id=1, source_target_pairs={{0,4},{1,5},{2,6},{3,7},{4,0},{5,1},{6,2},{7,3},{8,12},{9,13},{10,... | collective-permute-start | bytes 589832 | tf_op jit(solution)/shard_map/ppermute | solution.py:41
  66.9 6.3 %collective-permute-start.22 = (f32[32,1536]{1,0:T(8,128)S(1)}, f32[32,1536]{1,0:T(8,128)S(1)}, u32[]{:S(2)}, u32[]{:S(2)}) collective-permute-start(f32[32,1536]{1,0:T(8,128)S(1)} %get-tuple-element.92), channel_id=1, source_target_pairs={{0,2},{1,3},{2,0},{3,1},{4,6},{5,7},{6,4},{7,5},{8,10},{9,11},{10,... | collective-permute-start | bytes 589832 | tf_op jit(solution)/shard_map/ppermute | solution.py:41
  67.2 6.0 %collective-permute-start.23 = (f32[32,1536]{1,0:T(8,128)S(1)}, f32[32,1536]{1,0:T(8,128)S(1)}, u32[]{:S(2)}, u32[]{:S(2)}) collective-permute-start(f32[32,1536]{1,0:T(8,128)S(1)} %get-tuple-element.93), channel_id=1, source_target_pairs={{0,1},{1,0},{2,3},{3,2},{4,5},{5,4},{6,7},{7,6},{8,9},{9,8},{10,11... | collective-permute-start | bytes 589832 | tf_op jit(solution)/shard_map/ppermute | solution.py:41

commit v9 on v6

--- a/solution.py
+++ b/solution.py
@@ -12,8 +12,9 @@
 PACK = 4
 CHUNK = 1024
 SUBLANES = 8
-STEP = 4
+STEP = 8
 COPIES = 8
+GROUP = 128
 F32 = jnp.float32
 BF16 = jnp.bfloat16
 VMEM = pl.BlockSpec(memory_space=pltpu.VMEM)
@@ -360,7 +361,7 @@
 def product(src, dst, count, block, own, ghosts, matrix, tiles, with_rows):
     columns, states = block.shape
     rest, tile_size, _ = tiles.shape
-    group = 64
+    group = GROUP
     while rest % group:
         group //= 2
     outs = [vmem_out((3 * columns, states), BF16), vmem_out((columns * columns // LANES, LANES), F32)]

time: 89.3 us -> 88 us (0.985)
  Pallas kernels: 45.1 us -> 40 us
  starting transfers between devices: 30.3 us -> 32.3 us
  waiting for transfers between devices: 12.5 us -> 13.4 us
    pallas_call x3, Pallas kernels: 12.7 us -> 8.91 us  [product(): pl.pallas_call(functools.partial(product_kernel, len(ghosts), group, with...]
    ppermute x30, starting transfers between devices: 30.3 us -> 32.3 us  [swapped(): return lax.ppermute(x, 'dom', [(i, i ^ mask) for i in range(size)])]
    ppermute x30, waiting for transfers between devices: 12.5 us -> 13.4 us  [swapped(): return lax.ppermute(x, 'dom', [(i, i ^ mask) for i in range(size)])]
where the time goes in v9:
time: 88 us; the launch traced here: 87.8 us
  Pallas kernels  40 us (45%)
  starting transfers between devices  32.3 us (37%)
  waiting for transfers between devices  13.4 us (15%)
  between operations  1.05 us (1%)
    ppermute x30, starting transfers between devices, swapped(): return lax.ppermute(x, 'dom', [(i, i ^ mask) for i in range(size)])  32.3 us
    pallas_call x4, Pallas kernels, gather_colours(): pl.pallas_call(gather_kernel, out_shape=[vmem_out((columns, indices // co...  15.3 us
    ppermute x30, waiting for transfers between devices, swapped(): return lax.ppermute(x, 'dom', [(i, i ^ mask) for i in range(size)])  13.4 us
    pallas_call x3, Pallas kernels, product(): pl.pallas_call(functools.partial(product_kernel, len(ghosts), group, with...  8.91 us
    pallas_call x2, Pallas kernels, start_gather(): pl.pallas_call(functools.partial(start_kernel, count, first, make_rows),...  8.72 us
    pallas_call x2, Pallas kernels, later_own(): pl.pallas_call(functools.partial(later_own_kernel, total_states), out_sha...  4.15 us
    pallas_call x1, Pallas kernels, final(): pl.pallas_call(functools.partial(final_kernel, total_states), out_shape=j...  2.27 us
  transfers between devices with their start and end apart: 30, of which 12 were waited for; matrix products, arithmetic and copies ran while one was open for 0% of the time, Pallas kernels for 27%

profile of v9, /device:TPU:0, one launch (start us, length us, event | category | flops | bytes accessed | tf_op | source)
XLA Modules:
  0.0 87.8 jit_solution(14574934179732641120)
XLA Ops:
  0.0 0.8 add_select_fusion
  0.8 0.1 slice_reduce_fusion.1
  1.0 5.0 %start_gather.2 = (bf16[32,1536]{1,0:T(8,128)(2,1)S(1)}, bf16[32,1536]{1,0:T(8,128)(2,1)S(1)}, bf16[256,128,128]{2,1,0:T(8,128)(2,1)S(1)}, f32[2048,128]{1,0:T(8,128)S(1)}, bf16[32,8192]{1,0:T(8,128)(2,1)S(1)}) custom-call(s32[3072]{0:T(1024)S(1)} %pad_add_fusion.row_ref, s32[24,128]{1,0:T(8,128)S(1)} %pad_add_fusion.1.part_ref, ...), custom_call_target="tpu_custom_call" | custom-call | bytes 1024 | tf_op jit(solution)/shard_map/start_gather/pallas_call | solution.py:226
  6.0 4.1 %collective-permute-start = (bf16[32,1536]{1,0:T(8,128)(2,1)S(1)}, bf16[32,1536]{1,0:T(8,128)(2,1)S(1)}, u32[]{:S(2)}, u32[]{:S(2)}) collective-permute-start(bf16[32,1536]{1,0:T(8,128)(2,1)S(1)} %get-tuple-element.54), channel_id=1, source_target_pairs={{0,8},{1,9},{2,10},{3,11},{4,12},{5,13},{6,14},{7,15},{8,0},{9,1},... | collective-permute-start | bytes 294920 | tf_op jit(solution)/shard_map/ppermute | solution.py:41
  10.1 1.6 %collective-permute-start.1 = (bf16[32,1536]{1,0:T(8,128)(2,1)S(1)}, bf16[32,1536]{1,0:T(8,128)(2,1)S(1)}, u32[]{:S(2)}, u32[]{:S(2)}) collective-permute-start(bf16[32,1536]{1,0:T(8,128)(2,1)S(1)} %get-tuple-element.55), channel_id=1, source_target_pairs={{0,4},{1,5},{2,6},{3,7},{4,0},{5,1},{6,2},{7,3},{8,12},{9,13},{10,... | collective-permute-start | bytes 294920 | tf_op jit(solution)/shard_map/ppermute | solution.py:41
  11.7 3.7 %start_gather.3 = (bf16[32,1536]{1,0:T(8,128)(2,1)S(1)}, bf16[32,1536]{1,0:T(8,128)(2,1)S(1)}, bf16[64,128,128]{2,1,0:T(8,128)(2,1)S(1)}) custom-call(s32[3072]{0:T(1024)S(1)} %pad_add_fusion.2.row_ref, s32[24,128]{1,0:T(8,128)S(1)} %pad_add_fusion.3.part_ref, f32[2048,128]{1,0:T(8,128)S(1)} %get-tuple-element.52.source_ref, bf16[320,128,128]{2,1,0:T(8,128)(2,1)} %tiles_ref.3), custom_call_target="tpu_custom_call" | custom-call | bytes 1024 | tf_op jit(solution)/shard_map/start_gather/pallas_call | solution.py:226
  15.4 0.0 copy-start
  15.4 0.0 copy-start.1
  15.4 1.6 %collective-permute-start.2 = (bf16[32,1536]{1,0:T(8,128)(2,1)S(1)}, bf16[32,1536]{1,0:T(8,128)(2,1)S(1)}, u32[]{:S(2)}, u32[]{:S(2)}) collective-permute-start(bf16[32,1536]{1,0:T(8,128)(2,1)S(1)} %get-tuple-element.56), channel_id=1, source_target_pairs={{0,2},{1,3},{2,0},{3,1},{4,6},{5,7},{6,4},{7,5},{8,10},{9,11},{10,... | collective-permute-start | bytes 294920 | tf_op jit(solution)/shard_map/ppermute | solution.py:41
  17.0 0.0 collective-permute-start.3
  17.7 0.7 first_own.1.refs_4_
  18.3 0.0 collective-permute-done.refs_5_
  18.3 1.8 %collective-permute-done.2.refs_7_ = bf16[32,1536]{1,0:T(8,128)(2,1)S(1)} collective-permute-done((bf16[32,1536]{1,0:T(8,128)(2,1)S(1)}, bf16[32,1536]{1,0:T(8,128)(2,1)S(1)}, u32[]{:S(2)}, u32[]{:S(2)}) %collective-permute-start.2) | collective-permute-done | bytes 98336 | tf_op jit(solution)/shard_map/ppermute | solution.py:41
  20.1 2.7 %product.3 = (bf16[96,8192]{1,0:T(8,128)(2,1)S(1)}, f32[8,128]{1,0:T(8,128)S(1)}, f32[2048,128]{1,0:T(8,128)S(1)}) custom-call(s32[320]{0:T(512)S(1)} %copy-done, s32[320]{0:T(512)S(1)} %copy-done.1, s32[1]{0:T(128)S(6)} %copy.7.refs_2_, bf16[32,8192]{1,0:T(8,128)(2,1)S(1)} %get-tuple-element.51.block_ref.refs_3_, f32[32,8192]{1,0:T(8,128)S(1)} %first_own.1.refs_4_, ...), custom_call_target="tpu_custom_call" | custom-call | bytes 1024 | tf_op jit(solution)/shard_map/product/pallas_call | solution.py:372
  22.8 0.1 collective-permute-start.6
  22.9 1.9 %collective-permute-start.5 = (f32[8,128]{1,0:T(8,128)S(1)}, f32[8,128]{1,0:T(8,128)S(1)}, u32[]{:S(2)}, u32[]{:S(2)}) collective-permute-start(f32[8,128]{1,0:T(8,128)S(1)} %get-tuple-element.60), channel_id=1, source_target_pairs={{0,8},{1,9},{2,10},{3,11},{4,12},{5,13},{6,14},{7,15},{8,0},{9,1},... | collective-permute-start | bytes 12296 | tf_op jit(solution)/shard_map/ppermute | solution.py:41
  24.8 2.5 %collective-permute-start.4 = (f32[8,128]{1,0:T(8,128)S(1)}, f32[8,128]{1,0:T(8,128)S(1)}, u32[]{:S(2)}, u32[]{:S(2)}) collective-permute-start(f32[8,128]{1,0:T(8,128)S(1)} %get-tuple-element.60), channel_id=1, source_target_pairs={{0,4},{1,5},{2,6},{3,7},{4,0},{5,1},{6,2},{7,3},{8,12},{9,13},{10,... | collective-permute-start | bytes 12296 | tf_op jit(solution)/shard_map/ppermute | solution.py:41
  27.3 3.8 %gather_rows.4 = (f32[32,1536]{1,0:T(8,128)S(1)}, f32[32,1536]{1,0:T(8,128)S(1)}) custom-call(s32[3072]{0:T(1024)S(1)} %pad_add_fusion.row_ref, s32[24,128]{1,0:T(8,128)S(1)} %pad_add_fusion.1.part_ref, f32[2048,128]{1,0:T(8,128)S(1)} %get-tuple-element.73.rows_ref), custom_call_target="tpu_custom_call" | custom-call | bytes 1024 | tf_op jit(solution)/shard_map/gather_rows/pallas_call | solution.py:176
  31.1 0.0 collective-permute-done.5
  31.1 0.0 collective-permute-done.4
  31.2 0.1 collective-permute-start.9
  31.2 1.6 %collective-permute-start.8 = (f32[8,128]{1,0:T(8,128)S(1)}, f32[8,128]{1,0:T(8,128)S(1)}, u32[]{:S(2)}, u32[]{:S(2)}) collective-permute-start(f32[8,128]{1,0:T(8,128)S(1)} %add_add_fusion.2.refs_0_), channel_id=1, source_target_pairs={{0,2},{1,3},{2,0},{3,1},{4,6},{5,7},{6,4},{7,5},{8,10},{9,11},{10,... | collective-permute-start | bytes 12296 | tf_op jit(solution)/shard_map/ppermute | solution.py:41
  32.8 0.3 collective-permute-start.7
  33.1 0.5 collective-permute-start.10
  33.6 0.2 collective-permute-start.11
  33.8 0.5 collective-permute-done.9.refs_3_
  34.3 0.7 collective-permute-done.8.refs_2_
  34.9 0.0 collective-permute-done.7.refs_1_
  34.9 3.8 %gather_rows.5 = (f32[32,1536]{1,0:T(8,128)S(1)}, f32[32,1536]{1,0:T(8,128)S(1)}) custom-call(s32[3072]{0:T(1024)S(1)} %pad_add_fusion.2.row_ref, s32[24,128]{1,0:T(8,128)S(1)} %pad_add_fusion.3.part_ref, f32[2048,128]{1,0:T(8,128)S(1)} %get-tuple-element.73.rows_ref), custom_call_target="tpu_custom_call" | custom-call | bytes 1024 | tf_op jit(solution)/shard_map/gather_rows/pallas_call | solution.py:176
  38.8 1.6 %collective-permute-start.12 = (f32[32,1536]{1,0:T(8,128)S(1)}, f32[32,1536]{1,0:T(8,128)S(1)}, u32[]{:S(2)}, u32[]{:S(2)}) collective-permute-start(f32[32,1536]{1,0:T(8,128)S(1)} %get-tuple-element.74), channel_id=1, source_target_pairs={{0,2},{1,3},{2,0},{3,1},{4,6},{5,7},{6,4},{7,5},{8,10},{9,11},{10,... | collective-permute-start | bytes 589832 | tf_op jit(solution)/shard_map/ppermute | solution.py:41
  40.3 0.0 collective-permute-start.13
  40.4 2.1 %later_own.2 = (bf16[32,8192]{1,0:T(8,128)(2,1)S(1)}, bf16[96,96]{1,0:T(8,128)(2,1)S(1)}, f32[32,8192]{1,0:T(8,128)S(1)}) custom-call(f32[8,128]{1,0:T(8,128)S(1)} %add_add_fusion.2.refs_0_, f32[8,128]{1,0:T(8,128)S(1)} %collective-permute-done.7.refs_1_, f32[8,128]{1,0:T(8,128)S(1)} %collective-permute-done.8.refs_2_, ...), custom_call_target="tpu_custom_call" | custom-call | bytes 1024 | tf_op jit(solution)/shard_map/later_own/pallas_call | solution.py:273
  42.4 2.3 %collective-permute-done.10.refs_5_ = f32[32,1536]{1,0:T(8,128)S(1)} collective-permute-done((f32[32,1536]{1,0:T(8,128)S(1)}, f32[32,1536]{1,0:T(8,128)S(1)}, u32[]{:S(2)}, u32[]{:S(2)}) %collective-permute-start.10) | collective-permute-done | bytes 196640 | tf_op jit(solution)/shard_map/ppermute | solution.py:41
  44.7 0.0 collective-permute-done.11.refs_6_
  44.7 1.4 %collective-permute-done.12.refs_7_ = f32[32,1536]{1,0:T(8,128)S(1)} collective-permute-done((f32[32,1536]{1,0:T(8,128)S(1)}, f32[32,1536]{1,0:T(8,128)S(1)}, u32[]{:S(2)}, u32[]{:S(2)}) %collective-permute-start.12) | collective-permute-done | bytes 196640 | tf_op jit(solution)/shard_map/ppermute | solution.py:41
  46.1 0.0 collective-permute-done.13.refs_8_
  46.1 3.2 %product.4 = (bf16[96,8192]{1,0:T(8,128)(2,1)S(1)}, f32[8,128]{1,0:T(8,128)S(1)}, f32[2048,128]{1,0:T(8,128)S(1)}) custom-call(s32[320]{0:T(512)S(1)} %copy-done, s32[320]{0:T(512)S(1)} %copy-done.1, s32[1]{0:T(128)S(6)} %copy.7.refs_2_, bf16[32,8192]{1,0:T(8,128)(2,1)S(1)} %get-tuple-element.69.refs_3_, f32[32,8192]{1,0:T(8,128)S(1)} %get-tuple-element.70.refs_4_, ...), custom_call_target="tpu_custom_call" | custom-call | bytes 1024 | tf_op jit(solution)/shard_map/product/pallas_call | solution.py:372
  49.3 1.9 %collective-permute-start.16 = (f32[8,128]{1,0:T(8,128)S(1)}, f32[8,128]{1,0:T(8,128)S(1)}, u32[]{:S(2)}, u32[]{:S(2)}) collective-permute-start(f32[8,128]{1,0:T(8,128)S(1)} %get-tuple-element.78), channel_id=1, source_target_pairs={{0,12},{1,13},{2,14},{3,15},{4,8},{5,9},{6,10},{7,11},{8,4},{9,5},... | collective-permute-start | bytes 12296 | tf_op jit(solution)/shard_map/ppermute | solution.py:41
  51.2 2.6 %collective-permute-start.14 = (f32[8,128]{1,0:T(8,128)S(1)}, f32[8,128]{1,0:T(8,128)S(1)}, u32[]{:S(2)}, u32[]{:S(2)}) collective-permute-start(f32[8,128]{1,0:T(8,128)S(1)} %get-tuple-element.78), channel_id=1, source_target_pairs={{0,4},{1,5},{2,6},{3,7},{4,0},{5,1},{6,2},{7,3},{8,12},{9,13},{10,... | collective-permute-start | bytes 12296 | tf_op jit(solution)/shard_map/ppermute | solution.py:41
  53.8 3.8 %gather_rows.6 = (f32[32,1536]{1,0:T(8,128)S(1)}, f32[32,1536]{1,0:T(8,128)S(1)}) custom-call(s32[3072]{0:T(1024)S(1)} %pad_add_fusion.row_ref, s32[24,128]{1,0:T(8,128)S(1)} %pad_add_fusion.1.part_ref, f32[2048,128]{1,0:T(8,128)S(1)} %get-tuple-element.91.rows_ref), custom_call_target="tpu_custom_call" | custom-call | bytes 1024 | tf_op jit(solution)/shard_map/gather_rows/pallas_call | solution.py:176
  57.6 0.0 collective-permute-done.15
  57.6 0.1 collective-permute-start.19
  57.7 0.6 collective-permute-start.18
  58.3 1.2 %collective-permute-start.17 = (f32[8,128]{1,0:T(8,128)S(1)}, f32[8,128]{1,0:T(8,128)S(1)}, u32[]{:S(2)}, u32[]{:S(2)}) collective-permute-start(f32[8,128]{1,0:T(8,128)S(1)} %add_add_fusion.1.refs_0_), channel_id=1, source_target_pairs={{0,1},{1,0},{2,3},{3,2},{4,5},{5,4},{6,7},{7,6},{8,9},{9,8},{10,11... | collective-permute-start | bytes 12296 | tf_op jit(solution)/shard_map/ppermute | solution.py:41
  59.6 0.8 collective-permute-start.20
  60.4 1.6 %collective-permute-start.21 = (f32[32,1536]{1,0:T(8,128)S(1)}, f32[32,1536]{1,0:T(8,128)S(1)}, u32[]{:S(2)}, u32[]{:S(2)}) collective-permute-start(f32[32,1536]{1,0:T(8,128)S(1)} %get-tuple-element.90), channel_id=1, source_target_pairs={{0,4},{1,5},{2,6},{3,7},{4,0},{5,1},{6,2},{7,3},{8,12},{9,13},{10,... | collective-permute-start | bytes 589832 | tf_op jit(solution)/shard_map/ppermute | solution.py:41
  62.0 0.0 collective-permute-done.18.refs_2_
  62.0 3.8 %gather_rows.7 = (f32[32,1536]{1,0:T(8,128)S(1)}, f32[32,1536]{1,0:T(8,128)S(1)}) custom-call(s32[3072]{0:T(1024)S(1)} %pad_add_fusion.2.row_ref, s32[24,128]{1,0:T(8,128)S(1)} %pad_add_fusion.3.part_ref, f32[2048,128]{1,0:T(8,128)S(1)} %get-tuple-element.91.rows_ref), custom_call_target="tpu_custom_call" | custom-call | bytes 1024 | tf_op jit(solution)/shard_map/gather_rows/pallas_call | solution.py:176
  65.8 1.3 %collective-permute-start.22 = (f32[32,1536]{1,0:T(8,128)S(1)}, f32[32,1536]{1,0:T(8,128)S(1)}, u32[]{:S(2)}, u32[]{:S(2)}) collective-permute-start(f32[32,1536]{1,0:T(8,128)S(1)} %get-tuple-element.92), channel_id=1, source_target_pairs={{0,2},{1,3},{2,0},{3,1},{4,6},{5,7},{6,4},{7,5},{8,10},{9,11},{10,... | collective-permute-start | bytes 589832 | tf_op jit(solution)/shard_map/ppermute | solution.py:41
  67.1 2.1 %later_own.3 = (bf16[32,8192]{1,0:T(8,128)(2,1)S(1)}, bf16[96,96]{1,0:T(8,128)(2,1)S(1)}, f32[32,8192]{1,0:T(8,128)S(1)}) custom-call(f32[8,128]{1,0:T(8,128)S(1)} %add_add_fusion.1.refs_0_, f32[8,128]{1,0:T(8,128)S(1)} %collective-permute-done.17.refs_1_, f32[8,128]{1,0:T(8,128)S(1)} %collective-permute-done.18.refs_2_, ...), custom_call_target="tpu_custom_call" | custom-call | bytes 1024 | tf_op jit(solution)/shard_map/later_own/pallas_call | solution.py:273
  69.2 1.8 %collective-permute-done.20.refs_5_ = f32[32,1536]{1,0:T(8,128)S(1)} collective-permute-done((f32[32,1536]{1,0:T(8,128)S(1)}, f32[32,1536]{1,0:T(8,128)S(1)}, u32[]{:S(2)}, u32[]{:S(2)}) %collective-permute-start.20) | collective-permute-done | bytes 196640 | tf_op jit(solution)/shard_map/ppermute | solution.py:41
  71.0 0.1 collective-permute-done.21.refs_6_
  71.1 1.0 %collective-permute-done.22.refs_7_ = f32[32,1536]{1,0:T(8,128)S(1)} collective-permute-done((f32[32,1536]{1,0:T(8,128)S(1)}, f32[32,1536]{1,0:T(8,128)S(1)}, u32[]{:S(2)}, u32[]{:S(2)}) %collective-permute-start.22) | collective-permute-done | bytes 196640 | tf_op jit(solution)/shard_map/ppermute | solution.py:41
  72.1 3.0 %product.5 = (bf16[96,8192]{1,0:T(8,128)(2,1)S(1)}, f32[8,128]{1,0:T(8,128)S(1)}) custom-call(s32[320]{0:T(512)S(1)} %copy-done, s32[320]{0:T(512)S(1)} %copy-done.1, s32[1]{0:T(128)S(6)} %copy.7.refs_2_, bf16[32,8192]{1,0:T(8,128)(2,1)S(1)} %get-tuple-element.87.refs_3_, f32[32,8192]{1,0:T(8,128)S(1)} %get-tuple-element.88.refs_4_, ...), custom_call_target="tpu_custom_call" | custom-call | bytes 1024 | tf_op jit(solution)/shard_map/product/pallas_call | solution.py:372
  75.1 2.0 %collective-permute-start.26 = (f32[8,128]{1,0:T(8,128)S(1)}, f32[8,128]{1,0:T(8,128)S(1)}, u32[]{:S(2)}, u32[]{:S(2)}) collective-permute-start(f32[8,128]{1,0:T(8,128)S(1)} %get-tuple-element.95), channel_id=1, source_target_pairs={{0,12},{1,13},{2,14},{3,15},{4,8},{5,9},{6,10},{7,11},{8,4},{9,5},... | collective-permute-start | bytes 12296 | tf_op jit(solution)/shard_map/ppermute | solution.py:41
  77.1 2.4 %collective-permute-start.24 = (f32[8,128]{1,0:T(8,128)S(1)}, f32[8,128]{1,0:T(8,128)S(1)}, u32[]{:S(2)}, u32[]{:S(2)}) collective-permute-start(f32[8,128]{1,0:T(8,128)S(1)} %get-tuple-element.95), channel_id=1, source_target_pairs={{0,4},{1,5},{2,6},{3,7},{4,0},{5,1},{6,2},{7,3},{8,12},{9,13},{10,... | collective-permute-start | bytes 12296 | tf_op jit(solution)/shard_map/ppermute | solution.py:41
  79.5 1.0 %collective-permute-done.26 = f32[8,128]{1,0:T(8,128)S(1)} collective-permute-done((f32[8,128]{1,0:T(8,128)S(1)}, f32[8,128]{1,0:T(8,128)S(1)}, u32[]{:S(2)}, u32[]{:S(2)}) %collective-permute-start.26) | collective-permute-done | bytes 4128 | tf_op jit(solution)/shard_map/ppermute | solution.py:41
  80.5 1.1 %collective-permute-done.25 = f32[8,128]{1,0:T(8,128)S(1)} collective-permute-done((f32[8,128]{1,0:T(8,128)S(1)}, f32[8,128]{1,0:T(8,128)S(1)}, u32[]{:S(2)}, u32[]{:S(2)}) %collective-permute-start.25) | collective-permute-done | bytes 4128 | tf_op jit(solution)/shard_map/ppermute | solution.py:41
  81.6 0.1 collective-permute-start.29
  81.7 0.9 collective-permute-start.28
  82.6 1.0 %collective-permute-start.27 = (f32[8,128]{1,0:T(8,128)S(1)}, f32[8,128]{1,0:T(8,128)S(1)}, u32[]{:S(2)}, u32[]{:S(2)}) collective-permute-start(f32[8,128]{1,0:T(8,128)S(1)} %add_add_fusion.refs_0_), channel_id=1, source_target_pairs={{0,1},{1,0},{2,3},{3,2},{4,5},{5,4},{6,7},{7,6},{8,9},{9,8},{10,11... | collective-permute-start | bytes 12296 | tf_op jit(solution)/shard_map/ppermute | solution.py:41
  83.6 1.2 %collective-permute-done.29.refs_3_ = f32[8,128]{1,0:T(8,128)S(1)} collective-permute-done((f32[8,128]{1,0:T(8,128)S(1)}, f32[8,128]{1,0:T(8,128)S(1)}, u32[]{:S(2)}, u32[]{:S(2)}) %collective-permute-start.29) | collective-permute-done | bytes 4128 | tf_op jit(solution)/shard_map/ppermute | solution.py:41
  84.7 0.7 collective-permute-done.28.refs_2_
  85.4 2.3 %final.1 = f32[32,8192]{1,0:T(8,128)} custom-call(f32[8,128]{1,0:T(8,128)S(1)} %add_add_fusion.refs_0_, f32[8,128]{1,0:T(8,128)S(1)} %collective-permute-done.27.refs_1_, f32[8,128]{1,0:T(8,128)S(1)} %collective-permute-done.28.refs_2_, f32[8,128]{1,0:T(8,128)S(1)} %collective-permute-done.29.refs_3_, bf16[96,8192]{1,0:T(8,128)(2,1)S(1)} %get-tuple-element.96.refs_4_), custom_call_target="tpu_custom_call" | custom-call | bytes 1024 | tf_op jit(solution)/shard_map/final/pallas_call | solution.py:399
  (22 shorter events, 0.1 us)
Async XLA Ops:
  6.0 12.4 %collective-permute-start = (bf16[32,1536]{1,0:T(8,128)(2,1)S(1)}, bf16[32,1536]{1,0:T(8,128)(2,1)S(1)}, u32[]{:S(2)}, u32[]{:S(2)}) collective-permute-start(bf16[32,1536]{1,0:T(8,128)(2,1)S(1)} %get-tuple-element.54), channel_id=1, source_target_pairs={{0,8},{1,9},{2,10},{3,11},{4,12},{5,13},{6,14},{7,15},{8,0},{9,1},... | collective-permute-start | bytes 294920 | tf_op jit(solution)/shard_map/ppermute | solution.py:41
  10.1 8.3 %collective-permute-start.1 = (bf16[32,1536]{1,0:T(8,128)(2,1)S(1)}, bf16[32,1536]{1,0:T(8,128)(2,1)S(1)}, u32[]{:S(2)}, u32[]{:S(2)}) collective-permute-start(bf16[32,1536]{1,0:T(8,128)(2,1)S(1)} %get-tuple-element.55), channel_id=1, source_target_pairs={{0,4},{1,5},{2,6},{3,7},{4,0},{5,1},{6,2},{7,3},{8,12},{9,13},{10,... | collective-permute-start | bytes 294920 | tf_op jit(solution)/shard_map/ppermute | solution.py:41
  15.4 4.7 %copy-start = (s32[320]{0:T(512)S(1)}, s32[320]{0:T(512)}, u32[]{:S(2)}) copy-start(s32[320]{0:T(512)} %refs_0_.5) | copy-start | bytes 3844
  15.4 4.7 %copy-start.1 = (s32[320]{0:T(512)S(1)}, s32[320]{0:T(512)}, u32[]{:S(2)}) copy-start(s32[320]{0:T(512)} %refs_1_.5) | copy-start | bytes 3844
  15.4 4.7 %collective-permute-start.2 = (bf16[32,1536]{1,0:T(8,128)(2,1)S(1)}, bf16[32,1536]{1,0:T(8,128)(2,1)S(1)}, u32[]{:S(2)}, u32[]{:S(2)}) collective-permute-start(bf16[32,1536]{1,0:T(8,128)(2,1)S(1)} %get-tuple-element.56), channel_id=1, source_target_pairs={{0,2},{1,3},{2,0},{3,1},{4,6},{5,7},{6,4},{7,5},{8,10},{9,11},{10,... | collective-permute-start | bytes 294920 | tf_op jit(solution)/shard_map/ppermute | solution.py:41
  17.0 3.1 %collective-permute-start.3 = (bf16[32,1536]{1,0:T(8,128)(2,1)S(1)}, bf16[32,1536]{1,0:T(8,128)(2,1)S(1)}, u32[]{:S(2)}, u32[]{:S(2)}) collective-permute-start(bf16[32,1536]{1,0:T(8,128)(2,1)S(1)} %get-tuple-element.57), channel_id=1, source_target_pairs={{0,1},{1,0},{2,3},{3,2},{4,5},{5,4},{6,7},{7,6},{8,9},{9,8},{10,11... | collective-permute-start | bytes 294920 | tf_op jit(solution)/shard_map/ppermute | solution.py:41
  22.8 8.3 %collective-permute-start.6 = (f32[8,128]{1,0:T(8,128)S(1)}, f32[8,128]{1,0:T(8,128)S(1)}, u32[]{:S(2)}, u32[]{:S(2)}) collective-permute-start(f32[8,128]{1,0:T(8,128)S(1)} %get-tuple-element.60), channel_id=1, source_target_pairs={{0,12},{1,13},{2,14},{3,15},{4,8},{5,9},{6,10},{7,11},{8,4},{9,5},... | collective-permute-start | bytes 12296 | tf_op jit(solution)/shard_map/ppermute | solution.py:41
  22.9 8.2 %collective-permute-start.5 = (f32[8,128]{1,0:T(8,128)S(1)}, f32[8,128]{1,0:T(8,128)S(1)}, u32[]{:S(2)}, u32[]{:S(2)}) collective-permute-start(f32[8,128]{1,0:T(8,128)S(1)} %get-tuple-element.60), channel_id=1, source_target_pairs={{0,8},{1,9},{2,10},{3,11},{4,12},{5,13},{6,14},{7,15},{8,0},{9,1},... | collective-permute-start | bytes 12296 | tf_op jit(solution)/shard_map/ppermute | solution.py:41
  24.8 6.3 %collective-permute-start.4 = (f32[8,128]{1,0:T(8,128)S(1)}, f32[8,128]{1,0:T(8,128)S(1)}, u32[]{:S(2)}, u32[]{:S(2)}) collective-permute-start(f32[8,128]{1,0:T(8,128)S(1)} %get-tuple-element.60), channel_id=1, source_target_pairs={{0,4},{1,5},{2,6},{3,7},{4,0},{5,1},{6,2},{7,3},{8,12},{9,13},{10,... | collective-permute-start | bytes 12296 | tf_op jit(solution)/shard_map/ppermute | solution.py:41
  31.2 3.1 %collective-permute-start.9 = (f32[8,128]{1,0:T(8,128)S(1)}, f32[8,128]{1,0:T(8,128)S(1)}, u32[]{:S(2)}, u32[]{:S(2)}) collective-permute-start(f32[8,128]{1,0:T(8,128)S(1)} %add_add_fusion.2.refs_0_), channel_id=1, source_target_pairs={{0,3},{1,2},{2,1},{3,0},{4,7},{5,6},{6,5},{7,4},{8,11},{9,10},{10,... | collective-permute-start | bytes 12296 | tf_op jit(solution)/shard_map/ppermute | solution.py:41
  31.2 3.7 %collective-permute-start.8 = (f32[8,128]{1,0:T(8,128)S(1)}, f32[8,128]{1,0:T(8,128)S(1)}, u32[]{:S(2)}, u32[]{:S(2)}) collective-permute-start(f32[8,128]{1,0:T(8,128)S(1)} %add_add_fusion.2.refs_0_), channel_id=1, source_target_pairs={{0,2},{1,3},{2,0},{3,1},{4,6},{5,7},{6,4},{7,5},{8,10},{9,11},{10,... | collective-permute-start | bytes 12296 | tf_op jit(solution)/shard_map/ppermute | solution.py:41
  32.8 2.1 %collective-permute-start.7 = (f32[8,128]{1,0:T(8,128)S(1)}, f32[8,128]{1,0:T(8,128)S(1)}, u32[]{:S(2)}, u32[]{:S(2)}) collective-permute-start(f32[8,128]{1,0:T(8,128)S(1)} %add_add_fusion.2.refs_0_), channel_id=1, source_target_pairs={{0,1},{1,0},{2,3},{3,2},{4,5},{5,4},{6,7},{7,6},{8,9},{9,8},{10,11... | collective-permute-start | bytes 12296 | tf_op jit(solution)/shard_map/ppermute | solution.py:41
  33.1 11.6 %collective-permute-start.10 = (f32[32,1536]{1,0:T(8,128)S(1)}, f32[32,1536]{1,0:T(8,128)S(1)}, u32[]{:S(2)}, u32[]{:S(2)}) collective-permute-start(f32[32,1536]{1,0:T(8,128)S(1)} %get-tuple-element.71), channel_id=1, source_target_pairs={{0,8},{1,9},{2,10},{3,11},{4,12},{5,13},{6,14},{7,15},{8,0},{9,1},... | collective-permute-start | bytes 589832 | tf_op jit(solution)/shard_map/ppermute | solution.py:41
  33.6 11.1 %collective-permute-start.11 = (f32[32,1536]{1,0:T(8,128)S(1)}, f32[32,1536]{1,0:T(8,128)S(1)}, u32[]{:S(2)}, u32[]{:S(2)}) collective-permute-start(f32[32,1536]{1,0:T(8,128)S(1)} %get-tuple-element.72), channel_id=1, source_target_pairs={{0,4},{1,5},{2,6},{3,7},{4,0},{5,1},{6,2},{7,3},{8,12},{9,13},{10,... | collective-permute-start | bytes 589832 | tf_op jit(solution)/shard_map/ppermute | solution.py:41
  38.8 7.3 %collective-permute-start.12 = (f32[32,1536]{1,0:T(8,128)S(1)}, f32[32,1536]{1,0:T(8,128)S(1)}, u32[]{:S(2)}, u32[]{:S(2)}) collective-permute-start(f32[32,1536]{1,0:T(8,128)S(1)} %get-tuple-element.74), channel_id=1, source_target_pairs={{0,2},{1,3},{2,0},{3,1},{4,6},{5,7},{6,4},{7,5},{8,10},{9,11},{10,... | collective-permute-start | bytes 589832 | tf_op jit(solution)/shard_map/ppermute | solution.py:41
  40.3 5.7 %collective-permute-start.13 = (f32[32,1536]{1,0:T(8,128)S(1)}, f32[32,1536]{1,0:T(8,128)S(1)}, u32[]{:S(2)}, u32[]{:S(2)}) collective-permute-start(f32[32,1536]{1,0:T(8,128)S(1)} %get-tuple-element.75), channel_id=1, source_target_pairs={{0,1},{1,0},{2,3},{3,2},{4,5},{5,4},{6,7},{7,6},{8,9},{9,8},{10,11... | collective-permute-start | bytes 589832 | tf_op jit(solution)/shard_map/ppermute | solution.py:41
  49.3 8.3 %collective-permute-start.16 = (f32[8,128]{1,0:T(8,128)S(1)}, f32[8,128]{1,0:T(8,128)S(1)}, u32[]{:S(2)}, u32[]{:S(2)}) collective-permute-start(f32[8,128]{1,0:T(8,128)S(1)} %get-tuple-element.78), channel_id=1, source_target_pairs={{0,12},{1,13},{2,14},{3,15},{4,8},{5,9},{6,10},{7,11},{8,4},{9,5},... | collective-permute-start | bytes 12296 | tf_op jit(solution)/shard_map/ppermute | solution.py:41
  51.2 6.4 %collective-permute-start.15 = (f32[8,128]{1,0:T(8,128)S(1)}, f32[8,128]{1,0:T(8,128)S(1)}, u32[]{:S(2)}, u32[]{:S(2)}) collective-permute-start(f32[8,128]{1,0:T(8,128)S(1)} %get-tuple-element.78), channel_id=1, source_target_pairs={{0,8},{1,9},{2,10},{3,11},{4,12},{5,13},{6,14},{7,15},{8,0},{9,1},... | collective-permute-start | bytes 12296 | tf_op jit(solution)/shard_map/ppermute | solution.py:41
  51.2 6.4 %collective-permute-start.14 = (f32[8,128]{1,0:T(8,128)S(1)}, f32[8,128]{1,0:T(8,128)S(1)}, u32[]{:S(2)}, u32[]{:S(2)}) collective-permute-start(f32[8,128]{1,0:T(8,128)S(1)} %get-tuple-element.78), channel_id=1, source_target_pairs={{0,4},{1,5},{2,6},{3,7},{4,0},{5,1},{6,2},{7,3},{8,12},{9,13},{10,... | collective-permute-start | bytes 12296 | tf_op jit(solution)/shard_map/ppermute | solution.py:41
  57.6 4.3 %collective-permute-start.19 = (f32[8,128]{1,0:T(8,128)S(1)}, f32[8,128]{1,0:T(8,128)S(1)}, u32[]{:S(2)}, u32[]{:S(2)}) collective-permute-start(f32[8,128]{1,0:T(8,128)S(1)} %add_add_fusion.1.refs_0_), channel_id=1, source_target_pairs={{0,3},{1,2},{2,1},{3,0},{4,7},{5,6},{6,5},{7,4},{8,11},{9,10},{10,... | collective-permute-start | bytes 12296 | tf_op jit(solution)/shard_map/ppermute | solution.py:41
  57.7 4.2 %collective-permute-start.18 = (f32[8,128]{1,0:T(8,128)S(1)}, f32[8,128]{1,0:T(8,128)S(1)}, u32[]{:S(2)}, u32[]{:S(2)}) collective-permute-start(f32[8,128]{1,0:T(8,128)S(1)} %add_add_fusion.1.refs_0_), channel_id=1, source_target_pairs={{0,2},{1,3},{2,0},{3,1},{4,6},{5,7},{6,4},{7,5},{8,10},{9,11},{10,... | collective-permute-start | bytes 12296 | tf_op jit(solution)/shard_map/ppermute | solution.py:41
  58.3 3.6 %collective-permute-start.17 = (f32[8,128]{1,0:T(8,128)S(1)}, f32[8,128]{1,0:T(8,128)S(1)}, u32[]{:S(2)}, u32[]{:S(2)}) collective-permute-start(f32[8,128]{1,0:T(8,128)S(1)} %add_add_fusion.1.refs_0_), channel_id=1, source_target_pairs={{0,1},{1,0},{2,3},{3,2},{4,5},{5,4},{6,7},{7,6},{8,9},{9,8},{10,11... | collective-permute-start | bytes 12296 | tf_op jit(solution)/shard_map/ppermute | solution.py:41
  59.6 11.5 %collective-permute-start.20 = (f32[32,1536]{1,0:T(8,128)S(1)}, f32[32,1536]{1,0:T(8,128)S(1)}, u32[]{:S(2)}, u32[]{:S(2)}) collective-permute-start(f32[32,1536]{1,0:T(8,128)S(1)} %get-tuple-element.89), channel_id=1, source_target_pairs={{0,8},{1,9},{2,10},{3,11},{4,12},{5,13},{6,14},{7,15},{8,0},{9,1},... | collective-permute-start | bytes 589832 | tf_op jit(solution)/shard_map/ppermute | solution.py:41
  60.4 10.7 %collective-permute-start.21 = (f32[32,1536]{1,0:T(8,128)S(1)}, f32[32,1536]{1,0:T(8,128)S(1)}, u32[]{:S(2)}, u32[]{:S(2)}) collective-permute-start(f32[32,1536]{1,0:T(8,128)S(1)} %get-tuple-element.90), channel_id=1, source_target_pairs={{0,4},{1,5},{2,6},{3,7},{4,0},{5,1},{6,2},{7,3},{8,12},{9,13},{10,... | collective-permute-start | bytes 589832 | tf_op jit(solution)/shard_map/ppermute | solution.py:41
  65.8 6.3 %collective-permute-start.22 = (f32[32,1536]{1,0:T(8,128)S(1)}, f32[32,1536]{1,0:T(8,128)S(1)}, u32[]{:S(2)}, u32[]{:S(2)}) collective-permute-start(f32[32,1536]{1,0:T(8,128)S(1)} %get-tuple-element.92), channel_id=1, source_target_pairs={{0,2},{1,3},{2,0},{3,1},{4,6},{5,7},{6,4},{7,5},{8,10},{9,11},{10,... | collective-permute-start | bytes 589832 | tf_op jit(solution)/shard_map/ppermute | solution.py:41
  67.1 5.0 %collective-permute-start.23 = (f32[32,1536]{1,0:T(8,128)S(1)}, f32[32,1536]{1,0:T(8,128)S(1)}, u32[]{:S(2)}, u32[]{:S(2)}) collective-permute-start(f32[32,1536]{1,0:T(8,128)S(1)} %get-tuple-element.93), channel_id=1, source_target_pairs={{0,1},{1,0},{2,3},{3,2},{4,5},{5,4},{6,7},{7,6},{8,9},{9,8},{10,11... | collective-permute-start | bytes 589832 | tf_op jit(solution)/shard_map/ppermute | solution.py:41
  75.1 5.4 %collective-permute-start.26 = (f32[8,128]{1,0:T(8,128)S(1)}, f32[8,128]{1,0:T(8,128)S(1)}, u32[]{:S(2)}, u32[]{:S(2)}) collective-permute-start(f32[8,128]{1,0:T(8,128)S(1)} %get-tuple-element.95), channel_id=1, source_target_pairs={{0,12},{1,13},{2,14},{3,15},{4,8},{5,9},{6,10},{7,11},{8,4},{9,5},... | collective-permute-start | bytes 12296 | tf_op jit(solution)/shard_map/ppermute | solution.py:41
  77.1 4.5 %collective-permute-start.25 = (f32[8,128]{1,0:T(8,128)S(1)}, f32[8,128]{1,0:T(8,128)S(1)}, u32[]{:S(2)}, u32[]{:S(2)}) collective-permute-start(f32[8,128]{1,0:T(8,128)S(1)} %get-tuple-element.95), channel_id=1, source_target_pairs={{0,8},{1,9},{2,10},{3,11},{4,12},{5,13},{6,14},{7,15},{8,0},{9,1},... | collective-permute-start | bytes 12296 | tf_op jit(solution)/shard_map/ppermute | solution.py:41
  77.1 4.5 %collective-permute-start.24 = (f32[8,128]{1,0:T(8,128)S(1)}, f32[8,128]{1,0:T(8,128)S(1)}, u32[]{:S(2)}, u32[]{:S(2)}) collective-permute-start(f32[8,128]{1,0:T(8,128)S(1)} %get-tuple-element.95), channel_id=1, source_target_pairs={{0,4},{1,5},{2,6},{3,7},{4,0},{5,1},{6,2},{7,3},{8,12},{9,13},{10,... | collective-permute-start | bytes 12296 | tf_op jit(solution)/shard_map/ppermute | solution.py:41
  81.6 3.1 %collective-permute-start.29 = (f32[8,128]{1,0:T(8,128)S(1)}, f32[8,128]{1,0:T(8,128)S(1)}, u32[]{:S(2)}, u32[]{:S(2)}) collective-permute-start(f32[8,128]{1,0:T(8,128)S(1)} %add_add_fusion.refs_0_), channel_id=1, source_target_pairs={{0,3},{1,2},{2,1},{3,0},{4,7},{5,6},{6,5},{7,4},{8,11},{9,10},{10,... | collective-permute-start | bytes 12296 | tf_op jit(solution)/shard_map/ppermute | solution.py:41
  81.7 3.7 %collective-permute-start.28 = (f32[8,128]{1,0:T(8,128)S(1)}, f32[8,128]{1,0:T(8,128)S(1)}, u32[]{:S(2)}, u32[]{:S(2)}) collective-permute-start(f32[8,128]{1,0:T(8,128)S(1)} %add_add_fusion.refs_0_), channel_id=1, source_target_pairs={{0,2},{1,3},{2,0},{3,1},{4,6},{5,7},{6,4},{7,5},{8,10},{9,11},{10,... | collective-permute-start | bytes 12296 | tf_op jit(solution)/shard_map/ppermute | solution.py:41
  82.6 2.8 %collective-permute-start.27 = (f32[8,128]{1,0:T(8,128)S(1)}, f32[8,128]{1,0:T(8,128)S(1)}, u32[]{:S(2)}, u32[]{:S(2)}) collective-permute-start(f32[8,128]{1,0:T(8,128)S(1)} %add_add_fusion.refs_0_), channel_id=1, source_target_pairs={{0,1},{1,0},{2,3},{3,2},{4,5},{5,4},{6,7},{7,6},{8,9},{9,8},{10,11... | collective-permute-start | bytes 12296 | tf_op jit(solution)/shard_map/ppermute | solution.py:41

commit v10 on v9

--- a/solution.py
+++ b/solution.py
@@ -167,7 +167,7 @@
 
 
 def gather_kernel(row_ref, part_ref, rows_ref, *rest):
-    gathered_into(64, row_ref, part_ref, rows_ref, rest[-1], rest[:-1])
+    gathered_into(128, row_ref, part_ref, rows_ref, rest[-1], rest[:-1])
 
 
 def gather_colours(rows, row_list, part_list, count):
@@ -209,7 +209,7 @@
     if make_rows:
         rows_ref = refs[0]
         transposed_into(block_ref, rows_ref)
-    gathered_into(64, row_ref, part_ref, rows_ref, picked, outs)
+    gathered_into(128, row_ref, part_ref, rows_ref, picked, outs)
     for copy in copies:
         copy.wait()
 

time: 88 us -> 87.4 us (level)
  transfers between devices with their start and end apart: 30 -> 30, of which waited for: 12 -> 11; matrix products, arithmetic and copies ran while one was open for 0% -> 0% of each run, Pallas kernels for 27% -> 27%
where the time goes in v10:
time: 87.4 us; the launch traced here: 87.2 us
  Pallas kernels  39.4 us (45%)
  starting transfers between devices  32.4 us (37%)
  waiting for transfers between devices  13.4 us (15%)
  between operations  1.05 us (1%)
    ppermute x30, starting transfers between devices, swapped(): return lax.ppermute(x, 'dom', [(i, i ^ mask) for i in range(size)])  32.4 us
    pallas_call x4, Pallas kernels, gather_colours(): pl.pallas_call(gather_kernel, out_shape=[vmem_out((columns, indices // co...  14.9 us
    ppermute x30, waiting for transfers between devices, swapped(): return lax.ppermute(x, 'dom', [(i, i ^ mask) for i in range(size)])  13.4 us
    pallas_call x3, Pallas kernels, product(): pl.pallas_call(functools.partial(product_kernel, len(ghosts), group, with...  8.91 us
    pallas_call x2, Pallas kernels, start_gather(): pl.pallas_call(functools.partial(start_kernel, count, first, make_rows),...  8.52 us
    pallas_call x2, Pallas kernels, later_own(): pl.pallas_call(functools.partial(later_own_kernel, total_states), out_sha...  4.15 us
    pallas_call x1, Pallas kernels, final(): pl.pallas_call(functools.partial(final_kernel, total_states), out_shape=j...  2.27 us
  transfers between devices with their start and end apart: 30, of which 11 were waited for; matrix products, arithmetic and copies ran while one was open for 0% of the time, Pallas kernels for 27%

profile of v10, /device:TPU:0, one launch (start us, length us, event | category | flops | bytes accessed | tf_op | source)
XLA Modules:
  0.0 87.2 jit_solution(14264510212132465449)
XLA Ops:
  0.0 0.8 add_select_fusion
  0.8 0.1 slice_reduce_fusion.1
  1.0 4.9 %start_gather.2 = (bf16[32,1536]{1,0:T(8,128)(2,1)S(1)}, bf16[32,1536]{1,0:T(8,128)(2,1)S(1)}, bf16[256,128,128]{2,1,0:T(8,128)(2,1)S(1)}, f32[2048,128]{1,0:T(8,128)S(1)}, bf16[32,8192]{1,0:T(8,128)(2,1)S(1)}) custom-call(s32[3072]{0:T(1024)S(1)} %pad_add_fusion.row_ref, s32[24,128]{1,0:T(8,128)S(1)} %pad_add_fusion.1.part_ref, ...), custom_call_target="tpu_custom_call" | custom-call | bytes 1024 | tf_op jit(solution)/shard_map/start_gather/pallas_call | solution.py:226
  5.9 4.1 %collective-permute-start = (bf16[32,1536]{1,0:T(8,128)(2,1)S(1)}, bf16[32,1536]{1,0:T(8,128)(2,1)S(1)}, u32[]{:S(2)}, u32[]{:S(2)}) collective-permute-start(bf16[32,1536]{1,0:T(8,128)(2,1)S(1)} %get-tuple-element.54), channel_id=1, source_target_pairs={{0,8},{1,9},{2,10},{3,11},{4,12},{5,13},{6,14},{7,15},{8,0},{9,1},... | collective-permute-start | bytes 294920 | tf_op jit(solution)/shard_map/ppermute | solution.py:41
  10.0 1.6 %collective-permute-start.1 = (bf16[32,1536]{1,0:T(8,128)(2,1)S(1)}, bf16[32,1536]{1,0:T(8,128)(2,1)S(1)}, u32[]{:S(2)}, u32[]{:S(2)}) collective-permute-start(bf16[32,1536]{1,0:T(8,128)(2,1)S(1)} %get-tuple-element.55), channel_id=1, source_target_pairs={{0,4},{1,5},{2,6},{3,7},{4,0},{5,1},{6,2},{7,3},{8,12},{9,13},{10,... | collective-permute-start | bytes 294920 | tf_op jit(solution)/shard_map/ppermute | solution.py:41
  11.6 3.6 %start_gather.3 = (bf16[32,1536]{1,0:T(8,128)(2,1)S(1)}, bf16[32,1536]{1,0:T(8,128)(2,1)S(1)}, bf16[64,128,128]{2,1,0:T(8,128)(2,1)S(1)}) custom-call(s32[3072]{0:T(1024)S(1)} %pad_add_fusion.2.row_ref, s32[24,128]{1,0:T(8,128)S(1)} %pad_add_fusion.3.part_ref, f32[2048,128]{1,0:T(8,128)S(1)} %get-tuple-element.52.source_ref, bf16[320,128,128]{2,1,0:T(8,128)(2,1)} %tiles_ref.3), custom_call_target="tpu_custom_call" | custom-call | bytes 1024 | tf_op jit(solution)/shard_map/start_gather/pallas_call | solution.py:226
  15.2 0.0 copy-start
  15.2 0.0 copy-start.1
  15.2 1.6 %collective-permute-start.2 = (bf16[32,1536]{1,0:T(8,128)(2,1)S(1)}, bf16[32,1536]{1,0:T(8,128)(2,1)S(1)}, u32[]{:S(2)}, u32[]{:S(2)}) collective-permute-start(bf16[32,1536]{1,0:T(8,128)(2,1)S(1)} %get-tuple-element.56), channel_id=1, source_target_pairs={{0,2},{1,3},{2,0},{3,1},{4,6},{5,7},{6,4},{7,5},{8,10},{9,11},{10,... | collective-permute-start | bytes 294920 | tf_op jit(solution)/shard_map/ppermute | solution.py:41
  16.8 0.0 collective-permute-start.3
  17.5 0.7 first_own.1.refs_4_
  18.1 1.8 %collective-permute-done.2.refs_7_ = bf16[32,1536]{1,0:T(8,128)(2,1)S(1)} collective-permute-done((bf16[32,1536]{1,0:T(8,128)(2,1)S(1)}, bf16[32,1536]{1,0:T(8,128)(2,1)S(1)}, u32[]{:S(2)}, u32[]{:S(2)}) %collective-permute-start.2) | collective-permute-done | bytes 98336 | tf_op jit(solution)/shard_map/ppermute | solution.py:41
  19.9 0.0 collective-permute-done.3.refs_8_
  19.9 2.7 %product.3 = (bf16[96,8192]{1,0:T(8,128)(2,1)S(1)}, f32[8,128]{1,0:T(8,128)S(1)}, f32[2048,128]{1,0:T(8,128)S(1)}) custom-call(s32[320]{0:T(512)S(1)} %copy-done, s32[320]{0:T(512)S(1)} %copy-done.1, s32[1]{0:T(128)S(6)} %copy.7.refs_2_, bf16[32,8192]{1,0:T(8,128)(2,1)S(1)} %get-tuple-element.51.block_ref.refs_3_, f32[32,8192]{1,0:T(8,128)S(1)} %first_own.1.refs_4_, ...), custom_call_target="tpu_custom_call" | custom-call | bytes 1024 | tf_op jit(solution)/shard_map/product/pallas_call | solution.py:372
  22.6 0.1 collective-permute-start.6
  22.7 1.9 %collective-permute-start.5 = (f32[8,128]{1,0:T(8,128)S(1)}, f32[8,128]{1,0:T(8,128)S(1)}, u32[]{:S(2)}, u32[]{:S(2)}) collective-permute-start(f32[8,128]{1,0:T(8,128)S(1)} %get-tuple-element.60), channel_id=1, source_target_pairs={{0,8},{1,9},{2,10},{3,11},{4,12},{5,13},{6,14},{7,15},{8,0},{9,1},... | collective-permute-start | bytes 12296 | tf_op jit(solution)/shard_map/ppermute | solution.py:41
  24.6 2.5 %collective-permute-start.4 = (f32[8,128]{1,0:T(8,128)S(1)}, f32[8,128]{1,0:T(8,128)S(1)}, u32[]{:S(2)}, u32[]{:S(2)}) collective-permute-start(f32[8,128]{1,0:T(8,128)S(1)} %get-tuple-element.60), channel_id=1, source_target_pairs={{0,4},{1,5},{2,6},{3,7},{4,0},{5,1},{6,2},{7,3},{8,12},{9,13},{10,... | collective-permute-start | bytes 12296 | tf_op jit(solution)/shard_map/ppermute | solution.py:41
  27.1 3.7 %gather_rows.4 = (f32[32,1536]{1,0:T(8,128)S(1)}, f32[32,1536]{1,0:T(8,128)S(1)}) custom-call(s32[3072]{0:T(1024)S(1)} %pad_add_fusion.row_ref, s32[24,128]{1,0:T(8,128)S(1)} %pad_add_fusion.1.part_ref, f32[2048,128]{1,0:T(8,128)S(1)} %get-tuple-element.73.rows_ref), custom_call_target="tpu_custom_call" | custom-call | bytes 1024 | tf_op jit(solution)/shard_map/gather_rows/pallas_call | solution.py:176
  30.8 0.0 collective-permute-done.4
  30.9 0.1 collective-permute-start.9
  30.9 1.6 %collective-permute-start.8 = (f32[8,128]{1,0:T(8,128)S(1)}, f32[8,128]{1,0:T(8,128)S(1)}, u32[]{:S(2)}, u32[]{:S(2)}) collective-permute-start(f32[8,128]{1,0:T(8,128)S(1)} %add_add_fusion.2.refs_0_), channel_id=1, source_target_pairs={{0,2},{1,3},{2,0},{3,1},{4,6},{5,7},{6,4},{7,5},{8,10},{9,11},{10,... | collective-permute-start | bytes 12296 | tf_op jit(solution)/shard_map/ppermute | solution.py:41
  32.5 0.3 collective-permute-start.7
  32.8 0.7 collective-permute-start.11
  33.5 0.4 collective-permute-done.9.refs_3_
  34.0 0.7 collective-permute-done.8.refs_2_
  34.6 0.0 collective-permute-done.7.refs_1_
  34.6 3.7 %gather_rows.5 = (f32[32,1536]{1,0:T(8,128)S(1)}, f32[32,1536]{1,0:T(8,128)S(1)}) custom-call(s32[3072]{0:T(1024)S(1)} %pad_add_fusion.2.row_ref, s32[24,128]{1,0:T(8,128)S(1)} %pad_add_fusion.3.part_ref, f32[2048,128]{1,0:T(8,128)S(1)} %get-tuple-element.73.rows_ref), custom_call_target="tpu_custom_call" | custom-call | bytes 1024 | tf_op jit(solution)/shard_map/gather_rows/pallas_call | solution.py:176
  38.4 1.6 %collective-permute-start.12 = (f32[32,1536]{1,0:T(8,128)S(1)}, f32[32,1536]{1,0:T(8,128)S(1)}, u32[]{:S(2)}, u32[]{:S(2)}) collective-permute-start(f32[32,1536]{1,0:T(8,128)S(1)} %get-tuple-element.74), channel_id=1, source_target_pairs={{0,2},{1,3},{2,0},{3,1},{4,6},{5,7},{6,4},{7,5},{8,10},{9,11},{10,... | collective-permute-start | bytes 589832 | tf_op jit(solution)/shard_map/ppermute | solution.py:41
  39.9 0.0 collective-permute-start.13
  39.9 2.1 %later_own.2 = (bf16[32,8192]{1,0:T(8,128)(2,1)S(1)}, bf16[96,96]{1,0:T(8,128)(2,1)S(1)}, f32[32,8192]{1,0:T(8,128)S(1)}) custom-call(f32[8,128]{1,0:T(8,128)S(1)} %add_add_fusion.2.refs_0_, f32[8,128]{1,0:T(8,128)S(1)} %collective-permute-done.7.refs_1_, f32[8,128]{1,0:T(8,128)S(1)} %collective-permute-done.8.refs_2_, ...), custom_call_target="tpu_custom_call" | custom-call | bytes 1024 | tf_op jit(solution)/shard_map/later_own/pallas_call | solution.py:273
  42.0 2.4 %collective-permute-done.10.refs_5_ = f32[32,1536]{1,0:T(8,128)S(1)} collective-permute-done((f32[32,1536]{1,0:T(8,128)S(1)}, f32[32,1536]{1,0:T(8,128)S(1)}, u32[]{:S(2)}, u32[]{:S(2)}) %collective-permute-start.10) | collective-permute-done | bytes 196640 | tf_op jit(solution)/shard_map/ppermute | solution.py:41
  44.4 0.0 collective-permute-done.11.refs_6_
  44.4 1.3 %collective-permute-done.12.refs_7_ = f32[32,1536]{1,0:T(8,128)S(1)} collective-permute-done((f32[32,1536]{1,0:T(8,128)S(1)}, f32[32,1536]{1,0:T(8,128)S(1)}, u32[]{:S(2)}, u32[]{:S(2)}) %collective-permute-start.12) | collective-permute-done | bytes 196640 | tf_op jit(solution)/shard_map/ppermute | solution.py:41
  45.7 0.0 collective-permute-done.13.refs_8_
  45.7 3.2 %product.4 = (bf16[96,8192]{1,0:T(8,128)(2,1)S(1)}, f32[8,128]{1,0:T(8,128)S(1)}, f32[2048,128]{1,0:T(8,128)S(1)}) custom-call(s32[320]{0:T(512)S(1)} %copy-done, s32[320]{0:T(512)S(1)} %copy-done.1, s32[1]{0:T(128)S(6)} %copy.7.refs_2_, bf16[32,8192]{1,0:T(8,128)(2,1)S(1)} %get-tuple-element.69.refs_3_, f32[32,8192]{1,0:T(8,128)S(1)} %get-tuple-element.70.refs_4_, ...), custom_call_target="tpu_custom_call" | custom-call | bytes 1024 | tf_op jit(solution)/shard_map/product/pallas_call | solution.py:372
  48.9 1.9 %collective-permute-start.16 = (f32[8,128]{1,0:T(8,128)S(1)}, f32[8,128]{1,0:T(8,128)S(1)}, u32[]{:S(2)}, u32[]{:S(2)}) collective-permute-start(f32[8,128]{1,0:T(8,128)S(1)} %get-tuple-element.78), channel_id=1, source_target_pairs={{0,12},{1,13},{2,14},{3,15},{4,8},{5,9},{6,10},{7,11},{8,4},{9,5},... | collective-permute-start | bytes 12296 | tf_op jit(solution)/shard_map/ppermute | solution.py:41
  50.8 0.0 collective-permute-start.15
  50.8 2.6 %collective-permute-start.14 = (f32[8,128]{1,0:T(8,128)S(1)}, f32[8,128]{1,0:T(8,128)S(1)}, u32[]{:S(2)}, u32[]{:S(2)}) collective-permute-start(f32[8,128]{1,0:T(8,128)S(1)} %get-tuple-element.78), channel_id=1, source_target_pairs={{0,4},{1,5},{2,6},{3,7},{4,0},{5,1},{6,2},{7,3},{8,12},{9,13},{10,... | collective-permute-start | bytes 12296 | tf_op jit(solution)/shard_map/ppermute | solution.py:41
  53.3 3.7 %gather_rows.6 = (f32[32,1536]{1,0:T(8,128)S(1)}, f32[32,1536]{1,0:T(8,128)S(1)}) custom-call(s32[3072]{0:T(1024)S(1)} %pad_add_fusion.row_ref, s32[24,128]{1,0:T(8,128)S(1)} %pad_add_fusion.1.part_ref, f32[2048,128]{1,0:T(8,128)S(1)} %get-tuple-element.91.rows_ref), custom_call_target="tpu_custom_call" | custom-call | bytes 1024 | tf_op jit(solution)/shard_map/gather_rows/pallas_call | solution.py:176
  57.1 0.0 collective-permute-done.15
  57.1 0.0 collective-permute-done.14
  57.1 0.1 collective-permute-start.19
  57.2 0.6 collective-permute-start.18
  57.8 1.2 %collective-permute-start.17 = (f32[8,128]{1,0:T(8,128)S(1)}, f32[8,128]{1,0:T(8,128)S(1)}, u32[]{:S(2)}, u32[]{:S(2)}) collective-permute-start(f32[8,128]{1,0:T(8,128)S(1)} %add_add_fusion.1.refs_0_), channel_id=1, source_target_pairs={{0,1},{1,0},{2,3},{3,2},{4,5},{5,4},{6,7},{7,6},{8,9},{9,8},{10,11... | collective-permute-start | bytes 12296 | tf_op jit(solution)/shard_map/ppermute | solution.py:41
  59.1 0.4 collective-permute-start.20
  59.4 2.0 %collective-permute-start.21 = (f32[32,1536]{1,0:T(8,128)S(1)}, f32[32,1536]{1,0:T(8,128)S(1)}, u32[]{:S(2)}, u32[]{:S(2)}) collective-permute-start(f32[32,1536]{1,0:T(8,128)S(1)} %get-tuple-element.90), channel_id=1, source_target_pairs={{0,4},{1,5},{2,6},{3,7},{4,0},{5,1},{6,2},{7,3},{8,12},{9,13},{10,... | collective-permute-start | bytes 589832 | tf_op jit(solution)/shard_map/ppermute | solution.py:41
  61.4 0.0 collective-permute-done.19.refs_3_
  61.4 0.0 collective-permute-done.18.refs_2_
  61.5 3.7 %gather_rows.7 = (f32[32,1536]{1,0:T(8,128)S(1)}, f32[32,1536]{1,0:T(8,128)S(1)}) custom-call(s32[3072]{0:T(1024)S(1)} %pad_add_fusion.2.row_ref, s32[24,128]{1,0:T(8,128)S(1)} %pad_add_fusion.3.part_ref, f32[2048,128]{1,0:T(8,128)S(1)} %get-tuple-element.91.rows_ref), custom_call_target="tpu_custom_call" | custom-call | bytes 1024 | tf_op jit(solution)/shard_map/gather_rows/pallas_call | solution.py:176
  65.2 1.3 %collective-permute-start.22 = (f32[32,1536]{1,0:T(8,128)S(1)}, f32[32,1536]{1,0:T(8,128)S(1)}, u32[]{:S(2)}, u32[]{:S(2)}) collective-permute-start(f32[32,1536]{1,0:T(8,128)S(1)} %get-tuple-element.92), channel_id=1, source_target_pairs={{0,2},{1,3},{2,0},{3,1},{4,6},{5,7},{6,4},{7,5},{8,10},{9,11},{10,... | collective-permute-start | bytes 589832 | tf_op jit(solution)/shard_map/ppermute | solution.py:41
  66.5 2.1 %later_own.3 = (bf16[32,8192]{1,0:T(8,128)(2,1)S(1)}, bf16[96,96]{1,0:T(8,128)(2,1)S(1)}, f32[32,8192]{1,0:T(8,128)S(1)}) custom-call(f32[8,128]{1,0:T(8,128)S(1)} %add_add_fusion.1.refs_0_, f32[8,128]{1,0:T(8,128)S(1)} %collective-permute-done.17.refs_1_, f32[8,128]{1,0:T(8,128)S(1)} %collective-permute-done.18.refs_2_, ...), custom_call_target="tpu_custom_call" | custom-call | bytes 1024 | tf_op jit(solution)/shard_map/later_own/pallas_call | solution.py:273
  68.6 1.8 %collective-permute-done.20.refs_5_ = f32[32,1536]{1,0:T(8,128)S(1)} collective-permute-done((f32[32,1536]{1,0:T(8,128)S(1)}, f32[32,1536]{1,0:T(8,128)S(1)}, u32[]{:S(2)}, u32[]{:S(2)}) %collective-permute-start.20) | collective-permute-done | bytes 196640 | tf_op jit(solution)/shard_map/ppermute | solution.py:41
  70.4 1.1 %collective-permute-done.22.refs_7_ = f32[32,1536]{1,0:T(8,128)S(1)} collective-permute-done((f32[32,1536]{1,0:T(8,128)S(1)}, f32[32,1536]{1,0:T(8,128)S(1)}, u32[]{:S(2)}, u32[]{:S(2)}) %collective-permute-start.22) | collective-permute-done | bytes 196640 | tf_op jit(solution)/shard_map/ppermute | solution.py:41
  71.5 3.0 %product.5 = (bf16[96,8192]{1,0:T(8,128)(2,1)S(1)}, f32[8,128]{1,0:T(8,128)S(1)}) custom-call(s32[320]{0:T(512)S(1)} %copy-done, s32[320]{0:T(512)S(1)} %copy-done.1, s32[1]{0:T(128)S(6)} %copy.7.refs_2_, bf16[32,8192]{1,0:T(8,128)(2,1)S(1)} %get-tuple-element.87.refs_3_, f32[32,8192]{1,0:T(8,128)S(1)} %get-tuple-element.88.refs_4_, ...), custom_call_target="tpu_custom_call" | custom-call | bytes 1024 | tf_op jit(solution)/shard_map/product/pallas_call | solution.py:372
  74.5 2.0 %collective-permute-start.26 = (f32[8,128]{1,0:T(8,128)S(1)}, f32[8,128]{1,0:T(8,128)S(1)}, u32[]{:S(2)}, u32[]{:S(2)}) collective-permute-start(f32[8,128]{1,0:T(8,128)S(1)} %get-tuple-element.95), channel_id=1, source_target_pairs={{0,12},{1,13},{2,14},{3,15},{4,8},{5,9},{6,10},{7,11},{8,4},{9,5},... | collective-permute-start | bytes 12296 | tf_op jit(solution)/shard_map/ppermute | solution.py:41
  76.5 2.4 %collective-permute-start.24 = (f32[8,128]{1,0:T(8,128)S(1)}, f32[8,128]{1,0:T(8,128)S(1)}, u32[]{:S(2)}, u32[]{:S(2)}) collective-permute-start(f32[8,128]{1,0:T(8,128)S(1)} %get-tuple-element.95), channel_id=1, source_target_pairs={{0,4},{1,5},{2,6},{3,7},{4,0},{5,1},{6,2},{7,3},{8,12},{9,13},{10,... | collective-permute-start | bytes 12296 | tf_op jit(solution)/shard_map/ppermute | solution.py:41
  78.9 1.0 %collective-permute-done.26 = f32[8,128]{1,0:T(8,128)S(1)} collective-permute-done((f32[8,128]{1,0:T(8,128)S(1)}, f32[8,128]{1,0:T(8,128)S(1)}, u32[]{:S(2)}, u32[]{:S(2)}) %collective-permute-start.26) | collective-permute-done | bytes 4128 | tf_op jit(solution)/shard_map/ppermute | solution.py:41
  79.9 1.1 %collective-permute-done.25 = f32[8,128]{1,0:T(8,128)S(1)} collective-permute-done((f32[8,128]{1,0:T(8,128)S(1)}, f32[8,128]{1,0:T(8,128)S(1)}, u32[]{:S(2)}, u32[]{:S(2)}) %collective-permute-start.25) | collective-permute-done | bytes 4128 | tf_op jit(solution)/shard_map/ppermute | solution.py:41
  81.0 0.1 collective-permute-start.29
  81.1 0.8 collective-permute-start.28
  82.0 1.0 %collective-permute-start.27 = (f32[8,128]{1,0:T(8,128)S(1)}, f32[8,128]{1,0:T(8,128)S(1)}, u32[]{:S(2)}, u32[]{:S(2)}) collective-permute-start(f32[8,128]{1,0:T(8,128)S(1)} %add_add_fusion.refs_0_), channel_id=1, source_target_pairs={{0,1},{1,0},{2,3},{3,2},{4,5},{5,4},{6,7},{7,6},{8,9},{9,8},{10,11... | collective-permute-start | bytes 12296 | tf_op jit(solution)/shard_map/ppermute | solution.py:41
  83.0 1.2 %collective-permute-done.29.refs_3_ = f32[8,128]{1,0:T(8,128)S(1)} collective-permute-done((f32[8,128]{1,0:T(8,128)S(1)}, f32[8,128]{1,0:T(8,128)S(1)}, u32[]{:S(2)}, u32[]{:S(2)}) %collective-permute-start.29) | collective-permute-done | bytes 4128 | tf_op jit(solution)/shard_map/ppermute | solution.py:41
  84.1 0.7 collective-permute-done.28.refs_2_
  84.8 2.3 %final.1 = f32[32,8192]{1,0:T(8,128)} custom-call(f32[8,128]{1,0:T(8,128)S(1)} %add_add_fusion.refs_0_, f32[8,128]{1,0:T(8,128)S(1)} %collective-permute-done.27.refs_1_, f32[8,128]{1,0:T(8,128)S(1)} %collective-permute-done.28.refs_2_, f32[8,128]{1,0:T(8,128)S(1)} %collective-permute-done.29.refs_3_, bf16[96,8192]{1,0:T(8,128)(2,1)S(1)} %get-tuple-element.96.refs_4_), custom_call_target="tpu_custom_call" | custom-call | bytes 1024 | tf_op jit(solution)/shard_map/final/pallas_call | solution.py:399
  (22 shorter events, 0.1 us)
Async XLA Ops:
  5.9 12.3 %collective-permute-start = (bf16[32,1536]{1,0:T(8,128)(2,1)S(1)}, bf16[32,1536]{1,0:T(8,128)(2,1)S(1)}, u32[]{:S(2)}, u32[]{:S(2)}) collective-permute-start(bf16[32,1536]{1,0:T(8,128)(2,1)S(1)} %get-tuple-element.54), channel_id=1, source_target_pairs={{0,8},{1,9},{2,10},{3,11},{4,12},{5,13},{6,14},{7,15},{8,0},{9,1},... | collective-permute-start | bytes 294920 | tf_op jit(solution)/shard_map/ppermute | solution.py:41
  10.0 8.2 %collective-permute-start.1 = (bf16[32,1536]{1,0:T(8,128)(2,1)S(1)}, bf16[32,1536]{1,0:T(8,128)(2,1)S(1)}, u32[]{:S(2)}, u32[]{:S(2)}) collective-permute-start(bf16[32,1536]{1,0:T(8,128)(2,1)S(1)} %get-tuple-element.55), channel_id=1, source_target_pairs={{0,4},{1,5},{2,6},{3,7},{4,0},{5,1},{6,2},{7,3},{8,12},{9,13},{10,... | collective-permute-start | bytes 294920 | tf_op jit(solution)/shard_map/ppermute | solution.py:41
  15.2 4.7 %copy-start = (s32[320]{0:T(512)S(1)}, s32[320]{0:T(512)}, u32[]{:S(2)}) copy-start(s32[320]{0:T(512)} %refs_0_.5) | copy-start | bytes 3844
  15.2 4.7 %copy-start.1 = (s32[320]{0:T(512)S(1)}, s32[320]{0:T(512)}, u32[]{:S(2)}) copy-start(s32[320]{0:T(512)} %refs_1_.5) | copy-start | bytes 3844
  15.2 4.7 %collective-permute-start.2 = (bf16[32,1536]{1,0:T(8,128)(2,1)S(1)}, bf16[32,1536]{1,0:T(8,128)(2,1)S(1)}, u32[]{:S(2)}, u32[]{:S(2)}) collective-permute-start(bf16[32,1536]{1,0:T(8,128)(2,1)S(1)} %get-tuple-element.56), channel_id=1, source_target_pairs={{0,2},{1,3},{2,0},{3,1},{4,6},{5,7},{6,4},{7,5},{8,10},{9,11},{10,... | collective-permute-start | bytes 294920 | tf_op jit(solution)/shard_map/ppermute | solution.py:41
  16.8 3.1 %collective-permute-start.3 = (bf16[32,1536]{1,0:T(8,128)(2,1)S(1)}, bf16[32,1536]{1,0:T(8,128)(2,1)S(1)}, u32[]{:S(2)}, u32[]{:S(2)}) collective-permute-start(bf16[32,1536]{1,0:T(8,128)(2,1)S(1)} %get-tuple-element.57), channel_id=1, source_target_pairs={{0,1},{1,0},{2,3},{3,2},{4,5},{5,4},{6,7},{7,6},{8,9},{9,8},{10,11... | collective-permute-start | bytes 294920 | tf_op jit(solution)/shard_map/ppermute | solution.py:41
  22.6 8.2 %collective-permute-start.6 = (f32[8,128]{1,0:T(8,128)S(1)}, f32[8,128]{1,0:T(8,128)S(1)}, u32[]{:S(2)}, u32[]{:S(2)}) collective-permute-start(f32[8,128]{1,0:T(8,128)S(1)} %get-tuple-element.60), channel_id=1, source_target_pairs={{0,12},{1,13},{2,14},{3,15},{4,8},{5,9},{6,10},{7,11},{8,4},{9,5},... | collective-permute-start | bytes 12296 | tf_op jit(solution)/shard_map/ppermute | solution.py:41
  22.7 8.1 %collective-permute-start.5 = (f32[8,128]{1,0:T(8,128)S(1)}, f32[8,128]{1,0:T(8,128)S(1)}, u32[]{:S(2)}, u32[]{:S(2)}) collective-permute-start(f32[8,128]{1,0:T(8,128)S(1)} %get-tuple-element.60), channel_id=1, source_target_pairs={{0,8},{1,9},{2,10},{3,11},{4,12},{5,13},{6,14},{7,15},{8,0},{9,1},... | collective-permute-start | bytes 12296 | tf_op jit(solution)/shard_map/ppermute | solution.py:41
  24.6 6.2 %collective-permute-start.4 = (f32[8,128]{1,0:T(8,128)S(1)}, f32[8,128]{1,0:T(8,128)S(1)}, u32[]{:S(2)}, u32[]{:S(2)}) collective-permute-start(f32[8,128]{1,0:T(8,128)S(1)} %get-tuple-element.60), channel_id=1, source_target_pairs={{0,4},{1,5},{2,6},{3,7},{4,0},{5,1},{6,2},{7,3},{8,12},{9,13},{10,... | collective-permute-start | bytes 12296 | tf_op jit(solution)/shard_map/ppermute | solution.py:41
  30.9 3.1 %collective-permute-start.9 = (f32[8,128]{1,0:T(8,128)S(1)}, f32[8,128]{1,0:T(8,128)S(1)}, u32[]{:S(2)}, u32[]{:S(2)}) collective-permute-start(f32[8,128]{1,0:T(8,128)S(1)} %add_add_fusion.2.refs_0_), channel_id=1, source_target_pairs={{0,3},{1,2},{2,1},{3,0},{4,7},{5,6},{6,5},{7,4},{8,11},{9,10},{10,... | collective-permute-start | bytes 12296 | tf_op jit(solution)/shard_map/ppermute | solution.py:41
  30.9 3.7 %collective-permute-start.8 = (f32[8,128]{1,0:T(8,128)S(1)}, f32[8,128]{1,0:T(8,128)S(1)}, u32[]{:S(2)}, u32[]{:S(2)}) collective-permute-start(f32[8,128]{1,0:T(8,128)S(1)} %add_add_fusion.2.refs_0_), channel_id=1, source_target_pairs={{0,2},{1,3},{2,0},{3,1},{4,6},{5,7},{6,4},{7,5},{8,10},{9,11},{10,... | collective-permute-start | bytes 12296 | tf_op jit(solution)/shard_map/ppermute | solution.py:41
  32.5 2.1 %collective-permute-start.7 = (f32[8,128]{1,0:T(8,128)S(1)}, f32[8,128]{1,0:T(8,128)S(1)}, u32[]{:S(2)}, u32[]{:S(2)}) collective-permute-start(f32[8,128]{1,0:T(8,128)S(1)} %add_add_fusion.2.refs_0_), channel_id=1, source_target_pairs={{0,1},{1,0},{2,3},{3,2},{4,5},{5,4},{6,7},{7,6},{8,9},{9,8},{10,11... | collective-permute-start | bytes 12296 | tf_op jit(solution)/shard_map/ppermute | solution.py:41
  32.8 11.6 %collective-permute-start.10 = (f32[32,1536]{1,0:T(8,128)S(1)}, f32[32,1536]{1,0:T(8,128)S(1)}, u32[]{:S(2)}, u32[]{:S(2)}) collective-permute-start(f32[32,1536]{1,0:T(8,128)S(1)} %get-tuple-element.71), channel_id=1, source_target_pairs={{0,8},{1,9},{2,10},{3,11},{4,12},{5,13},{6,14},{7,15},{8,0},{9,1},... | collective-permute-start | bytes 589832 | tf_op jit(solution)/shard_map/ppermute | solution.py:41
  32.8 11.6 %collective-permute-start.11 = (f32[32,1536]{1,0:T(8,128)S(1)}, f32[32,1536]{1,0:T(8,128)S(1)}, u32[]{:S(2)}, u32[]{:S(2)}) collective-permute-start(f32[32,1536]{1,0:T(8,128)S(1)} %get-tuple-element.72), channel_id=1, source_target_pairs={{0,4},{1,5},{2,6},{3,7},{4,0},{5,1},{6,2},{7,3},{8,12},{9,13},{10,... | collective-permute-start | bytes 589832 | tf_op jit(solution)/shard_map/ppermute | solution.py:41
  38.4 7.3 %collective-permute-start.12 = (f32[32,1536]{1,0:T(8,128)S(1)}, f32[32,1536]{1,0:T(8,128)S(1)}, u32[]{:S(2)}, u32[]{:S(2)}) collective-permute-start(f32[32,1536]{1,0:T(8,128)S(1)} %get-tuple-element.74), channel_id=1, source_target_pairs={{0,2},{1,3},{2,0},{3,1},{4,6},{5,7},{6,4},{7,5},{8,10},{9,11},{10,... | collective-permute-start | bytes 589832 | tf_op jit(solution)/shard_map/ppermute | solution.py:41
  39.9 5.7 %collective-permute-start.13 = (f32[32,1536]{1,0:T(8,128)S(1)}, f32[32,1536]{1,0:T(8,128)S(1)}, u32[]{:S(2)}, u32[]{:S(2)}) collective-permute-start(f32[32,1536]{1,0:T(8,128)S(1)} %get-tuple-element.75), channel_id=1, source_target_pairs={{0,1},{1,0},{2,3},{3,2},{4,5},{5,4},{6,7},{7,6},{8,9},{9,8},{10,11... | collective-permute-start | bytes 589832 | tf_op jit(solution)/shard_map/ppermute | solution.py:41
  48.9 8.2 %collective-permute-start.16 = (f32[8,128]{1,0:T(8,128)S(1)}, f32[8,128]{1,0:T(8,128)S(1)}, u32[]{:S(2)}, u32[]{:S(2)}) collective-permute-start(f32[8,128]{1,0:T(8,128)S(1)} %get-tuple-element.78), channel_id=1, source_target_pairs={{0,12},{1,13},{2,14},{3,15},{4,8},{5,9},{6,10},{7,11},{8,4},{9,5},... | collective-permute-start | bytes 12296 | tf_op jit(solution)/shard_map/ppermute | solution.py:41
  50.8 6.3 %collective-permute-start.15 = (f32[8,128]{1,0:T(8,128)S(1)}, f32[8,128]{1,0:T(8,128)S(1)}, u32[]{:S(2)}, u32[]{:S(2)}) collective-permute-start(f32[8,128]{1,0:T(8,128)S(1)} %get-tuple-element.78), channel_id=1, source_target_pairs={{0,8},{1,9},{2,10},{3,11},{4,12},{5,13},{6,14},{7,15},{8,0},{9,1},... | collective-permute-start | bytes 12296 | tf_op jit(solution)/shard_map/ppermute | solution.py:41
  50.8 6.3 %collective-permute-start.14 = (f32[8,128]{1,0:T(8,128)S(1)}, f32[8,128]{1,0:T(8,128)S(1)}, u32[]{:S(2)}, u32[]{:S(2)}) collective-permute-start(f32[8,128]{1,0:T(8,128)S(1)} %get-tuple-element.78), channel_id=1, source_target_pairs={{0,4},{1,5},{2,6},{3,7},{4,0},{5,1},{6,2},{7,3},{8,12},{9,13},{10,... | collective-permute-start | bytes 12296 | tf_op jit(solution)/shard_map/ppermute | solution.py:41
  57.1 4.3 %collective-permute-start.19 = (f32[8,128]{1,0:T(8,128)S(1)}, f32[8,128]{1,0:T(8,128)S(1)}, u32[]{:S(2)}, u32[]{:S(2)}) collective-permute-start(f32[8,128]{1,0:T(8,128)S(1)} %add_add_fusion.1.refs_0_), channel_id=1, source_target_pairs={{0,3},{1,2},{2,1},{3,0},{4,7},{5,6},{6,5},{7,4},{8,11},{9,10},{10,... | collective-permute-start | bytes 12296 | tf_op jit(solution)/shard_map/ppermute | solution.py:41
  57.2 4.2 %collective-permute-start.18 = (f32[8,128]{1,0:T(8,128)S(1)}, f32[8,128]{1,0:T(8,128)S(1)}, u32[]{:S(2)}, u32[]{:S(2)}) collective-permute-start(f32[8,128]{1,0:T(8,128)S(1)} %add_add_fusion.1.refs_0_), channel_id=1, source_target_pairs={{0,2},{1,3},{2,0},{3,1},{4,6},{5,7},{6,4},{7,5},{8,10},{9,11},{10,... | collective-permute-start | bytes 12296 | tf_op jit(solution)/shard_map/ppermute | solution.py:41
  57.8 3.6 %collective-permute-start.17 = (f32[8,128]{1,0:T(8,128)S(1)}, f32[8,128]{1,0:T(8,128)S(1)}, u32[]{:S(2)}, u32[]{:S(2)}) collective-permute-start(f32[8,128]{1,0:T(8,128)S(1)} %add_add_fusion.1.refs_0_), channel_id=1, source_target_pairs={{0,1},{1,0},{2,3},{3,2},{4,5},{5,4},{6,7},{7,6},{8,9},{9,8},{10,11... | collective-permute-start | bytes 12296 | tf_op jit(solution)/shard_map/ppermute | solution.py:41
  59.1 11.4 %collective-permute-start.20 = (f32[32,1536]{1,0:T(8,128)S(1)}, f32[32,1536]{1,0:T(8,128)S(1)}, u32[]{:S(2)}, u32[]{:S(2)}) collective-permute-start(f32[32,1536]{1,0:T(8,128)S(1)} %get-tuple-element.89), channel_id=1, source_target_pairs={{0,8},{1,9},{2,10},{3,11},{4,12},{5,13},{6,14},{7,15},{8,0},{9,1},... | collective-permute-start | bytes 589832 | tf_op jit(solution)/shard_map/ppermute | solution.py:41
  59.4 11.0 %collective-permute-start.21 = (f32[32,1536]{1,0:T(8,128)S(1)}, f32[32,1536]{1,0:T(8,128)S(1)}, u32[]{:S(2)}, u32[]{:S(2)}) collective-permute-start(f32[32,1536]{1,0:T(8,128)S(1)} %get-tuple-element.90), channel_id=1, source_target_pairs={{0,4},{1,5},{2,6},{3,7},{4,0},{5,1},{6,2},{7,3},{8,12},{9,13},{10,... | collective-permute-start | bytes 589832 | tf_op jit(solution)/shard_map/ppermute | solution.py:41
  65.2 6.3 %collective-permute-start.22 = (f32[32,1536]{1,0:T(8,128)S(1)}, f32[32,1536]{1,0:T(8,128)S(1)}, u32[]{:S(2)}, u32[]{:S(2)}) collective-permute-start(f32[32,1536]{1,0:T(8,128)S(1)} %get-tuple-element.92), channel_id=1, source_target_pairs={{0,2},{1,3},{2,0},{3,1},{4,6},{5,7},{6,4},{7,5},{8,10},{9,11},{10,... | collective-permute-start | bytes 589832 | tf_op jit(solution)/shard_map/ppermute | solution.py:41
  66.5 5.0 %collective-permute-start.23 = (f32[32,1536]{1,0:T(8,128)S(1)}, f32[32,1536]{1,0:T(8,128)S(1)}, u32[]{:S(2)}, u32[]{:S(2)}) collective-permute-start(f32[32,1536]{1,0:T(8,128)S(1)} %get-tuple-element.93), channel_id=1, source_target_pairs={{0,1},{1,0},{2,3},{3,2},{4,5},{5,4},{6,7},{7,6},{8,9},{9,8},{10,11... | collective-permute-start | bytes 589832 | tf_op jit(solution)/shard_map/ppermute | solution.py:41
  74.5 5.4 %collective-permute-start.26 = (f32[8,128]{1,0:T(8,128)S(1)}, f32[8,128]{1,0:T(8,128)S(1)}, u32[]{:S(2)}, u32[]{:S(2)}) collective-permute-start(f32[8,128]{1,0:T(8,128)S(1)} %get-tuple-element.95), channel_id=1, source_target_pairs={{0,12},{1,13},{2,14},{3,15},{4,8},{5,9},{6,10},{7,11},{8,4},{9,5},... | collective-permute-start | bytes 12296 | tf_op jit(solution)/shard_map/ppermute | solution.py:41
  76.5 4.5 %collective-permute-start.25 = (f32[8,128]{1,0:T(8,128)S(1)}, f32[8,128]{1,0:T(8,128)S(1)}, u32[]{:S(2)}, u32[]{:S(2)}) collective-permute-start(f32[8,128]{1,0:T(8,128)S(1)} %get-tuple-element.95), channel_id=1, source_target_pairs={{0,8},{1,9},{2,10},{3,11},{4,12},{5,13},{6,14},{7,15},{8,0},{9,1},... | collective-permute-start | bytes 12296 | tf_op jit(solution)/shard_map/ppermute | solution.py:41
  76.5 4.5 %collective-permute-start.24 = (f32[8,128]{1,0:T(8,128)S(1)}, f32[8,128]{1,0:T(8,128)S(1)}, u32[]{:S(2)}, u32[]{:S(2)}) collective-permute-start(f32[8,128]{1,0:T(8,128)S(1)} %get-tuple-element.95), channel_id=1, source_target_pairs={{0,4},{1,5},{2,6},{3,7},{4,0},{5,1},{6,2},{7,3},{8,12},{9,13},{10,... | collective-permute-start | bytes 12296 | tf_op jit(solution)/shard_map/ppermute | solution.py:41
  81.0 3.1 %collective-permute-start.29 = (f32[8,128]{1,0:T(8,128)S(1)}, f32[8,128]{1,0:T(8,128)S(1)}, u32[]{:S(2)}, u32[]{:S(2)}) collective-permute-start(f32[8,128]{1,0:T(8,128)S(1)} %add_add_fusion.refs_0_), channel_id=1, source_target_pairs={{0,3},{1,2},{2,1},{3,0},{4,7},{5,6},{6,5},{7,4},{8,11},{9,10},{10,... | collective-permute-start | bytes 12296 | tf_op jit(solution)/shard_map/ppermute | solution.py:41
  81.1 3.7 %collective-permute-start.28 = (f32[8,128]{1,0:T(8,128)S(1)}, f32[8,128]{1,0:T(8,128)S(1)}, u32[]{:S(2)}, u32[]{:S(2)}) collective-permute-start(f32[8,128]{1,0:T(8,128)S(1)} %add_add_fusion.refs_0_), channel_id=1, source_target_pairs={{0,2},{1,3},{2,0},{3,1},{4,6},{5,7},{6,4},{7,5},{8,10},{9,11},{10,... | collective-permute-start | bytes 12296 | tf_op jit(solution)/shard_map/ppermute | solution.py:41
  82.0 2.8 %collective-permute-start.27 = (f32[8,128]{1,0:T(8,128)S(1)}, f32[8,128]{1,0:T(8,128)S(1)}, u32[]{:S(2)}, u32[]{:S(2)}) collective-permute-start(f32[8,128]{1,0:T(8,128)S(1)} %add_add_fusion.refs_0_), channel_id=1, source_target_pairs={{0,1},{1,0},{2,3},{3,2},{4,5},{5,4},{6,7},{7,6},{8,9},{9,8},{10,11... | collective-permute-start | bytes 12296 | tf_op jit(solution)/shard_map/ppermute | solution.py:41

commit v11 on v10

--- a/solution.py
+++ b/solution.py
@@ -144,30 +144,36 @@
         rows_ref[g * LANES : (g + 1) * LANES, :] = jnp.concatenate(pieces, axis=0).T
 
 
-def gathered_into(unroll, row_ref, part_ref, rows_ref, picked, outs):
-    count = picked.shape[0]
-    columns = outs[0].shape[0]
-
-    def pick(i, carry):
-        for u in range(unroll):
-            m = i * unroll + u
-            picked[pl.ds(m, 1), :] = rows_ref[pl.ds(row_ref[m], 1), :]
-        return carry
-
-    lax.fori_loop(0, count // unroll, pick, 0)
-    tiles_out = outs[0].shape[1] // LANES
-    for g in range(count // LANES):
-        y = picked[g * LANES : (g + 1) * LANES, :].T
-        part = jnp.broadcast_to(part_ref[g : g + 1, :], (columns, LANES))
+def gathered_into(row_ref, part_ref, rows_ref, picked, outs):
+    columns, width = outs[0].shape
+    tiles_out = width // LANES
+
+    def turn(g, t, out):
+        y = picked[pl.ds(pl.multiple_of(g * LANES, LANES), LANES), :].T
+        part = jnp.broadcast_to(part_ref[pl.ds(g, 1), :], (columns, LANES))
         value = y[:columns]
         for b in range(1, PACK):
             value = jnp.where(part == b, y[b * columns : (b + 1) * columns], value)
-        out, t = outs[g // tiles_out], g % tiles_out
-        out[:, t * LANES : (t + 1) * LANES] = value.astype(out.dtype)
+        at = pl.ds(pl.multiple_of(t * LANES, LANES), LANES)
+        out[:, at] = value.astype(out.dtype)
+
+    for n, out in enumerate(outs):
+        first = n * tiles_out
+
+        def step(i, carry, first=first, out=out):
+            before = jnp.maximum(i - 1, 0)
+            turn(first + before, before, out)
+            base = (first + i) * LANES
+            for u in range(LANES):
+                picked[pl.ds(base + u, 1), :] = rows_ref[pl.ds(row_ref[base + u], 1), :]
+            return carry
+
+        lax.fori_loop(0, tiles_out, step, 0)
+        turn(first + tiles_out - 1, tiles_out - 1, out)
 
 
 def gather_kernel(row_ref, part_ref, rows_ref, *rest):
-    gathered_into(128, row_ref, part_ref, rows_ref, rest[-1], rest[:-1])
+    gathered_into(row_ref, part_ref, rows_ref, rest[-1], rest[:-1])
 
 
 def gather_colours(rows, row_list, part_list, count):
@@ -209,7 +215,7 @@
     if make_rows:
         rows_ref = refs[0]
         transposed_into(block_ref, rows_ref)
-    gathered_into(128, row_ref, part_ref, rows_ref, picked, outs)
+    gathered_into(row_ref, part_ref, rows_ref, picked, outs)
     for copy in copies:
         copy.wait()
 

time: 87.4 us -> 87.3 us (level)
  transfers between devices with their start and end apart: 30 -> 30, of which waited for: 11 -> 11; matrix products, arithmetic and copies ran while one was open for 0% -> 0% of each run, Pallas kernels for 27% -> 26%
where the time goes in v11:
time: 87.3 us; the launch traced here: 86.4 us
  Pallas kernels  38.6 us (44%)
  starting transfers between devices  32.6 us (37%)
  waiting for transfers between devices  13.2 us (15%)
  between operations  1.05 us (1%)
    ppermute x30, starting transfers between devices, swapped(): return lax.ppermute(x, 'dom', [(i, i ^ mask) for i in range(size)])  32.6 us
    pallas_call x4, Pallas kernels, gather_colours(): pl.pallas_call(gather_kernel, out_shape=[vmem_out((columns, indices // co...  14.1 us
    ppermute x30, waiting for transfers between devices, swapped(): return lax.ppermute(x, 'dom', [(i, i ^ mask) for i in range(size)])  13.2 us
    pallas_call x3, Pallas kernels, product(): pl.pallas_call(functools.partial(product_kernel, len(ghosts), group, with...  8.91 us
    pallas_call x2, Pallas kernels, start_gather(): pl.pallas_call(functools.partial(start_kernel, count, first, make_rows),...  8.54 us
    pallas_call x2, Pallas kernels, later_own(): pl.pallas_call(functools.partial(later_own_kernel, total_states), out_sha...  4.15 us
    pallas_call x1, Pallas kernels, final(): pl.pallas_call(functools.partial(final_kernel, total_states), out_shape=j...  2.27 us
  transfers between devices with their start and end apart: 30, of which 11 were waited for; matrix products, arithmetic and copies ran while one was open for 0% of the time, Pallas kernels for 26%

profile of v11, /device:TPU:0, one launch (start us, length us, event | category | flops | bytes accessed | tf_op | source)
XLA Modules:
  0.0 86.4 jit_solution(14341426132719066198)
XLA Ops:
  0.0 0.8 add_select_fusion
  0.8 0.1 slice_reduce_fusion.1
  1.0 4.9 %start_gather.2 = (bf16[32,1536]{1,0:T(8,128)(2,1)S(1)}, bf16[32,1536]{1,0:T(8,128)(2,1)S(1)}, bf16[256,128,128]{2,1,0:T(8,128)(2,1)S(1)}, f32[2048,128]{1,0:T(8,128)S(1)}, bf16[32,8192]{1,0:T(8,128)(2,1)S(1)}) custom-call(s32[3072]{0:T(1024)S(1)} %pad_add_fusion.row_ref, s32[24,128]{1,0:T(8,128)S(1)} %pad_add_fusion.1.part_ref, ...), custom_call_target="tpu_custom_call" | custom-call | bytes 1024 | tf_op jit(solution)/shard_map/start_gather/pallas_call | solution.py:232
  5.9 4.1 %collective-permute-start = (bf16[32,1536]{1,0:T(8,128)(2,1)S(1)}, bf16[32,1536]{1,0:T(8,128)(2,1)S(1)}, u32[]{:S(2)}, u32[]{:S(2)}) collective-permute-start(bf16[32,1536]{1,0:T(8,128)(2,1)S(1)} %get-tuple-element.54), channel_id=1, source_target_pairs={{0,8},{1,9},{2,10},{3,11},{4,12},{5,13},{6,14},{7,15},{8,0},{9,1},... | collective-permute-start | bytes 294920 | tf_op jit(solution)/shard_map/ppermute | solution.py:41
  10.0 1.6 %collective-permute-start.1 = (bf16[32,1536]{1,0:T(8,128)(2,1)S(1)}, bf16[32,1536]{1,0:T(8,128)(2,1)S(1)}, u32[]{:S(2)}, u32[]{:S(2)}) collective-permute-start(bf16[32,1536]{1,0:T(8,128)(2,1)S(1)} %get-tuple-element.55), channel_id=1, source_target_pairs={{0,4},{1,5},{2,6},{3,7},{4,0},{5,1},{6,2},{7,3},{8,12},{9,13},{10,... | collective-permute-start | bytes 294920 | tf_op jit(solution)/shard_map/ppermute | solution.py:41
  11.6 3.7 %start_gather.3 = (bf16[32,1536]{1,0:T(8,128)(2,1)S(1)}, bf16[32,1536]{1,0:T(8,128)(2,1)S(1)}, bf16[64,128,128]{2,1,0:T(8,128)(2,1)S(1)}) custom-call(s32[3072]{0:T(1024)S(1)} %pad_add_fusion.2.row_ref, s32[24,128]{1,0:T(8,128)S(1)} %pad_add_fusion.3.part_ref, f32[2048,128]{1,0:T(8,128)S(1)} %get-tuple-element.52.source_ref, bf16[320,128,128]{2,1,0:T(8,128)(2,1)} %tiles_ref.3), custom_call_target="tpu_custom_call" | custom-call | bytes 1024 | tf_op jit(solution)/shard_map/start_gather/pallas_call | solution.py:232
  15.2 0.0 copy-start
  15.2 0.0 copy-start.1
  15.3 1.6 %collective-permute-start.2 = (bf16[32,1536]{1,0:T(8,128)(2,1)S(1)}, bf16[32,1536]{1,0:T(8,128)(2,1)S(1)}, u32[]{:S(2)}, u32[]{:S(2)}) collective-permute-start(bf16[32,1536]{1,0:T(8,128)(2,1)S(1)} %get-tuple-element.56), channel_id=1, source_target_pairs={{0,2},{1,3},{2,0},{3,1},{4,6},{5,7},{6,4},{7,5},{8,10},{9,11},{10,... | collective-permute-start | bytes 294920 | tf_op jit(solution)/shard_map/ppermute | solution.py:41
  17.5 0.7 first_own.1.refs_4_
  18.2 0.0 collective-permute-done.refs_5_
  18.2 0.0 collective-permute-done.1.refs_6_
  18.2 1.8 %collective-permute-done.2.refs_7_ = bf16[32,1536]{1,0:T(8,128)(2,1)S(1)} collective-permute-done((bf16[32,1536]{1,0:T(8,128)(2,1)S(1)}, bf16[32,1536]{1,0:T(8,128)(2,1)S(1)}, u32[]{:S(2)}, u32[]{:S(2)}) %collective-permute-start.2) | collective-permute-done | bytes 98336 | tf_op jit(solution)/shard_map/ppermute | solution.py:41
  19.9 0.0 collective-permute-done.3.refs_8_
  20.0 2.7 %product.3 = (bf16[96,8192]{1,0:T(8,128)(2,1)S(1)}, f32[8,128]{1,0:T(8,128)S(1)}, f32[2048,128]{1,0:T(8,128)S(1)}) custom-call(s32[320]{0:T(512)S(1)} %copy-done, s32[320]{0:T(512)S(1)} %copy-done.1, s32[1]{0:T(128)S(6)} %copy.7.refs_2_, bf16[32,8192]{1,0:T(8,128)(2,1)S(1)} %get-tuple-element.51.block_ref.refs_3_, f32[32,8192]{1,0:T(8,128)S(1)} %first_own.1.refs_4_, ...), custom_call_target="tpu_custom_call" | custom-call | bytes 1024 | tf_op jit(solution)/shard_map/product/pallas_call | solution.py:378
  22.6 0.1 collective-permute-start.6
  22.7 1.9 %collective-permute-start.5 = (f32[8,128]{1,0:T(8,128)S(1)}, f32[8,128]{1,0:T(8,128)S(1)}, u32[]{:S(2)}, u32[]{:S(2)}) collective-permute-start(f32[8,128]{1,0:T(8,128)S(1)} %get-tuple-element.60), channel_id=1, source_target_pairs={{0,8},{1,9},{2,10},{3,11},{4,12},{5,13},{6,14},{7,15},{8,0},{9,1},... | collective-permute-start | bytes 12296 | tf_op jit(solution)/shard_map/ppermute | solution.py:41
  24.6 2.5 %collective-permute-start.4 = (f32[8,128]{1,0:T(8,128)S(1)}, f32[8,128]{1,0:T(8,128)S(1)}, u32[]{:S(2)}, u32[]{:S(2)}) collective-permute-start(f32[8,128]{1,0:T(8,128)S(1)} %get-tuple-element.60), channel_id=1, source_target_pairs={{0,4},{1,5},{2,6},{3,7},{4,0},{5,1},{6,2},{7,3},{8,12},{9,13},{10,... | collective-permute-start | bytes 12296 | tf_op jit(solution)/shard_map/ppermute | solution.py:41
  27.1 3.5 %gather_rows.4 = (f32[32,1536]{1,0:T(8,128)S(1)}, f32[32,1536]{1,0:T(8,128)S(1)}) custom-call(s32[3072]{0:T(1024)S(1)} %pad_add_fusion.row_ref, s32[24,128]{1,0:T(8,128)S(1)} %pad_add_fusion.1.part_ref, f32[2048,128]{1,0:T(8,128)S(1)} %get-tuple-element.73.rows_ref), custom_call_target="tpu_custom_call" | custom-call | bytes 1024 | tf_op jit(solution)/shard_map/gather_rows/pallas_call | solution.py:182
  30.7 0.0 collective-permute-done.4
  30.7 0.1 collective-permute-start.9
  30.8 1.6 %collective-permute-start.8 = (f32[8,128]{1,0:T(8,128)S(1)}, f32[8,128]{1,0:T(8,128)S(1)}, u32[]{:S(2)}, u32[]{:S(2)}) collective-permute-start(f32[8,128]{1,0:T(8,128)S(1)} %add_add_fusion.2.refs_0_), channel_id=1, source_target_pairs={{0,2},{1,3},{2,0},{3,1},{4,6},{5,7},{6,4},{7,5},{8,10},{9,11},{10,... | collective-permute-start | bytes 12296 | tf_op jit(solution)/shard_map/ppermute | solution.py:41
  32.3 0.3 collective-permute-start.7
  32.6 0.9 %collective-permute-start.11 = (f32[32,1536]{1,0:T(8,128)S(1)}, f32[32,1536]{1,0:T(8,128)S(1)}, u32[]{:S(2)}, u32[]{:S(2)}) collective-permute-start(f32[32,1536]{1,0:T(8,128)S(1)} %get-tuple-element.72), channel_id=1, source_target_pairs={{0,4},{1,5},{2,6},{3,7},{4,0},{5,1},{6,2},{7,3},{8,12},{9,13},{10,... | collective-permute-start | bytes 589832 | tf_op jit(solution)/shard_map/ppermute | solution.py:41
  33.5 0.2 collective-permute-done.9.refs_3_
  33.8 0.7 collective-permute-done.8.refs_2_
  34.4 0.0 collective-permute-done.7.refs_1_
  34.4 3.5 %gather_rows.5 = (f32[32,1536]{1,0:T(8,128)S(1)}, f32[32,1536]{1,0:T(8,128)S(1)}) custom-call(s32[3072]{0:T(1024)S(1)} %pad_add_fusion.2.row_ref, s32[24,128]{1,0:T(8,128)S(1)} %pad_add_fusion.3.part_ref, f32[2048,128]{1,0:T(8,128)S(1)} %get-tuple-element.73.rows_ref), custom_call_target="tpu_custom_call" | custom-call | bytes 1024 | tf_op jit(solution)/shard_map/gather_rows/pallas_call | solution.py:182
  38.0 1.6 %collective-permute-start.12 = (f32[32,1536]{1,0:T(8,128)S(1)}, f32[32,1536]{1,0:T(8,128)S(1)}, u32[]{:S(2)}, u32[]{:S(2)}) collective-permute-start(f32[32,1536]{1,0:T(8,128)S(1)} %get-tuple-element.74), channel_id=1, source_target_pairs={{0,2},{1,3},{2,0},{3,1},{4,6},{5,7},{6,4},{7,5},{8,10},{9,11},{10,... | collective-permute-start | bytes 589832 | tf_op jit(solution)/shard_map/ppermute | solution.py:41
  39.5 0.0 collective-permute-start.13
  39.5 2.1 %later_own.2 = (bf16[32,8192]{1,0:T(8,128)(2,1)S(1)}, bf16[96,96]{1,0:T(8,128)(2,1)S(1)}, f32[32,8192]{1,0:T(8,128)S(1)}) custom-call(f32[8,128]{1,0:T(8,128)S(1)} %add_add_fusion.2.refs_0_, f32[8,128]{1,0:T(8,128)S(1)} %collective-permute-done.7.refs_1_, f32[8,128]{1,0:T(8,128)S(1)} %collective-permute-done.8.refs_2_, ...), custom_call_target="tpu_custom_call" | custom-call | bytes 1024 | tf_op jit(solution)/shard_map/later_own/pallas_call | solution.py:279
  41.6 2.6 %collective-permute-done.10.refs_5_ = f32[32,1536]{1,0:T(8,128)S(1)} collective-permute-done((f32[32,1536]{1,0:T(8,128)S(1)}, f32[32,1536]{1,0:T(8,128)S(1)}, u32[]{:S(2)}, u32[]{:S(2)}) %collective-permute-start.10) | collective-permute-done | bytes 196640 | tf_op jit(solution)/shard_map/ppermute | solution.py:41
  44.2 0.0 collective-permute-done.11.refs_6_
  44.2 1.1 %collective-permute-done.12.refs_7_ = f32[32,1536]{1,0:T(8,128)S(1)} collective-permute-done((f32[32,1536]{1,0:T(8,128)S(1)}, f32[32,1536]{1,0:T(8,128)S(1)}, u32[]{:S(2)}, u32[]{:S(2)}) %collective-permute-start.12) | collective-permute-done | bytes 196640 | tf_op jit(solution)/shard_map/ppermute | solution.py:41
  45.3 0.0 collective-permute-done.13.refs_8_
  45.3 3.2 %product.4 = (bf16[96,8192]{1,0:T(8,128)(2,1)S(1)}, f32[8,128]{1,0:T(8,128)S(1)}, f32[2048,128]{1,0:T(8,128)S(1)}) custom-call(s32[320]{0:T(512)S(1)} %copy-done, s32[320]{0:T(512)S(1)} %copy-done.1, s32[1]{0:T(128)S(6)} %copy.7.refs_2_, bf16[32,8192]{1,0:T(8,128)(2,1)S(1)} %get-tuple-element.69.refs_3_, f32[32,8192]{1,0:T(8,128)S(1)} %get-tuple-element.70.refs_4_, ...), custom_call_target="tpu_custom_call" | custom-call | bytes 1024 | tf_op jit(solution)/shard_map/product/pallas_call | solution.py:378
  48.5 1.9 %collective-permute-start.16 = (f32[8,128]{1,0:T(8,128)S(1)}, f32[8,128]{1,0:T(8,128)S(1)}, u32[]{:S(2)}, u32[]{:S(2)}) collective-permute-start(f32[8,128]{1,0:T(8,128)S(1)} %get-tuple-element.78), channel_id=1, source_target_pairs={{0,12},{1,13},{2,14},{3,15},{4,8},{5,9},{6,10},{7,11},{8,4},{9,5},... | collective-permute-start | bytes 12296 | tf_op jit(solution)/shard_map/ppermute | solution.py:41
  50.4 2.6 %collective-permute-start.14 = (f32[8,128]{1,0:T(8,128)S(1)}, f32[8,128]{1,0:T(8,128)S(1)}, u32[]{:S(2)}, u32[]{:S(2)}) collective-permute-start(f32[8,128]{1,0:T(8,128)S(1)} %get-tuple-element.78), channel_id=1, source_target_pairs={{0,4},{1,5},{2,6},{3,7},{4,0},{5,1},{6,2},{7,3},{8,12},{9,13},{10,... | collective-permute-start | bytes 12296 | tf_op jit(solution)/shard_map/ppermute | solution.py:41
  53.0 3.5 %gather_rows.6 = (f32[32,1536]{1,0:T(8,128)S(1)}, f32[32,1536]{1,0:T(8,128)S(1)}) custom-call(s32[3072]{0:T(1024)S(1)} %pad_add_fusion.row_ref, s32[24,128]{1,0:T(8,128)S(1)} %pad_add_fusion.1.part_ref, f32[2048,128]{1,0:T(8,128)S(1)} %get-tuple-element.91.rows_ref), custom_call_target="tpu_custom_call" | custom-call | bytes 1024 | tf_op jit(solution)/shard_map/gather_rows/pallas_call | solution.py:182
  56.5 0.0 collective-permute-done.16
  56.5 0.0 collective-permute-done.14
  56.5 0.1 collective-permute-start.19
  56.6 0.6 collective-permute-start.18
  57.2 1.2 %collective-permute-start.17 = (f32[8,128]{1,0:T(8,128)S(1)}, f32[8,128]{1,0:T(8,128)S(1)}, u32[]{:S(2)}, u32[]{:S(2)}) collective-permute-start(f32[8,128]{1,0:T(8,128)S(1)} %add_add_fusion.1.refs_0_), channel_id=1, source_target_pairs={{0,1},{1,0},{2,3},{3,2},{4,5},{5,4},{6,7},{7,6},{8,9},{9,8},{10,11... | collective-permute-start | bytes 12296 | tf_op jit(solution)/shard_map/ppermute | solution.py:41
  58.5 0.3 collective-permute-start.20
  58.8 2.0 %collective-permute-start.21 = (f32[32,1536]{1,0:T(8,128)S(1)}, f32[32,1536]{1,0:T(8,128)S(1)}, u32[]{:S(2)}, u32[]{:S(2)}) collective-permute-start(f32[32,1536]{1,0:T(8,128)S(1)} %get-tuple-element.90), channel_id=1, source_target_pairs={{0,4},{1,5},{2,6},{3,7},{4,0},{5,1},{6,2},{7,3},{8,12},{9,13},{10,... | collective-permute-start | bytes 589832 | tf_op jit(solution)/shard_map/ppermute | solution.py:41
  60.8 0.0 collective-permute-done.18.refs_2_
  60.8 0.0 collective-permute-done.17.refs_1_
  60.8 3.5 %gather_rows.7 = (f32[32,1536]{1,0:T(8,128)S(1)}, f32[32,1536]{1,0:T(8,128)S(1)}) custom-call(s32[3072]{0:T(1024)S(1)} %pad_add_fusion.2.row_ref, s32[24,128]{1,0:T(8,128)S(1)} %pad_add_fusion.3.part_ref, f32[2048,128]{1,0:T(8,128)S(1)} %get-tuple-element.91.rows_ref), custom_call_target="tpu_custom_call" | custom-call | bytes 1024 | tf_op jit(solution)/shard_map/gather_rows/pallas_call | solution.py:182
  64.4 1.4 %collective-permute-start.22 = (f32[32,1536]{1,0:T(8,128)S(1)}, f32[32,1536]{1,0:T(8,128)S(1)}, u32[]{:S(2)}, u32[]{:S(2)}) collective-permute-start(f32[32,1536]{1,0:T(8,128)S(1)} %get-tuple-element.92), channel_id=1, source_target_pairs={{0,2},{1,3},{2,0},{3,1},{4,6},{5,7},{6,4},{7,5},{8,10},{9,11},{10,... | collective-permute-start | bytes 589832 | tf_op jit(solution)/shard_map/ppermute | solution.py:41
  65.7 2.1 %later_own.3 = (bf16[32,8192]{1,0:T(8,128)(2,1)S(1)}, bf16[96,96]{1,0:T(8,128)(2,1)S(1)}, f32[32,8192]{1,0:T(8,128)S(1)}) custom-call(f32[8,128]{1,0:T(8,128)S(1)} %add_add_fusion.1.refs_0_, f32[8,128]{1,0:T(8,128)S(1)} %collective-permute-done.17.refs_1_, f32[8,128]{1,0:T(8,128)S(1)} %collective-permute-done.18.refs_2_, ...), custom_call_target="tpu_custom_call" | custom-call | bytes 1024 | tf_op jit(solution)/shard_map/later_own/pallas_call | solution.py:279
  67.8 2.0 %collective-permute-done.20.refs_5_ = f32[32,1536]{1,0:T(8,128)S(1)} collective-permute-done((f32[32,1536]{1,0:T(8,128)S(1)}, f32[32,1536]{1,0:T(8,128)S(1)}, u32[]{:S(2)}, u32[]{:S(2)}) %collective-permute-start.20) | collective-permute-done | bytes 196640 | tf_op jit(solution)/shard_map/ppermute | solution.py:41
  69.8 0.9 collective-permute-done.22.refs_7_
  70.7 3.0 %product.5 = (bf16[96,8192]{1,0:T(8,128)(2,1)S(1)}, f32[8,128]{1,0:T(8,128)S(1)}) custom-call(s32[320]{0:T(512)S(1)} %copy-done, s32[320]{0:T(512)S(1)} %copy-done.1, s32[1]{0:T(128)S(6)} %copy.7.refs_2_, bf16[32,8192]{1,0:T(8,128)(2,1)S(1)} %get-tuple-element.87.refs_3_, f32[32,8192]{1,0:T(8,128)S(1)} %get-tuple-element.88.refs_4_, ...), custom_call_target="tpu_custom_call" | custom-call | bytes 1024 | tf_op jit(solution)/shard_map/product/pallas_call | solution.py:378
  73.7 2.0 %collective-permute-start.26 = (f32[8,128]{1,0:T(8,128)S(1)}, f32[8,128]{1,0:T(8,128)S(1)}, u32[]{:S(2)}, u32[]{:S(2)}) collective-permute-start(f32[8,128]{1,0:T(8,128)S(1)} %get-tuple-element.95), channel_id=1, source_target_pairs={{0,12},{1,13},{2,14},{3,15},{4,8},{5,9},{6,10},{7,11},{8,4},{9,5},... | collective-permute-start | bytes 12296 | tf_op jit(solution)/shard_map/ppermute | solution.py:41
  75.7 2.4 %collective-permute-start.24 = (f32[8,128]{1,0:T(8,128)S(1)}, f32[8,128]{1,0:T(8,128)S(1)}, u32[]{:S(2)}, u32[]{:S(2)}) collective-permute-start(f32[8,128]{1,0:T(8,128)S(1)} %get-tuple-element.95), channel_id=1, source_target_pairs={{0,4},{1,5},{2,6},{3,7},{4,0},{5,1},{6,2},{7,3},{8,12},{9,13},{10,... | collective-permute-start | bytes 12296 | tf_op jit(solution)/shard_map/ppermute | solution.py:41
  78.1 1.0 %collective-permute-done.26 = f32[8,128]{1,0:T(8,128)S(1)} collective-permute-done((f32[8,128]{1,0:T(8,128)S(1)}, f32[8,128]{1,0:T(8,128)S(1)}, u32[]{:S(2)}, u32[]{:S(2)}) %collective-permute-start.26) | collective-permute-done | bytes 4128 | tf_op jit(solution)/shard_map/ppermute | solution.py:41
  79.1 1.1 %collective-permute-done.25 = f32[8,128]{1,0:T(8,128)S(1)} collective-permute-done((f32[8,128]{1,0:T(8,128)S(1)}, f32[8,128]{1,0:T(8,128)S(1)}, u32[]{:S(2)}, u32[]{:S(2)}) %collective-permute-start.25) | collective-permute-done | bytes 4128 | tf_op jit(solution)/shard_map/ppermute | solution.py:41
  80.2 0.1 collective-permute-start.29
  80.3 0.9 collective-permute-start.28
  81.2 1.0 %collective-permute-start.27 = (f32[8,128]{1,0:T(8,128)S(1)}, f32[8,128]{1,0:T(8,128)S(1)}, u32[]{:S(2)}, u32[]{:S(2)}) collective-permute-start(f32[8,128]{1,0:T(8,128)S(1)} %add_add_fusion.refs_0_), channel_id=1, source_target_pairs={{0,1},{1,0},{2,3},{3,2},{4,5},{5,4},{6,7},{7,6},{8,9},{9,8},{10,11... | collective-permute-start | bytes 12296 | tf_op jit(solution)/shard_map/ppermute | solution.py:41
  82.2 1.2 %collective-permute-done.29.refs_3_ = f32[8,128]{1,0:T(8,128)S(1)} collective-permute-done((f32[8,128]{1,0:T(8,128)S(1)}, f32[8,128]{1,0:T(8,128)S(1)}, u32[]{:S(2)}, u32[]{:S(2)}) %collective-permute-start.29) | collective-permute-done | bytes 4128 | tf_op jit(solution)/shard_map/ppermute | solution.py:41
  83.3 0.7 collective-permute-done.28.refs_2_
  84.0 2.3 %final.1 = f32[32,8192]{1,0:T(8,128)} custom-call(f32[8,128]{1,0:T(8,128)S(1)} %add_add_fusion.refs_0_, f32[8,128]{1,0:T(8,128)S(1)} %collective-permute-done.27.refs_1_, f32[8,128]{1,0:T(8,128)S(1)} %collective-permute-done.28.refs_2_, f32[8,128]{1,0:T(8,128)S(1)} %collective-permute-done.29.refs_3_, bf16[96,8192]{1,0:T(8,128)(2,1)S(1)} %get-tuple-element.96.refs_4_), custom_call_target="tpu_custom_call" | custom-call | bytes 1024 | tf_op jit(solution)/shard_map/final/pallas_call | solution.py:405
  (22 shorter events, 0.1 us)
Async XLA Ops:
  5.9 12.3 %collective-permute-start = (bf16[32,1536]{1,0:T(8,128)(2,1)S(1)}, bf16[32,1536]{1,0:T(8,128)(2,1)S(1)}, u32[]{:S(2)}, u32[]{:S(2)}) collective-permute-start(bf16[32,1536]{1,0:T(8,128)(2,1)S(1)} %get-tuple-element.54), channel_id=1, source_target_pairs={{0,8},{1,9},{2,10},{3,11},{4,12},{5,13},{6,14},{7,15},{8,0},{9,1},... | collective-permute-start | bytes 294920 | tf_op jit(solution)/shard_map/ppermute | solution.py:41
  10.0 8.2 %collective-permute-start.1 = (bf16[32,1536]{1,0:T(8,128)(2,1)S(1)}, bf16[32,1536]{1,0:T(8,128)(2,1)S(1)}, u32[]{:S(2)}, u32[]{:S(2)}) collective-permute-start(bf16[32,1536]{1,0:T(8,128)(2,1)S(1)} %get-tuple-element.55), channel_id=1, source_target_pairs={{0,4},{1,5},{2,6},{3,7},{4,0},{5,1},{6,2},{7,3},{8,12},{9,13},{10,... | collective-permute-start | bytes 294920 | tf_op jit(solution)/shard_map/ppermute | solution.py:41
  15.2 4.7 %copy-start = (s32[320]{0:T(512)S(1)}, s32[320]{0:T(512)}, u32[]{:S(2)}) copy-start(s32[320]{0:T(512)} %refs_0_.5) | copy-start | bytes 3844
  15.2 4.7 %copy-start.1 = (s32[320]{0:T(512)S(1)}, s32[320]{0:T(512)}, u32[]{:S(2)}) copy-start(s32[320]{0:T(512)} %refs_1_.5) | copy-start | bytes 3844
  15.3 4.7 %collective-permute-start.2 = (bf16[32,1536]{1,0:T(8,128)(2,1)S(1)}, bf16[32,1536]{1,0:T(8,128)(2,1)S(1)}, u32[]{:S(2)}, u32[]{:S(2)}) collective-permute-start(bf16[32,1536]{1,0:T(8,128)(2,1)S(1)} %get-tuple-element.56), channel_id=1, source_target_pairs={{0,2},{1,3},{2,0},{3,1},{4,6},{5,7},{6,4},{7,5},{8,10},{9,11},{10,... | collective-permute-start | bytes 294920 | tf_op jit(solution)/shard_map/ppermute | solution.py:41
  16.8 3.1 %collective-permute-start.3 = (bf16[32,1536]{1,0:T(8,128)(2,1)S(1)}, bf16[32,1536]{1,0:T(8,128)(2,1)S(1)}, u32[]{:S(2)}, u32[]{:S(2)}) collective-permute-start(bf16[32,1536]{1,0:T(8,128)(2,1)S(1)} %get-tuple-element.57), channel_id=1, source_target_pairs={{0,1},{1,0},{2,3},{3,2},{4,5},{5,4},{6,7},{7,6},{8,9},{9,8},{10,11... | collective-permute-start | bytes 294920 | tf_op jit(solution)/shard_map/ppermute | solution.py:41
  22.6 8.0 %collective-permute-start.6 = (f32[8,128]{1,0:T(8,128)S(1)}, f32[8,128]{1,0:T(8,128)S(1)}, u32[]{:S(2)}, u32[]{:S(2)}) collective-permute-start(f32[8,128]{1,0:T(8,128)S(1)} %get-tuple-element.60), channel_id=1, source_target_pairs={{0,12},{1,13},{2,14},{3,15},{4,8},{5,9},{6,10},{7,11},{8,4},{9,5},... | collective-permute-start | bytes 12296 | tf_op jit(solution)/shard_map/ppermute | solution.py:41
  22.7 7.9 %collective-permute-start.5 = (f32[8,128]{1,0:T(8,128)S(1)}, f32[8,128]{1,0:T(8,128)S(1)}, u32[]{:S(2)}, u32[]{:S(2)}) collective-permute-start(f32[8,128]{1,0:T(8,128)S(1)} %get-tuple-element.60), channel_id=1, source_target_pairs={{0,8},{1,9},{2,10},{3,11},{4,12},{5,13},{6,14},{7,15},{8,0},{9,1},... | collective-permute-start | bytes 12296 | tf_op jit(solution)/shard_map/ppermute | solution.py:41
  24.6 6.0 %collective-permute-start.4 = (f32[8,128]{1,0:T(8,128)S(1)}, f32[8,128]{1,0:T(8,128)S(1)}, u32[]{:S(2)}, u32[]{:S(2)}) collective-permute-start(f32[8,128]{1,0:T(8,128)S(1)} %get-tuple-element.60), channel_id=1, source_target_pairs={{0,4},{1,5},{2,6},{3,7},{4,0},{5,1},{6,2},{7,3},{8,12},{9,13},{10,... | collective-permute-start | bytes 12296 | tf_op jit(solution)/shard_map/ppermute | solution.py:41
  30.7 3.1 %collective-permute-start.9 = (f32[8,128]{1,0:T(8,128)S(1)}, f32[8,128]{1,0:T(8,128)S(1)}, u32[]{:S(2)}, u32[]{:S(2)}) collective-permute-start(f32[8,128]{1,0:T(8,128)S(1)} %add_add_fusion.2.refs_0_), channel_id=1, source_target_pairs={{0,3},{1,2},{2,1},{3,0},{4,7},{5,6},{6,5},{7,4},{8,11},{9,10},{10,... | collective-permute-start | bytes 12296 | tf_op jit(solution)/shard_map/ppermute | solution.py:41
  30.8 3.7 %collective-permute-start.8 = (f32[8,128]{1,0:T(8,128)S(1)}, f32[8,128]{1,0:T(8,128)S(1)}, u32[]{:S(2)}, u32[]{:S(2)}) collective-permute-start(f32[8,128]{1,0:T(8,128)S(1)} %add_add_fusion.2.refs_0_), channel_id=1, source_target_pairs={{0,2},{1,3},{2,0},{3,1},{4,6},{5,7},{6,4},{7,5},{8,10},{9,11},{10,... | collective-permute-start | bytes 12296 | tf_op jit(solution)/shard_map/ppermute | solution.py:41
  32.3 2.1 %collective-permute-start.7 = (f32[8,128]{1,0:T(8,128)S(1)}, f32[8,128]{1,0:T(8,128)S(1)}, u32[]{:S(2)}, u32[]{:S(2)}) collective-permute-start(f32[8,128]{1,0:T(8,128)S(1)} %add_add_fusion.2.refs_0_), channel_id=1, source_target_pairs={{0,1},{1,0},{2,3},{3,2},{4,5},{5,4},{6,7},{7,6},{8,9},{9,8},{10,11... | collective-permute-start | bytes 12296 | tf_op jit(solution)/shard_map/ppermute | solution.py:41
  32.6 11.6 %collective-permute-start.10 = (f32[32,1536]{1,0:T(8,128)S(1)}, f32[32,1536]{1,0:T(8,128)S(1)}, u32[]{:S(2)}, u32[]{:S(2)}) collective-permute-start(f32[32,1536]{1,0:T(8,128)S(1)} %get-tuple-element.71), channel_id=1, source_target_pairs={{0,8},{1,9},{2,10},{3,11},{4,12},{5,13},{6,14},{7,15},{8,0},{9,1},... | collective-permute-start | bytes 589832 | tf_op jit(solution)/shard_map/ppermute | solution.py:41
  32.6 11.6 %collective-permute-start.11 = (f32[32,1536]{1,0:T(8,128)S(1)}, f32[32,1536]{1,0:T(8,128)S(1)}, u32[]{:S(2)}, u32[]{:S(2)}) collective-permute-start(f32[32,1536]{1,0:T(8,128)S(1)} %get-tuple-element.72), channel_id=1, source_target_pairs={{0,4},{1,5},{2,6},{3,7},{4,0},{5,1},{6,2},{7,3},{8,12},{9,13},{10,... | collective-permute-start | bytes 589832 | tf_op jit(solution)/shard_map/ppermute | solution.py:41
  38.0 7.3 %collective-permute-start.12 = (f32[32,1536]{1,0:T(8,128)S(1)}, f32[32,1536]{1,0:T(8,128)S(1)}, u32[]{:S(2)}, u32[]{:S(2)}) collective-permute-start(f32[32,1536]{1,0:T(8,128)S(1)} %get-tuple-element.74), channel_id=1, source_target_pairs={{0,2},{1,3},{2,0},{3,1},{4,6},{5,7},{6,4},{7,5},{8,10},{9,11},{10,... | collective-permute-start | bytes 589832 | tf_op jit(solution)/shard_map/ppermute | solution.py:41
  39.5 5.7 %collective-permute-start.13 = (f32[32,1536]{1,0:T(8,128)S(1)}, f32[32,1536]{1,0:T(8,128)S(1)}, u32[]{:S(2)}, u32[]{:S(2)}) collective-permute-start(f32[32,1536]{1,0:T(8,128)S(1)} %get-tuple-element.75), channel_id=1, source_target_pairs={{0,1},{1,0},{2,3},{3,2},{4,5},{5,4},{6,7},{7,6},{8,9},{9,8},{10,11... | collective-permute-start | bytes 589832 | tf_op jit(solution)/shard_map/ppermute | solution.py:41
  48.5 8.0 %collective-permute-start.16 = (f32[8,128]{1,0:T(8,128)S(1)}, f32[8,128]{1,0:T(8,128)S(1)}, u32[]{:S(2)}, u32[]{:S(2)}) collective-permute-start(f32[8,128]{1,0:T(8,128)S(1)} %get-tuple-element.78), channel_id=1, source_target_pairs={{0,12},{1,13},{2,14},{3,15},{4,8},{5,9},{6,10},{7,11},{8,4},{9,5},... | collective-permute-start | bytes 12296 | tf_op jit(solution)/shard_map/ppermute | solution.py:41
  50.4 6.1 %collective-permute-start.15 = (f32[8,128]{1,0:T(8,128)S(1)}, f32[8,128]{1,0:T(8,128)S(1)}, u32[]{:S(2)}, u32[]{:S(2)}) collective-permute-start(f32[8,128]{1,0:T(8,128)S(1)} %get-tuple-element.78), channel_id=1, source_target_pairs={{0,8},{1,9},{2,10},{3,11},{4,12},{5,13},{6,14},{7,15},{8,0},{9,1},... | collective-permute-start | bytes 12296 | tf_op jit(solution)/shard_map/ppermute | solution.py:41
  50.4 6.1 %collective-permute-start.14 = (f32[8,128]{1,0:T(8,128)S(1)}, f32[8,128]{1,0:T(8,128)S(1)}, u32[]{:S(2)}, u32[]{:S(2)}) collective-permute-start(f32[8,128]{1,0:T(8,128)S(1)} %get-tuple-element.78), channel_id=1, source_target_pairs={{0,4},{1,5},{2,6},{3,7},{4,0},{5,1},{6,2},{7,3},{8,12},{9,13},{10,... | collective-permute-start | bytes 12296 | tf_op jit(solution)/shard_map/ppermute | solution.py:41
  56.5 4.3 %collective-permute-start.19 = (f32[8,128]{1,0:T(8,128)S(1)}, f32[8,128]{1,0:T(8,128)S(1)}, u32[]{:S(2)}, u32[]{:S(2)}) collective-permute-start(f32[8,128]{1,0:T(8,128)S(1)} %add_add_fusion.1.refs_0_), channel_id=1, source_target_pairs={{0,3},{1,2},{2,1},{3,0},{4,7},{5,6},{6,5},{7,4},{8,11},{9,10},{10,... | collective-permute-start | bytes 12296 | tf_op jit(solution)/shard_map/ppermute | solution.py:41
  56.6 4.2 %collective-permute-start.18 = (f32[8,128]{1,0:T(8,128)S(1)}, f32[8,128]{1,0:T(8,128)S(1)}, u32[]{:S(2)}, u32[]{:S(2)}) collective-permute-start(f32[8,128]{1,0:T(8,128)S(1)} %add_add_fusion.1.refs_0_), channel_id=1, source_target_pairs={{0,2},{1,3},{2,0},{3,1},{4,6},{5,7},{6,4},{7,5},{8,10},{9,11},{10,... | collective-permute-start | bytes 12296 | tf_op jit(solution)/shard_map/ppermute | solution.py:41
  57.2 3.6 %collective-permute-start.17 = (f32[8,128]{1,0:T(8,128)S(1)}, f32[8,128]{1,0:T(8,128)S(1)}, u32[]{:S(2)}, u32[]{:S(2)}) collective-permute-start(f32[8,128]{1,0:T(8,128)S(1)} %add_add_fusion.1.refs_0_), channel_id=1, source_target_pairs={{0,1},{1,0},{2,3},{3,2},{4,5},{5,4},{6,7},{7,6},{8,9},{9,8},{10,11... | collective-permute-start | bytes 12296 | tf_op jit(solution)/shard_map/ppermute | solution.py:41
  58.5 11.4 %collective-permute-start.20 = (f32[32,1536]{1,0:T(8,128)S(1)}, f32[32,1536]{1,0:T(8,128)S(1)}, u32[]{:S(2)}, u32[]{:S(2)}) collective-permute-start(f32[32,1536]{1,0:T(8,128)S(1)} %get-tuple-element.89), channel_id=1, source_target_pairs={{0,8},{1,9},{2,10},{3,11},{4,12},{5,13},{6,14},{7,15},{8,0},{9,1},... | collective-permute-start | bytes 589832 | tf_op jit(solution)/shard_map/ppermute | solution.py:41
  58.8 11.0 %collective-permute-start.21 = (f32[32,1536]{1,0:T(8,128)S(1)}, f32[32,1536]{1,0:T(8,128)S(1)}, u32[]{:S(2)}, u32[]{:S(2)}) collective-permute-start(f32[32,1536]{1,0:T(8,128)S(1)} %get-tuple-element.90), channel_id=1, source_target_pairs={{0,4},{1,5},{2,6},{3,7},{4,0},{5,1},{6,2},{7,3},{8,12},{9,13},{10,... | collective-permute-start | bytes 589832 | tf_op jit(solution)/shard_map/ppermute | solution.py:41
  64.4 6.3 %collective-permute-start.22 = (f32[32,1536]{1,0:T(8,128)S(1)}, f32[32,1536]{1,0:T(8,128)S(1)}, u32[]{:S(2)}, u32[]{:S(2)}) collective-permute-start(f32[32,1536]{1,0:T(8,128)S(1)} %get-tuple-element.92), channel_id=1, source_target_pairs={{0,2},{1,3},{2,0},{3,1},{4,6},{5,7},{6,4},{7,5},{8,10},{9,11},{10,... | collective-permute-start | bytes 589832 | tf_op jit(solution)/shard_map/ppermute | solution.py:41
  65.7 5.0 %collective-permute-start.23 = (f32[32,1536]{1,0:T(8,128)S(1)}, f32[32,1536]{1,0:T(8,128)S(1)}, u32[]{:S(2)}, u32[]{:S(2)}) collective-permute-start(f32[32,1536]{1,0:T(8,128)S(1)} %get-tuple-element.93), channel_id=1, source_target_pairs={{0,1},{1,0},{2,3},{3,2},{4,5},{5,4},{6,7},{7,6},{8,9},{9,8},{10,11... | collective-permute-start | bytes 589832 | tf_op jit(solution)/shard_map/ppermute | solution.py:41
  73.7 5.4 %collective-permute-start.26 = (f32[8,128]{1,0:T(8,128)S(1)}, f32[8,128]{1,0:T(8,128)S(1)}, u32[]{:S(2)}, u32[]{:S(2)}) collective-permute-start(f32[8,128]{1,0:T(8,128)S(1)} %get-tuple-element.95), channel_id=1, source_target_pairs={{0,12},{1,13},{2,14},{3,15},{4,8},{5,9},{6,10},{7,11},{8,4},{9,5},... | collective-permute-start | bytes 12296 | tf_op jit(solution)/shard_map/ppermute | solution.py:41
  75.7 4.5 %collective-permute-start.25 = (f32[8,128]{1,0:T(8,128)S(1)}, f32[8,128]{1,0:T(8,128)S(1)}, u32[]{:S(2)}, u32[]{:S(2)}) collective-permute-start(f32[8,128]{1,0:T(8,128)S(1)} %get-tuple-element.95), channel_id=1, source_target_pairs={{0,8},{1,9},{2,10},{3,11},{4,12},{5,13},{6,14},{7,15},{8,0},{9,1},... | collective-permute-start | bytes 12296 | tf_op jit(solution)/shard_map/ppermute | solution.py:41
  75.7 4.5 %collective-permute-start.24 = (f32[8,128]{1,0:T(8,128)S(1)}, f32[8,128]{1,0:T(8,128)S(1)}, u32[]{:S(2)}, u32[]{:S(2)}) collective-permute-start(f32[8,128]{1,0:T(8,128)S(1)} %get-tuple-element.95), channel_id=1, source_target_pairs={{0,4},{1,5},{2,6},{3,7},{4,0},{5,1},{6,2},{7,3},{8,12},{9,13},{10,... | collective-permute-start | bytes 12296 | tf_op jit(solution)/shard_map/ppermute | solution.py:41
  80.2 3.1 %collective-permute-start.29 = (f32[8,128]{1,0:T(8,128)S(1)}, f32[8,128]{1,0:T(8,128)S(1)}, u32[]{:S(2)}, u32[]{:S(2)}) collective-permute-start(f32[8,128]{1,0:T(8,128)S(1)} %add_add_fusion.refs_0_), channel_id=1, source_target_pairs={{0,3},{1,2},{2,1},{3,0},{4,7},{5,6},{6,5},{7,4},{8,11},{9,10},{10,... | collective-permute-start | bytes 12296 | tf_op jit(solution)/shard_map/ppermute | solution.py:41
  80.3 3.7 %collective-permute-start.28 = (f32[8,128]{1,0:T(8,128)S(1)}, f32[8,128]{1,0:T(8,128)S(1)}, u32[]{:S(2)}, u32[]{:S(2)}) collective-permute-start(f32[8,128]{1,0:T(8,128)S(1)} %add_add_fusion.refs_0_), channel_id=1, source_target_pairs={{0,2},{1,3},{2,0},{3,1},{4,6},{5,7},{6,4},{7,5},{8,10},{9,11},{10,... | collective-permute-start | bytes 12296 | tf_op jit(solution)/shard_map/ppermute | solution.py:41
  81.2 2.8 %collective-permute-start.27 = (f32[8,128]{1,0:T(8,128)S(1)}, f32[8,128]{1,0:T(8,128)S(1)}, u32[]{:S(2)}, u32[]{:S(2)}) collective-permute-start(f32[8,128]{1,0:T(8,128)S(1)} %add_add_fusion.refs_0_), channel_id=1, source_target_pairs={{0,1},{1,0},{2,3},{3,2},{4,5},{5,4},{6,7},{7,6},{8,9},{9,8},{10,11... | collective-permute-start | bytes 12296 | tf_op jit(solution)/shard_map/ppermute | solution.py:41

commit v12 on v11

--- a/solution.py
+++ b/solution.py
@@ -10,7 +10,7 @@
 ITERS = 3
 LANES = 128
 PACK = 4
-CHUNK = 1024
+CHUNK = 2048
 SUBLANES = 8
 STEP = 8
 COPIES = 8

time: 87.3 us -> 86.6 us (level)
  no operation moved by 1% of the time
where the time goes in v12:
time: 86.6 us; the launch traced here: 86.4 us
  Pallas kernels  38.6 us (45%)
  starting transfers between devices  32.6 us (38%)
  waiting for transfers between devices  13.2 us (15%)
  between operations  1.04 us (1%)
  other arithmetic  0.87 us (1%)
    ppermute x30, starting transfers between devices, swapped(): return lax.ppermute(x, 'dom', [(i, i ^ mask) for i in range(size)])  32.6 us
    pallas_call x4, Pallas kernels, gather_colours(): pl.pallas_call(gather_kernel, out_shape=[vmem_out((columns, indices // co...  14.1 us
    ppermute x30, waiting for transfers between devices, swapped(): return lax.ppermute(x, 'dom', [(i, i ^ mask) for i in range(size)])  13.2 us
    pallas_call x3, Pallas kernels, product(): pl.pallas_call(functools.partial(product_kernel, len(ghosts), group, with...  8.91 us
    pallas_call x2, Pallas kernels, start_gather(): pl.pallas_call(functools.partial(start_kernel, count, first, make_rows),...  8.53 us
    pallas_call x2, Pallas kernels, later_own(): pl.pallas_call(functools.partial(later_own_kernel, total_states), out_sha...  4.15 us
    pallas_call x1, Pallas kernels, final(): pl.pallas_call(functools.partial(final_kernel, total_states), out_shape=j...  2.28 us
  transfers between devices with their start and end apart: 30, of which 11 were waited for; matrix products, arithmetic and copies ran while one was open for 0% of the time, Pallas kernels for 26%

profile of v12, /device:TPU:0, one launch (start us, length us, event | category | flops | bytes accessed | tf_op | source)
XLA Modules:
  0.0 86.4 jit_solution(2737434352564787280)
XLA Ops:
  0.0 0.8 add_select_fusion
  0.8 0.1 slice_reduce_fusion.1
  1.0 4.9 %start_gather.2 = (bf16[32,1536]{1,0:T(8,128)(2,1)S(1)}, bf16[32,1536]{1,0:T(8,128)(2,1)S(1)}, bf16[256,128,128]{2,1,0:T(8,128)(2,1)S(1)}, f32[2048,128]{1,0:T(8,128)S(1)}, bf16[32,8192]{1,0:T(8,128)(2,1)S(1)}) custom-call(s32[3072]{0:T(1024)S(1)} %pad_add_fusion.row_ref, s32[24,128]{1,0:T(8,128)S(1)} %pad_add_fusion.1.part_ref, ...), custom_call_target="tpu_custom_call" | custom-call | bytes 1024 | tf_op jit(solution)/shard_map/start_gather/pallas_call | solution.py:232
  5.9 4.1 %collective-permute-start = (bf16[32,1536]{1,0:T(8,128)(2,1)S(1)}, bf16[32,1536]{1,0:T(8,128)(2,1)S(1)}, u32[]{:S(2)}, u32[]{:S(2)}) collective-permute-start(bf16[32,1536]{1,0:T(8,128)(2,1)S(1)} %get-tuple-element.54), channel_id=1, source_target_pairs={{0,8},{1,9},{2,10},{3,11},{4,12},{5,13},{6,14},{7,15},{8,0},{9,1},... | collective-permute-start | bytes 294920 | tf_op jit(solution)/shard_map/ppermute | solution.py:41
  10.0 1.6 %collective-permute-start.1 = (bf16[32,1536]{1,0:T(8,128)(2,1)S(1)}, bf16[32,1536]{1,0:T(8,128)(2,1)S(1)}, u32[]{:S(2)}, u32[]{:S(2)}) collective-permute-start(bf16[32,1536]{1,0:T(8,128)(2,1)S(1)} %get-tuple-element.55), channel_id=1, source_target_pairs={{0,4},{1,5},{2,6},{3,7},{4,0},{5,1},{6,2},{7,3},{8,12},{9,13},{10,... | collective-permute-start | bytes 294920 | tf_op jit(solution)/shard_map/ppermute | solution.py:41
  11.6 3.7 %start_gather.3 = (bf16[32,1536]{1,0:T(8,128)(2,1)S(1)}, bf16[32,1536]{1,0:T(8,128)(2,1)S(1)}, bf16[64,128,128]{2,1,0:T(8,128)(2,1)S(1)}) custom-call(s32[3072]{0:T(1024)S(1)} %pad_add_fusion.2.row_ref, s32[24,128]{1,0:T(8,128)S(1)} %pad_add_fusion.3.part_ref, f32[2048,128]{1,0:T(8,128)S(1)} %get-tuple-element.52.source_ref, bf16[320,128,128]{2,1,0:T(8,128)(2,1)} %tiles_ref.3), custom_call_target="tpu_custom_call" | custom-call | bytes 1024 | tf_op jit(solution)/shard_map/start_gather/pallas_call | solution.py:232
  15.2 0.0 copy-start
  15.2 0.0 copy-start.1
  15.3 1.6 %collective-permute-start.2 = (bf16[32,1536]{1,0:T(8,128)(2,1)S(1)}, bf16[32,1536]{1,0:T(8,128)(2,1)S(1)}, u32[]{:S(2)}, u32[]{:S(2)}) collective-permute-start(bf16[32,1536]{1,0:T(8,128)(2,1)S(1)} %get-tuple-element.56), channel_id=1, source_target_pairs={{0,2},{1,3},{2,0},{3,1},{4,6},{5,7},{6,4},{7,5},{8,10},{9,11},{10,... | collective-permute-start | bytes 294920 | tf_op jit(solution)/shard_map/ppermute | solution.py:41
  16.8 0.0 collective-permute-start.3
  17.5 0.7 first_own.1.refs_4_
  18.2 0.0 collective-permute-done.refs_5_
  18.2 0.0 collective-permute-done.1.refs_6_
  18.2 1.8 %collective-permute-done.2.refs_7_ = bf16[32,1536]{1,0:T(8,128)(2,1)S(1)} collective-permute-done((bf16[32,1536]{1,0:T(8,128)(2,1)S(1)}, bf16[32,1536]{1,0:T(8,128)(2,1)S(1)}, u32[]{:S(2)}, u32[]{:S(2)}) %collective-permute-start.2) | collective-permute-done | bytes 98336 | tf_op jit(solution)/shard_map/ppermute | solution.py:41
  19.9 0.0 collective-permute-done.3.refs_8_
  20.0 2.7 %product.3 = (bf16[96,8192]{1,0:T(8,128)(2,1)S(1)}, f32[8,128]{1,0:T(8,128)S(1)}, f32[2048,128]{1,0:T(8,128)S(1)}) custom-call(s32[320]{0:T(512)S(1)} %copy-done, s32[320]{0:T(512)S(1)} %copy-done.1, s32[1]{0:T(128)S(6)} %copy.7.refs_2_, bf16[32,8192]{1,0:T(8,128)(2,1)S(1)} %get-tuple-element.51.block_ref.refs_3_, f32[32,8192]{1,0:T(8,128)S(1)} %first_own.1.refs_4_, ...), custom_call_target="tpu_custom_call" | custom-call | bytes 1024 | tf_op jit(solution)/shard_map/product/pallas_call | solution.py:378
  22.6 0.1 collective-permute-start.6
  22.7 1.9 %collective-permute-start.5 = (f32[8,128]{1,0:T(8,128)S(1)}, f32[8,128]{1,0:T(8,128)S(1)}, u32[]{:S(2)}, u32[]{:S(2)}) collective-permute-start(f32[8,128]{1,0:T(8,128)S(1)} %get-tuple-element.60), channel_id=1, source_target_pairs={{0,8},{1,9},{2,10},{3,11},{4,12},{5,13},{6,14},{7,15},{8,0},{9,1},... | collective-permute-start | bytes 12296 | tf_op jit(solution)/shard_map/ppermute | solution.py:41
  24.6 2.5 %collective-permute-start.4 = (f32[8,128]{1,0:T(8,128)S(1)}, f32[8,128]{1,0:T(8,128)S(1)}, u32[]{:S(2)}, u32[]{:S(2)}) collective-permute-start(f32[8,128]{1,0:T(8,128)S(1)} %get-tuple-element.60), channel_id=1, source_target_pairs={{0,4},{1,5},{2,6},{3,7},{4,0},{5,1},{6,2},{7,3},{8,12},{9,13},{10,... | collective-permute-start | bytes 12296 | tf_op jit(solution)/shard_map/ppermute | solution.py:41
  27.1 3.5 %gather_rows.4 = (f32[32,1536]{1,0:T(8,128)S(1)}, f32[32,1536]{1,0:T(8,128)S(1)}) custom-call(s32[3072]{0:T(1024)S(1)} %pad_add_fusion.row_ref, s32[24,128]{1,0:T(8,128)S(1)} %pad_add_fusion.1.part_ref, f32[2048,128]{1,0:T(8,128)S(1)} %get-tuple-element.73.rows_ref), custom_call_target="tpu_custom_call" | custom-call | bytes 1024 | tf_op jit(solution)/shard_map/gather_rows/pallas_call | solution.py:182
  30.6 0.0 collective-permute-done.6
  30.7 0.1 collective-permute-start.9
  30.8 1.6 %collective-permute-start.8 = (f32[8,128]{1,0:T(8,128)S(1)}, f32[8,128]{1,0:T(8,128)S(1)}, u32[]{:S(2)}, u32[]{:S(2)}) collective-permute-start(f32[8,128]{1,0:T(8,128)S(1)} %add_add_fusion.2.refs_0_), channel_id=1, source_target_pairs={{0,2},{1,3},{2,0},{3,1},{4,6},{5,7},{6,4},{7,5},{8,10},{9,11},{10,... | collective-permute-start | bytes 12296 | tf_op jit(solution)/shard_map/ppermute | solution.py:41
  32.3 0.3 collective-permute-start.7
  32.6 0.0 collective-permute-start.10
  32.6 0.9 %collective-permute-start.11 = (f32[32,1536]{1,0:T(8,128)S(1)}, f32[32,1536]{1,0:T(8,128)S(1)}, u32[]{:S(2)}, u32[]{:S(2)}) collective-permute-start(f32[32,1536]{1,0:T(8,128)S(1)} %get-tuple-element.72), channel_id=1, source_target_pairs={{0,4},{1,5},{2,6},{3,7},{4,0},{5,1},{6,2},{7,3},{8,12},{9,13},{10,... | collective-permute-start | bytes 589832 | tf_op jit(solution)/shard_map/ppermute | solution.py:41
  33.5 0.2 collective-permute-done.9.refs_3_
  33.8 0.7 collective-permute-done.8.refs_2_
  34.4 0.0 collective-permute-done.7.refs_1_
  34.4 3.5 %gather_rows.5 = (f32[32,1536]{1,0:T(8,128)S(1)}, f32[32,1536]{1,0:T(8,128)S(1)}) custom-call(s32[3072]{0:T(1024)S(1)} %pad_add_fusion.2.row_ref, s32[24,128]{1,0:T(8,128)S(1)} %pad_add_fusion.3.part_ref, f32[2048,128]{1,0:T(8,128)S(1)} %get-tuple-element.73.rows_ref), custom_call_target="tpu_custom_call" | custom-call | bytes 1024 | tf_op jit(solution)/shard_map/gather_rows/pallas_call | solution.py:182
  38.0 1.6 %collective-permute-start.12 = (f32[32,1536]{1,0:T(8,128)S(1)}, f32[32,1536]{1,0:T(8,128)S(1)}, u32[]{:S(2)}, u32[]{:S(2)}) collective-permute-start(f32[32,1536]{1,0:T(8,128)S(1)} %get-tuple-element.74), channel_id=1, source_target_pairs={{0,2},{1,3},{2,0},{3,1},{4,6},{5,7},{6,4},{7,5},{8,10},{9,11},{10,... | collective-permute-start | bytes 589832 | tf_op jit(solution)/shard_map/ppermute | solution.py:41
  39.5 0.0 collective-permute-start.13
  39.5 2.1 %later_own.2 = (bf16[32,8192]{1,0:T(8,128)(2,1)S(1)}, bf16[96,96]{1,0:T(8,128)(2,1)S(1)}, f32[32,8192]{1,0:T(8,128)S(1)}) custom-call(f32[8,128]{1,0:T(8,128)S(1)} %add_add_fusion.2.refs_0_, f32[8,128]{1,0:T(8,128)S(1)} %collective-permute-done.7.refs_1_, f32[8,128]{1,0:T(8,128)S(1)} %collective-permute-done.8.refs_2_, ...), custom_call_target="tpu_custom_call" | custom-call | bytes 1024 | tf_op jit(solution)/shard_map/later_own/pallas_call | solution.py:279
  41.6 2.6 %collective-permute-done.10.refs_5_ = f32[32,1536]{1,0:T(8,128)S(1)} collective-permute-done((f32[32,1536]{1,0:T(8,128)S(1)}, f32[32,1536]{1,0:T(8,128)S(1)}, u32[]{:S(2)}, u32[]{:S(2)}) %collective-permute-start.10) | collective-permute-done | bytes 196640 | tf_op jit(solution)/shard_map/ppermute | solution.py:41
  44.2 0.0 collective-permute-done.11.refs_6_
  44.2 1.1 %collective-permute-done.12.refs_7_ = f32[32,1536]{1,0:T(8,128)S(1)} collective-permute-done((f32[32,1536]{1,0:T(8,128)S(1)}, f32[32,1536]{1,0:T(8,128)S(1)}, u32[]{:S(2)}, u32[]{:S(2)}) %collective-permute-start.12) | collective-permute-done | bytes 196640 | tf_op jit(solution)/shard_map/ppermute | solution.py:41
  45.3 3.2 %product.4 = (bf16[96,8192]{1,0:T(8,128)(2,1)S(1)}, f32[8,128]{1,0:T(8,128)S(1)}, f32[2048,128]{1,0:T(8,128)S(1)}) custom-call(s32[320]{0:T(512)S(1)} %copy-done, s32[320]{0:T(512)S(1)} %copy-done.1, s32[1]{0:T(128)S(6)} %copy.7.refs_2_, bf16[32,8192]{1,0:T(8,128)(2,1)S(1)} %get-tuple-element.69.refs_3_, f32[32,8192]{1,0:T(8,128)S(1)} %get-tuple-element.70.refs_4_, ...), custom_call_target="tpu_custom_call" | custom-call | bytes 1024 | tf_op jit(solution)/shard_map/product/pallas_call | solution.py:378
  48.5 1.9 %collective-permute-start.16 = (f32[8,128]{1,0:T(8,128)S(1)}, f32[8,128]{1,0:T(8,128)S(1)}, u32[]{:S(2)}, u32[]{:S(2)}) collective-permute-start(f32[8,128]{1,0:T(8,128)S(1)} %get-tuple-element.78), channel_id=1, source_target_pairs={{0,12},{1,13},{2,14},{3,15},{4,8},{5,9},{6,10},{7,11},{8,4},{9,5},... | collective-permute-start | bytes 12296 | tf_op jit(solution)/shard_map/ppermute | solution.py:41
  50.4 0.0 collective-permute-start.15
  50.4 2.6 %collective-permute-start.14 = (f32[8,128]{1,0:T(8,128)S(1)}, f32[8,128]{1,0:T(8,128)S(1)}, u32[]{:S(2)}, u32[]{:S(2)}) collective-permute-start(f32[8,128]{1,0:T(8,128)S(1)} %get-tuple-element.78), channel_id=1, source_target_pairs={{0,4},{1,5},{2,6},{3,7},{4,0},{5,1},{6,2},{7,3},{8,12},{9,13},{10,... | collective-permute-start | bytes 12296 | tf_op jit(solution)/shard_map/ppermute | solution.py:41
  53.0 3.5 %gather_rows.6 = (f32[32,1536]{1,0:T(8,128)S(1)}, f32[32,1536]{1,0:T(8,128)S(1)}) custom-call(s32[3072]{0:T(1024)S(1)} %pad_add_fusion.row_ref, s32[24,128]{1,0:T(8,128)S(1)} %pad_add_fusion.1.part_ref, f32[2048,128]{1,0:T(8,128)S(1)} %get-tuple-element.91.rows_ref), custom_call_target="tpu_custom_call" | custom-call | bytes 1024 | tf_op jit(solution)/shard_map/gather_rows/pallas_call | solution.py:182
  56.5 0.0 collective-permute-done.15
  56.5 0.0 collective-permute-done.14
  56.5 0.2 collective-permute-start.19
  56.7 0.5 collective-permute-start.18
  57.2 1.2 %collective-permute-start.17 = (f32[8,128]{1,0:T(8,128)S(1)}, f32[8,128]{1,0:T(8,128)S(1)}, u32[]{:S(2)}, u32[]{:S(2)}) collective-permute-start(f32[8,128]{1,0:T(8,128)S(1)} %add_add_fusion.1.refs_0_), channel_id=1, source_target_pairs={{0,1},{1,0},{2,3},{3,2},{4,5},{5,4},{6,7},{7,6},{8,9},{9,8},{10,11... | collective-permute-start | bytes 12296 | tf_op jit(solution)/shard_map/ppermute | solution.py:41
  58.5 0.4 collective-permute-start.20
  58.8 2.0 %collective-permute-start.21 = (f32[32,1536]{1,0:T(8,128)S(1)}, f32[32,1536]{1,0:T(8,128)S(1)}, u32[]{:S(2)}, u32[]{:S(2)}) collective-permute-start(f32[32,1536]{1,0:T(8,128)S(1)} %get-tuple-element.90), channel_id=1, source_target_pairs={{0,4},{1,5},{2,6},{3,7},{4,0},{5,1},{6,2},{7,3},{8,12},{9,13},{10,... | collective-permute-start | bytes 589832 | tf_op jit(solution)/shard_map/ppermute | solution.py:41
  60.9 3.5 %gather_rows.7 = (f32[32,1536]{1,0:T(8,128)S(1)}, f32[32,1536]{1,0:T(8,128)S(1)}) custom-call(s32[3072]{0:T(1024)S(1)} %pad_add_fusion.2.row_ref, s32[24,128]{1,0:T(8,128)S(1)} %pad_add_fusion.3.part_ref, f32[2048,128]{1,0:T(8,128)S(1)} %get-tuple-element.91.rows_ref), custom_call_target="tpu_custom_call" | custom-call | bytes 1024 | tf_op jit(solution)/shard_map/gather_rows/pallas_call | solution.py:182
  64.4 1.3 %collective-permute-start.22 = (f32[32,1536]{1,0:T(8,128)S(1)}, f32[32,1536]{1,0:T(8,128)S(1)}, u32[]{:S(2)}, u32[]{:S(2)}) collective-permute-start(f32[32,1536]{1,0:T(8,128)S(1)} %get-tuple-element.92), channel_id=1, source_target_pairs={{0,2},{1,3},{2,0},{3,1},{4,6},{5,7},{6,4},{7,5},{8,10},{9,11},{10,... | collective-permute-start | bytes 589832 | tf_op jit(solution)/shard_map/ppermute | solution.py:41
  65.7 2.1 %later_own.3 = (bf16[32,8192]{1,0:T(8,128)(2,1)S(1)}, bf16[96,96]{1,0:T(8,128)(2,1)S(1)}, f32[32,8192]{1,0:T(8,128)S(1)}) custom-call(f32[8,128]{1,0:T(8,128)S(1)} %add_add_fusion.1.refs_0_, f32[8,128]{1,0:T(8,128)S(1)} %collective-permute-done.17.refs_1_, f32[8,128]{1,0:T(8,128)S(1)} %collective-permute-done.18.refs_2_, ...), custom_call_target="tpu_custom_call" | custom-call | bytes 1024 | tf_op jit(solution)/shard_map/later_own/pallas_call | solution.py:279
  67.8 2.0 %collective-permute-done.20.refs_5_ = f32[32,1536]{1,0:T(8,128)S(1)} collective-permute-done((f32[32,1536]{1,0:T(8,128)S(1)}, f32[32,1536]{1,0:T(8,128)S(1)}, u32[]{:S(2)}, u32[]{:S(2)}) %collective-permute-start.20) | collective-permute-done | bytes 196640 | tf_op jit(solution)/shard_map/ppermute | solution.py:41
  69.9 0.9 collective-permute-done.22.refs_7_
  70.7 3.0 %product.5 = (bf16[96,8192]{1,0:T(8,128)(2,1)S(1)}, f32[8,128]{1,0:T(8,128)S(1)}) custom-call(s32[320]{0:T(512)S(1)} %copy-done, s32[320]{0:T(512)S(1)} %copy-done.1, s32[1]{0:T(128)S(6)} %copy.7.refs_2_, bf16[32,8192]{1,0:T(8,128)(2,1)S(1)} %get-tuple-element.87.refs_3_, f32[32,8192]{1,0:T(8,128)S(1)} %get-tuple-element.88.refs_4_, ...), custom_call_target="tpu_custom_call" | custom-call | bytes 1024 | tf_op jit(solution)/shard_map/product/pallas_call | solution.py:378
  73.7 2.0 %collective-permute-start.26 = (f32[8,128]{1,0:T(8,128)S(1)}, f32[8,128]{1,0:T(8,128)S(1)}, u32[]{:S(2)}, u32[]{:S(2)}) collective-permute-start(f32[8,128]{1,0:T(8,128)S(1)} %get-tuple-element.95), channel_id=1, source_target_pairs={{0,12},{1,13},{2,14},{3,15},{4,8},{5,9},{6,10},{7,11},{8,4},{9,5},... | collective-permute-start | bytes 12296 | tf_op jit(solution)/shard_map/ppermute | solution.py:41
  75.7 2.4 %collective-permute-start.24 = (f32[8,128]{1,0:T(8,128)S(1)}, f32[8,128]{1,0:T(8,128)S(1)}, u32[]{:S(2)}, u32[]{:S(2)}) collective-permute-start(f32[8,128]{1,0:T(8,128)S(1)} %get-tuple-element.95), channel_id=1, source_target_pairs={{0,4},{1,5},{2,6},{3,7},{4,0},{5,1},{6,2},{7,3},{8,12},{9,13},{10,... | collective-permute-start | bytes 12296 | tf_op jit(solution)/shard_map/ppermute | solution.py:41
  78.1 1.0 %collective-permute-done.26 = f32[8,128]{1,0:T(8,128)S(1)} collective-permute-done((f32[8,128]{1,0:T(8,128)S(1)}, f32[8,128]{1,0:T(8,128)S(1)}, u32[]{:S(2)}, u32[]{:S(2)}) %collective-permute-start.26) | collective-permute-done | bytes 4128 | tf_op jit(solution)/shard_map/ppermute | solution.py:41
  79.1 1.1 %collective-permute-done.25 = f32[8,128]{1,0:T(8,128)S(1)} collective-permute-done((f32[8,128]{1,0:T(8,128)S(1)}, f32[8,128]{1,0:T(8,128)S(1)}, u32[]{:S(2)}, u32[]{:S(2)}) %collective-permute-start.25) | collective-permute-done | bytes 4128 | tf_op jit(solution)/shard_map/ppermute | solution.py:41
  80.2 0.1 collective-permute-start.29
  80.3 0.9 %collective-permute-start.28 = (f32[8,128]{1,0:T(8,128)S(1)}, f32[8,128]{1,0:T(8,128)S(1)}, u32[]{:S(2)}, u32[]{:S(2)}) collective-permute-start(f32[8,128]{1,0:T(8,128)S(1)} %add_add_fusion.refs_0_), channel_id=1, source_target_pairs={{0,2},{1,3},{2,0},{3,1},{4,6},{5,7},{6,4},{7,5},{8,10},{9,11},{10,... | collective-permute-start | bytes 12296 | tf_op jit(solution)/shard_map/ppermute | solution.py:41
  81.2 1.0 %collective-permute-start.27 = (f32[8,128]{1,0:T(8,128)S(1)}, f32[8,128]{1,0:T(8,128)S(1)}, u32[]{:S(2)}, u32[]{:S(2)}) collective-permute-start(f32[8,128]{1,0:T(8,128)S(1)} %add_add_fusion.refs_0_), channel_id=1, source_target_pairs={{0,1},{1,0},{2,3},{3,2},{4,5},{5,4},{6,7},{7,6},{8,9},{9,8},{10,11... | collective-permute-start | bytes 12296 | tf_op jit(solution)/shard_map/ppermute | solution.py:41
  82.1 1.2 %collective-permute-done.29.refs_3_ = f32[8,128]{1,0:T(8,128)S(1)} collective-permute-done((f32[8,128]{1,0:T(8,128)S(1)}, f32[8,128]{1,0:T(8,128)S(1)}, u32[]{:S(2)}, u32[]{:S(2)}) %collective-permute-start.29) | collective-permute-done | bytes 4128 | tf_op jit(solution)/shard_map/ppermute | solution.py:41
  83.3 0.7 collective-permute-done.28.refs_2_
  84.0 2.3 %final.1 = f32[32,8192]{1,0:T(8,128)} custom-call(f32[8,128]{1,0:T(8,128)S(1)} %add_add_fusion.refs_0_, f32[8,128]{1,0:T(8,128)S(1)} %collective-permute-done.27.refs_1_, f32[8,128]{1,0:T(8,128)S(1)} %collective-permute-done.28.refs_2_, f32[8,128]{1,0:T(8,128)S(1)} %collective-permute-done.29.refs_3_, bf16[96,8192]{1,0:T(8,128)(2,1)S(1)} %get-tuple-element.96.refs_4_), custom_call_target="tpu_custom_call" | custom-call | bytes 1024 | tf_op jit(solution)/shard_map/final/pallas_call | solution.py:405
  (22 shorter events, 0.1 us)
Async XLA Ops:
  5.9 12.3 %collective-permute-start = (bf16[32,1536]{1,0:T(8,128)(2,1)S(1)}, bf16[32,1536]{1,0:T(8,128)(2,1)S(1)}, u32[]{:S(2)}, u32[]{:S(2)}) collective-permute-start(bf16[32,1536]{1,0:T(8,128)(2,1)S(1)} %get-tuple-element.54), channel_id=1, source_target_pairs={{0,8},{1,9},{2,10},{3,11},{4,12},{5,13},{6,14},{7,15},{8,0},{9,1},... | collective-permute-start | bytes 294920 | tf_op jit(solution)/shard_map/ppermute | solution.py:41
  10.0 8.2 %collective-permute-start.1 = (bf16[32,1536]{1,0:T(8,128)(2,1)S(1)}, bf16[32,1536]{1,0:T(8,128)(2,1)S(1)}, u32[]{:S(2)}, u32[]{:S(2)}) collective-permute-start(bf16[32,1536]{1,0:T(8,128)(2,1)S(1)} %get-tuple-element.55), channel_id=1, source_target_pairs={{0,4},{1,5},{2,6},{3,7},{4,0},{5,1},{6,2},{7,3},{8,12},{9,13},{10,... | collective-permute-start | bytes 294920 | tf_op jit(solution)/shard_map/ppermute | solution.py:41
  15.2 4.7 %copy-start = (s32[320]{0:T(512)S(1)}, s32[320]{0:T(512)}, u32[]{:S(2)}) copy-start(s32[320]{0:T(512)} %refs_0_.5) | copy-start | bytes 3844
  15.2 4.7 %copy-start.1 = (s32[320]{0:T(512)S(1)}, s32[320]{0:T(512)}, u32[]{:S(2)}) copy-start(s32[320]{0:T(512)} %refs_1_.5) | copy-start | bytes 3844
  15.3 4.7 %collective-permute-start.2 = (bf16[32,1536]{1,0:T(8,128)(2,1)S(1)}, bf16[32,1536]{1,0:T(8,128)(2,1)S(1)}, u32[]{:S(2)}, u32[]{:S(2)}) collective-permute-start(bf16[32,1536]{1,0:T(8,128)(2,1)S(1)} %get-tuple-element.56), channel_id=1, source_target_pairs={{0,2},{1,3},{2,0},{3,1},{4,6},{5,7},{6,4},{7,5},{8,10},{9,11},{10,... | collective-permute-start | bytes 294920 | tf_op jit(solution)/shard_map/ppermute | solution.py:41
  16.8 3.1 %collective-permute-start.3 = (bf16[32,1536]{1,0:T(8,128)(2,1)S(1)}, bf16[32,1536]{1,0:T(8,128)(2,1)S(1)}, u32[]{:S(2)}, u32[]{:S(2)}) collective-permute-start(bf16[32,1536]{1,0:T(8,128)(2,1)S(1)} %get-tuple-element.57), channel_id=1, source_target_pairs={{0,1},{1,0},{2,3},{3,2},{4,5},{5,4},{6,7},{7,6},{8,9},{9,8},{10,11... | collective-permute-start | bytes 294920 | tf_op jit(solution)/shard_map/ppermute | solution.py:41
  22.6 8.0 %collective-permute-start.6 = (f32[8,128]{1,0:T(8,128)S(1)}, f32[8,128]{1,0:T(8,128)S(1)}, u32[]{:S(2)}, u32[]{:S(2)}) collective-permute-start(f32[8,128]{1,0:T(8,128)S(1)} %get-tuple-element.60), channel_id=1, source_target_pairs={{0,12},{1,13},{2,14},{3,15},{4,8},{5,9},{6,10},{7,11},{8,4},{9,5},... | collective-permute-start | bytes 12296 | tf_op jit(solution)/shard_map/ppermute | solution.py:41
  22.7 7.9 %collective-permute-start.5 = (f32[8,128]{1,0:T(8,128)S(1)}, f32[8,128]{1,0:T(8,128)S(1)}, u32[]{:S(2)}, u32[]{:S(2)}) collective-permute-start(f32[8,128]{1,0:T(8,128)S(1)} %get-tuple-element.60), channel_id=1, source_target_pairs={{0,8},{1,9},{2,10},{3,11},{4,12},{5,13},{6,14},{7,15},{8,0},{9,1},... | collective-permute-start | bytes 12296 | tf_op jit(solution)/shard_map/ppermute | solution.py:41
  24.6 6.0 %collective-permute-start.4 = (f32[8,128]{1,0:T(8,128)S(1)}, f32[8,128]{1,0:T(8,128)S(1)}, u32[]{:S(2)}, u32[]{:S(2)}) collective-permute-start(f32[8,128]{1,0:T(8,128)S(1)} %get-tuple-element.60), channel_id=1, source_target_pairs={{0,4},{1,5},{2,6},{3,7},{4,0},{5,1},{6,2},{7,3},{8,12},{9,13},{10,... | collective-permute-start | bytes 12296 | tf_op jit(solution)/shard_map/ppermute | solution.py:41
  30.7 3.1 %collective-permute-start.9 = (f32[8,128]{1,0:T(8,128)S(1)}, f32[8,128]{1,0:T(8,128)S(1)}, u32[]{:S(2)}, u32[]{:S(2)}) collective-permute-start(f32[8,128]{1,0:T(8,128)S(1)} %add_add_fusion.2.refs_0_), channel_id=1, source_target_pairs={{0,3},{1,2},{2,1},{3,0},{4,7},{5,6},{6,5},{7,4},{8,11},{9,10},{10,... | collective-permute-start | bytes 12296 | tf_op jit(solution)/shard_map/ppermute | solution.py:41
  30.8 3.7 %collective-permute-start.8 = (f32[8,128]{1,0:T(8,128)S(1)}, f32[8,128]{1,0:T(8,128)S(1)}, u32[]{:S(2)}, u32[]{:S(2)}) collective-permute-start(f32[8,128]{1,0:T(8,128)S(1)} %add_add_fusion.2.refs_0_), channel_id=1, source_target_pairs={{0,2},{1,3},{2,0},{3,1},{4,6},{5,7},{6,4},{7,5},{8,10},{9,11},{10,... | collective-permute-start | bytes 12296 | tf_op jit(solution)/shard_map/ppermute | solution.py:41
  32.3 2.1 %collective-permute-start.7 = (f32[8,128]{1,0:T(8,128)S(1)}, f32[8,128]{1,0:T(8,128)S(1)}, u32[]{:S(2)}, u32[]{:S(2)}) collective-permute-start(f32[8,128]{1,0:T(8,128)S(1)} %add_add_fusion.2.refs_0_), channel_id=1, source_target_pairs={{0,1},{1,0},{2,3},{3,2},{4,5},{5,4},{6,7},{7,6},{8,9},{9,8},{10,11... | collective-permute-start | bytes 12296 | tf_op jit(solution)/shard_map/ppermute | solution.py:41
  32.6 11.6 %collective-permute-start.10 = (f32[32,1536]{1,0:T(8,128)S(1)}, f32[32,1536]{1,0:T(8,128)S(1)}, u32[]{:S(2)}, u32[]{:S(2)}) collective-permute-start(f32[32,1536]{1,0:T(8,128)S(1)} %get-tuple-element.71), channel_id=1, source_target_pairs={{0,8},{1,9},{2,10},{3,11},{4,12},{5,13},{6,14},{7,15},{8,0},{9,1},... | collective-permute-start | bytes 589832 | tf_op jit(solution)/shard_map/ppermute | solution.py:41
  32.6 11.6 %collective-permute-start.11 = (f32[32,1536]{1,0:T(8,128)S(1)}, f32[32,1536]{1,0:T(8,128)S(1)}, u32[]{:S(2)}, u32[]{:S(2)}) collective-permute-start(f32[32,1536]{1,0:T(8,128)S(1)} %get-tuple-element.72), channel_id=1, source_target_pairs={{0,4},{1,5},{2,6},{3,7},{4,0},{5,1},{6,2},{7,3},{8,12},{9,13},{10,... | collective-permute-start | bytes 589832 | tf_op jit(solution)/shard_map/ppermute | solution.py:41
  38.0 7.3 %collective-permute-start.12 = (f32[32,1536]{1,0:T(8,128)S(1)}, f32[32,1536]{1,0:T(8,128)S(1)}, u32[]{:S(2)}, u32[]{:S(2)}) collective-permute-start(f32[32,1536]{1,0:T(8,128)S(1)} %get-tuple-element.74), channel_id=1, source_target_pairs={{0,2},{1,3},{2,0},{3,1},{4,6},{5,7},{6,4},{7,5},{8,10},{9,11},{10,... | collective-permute-start | bytes 589832 | tf_op jit(solution)/shard_map/ppermute | solution.py:41
  39.5 5.7 %collective-permute-start.13 = (f32[32,1536]{1,0:T(8,128)S(1)}, f32[32,1536]{1,0:T(8,128)S(1)}, u32[]{:S(2)}, u32[]{:S(2)}) collective-permute-start(f32[32,1536]{1,0:T(8,128)S(1)} %get-tuple-element.75), channel_id=1, source_target_pairs={{0,1},{1,0},{2,3},{3,2},{4,5},{5,4},{6,7},{7,6},{8,9},{9,8},{10,11... | collective-permute-start | bytes 589832 | tf_op jit(solution)/shard_map/ppermute | solution.py:41
  48.5 8.0 %collective-permute-start.16 = (f32[8,128]{1,0:T(8,128)S(1)}, f32[8,128]{1,0:T(8,128)S(1)}, u32[]{:S(2)}, u32[]{:S(2)}) collective-permute-start(f32[8,128]{1,0:T(8,128)S(1)} %get-tuple-element.78), channel_id=1, source_target_pairs={{0,12},{1,13},{2,14},{3,15},{4,8},{5,9},{6,10},{7,11},{8,4},{9,5},... | collective-permute-start | bytes 12296 | tf_op jit(solution)/shard_map/ppermute | solution.py:41
  50.4 6.1 %collective-permute-start.15 = (f32[8,128]{1,0:T(8,128)S(1)}, f32[8,128]{1,0:T(8,128)S(1)}, u32[]{:S(2)}, u32[]{:S(2)}) collective-permute-start(f32[8,128]{1,0:T(8,128)S(1)} %get-tuple-element.78), channel_id=1, source_target_pairs={{0,8},{1,9},{2,10},{3,11},{4,12},{5,13},{6,14},{7,15},{8,0},{9,1},... | collective-permute-start | bytes 12296 | tf_op jit(solution)/shard_map/ppermute | solution.py:41
  50.4 6.1 %collective-permute-start.14 = (f32[8,128]{1,0:T(8,128)S(1)}, f32[8,128]{1,0:T(8,128)S(1)}, u32[]{:S(2)}, u32[]{:S(2)}) collective-permute-start(f32[8,128]{1,0:T(8,128)S(1)} %get-tuple-element.78), channel_id=1, source_target_pairs={{0,4},{1,5},{2,6},{3,7},{4,0},{5,1},{6,2},{7,3},{8,12},{9,13},{10,... | collective-permute-start | bytes 12296 | tf_op jit(solution)/shard_map/ppermute | solution.py:41
  56.5 4.3 %collective-permute-start.19 = (f32[8,128]{1,0:T(8,128)S(1)}, f32[8,128]{1,0:T(8,128)S(1)}, u32[]{:S(2)}, u32[]{:S(2)}) collective-permute-start(f32[8,128]{1,0:T(8,128)S(1)} %add_add_fusion.1.refs_0_), channel_id=1, source_target_pairs={{0,3},{1,2},{2,1},{3,0},{4,7},{5,6},{6,5},{7,4},{8,11},{9,10},{10,... | collective-permute-start | bytes 12296 | tf_op jit(solution)/shard_map/ppermute | solution.py:41
  56.7 4.2 %collective-permute-start.18 = (f32[8,128]{1,0:T(8,128)S(1)}, f32[8,128]{1,0:T(8,128)S(1)}, u32[]{:S(2)}, u32[]{:S(2)}) collective-permute-start(f32[8,128]{1,0:T(8,128)S(1)} %add_add_fusion.1.refs_0_), channel_id=1, source_target_pairs={{0,2},{1,3},{2,0},{3,1},{4,6},{5,7},{6,4},{7,5},{8,10},{9,11},{10,... | collective-permute-start | bytes 12296 | tf_op jit(solution)/shard_map/ppermute | solution.py:41
  57.2 3.6 %collective-permute-start.17 = (f32[8,128]{1,0:T(8,128)S(1)}, f32[8,128]{1,0:T(8,128)S(1)}, u32[]{:S(2)}, u32[]{:S(2)}) collective-permute-start(f32[8,128]{1,0:T(8,128)S(1)} %add_add_fusion.1.refs_0_), channel_id=1, source_target_pairs={{0,1},{1,0},{2,3},{3,2},{4,5},{5,4},{6,7},{7,6},{8,9},{9,8},{10,11... | collective-permute-start | bytes 12296 | tf_op jit(solution)/shard_map/ppermute | solution.py:41
  58.5 11.4 %collective-permute-start.20 = (f32[32,1536]{1,0:T(8,128)S(1)}, f32[32,1536]{1,0:T(8,128)S(1)}, u32[]{:S(2)}, u32[]{:S(2)}) collective-permute-start(f32[32,1536]{1,0:T(8,128)S(1)} %get-tuple-element.89), channel_id=1, source_target_pairs={{0,8},{1,9},{2,10},{3,11},{4,12},{5,13},{6,14},{7,15},{8,0},{9,1},... | collective-permute-start | bytes 589832 | tf_op jit(solution)/shard_map/ppermute | solution.py:41
  58.8 11.0 %collective-permute-start.21 = (f32[32,1536]{1,0:T(8,128)S(1)}, f32[32,1536]{1,0:T(8,128)S(1)}, u32[]{:S(2)}, u32[]{:S(2)}) collective-permute-start(f32[32,1536]{1,0:T(8,128)S(1)} %get-tuple-element.90), channel_id=1, source_target_pairs={{0,4},{1,5},{2,6},{3,7},{4,0},{5,1},{6,2},{7,3},{8,12},{9,13},{10,... | collective-permute-start | bytes 589832 | tf_op jit(solution)/shard_map/ppermute | solution.py:41
  64.4 6.3 %collective-permute-start.22 = (f32[32,1536]{1,0:T(8,128)S(1)}, f32[32,1536]{1,0:T(8,128)S(1)}, u32[]{:S(2)}, u32[]{:S(2)}) collective-permute-start(f32[32,1536]{1,0:T(8,128)S(1)} %get-tuple-element.92), channel_id=1, source_target_pairs={{0,2},{1,3},{2,0},{3,1},{4,6},{5,7},{6,4},{7,5},{8,10},{9,11},{10,... | collective-permute-start | bytes 589832 | tf_op jit(solution)/shard_map/ppermute | solution.py:41
  65.7 5.0 %collective-permute-start.23 = (f32[32,1536]{1,0:T(8,128)S(1)}, f32[32,1536]{1,0:T(8,128)S(1)}, u32[]{:S(2)}, u32[]{:S(2)}) collective-permute-start(f32[32,1536]{1,0:T(8,128)S(1)} %get-tuple-element.93), channel_id=1, source_target_pairs={{0,1},{1,0},{2,3},{3,2},{4,5},{5,4},{6,7},{7,6},{8,9},{9,8},{10,11... | collective-permute-start | bytes 589832 | tf_op jit(solution)/shard_map/ppermute | solution.py:41
  73.7 5.4 %collective-permute-start.26 = (f32[8,128]{1,0:T(8,128)S(1)}, f32[8,128]{1,0:T(8,128)S(1)}, u32[]{:S(2)}, u32[]{:S(2)}) collective-permute-start(f32[8,128]{1,0:T(8,128)S(1)} %get-tuple-element.95), channel_id=1, source_target_pairs={{0,12},{1,13},{2,14},{3,15},{4,8},{5,9},{6,10},{7,11},{8,4},{9,5},... | collective-permute-start | bytes 12296 | tf_op jit(solution)/shard_map/ppermute | solution.py:41
  75.7 4.5 %collective-permute-start.25 = (f32[8,128]{1,0:T(8,128)S(1)}, f32[8,128]{1,0:T(8,128)S(1)}, u32[]{:S(2)}, u32[]{:S(2)}) collective-permute-start(f32[8,128]{1,0:T(8,128)S(1)} %get-tuple-element.95), channel_id=1, source_target_pairs={{0,8},{1,9},{2,10},{3,11},{4,12},{5,13},{6,14},{7,15},{8,0},{9,1},... | collective-permute-start | bytes 12296 | tf_op jit(solution)/shard_map/ppermute | solution.py:41
  75.7 4.5 %collective-permute-start.24 = (f32[8,128]{1,0:T(8,128)S(1)}, f32[8,128]{1,0:T(8,128)S(1)}, u32[]{:S(2)}, u32[]{:S(2)}) collective-permute-start(f32[8,128]{1,0:T(8,128)S(1)} %get-tuple-element.95), channel_id=1, source_target_pairs={{0,4},{1,5},{2,6},{3,7},{4,0},{5,1},{6,2},{7,3},{8,12},{9,13},{10,... | collective-permute-start | bytes 12296 | tf_op jit(solution)/shard_map/ppermute | solution.py:41
  80.2 3.1 %collective-permute-start.29 = (f32[8,128]{1,0:T(8,128)S(1)}, f32[8,128]{1,0:T(8,128)S(1)}, u32[]{:S(2)}, u32[]{:S(2)}) collective-permute-start(f32[8,128]{1,0:T(8,128)S(1)} %add_add_fusion.refs_0_), channel_id=1, source_target_pairs={{0,3},{1,2},{2,1},{3,0},{4,7},{5,6},{6,5},{7,4},{8,11},{9,10},{10,... | collective-permute-start | bytes 12296 | tf_op jit(solution)/shard_map/ppermute | solution.py:41
  80.3 3.7 %collective-permute-start.28 = (f32[8,128]{1,0:T(8,128)S(1)}, f32[8,128]{1,0:T(8,128)S(1)}, u32[]{:S(2)}, u32[]{:S(2)}) collective-permute-start(f32[8,128]{1,0:T(8,128)S(1)} %add_add_fusion.refs_0_), channel_id=1, source_target_pairs={{0,2},{1,3},{2,0},{3,1},{4,6},{5,7},{6,4},{7,5},{8,10},{9,11},{10,... | collective-permute-start | bytes 12296 | tf_op jit(solution)/shard_map/ppermute | solution.py:41
  81.2 2.8 %collective-permute-start.27 = (f32[8,128]{1,0:T(8,128)S(1)}, f32[8,128]{1,0:T(8,128)S(1)}, u32[]{:S(2)}, u32[]{:S(2)}) collective-permute-start(f32[8,128]{1,0:T(8,128)S(1)} %add_add_fusion.refs_0_), channel_id=1, source_target_pairs={{0,1},{1,0},{2,3},{3,2},{4,5},{5,4},{6,7},{7,6},{8,9},{9,8},{10,11... | collective-permute-start | bytes 12296 | tf_op jit(solution)/shard_map/ppermute | solution.py:41
